TPU v7x, 32 devices: a whole 2x2x4 slice. The times are simulated.
32 devices in a mesh: rep: 2 (over y), dp: 4 (over z), tensor: 4 (over x, core).
Axes of the slice: x: 2, y: 2, z: 4, core: 2. Of those that a mesh axis runs over, the one named last changes fastest.
Arguments:
- tokens: bfloat16 [3, 1536, 8192], P(None, ('rep', 'dp'), 'tensor'), parts along dimension 1, may hold values from -6 to 6
- query_weight: bfloat16 [8192, 4096], P(None, 'tensor'), may hold values from -0.0625 to 0.0625
- adapter_down_weight: bfloat16 [32, 8192, 64], P('dp', 'tensor'), may hold values from -0.0625 to 0.0625
- adapter_up_weight: bfloat16 [32, 64, 4096], P('dp', None, 'tensor'), may hold values from -0.75 to 0.75
- cached_key_rows: bfloat16 [1536, 4, 48, 128], P(('rep', 'dp'), None, 'tensor'), parts along dimension 0, may hold values from -110 to 110
- cached_value_rows: bfloat16 [1536, 4, 48, 128], P(('rep', 'dp'), None, 'tensor'), parts along dimension 0, may hold values from -6 to 6
- incoming_key_rows: bfloat16 [3, 1536, 4, 128], P(None, ('rep', 'dp')), parts along dimension 1, may hold values from -6 to 6
- incoming_value_rows: bfloat16 [3, 1536, 4, 128], P(None, ('rep', 'dp')), parts along dimension 1, may hold values from -6 to 6
- cached_length_rows: int32 [1536], P(('rep', 'dp')), parts along dimension 0, may hold values from 1 to 48, as said below
- row_adapter_index: int32 [1536], P(('rep', 'dp')), parts along dimension 0, may hold values from 0 to 31, as said below
Outputs:
- attended: bfloat16 [3, 1536, 4096], P(None, ('rep', 'dp'), 'tensor'), parts along dimension 1
There are 2 independent parts, one for each index of `rep`. A program takes and returns all parts, laid end to end along the dimension named above; an argument that names none is the same for every part. Nothing has to cross between parts.
Inputs may be any that keep to these rules, and one draw needn't show every extreme that they name: `cached_length_rows`: group g (rows g * 192 to (g + 1) * 192 - 1) has lengths up to 48 * (g + 1) * 192 // 768, reached by its first row. `row_adapter_index`: adapter a belongs to owner a // 8. Among the 192 rows of one group at most 96 name adapters of one owner, and in every group some owner is named exactly 96 times.
All inputs are finite; a program needn't handle non-finite values.
Results may differ from a plain program's by a relative error of at most 0.011.
Values may be sent and summed in bfloat16 or wider, within the bound.
No kernel may reach another device: no remote copies, remote signals or barrier semaphores. Data moves between devices by JAX's collectives and lax.ppermute only.
A program may use at most 384 MiB of HBM per device.

v0:
```python
import jax
import jax.numpy as jnp
from jax import lax
from jax.sharding import PartitionSpec as P

QUERY_HEADS_HALF = 32
KVH = 4


def body(
    tokens,
    query_weight,
    adapter_down_weight,
    adapter_up_weight,
    cached_key_rows,
    cached_value_rows,
    incoming_key_rows,
    incoming_value_rows,
    cached_length_rows,
    row_adapter_index,
):
    step_count = tokens.shape[0]
    row_count = tokens.shape[1]
    width_local = query_weight.shape[1]
    head_size = cached_key_rows.shape[3]
    flat_tokens = tokens.reshape(step_count * row_count, tokens.shape[2])
    base_query = jnp.dot(
        lax.all_gather(flat_tokens, "tensor", axis=1, tiled=True),
        query_weight,
        preferred_element_type=jnp.float32,
    )
    owner_count = lax.axis_size("dp")
    adapter_count = adapter_down_weight.shape[0]
    capacity = 2 * row_count // owner_count
    owner_of = row_adapter_index // adapter_count
    within = row_adapter_index % adapter_count
    member = (owner_of[:, None] == jnp.arange(owner_count)[None, :]).astype(jnp.int32)
    position = jnp.sum(jnp.cumsum(member, axis=0) * member, axis=1) - 1
    slot_index = owner_of * capacity + position
    placing = slot_index[:, None] == jnp.arange(owner_count * capacity)[None, :]
    place_matrix = placing.astype(jnp.bfloat16).reshape(row_count, owner_count, capacity)
    outgoing = jnp.einsum(
        "rok,srd->oskd", place_matrix, tokens, preferred_element_type=jnp.float32
    ).astype(jnp.bfloat16)
    slot_adapter = jnp.sum(placing.astype(jnp.int32) * (within[:, None] + 1), axis=0) - 1
    slot_adapter = jnp.broadcast_to(
        slot_adapter.reshape(owner_count, 1, capacity), (owner_count, step_count, capacity)
    )
    incoming = lax.all_to_all(outgoing, "dp", split_axis=0, concat_axis=0, tiled=True)
    incoming_ids = lax.all_to_all(slot_adapter, "dp", split_axis=0, concat_axis=0, tiled=True)
    sources = incoming.shape[0]
    slot_ids = jnp.maximum(incoming_ids[:, 0], 0).reshape(-1)
    slot_down = jnp.take(adapter_down_weight, slot_ids, axis=0).reshape(
        sources, capacity, adapter_down_weight.shape[1], adapter_down_weight.shape[2]
    )
    partial_rank = jnp.einsum(
        "oskd,okdr->oskr", incoming, slot_down, preferred_element_type=jnp.float32
    )
    summed_rank = lax.psum(partial_rank, "tensor").astype(jnp.bfloat16)
    slot_up = jnp.take(adapter_up_weight, slot_ids, axis=0).reshape(
        sources, capacity, adapter_up_weight.shape[1], adapter_up_weight.shape[2]
    )
    corrections = jnp.einsum(
        "oskr,okrc->oskc", summed_rank, slot_up, preferred_element_type=jnp.float32
    ).astype(jnp.bfloat16)
    returned = lax.all_to_all(corrections, "dp", split_axis=0, concat_axis=0, tiled=True)
    delta_rows = jnp.einsum(
        "rok,oskc->src", place_matrix, returned, preferred_element_type=jnp.float32
    ).astype(jnp.bfloat16)
    delta_rows = delta_rows.reshape(step_count * row_count, width_local)
    query_rows = (base_query + delta_rows.astype(jnp.float32)).astype(jnp.bfloat16)
    query_rows = query_rows.reshape(step_count, row_count, width_local)
    full_query = lax.all_gather(query_rows, "tensor", axis=2, tiled=True)
    group_size = QUERY_HEADS_HALF // KVH
    heads_local = width_local // head_size
    full_heads = full_query.reshape(step_count, row_count, KVH, group_size, head_size)
    score_scale = head_size ** (-0.5)
    block_size = cached_key_rows.shape[2]
    scores = (
        jnp.einsum(
            "srkgd,rkpd->srkgp", full_heads, cached_key_rows, preferred_element_type=jnp.float32
        )
        * score_scale
    )
    cache_position = lax.axis_index("tensor") * block_size + jnp.arange(block_size)
    visible = cache_position[None, :] < cached_length_rows[:, None]
    visible_wide = visible[None, :, None, None, :]
    block_max = jnp.max(jnp.where(visible_wide, scores, -jnp.inf), axis=-1)
    safe_max = jnp.where(block_max > -jnp.inf, block_max, 0.0)
    raised = jnp.where(visible_wide, jnp.exp(scores - safe_max[..., None]), 0.0)
    block_weights = raised.astype(jnp.bfloat16)
    block_numerator = jnp.einsum(
        "srkgp,rkpd->srkgd", block_weights, cached_value_rows, preferred_element_type=jnp.float32
    )
    block_numerator = block_numerator.reshape(step_count, row_count, QUERY_HEADS_HALF, head_size)
    block_total = jnp.sum(raised, axis=-1).reshape(step_count, row_count, QUERY_HEADS_HALF)
    block_max = block_max.reshape(step_count, row_count, QUERY_HEADS_HALF)
    numerator_in, total_in, max_in = (
        lax.all_to_all(block_numerator[None], "tensor", split_axis=3, concat_axis=0, tiled=True),
        lax.all_to_all(block_total[None], "tensor", split_axis=3, concat_axis=0, tiled=True),
        lax.all_to_all(block_max[None], "tensor", split_axis=3, concat_axis=0, tiled=True),
    )
    head_index = lax.axis_index("tensor") * heads_local + jnp.arange(heads_local)
    kv_index = head_index // group_size
    own_keys = jnp.take(incoming_key_rows, kv_index, axis=2)
    own_values = jnp.take(incoming_value_rows, kv_index, axis=2)
    own_query = query_rows.reshape(step_count, row_count, heads_local, head_size)
    fresh_scores = (
        jnp.einsum("srhd,trhd->srht", own_query, own_keys, preferred_element_type=jnp.float32)
        * score_scale
    )
    earlier = jnp.arange(step_count)[None, :] <= jnp.arange(step_count)[:, None]
    step_mask = earlier[:, None, None, :]
    fresh_max = jnp.max(jnp.where(step_mask, fresh_scores, -jnp.inf), axis=-1)
    fresh_raised = jnp.where(step_mask, jnp.exp(fresh_scores - fresh_max[..., None]), 0.0)
    fresh_weights = fresh_raised.astype(jnp.bfloat16)
    fresh_numerator = jnp.einsum(
        "srht,trhd->srhd", fresh_weights, own_values, preferred_element_type=jnp.float32
    )
    fresh_total = jnp.sum(fresh_raised, axis=-1)
    overall = jnp.maximum(jnp.max(max_in, axis=0), fresh_max)
    factor = jnp.exp(max_in - overall[None])
    fresh_factor = jnp.exp(fresh_max - overall)
    numerator = (
        jnp.sum(factor[..., None] * numerator_in, axis=0)
        + fresh_factor[..., None] * fresh_numerator
    )
    total_sum = jnp.sum(factor * total_in, axis=0) + fresh_factor * fresh_total
    attended = (numerator / total_sum[..., None]).astype(jnp.bfloat16)
    return attended.reshape(step_count, row_count, width_local)


def solution(mesh):
    in_specs = (
        P(None, ("rep", "dp"), "tensor"),
        P(None, "tensor"),
        P("dp", "tensor", None),
        P("dp", None, "tensor"),
        P(("rep", "dp"), None, "tensor", None),
        P(("rep", "dp"), None, "tensor", None),
        P(None, ("rep", "dp"), None, None),
        P(None, ("rep", "dp"), None, None),
        P(("rep", "dp")),
        P(("rep", "dp")),
    )
    out_specs = P(None, ("rep", "dp"), "tensor")
    return jax.shard_map(body, mesh=mesh, in_specs=in_specs, out_specs=out_specs, check_vma=False)
```

profile of v0, /device:TPU:0, one launch (start us, length us, event | category | flops | bytes accessed | tf_op | source)
XLA Modules:
  0.0 518.5 jit_solution(6532656597735696665)
XLA Ops:
  6.5 0.8 and_select_fusion.2
  7.4 1.2 reduce-window.6
  9.9 6.3 %all-to-all-start = ((s32[4,3,96]{2,1,0:T(4,128)}), s32[4,3,96]{2,1,0:T(4,128)S(1)}, u32[]{:S(2)}, u32[]{:S(2)}) async-start(s32[4,3,96]{2,1,0:T(4,128)} %broadcast_in_dim.94), calls=%async_computation | async-start | bytes 16384 | tf_op jit(solution)/shard_map/all_to_all | solution.py:50
  16.8 5.4 %convert_bitcast_fusion = bf16[4,3,96,2048]{3,2,1,0:T(8,128)(2,1)} fusion(bf16[3,192,2048]{2,1,0:T(8,128)(2,1)} %param.12, s32[4,96]{1,0:T(4,128)S(1)} %multiply_add_fusion.1, s32[192]{0:T(256)S(1)} %add_add_fusion), kind=kOutput, calls=%fused_computation.29 | convolution fusion | flops 908402688 | bytes 7080192 | tf_op jit(solution)/shard_map/rok,srd->oskd/dot_general | solution.py:42
  22.1 5.1 all-to-all-start.1
  27.2 0.7 all-gather.3.cloned.1.call-update
  28.1 37.5 %gather_fusion.1 = bf16[384,2048,64]{1,2,0:T(8,128)(2,1)} fusion(bf16[8,2048,64]{1,2,0:T(8,128)(2,1)} %param.14, s32[1024]{0:T(1024)S(1)} %pad_clamp_fusion.1), kind=kCustom, calls=%fused_computation.3 | custom fusion | bytes 201328128 | tf_op jit(solution)/shard_map/jit(_take)/gather | solution.py:53
  65.6 19.2 %gather_fusion = bf16[384,64,1024]{2,1,0:T(8,128)(2,1)} fusion(bf16[8,64,1024]{2,1,0:T(8,128)(2,1)S(1)} %copy-done.1, s32[1024]{0:T(1024)S(1)} %pad_clamp_fusion.1), kind=kCustom, calls=%fused_computation.2 | custom fusion | bytes 100664832 | tf_op jit(solution)/shard_map/jit(_take)/gather | solution.py:60
  84.8 46.7 %all-to-all-done.1 = bf16[4,3,96,2048]{3,2,1,0:T(8,128)(2,1)} async-done(((bf16[4,3,96,2048]{3,2,1,0:T(8,128)(2,1)}), bf16[4,3,96,2048]{3,2,1,0:T(8,128)(2,1)}, u32[]{:S(2)}, u32[]{:S(2)}) %all-to-all-start.1) | async-done | bytes 4718624 | tf_op jit(solution)/shard_map/all_to_all | solution.py:49
  131.6 36.9 %fusion.41 = f32[4,3,96,64]{3,1,2,0:T(4,128)S(1)} fusion(bf16[4,3,96,2048]{3,2,1,0:T(8,128)(2,1)} %all-to-all-done.1, bf16[4,96,2048,64]{2,3,1,0:T(8,128)(2,1)} %bitcast.4, pred[4,96]{1,0:T(4,128)(4,1)S(1)} %bitcast.149), kind=kOutput, calls=%fused_computation.50 | convolution fusion | flops 352321536 | bytes 105677184 | tf_op jit(solution)/shard_map/oskd,okdr->oskr/dot_general | solution.py:56
  168.5 19.3 %all-reduce.2 = bf16[4,3,96,64]{3,1,2,0:T(4,128)(2,1)S(1)} all-reduce(f32[4,3,96,64]{3,1,2,0:T(4,128)S(1)} %fusion.41), channel_id=1, replica_groups=mesh['rep'=2,'dp'=4,'tensor'=4] {'tensor'}, use_global_device_ids=true, to_apply=%region_4.5 | all-reduce | flops 73728 | bytes 442368 | tf_op jit(solution)/shard_map/psum | solution.py:59
  187.8 19.3 %convert_bitcast_fusion.1 = bf16[4,3,96,1024]{3,1,2,0:T(4,128)(2,1)} fusion(bf16[4,96,64,1024]{3,2,1,0:T(8,128)(2,1)} %bitcast.136, pred[4,96]{1,0:T(4,128)(4,1)S(1)} %bitcast.150, bf16[4,3,96,64]{3,1,2,0:T(4,128)(2,1)S(1)} %all-reduce.2), kind=kOutput, calls=%fused_computation.35 | convolution fusion | flops 177340416 | bytes 52838784 | tf_op jit(solution)/shard_map/oskr,okrc->oskc/dot_general | solution.py:63
  207.1 2.8 copy.152
  210.0 56.4 %all_to_all.69 = bf16[4,3,96,1024]{3,2,1,0:T(8,128)(2,1)S(1)} all-to-all(bf16[4,3,96,1024]{3,2,1,0:T(8,128)(2,1)S(1)} %copy.152), channel_id=1, replica_groups=mesh['rep'=2,'dp'=4,'tensor'=4] {'dp'}, dimensions={0} | all-to-all | bytes 4718592 | tf_op jit(solution)/shard_map/all_to_all | solution.py:66
  266.4 2.4 fusion.40
  268.8 17.4 %fusion.28 = bf16[576,1024]{1,0:T(8,128)(2,1)} fusion(f32[3,1024,192]{1,2,0:T(8,128)} %fusion.40, bf16[576,8192]{1,0:T(8,128)(2,1)} %all-gather.3.cloned.1.call-done, bf16[8192,1024]{1,0:T(8,128)(2,1)} %param.13), kind=kOutput, calls=%fused_computation.37 | convolution fusion | flops 9664856064 | bytes 29753344 | tf_op jit(solution)/shard_map/dot_general | solution.py:27
  286.4 36.6 %all-gather.5.cloned.1.call-done = bf16[3,192,4096]{2,1,0:T(8,128)(2,1)} async-done(((bf16[3,192,1024]{2,1,0:T(8,128)(2,1)}), bf16[3,192,4096]{2,1,0:T(8,128)(2,1)}) %all-gather.5.cloned.1.call-update) | async-done | bytes 4718608 | tf_op jit(solution)/shard_map/all_gather | solution.py:73
  323.0 6.2 %copy.194 = bf16[72,8,32,128]{3,2,1,0:T(8,128)(2,1)} copy(bf16[72,8,32,128]{3,1,2,0:T(8,128)(2,1)} %bitcast.140) | data formatting | bytes 9437184
  329.2 10.2 %fusion.9 = (f32[3,192,4,8]{3,0,2,1:T(4,128)}, f32[192,4,3,8,12]{4,3,2,1,0:T(8,128)}) fusion(pred[192,12]{1,0:T(8,128)(4,1)S(1)} %broadcast_compare_fusion, bf16[192,4,12,128,1]{3,1,2,0,4:T(4,128)(2,1)S(1)} %bitcast.143, bf16[3,192,4,8,128]{4,3,2,1,0:T(8,128)(2,1)} %bitcast.138), kind=kOutput, calls=%fused_computation.16 | convolution fusion | flops 57268224 | bytes 8038656 | tf_op jit(solution)/shard_map/srkgd,rkpd->srkgp/dot_general | solution.py:80
  339.4 1.6 copy.155
  341.0 3.0 compare_select_fusion
  344.0 0.7 copy.156
  344.8 3.3 all-to-all-start.3
  348.1 9.9 %fusion.12 = f32[3,192,4,8]{3,0,2,1:T(4,128)} fusion(f32[192,4,3,8,12]{4,3,2,1,0:T(8,128)} %get-tuple-element.17, f32[3,192,4,8]{3,0,2,1:T(4,128)} %compare_select_fusion, pred[192,12]{1,0:T(8,128)(4,1)S(1)} %broadcast_compare_fusion), kind=kLoop, calls=%fused_computation.20 | loop fusion | flops 866304 | bytes 1034496 | tf_op jit(solution)/shard_map/reduce_sum | solution.py:96
  358.0 1.6 copy.174
  359.6 0.8 copy.175
  360.3 4.3 all-to-all-start.5
  364.7 10.1 %fusion.23 = f32[3,192,4,8,128]{4,3,0,2,1:T(8,128)} fusion(f32[192,4,3,8,12]{4,3,2,1,0:T(8,128)} %get-tuple-element.17, f32[3,192,4,8]{3,0,2,1:T(4,128)} %compare_select_fusion, pred[192,12]{1,0:T(8,128)(4,1)S(1)} %broadcast_compare_fusion, bf16[192,4,12,128,1]{3,1,2,0,4:T(4,128)(2,1)S(1)} %bitcast.135), kind=kOutput, calls=%fused_computation.32 | convolution fusion | flops 57507840 | bytes 12757248 | tf_op jit(solution)/shard_map/srkgp,rkpd->srkgd/dot_general | solution.py:92
  374.8 5.1 copy.225
  379.9 9.1 %copy.166 = f32[1,3,192,32,128]{4,2,1,0,3:T(8,128)} copy(f32[1,3,192,32,128]{4,3,2,1,0:T(8,128)S(1)} %bitcast.137) | data formatting | bytes 18874368 | tf_op jit(solution)/shard_map/broadcast_in_dim;reshape | solution.py:99
  389.0 6.1 %all-to-all-start.4 = ((f32[1,3,192,32,128]{4,2,1,0,3:T(8,128)}), f32[1,3,192,32,128]{4,2,1,0,3:T(8,128)}, u32[]{:S(2)}, u32[]{:S(2)}) async-start(f32[1,3,192,32,128]{4,2,1,0,3:T(8,128)} %copy.166), calls=%async_computation.4 | async-start | bytes 18874368 | tf_op jit(solution)/shard_map/all_to_all | solution.py:99
  395.1 4.9 gather_fusion.2
  400.1 4.9 gather_fusion.3
  405.0 2.0 select_bitcast_fusion
  407.4 3.4 fusion.37
  410.8 3.8 copy.160
  414.7 1.0 fusion.57
  416.2 2.2 fusion.60
  418.4 4.5 copy.172
  422.9 4.9 fusion.35
  427.9 1.6 fusion.55
  429.5 0.9 copy.169
  430.3 0.9 copy.179
  431.2 1.3 copy.163
  432.5 66.9 %all-to-all-done.4 = f32[1,3,192,32,128]{4,2,1,0,3:T(8,128)} async-done(((f32[1,3,192,32,128]{4,2,1,0,3:T(8,128)}), f32[1,3,192,32,128]{4,2,1,0,3:T(8,128)}, u32[]{:S(2)}, u32[]{:S(2)}) %all-to-all-start.4) | async-done | bytes 9437216 | tf_op jit(solution)/shard_map/all_to_all | solution.py:99
  499.5 9.0 %fusion.8 = f32[3,192,8,128]{3,2,1,0:T(8,128)S(1)} fusion(f32[1,3,192,32,128]{4,2,1,0,3:T(8,128)} %all-to-all-done.4, f32[4,3,192,8]{3,0,2,1:T(4,128)S(1)} %copy.163), kind=kLoop, calls=%fused_computation.13 | loop fusion | flops 4128768 | bytes 11870208 | tf_op jit(solution)/shard_map/reduce_sum | solution.py:125
  508.6 1.6 fusion.31
  510.1 1.4 reshape.167
  (77 shorter events, 3.2 us)
Async XLA Ops:
  6.5 358.1 %copy-start = (bf16[192,4,12,128]{3,1,2,0:T(4,128)(2,1)S(1)}, bf16[192,4,12,128]{3,1,2,0:T(4,128)(2,1)}, u32[]{:S(2)}) copy-start(bf16[192,4,12,128]{3,1,2,0:T(4,128)(2,1)} %param.17) | copy-start | bytes 7077892
  9.1 13.0 %copy-start.16 = (s32[192]{0:T(256)}, s32[192]{0:T(256)S(1)}, u32[]{:S(2)}) copy-start(s32[192]{0:T(256)S(1)} %add_add_fusion) | copy-start | bytes 2308
  9.9 12.2 %all-to-all-start = ((s32[4,3,96]{2,1,0:T(4,128)}), s32[4,3,96]{2,1,0:T(4,128)S(1)}, u32[]{:S(2)}, u32[]{:S(2)}) async-start(s32[4,3,96]{2,1,0:T(4,128)} %broadcast_in_dim.94), calls=%async_computation | async-start | bytes 16384 | tf_op jit(solution)/shard_map/all_to_all | solution.py:50
  16.2 0.5 copy-start.14
  22.1 109.4 %all-to-all-start.1 = ((bf16[4,3,96,2048]{3,2,1,0:T(8,128)(2,1)}), bf16[4,3,96,2048]{3,2,1,0:T(8,128)(2,1)}, u32[]{:S(2)}, u32[]{:S(2)}) async-start(bf16[4,3,96,2048]{3,2,1,0:T(8,128)(2,1)} %convert_bitcast_fusion), calls=%async_computation.1 | async-start | bytes 9437184 | tf_op jit(solution)/shard_map/all_to_all | solution.py:49
  27.2 241.6 %all-gather.3.cloned.1.call-start = ((), (), s32[]{:S(2)}) async-start(), calls=%async_computation.6 | async-start | bytes 11796480 | tf_op jit(solution)/shard_map/all_gather | solution.py:28
  27.9 295.1 %all-gather.5.cloned.1.call-start = ((), (), s32[]{:S(2)}) async-start(), calls=%async_computation.7 | async-start | bytes 5898240 | tf_op jit(solution)/shard_map/all_gather | solution.py:73
  28.1 37.5 %copy-start.1 = (bf16[8,64,1024]{2,1,0:T(8,128)(2,1)S(1)}, bf16[8,64,1024]{2,1,0:T(8,128)(2,1)}, u32[]{:S(2)}) copy-start(bf16[8,64,1024]{2,1,0:T(8,128)(2,1)} %param.15) | copy-start | bytes 3145732
  210.0 56.5 %copy-start.15 = (s32[4,96]{1,0:T(4,128)S(1)}, s32[4,96]{1,0:T(4,128)}, u32[]{:S(2)}) copy-start(s32[4,96]{1,0:T(4,128)} %copy-done.14) | copy-start | bytes 4612
  210.0 56.5 %copy-start.17 = (s32[192]{0:T(256)S(1)}, s32[192]{0:T(256)}, u32[]{:S(2)}) copy-start(s32[192]{0:T(256)} %copy-done.16) | copy-start | bytes 2308
  268.8 17.5 %copy-start.18 = (s32[192]{0:T(256)S(1)}, s32[192]{0:T(256)}, u32[]{:S(2)}) copy-start(s32[192]{0:T(256)} %param.20) | copy-start | bytes 2308
  323.0 6.2 %copy-start.6 = (bf16[192,4,12,128]{3,1,2,0:T(4,128)(2,1)S(1)}, bf16[192,4,12,128]{3,1,2,0:T(4,128)(2,1)}, u32[]{:S(2)}) copy-start(bf16[192,4,12,128]{3,1,2,0:T(4,128)(2,1)} %param.16) | copy-start | bytes 7077892
  344.8 15.6 %all-to-all-start.3 = ((f32[1,3,192,32]{2,0,1,3:T(1,128)}), f32[1,3,192,32]{2,0,1,3:T(1,128)S(1)}, u32[]{:S(2)}, u32[]{:S(2)}) async-start(f32[1,3,192,32]{2,0,1,3:T(1,128)} %copy.156), calls=%async_computation.3 | async-start | bytes 196608 | tf_op jit(solution)/shard_map/all_to_all | solution.py:101
  360.3 14.5 %copy-start.9 = (f32[1,3,192,32]{2,0,1,3:T(1,128)}, f32[1,3,192,32]{2,0,1,3:T(1,128)S(1)}, u32[]{:S(2)}) copy-start(f32[1,3,192,32]{2,0,1,3:T(1,128)S(1)} %all-to-all-done.3) | copy-start | bytes 221188
  360.3 28.6 %all-to-all-start.5 = ((f32[1,3,192,32]{2,0,1,3:T(1,128)}), f32[1,3,192,32]{2,0,1,3:T(1,128)}, u32[]{:S(2)}, u32[]{:S(2)}) async-start(f32[1,3,192,32]{2,0,1,3:T(1,128)} %copy.175), calls=%async_computation.5 | async-start | bytes 196608 | tf_op jit(solution)/shard_map/all_to_all | solution.py:100
  389.0 6.1 %copy-start.2 = (bf16[3,192,4,128]{3,2,1,0:T(4,128)(2,1)S(1)}, bf16[3,192,4,128]{3,2,1,0:T(4,128)(2,1)}, u32[]{:S(2)}) copy-start(bf16[3,192,4,128]{3,2,1,0:T(4,128)(2,1)} %param.18) | copy-start | bytes 1769476
  389.0 110.5 %all-to-all-start.4 = ((f32[1,3,192,32,128]{4,2,1,0,3:T(8,128)}), f32[1,3,192,32,128]{4,2,1,0,3:T(8,128)}, u32[]{:S(2)}, u32[]{:S(2)}) async-start(f32[1,3,192,32,128]{4,2,1,0,3:T(8,128)} %copy.166), calls=%async_computation.4 | async-start | bytes 18874368 | tf_op jit(solution)/shard_map/all_to_all | solution.py:99
  395.1 5.0 copy-start.3
  405.0 2.0 copy-start.5
  415.6 0.6 copy-start.11
  422.9 4.9 copy-start.10
  422.9 4.9 copy-start.12
  422.9 6.5 %copy-start.13 = (f32[3,192,8]{1,2,0:T(8,128)S(1)}, f32[3,192,8]{1,2,0:T(8,128)}, u32[]{:S(2)}) copy-start(f32[3,192,8]{1,2,0:T(8,128)} %get-tuple-element.10) | copy-start | bytes 55300
  499.5 9.1 %copy-start.4 = (f32[192,8,128,3]{2,3,1,0:T(4,128)S(1)}, f32[192,8,128,3]{2,3,1,0:T(4,128)}, u32[]{:S(2)}) copy-start(f32[192,8,128,3]{2,3,1,0:T(4,128)} %fusion.35) | copy-start | bytes 7077892
  499.5 9.1 %copy-start.7 = (f32[3,192,8]{2,1,0:T(8,128)S(1)}, f32[3,192,8]{2,1,0:T(8,128)}, u32[]{:S(2)}) copy-start(f32[3,192,8]{2,1,0:T(8,128)} %copy.169) | copy-start | bytes 55300
  499.5 9.1 %copy-start.8 = (f32[3,192,8]{2,1,0:T(8,128)S(1)}, f32[3,192,8]{2,1,0:T(8,128)}, u32[]{:S(2)}) copy-start(f32[3,192,8]{2,1,0:T(8,128)} %copy.179) | copy-start | bytes 55300
Sparse Core Ops, SparseCore 0:
  29.6 65.6 all-gather.2
  286.4 36.6 all-gather.4
where the time goes:
time: 527 us; the launch traced here: 519 us
  waiting for transfers between devices  151 us (29%)
  local copies, waits for them, and re-layouts  110 us (21%)
  matrix products  110 us (21%)
  blocking collectives  75.7 us (14%)
  other arithmetic  32.7 us (6%)
  starting transfers between devices  25.2 us (5%)
  between operations  14 us (3%)
    all_to_all x1, waiting for transfers between devices, body(): lax.all_to_all(block_numerator[None], 'tensor', split_axis=3, concat_axis...  66.9 us
    all_to_all x1, blocking collectives, body(): lax.all_to_all(corrections, 'dp', split_axis=0, concat_axis=0, tiled=True)  56.4 us
    all_to_all x1, waiting for transfers between devices, body(): lax.all_to_all(outgoing, 'dp', split_axis=0, concat_axis=0, tiled=True)  46.7 us
    gather x1, local copies, waits for them, and re-layouts, body(): jnp.take(adapter_down_weight, slot_ids, axis=0)  37.5 us
    dot_general x1, matrix products, body(): jnp.einsum('oskd,okdr->oskr', incoming, slot_down, preferred_element_type...  36.9 us
    all_gather x1, waiting for transfers between devices, body(): full_query = lax.all_gather(query_rows, 'tensor', axis=2, tiled=True)  36.6 us
    dot_general x1, matrix products, body(): jnp.einsum('oskr,okrc->oskc', summed_rank, slot_up, preferred_element_typ...  19.3 us
    psum x1, blocking collectives, body(): summed_rank = lax.psum(partial_rank, 'tensor').astype(jnp.bfloat16)  19.3 us
  transfers between devices with their start and end apart: 7, of which 3 were waited for; matrix products, arithmetic and copies ran while one was open for 38% of the time, Pallas kernels for 0%

commit v1 on v0

--- a/solution.py
+++ b/solution.py
@@ -1,13 +1,18 @@
+import functools
+
 import jax
 import jax.numpy as jnp
 from jax import lax
+from jax.experimental import pallas as pl
+from jax.experimental.pallas import tpu as pltpu
 from jax.sharding import PartitionSpec as P
 
 QUERY_HEADS_HALF = 32
 KVH = 4
-
-
-def body(
+VMEM_LIMIT = 56 * 1024 * 1024
+
+
+def general_body(
     tokens,
     query_weight,
     adapter_down_weight,
@@ -130,6 +135,356 @@
     return attended.reshape(step_count, row_count, width_local)
 
 
+def swap(array, bit, count):
+    return lax.ppermute(array, "tensor", [(i, i ^ bit) for i in range(count)])
+
+
+def project_pair(tensor_ids, first, second, weight, earlier=None):
+    rows, depth = first.shape
+    columns = weight.shape[1]
+    chunk = 512
+    chunks = depth // chunk
+
+    def kernel(ids_ref, *refs):
+        first_ref, first_weight, second_ref, second_weight = refs[:4]
+        out_ref = refs[-1]
+        product = jnp.dot(
+            first_ref[...], first_weight[...], preferred_element_type=jnp.float32
+        ) + jnp.dot(second_ref[...], second_weight[...], preferred_element_type=jnp.float32)
+
+        @pl.when(pl.program_id(0) == 0)
+        def _():
+            out_ref[...] = product if earlier is None else product + refs[4][...]
+
+        @pl.when(pl.program_id(0) > 0)
+        def _():
+            out_ref[...] += product
+
+    whole = pl.BlockSpec((rows, columns), lambda k, ids: (0, 0))
+    in_specs = [
+        pl.BlockSpec((rows, chunk), lambda k, ids: (0, k)),
+        pl.BlockSpec((chunk, columns), lambda k, ids: (ids[0] * chunks + k, 0)),
+        pl.BlockSpec((rows, chunk), lambda k, ids: (0, k)),
+        pl.BlockSpec((chunk, columns), lambda k, ids: (ids[1] * chunks + k, 0)),
+    ]
+    operands = [first, weight, second, weight]
+    if earlier is not None:
+        in_specs.append(whole)
+        operands.append(earlier)
+    return pl.pallas_call(
+        kernel,
+        out_shape=jax.ShapeDtypeStruct((rows, columns), jnp.float32),
+        grid_spec=pltpu.PrefetchScalarGridSpec(
+            num_scalar_prefetch=1, grid=(chunks,), in_specs=in_specs, out_specs=whole
+        ),
+        compiler_params=pltpu.CompilerParams(vmem_limit_bytes=VMEM_LIMIT),
+        cost_estimate=pl.CostEstimate(
+            flops=4 * rows * depth * columns,
+            bytes_accessed=4 * depth * (rows + columns) + 4 * rows * columns,
+            transcendentals=0,
+        ),
+        name="project",
+    )(tensor_ids, *operands)
+
+
+def adapter_rank(tokens, row_adapters, gathered_down, owners, per_block):
+    rows, depth = tokens.shape
+    halves = gathered_down.shape[0]
+    rank = gathered_down.shape[3]
+    blocks = halves * owners
+    width = per_block * rank
+    down = gathered_down.reshape(blocks, width, depth)
+
+    def kernel(tokens_ref, adapter_ref, down_ref, out_ref, acc_ref):
+        block = pl.program_id(0)
+        half, owner = block // owners, block % owners
+        product = lax.dot_general(
+            tokens_ref[...],
+            down_ref[0],
+            (((1,), (1,)), ((), ())),
+            preferred_element_type=jnp.float32,
+        )
+        start = owner * (halves * per_block) + half * per_block
+        column = lax.broadcasted_iota(jnp.int32, (rows, width), 1) // rank + start
+        kept = jnp.where(column == adapter_ref[...], product, 0.0)
+
+        @pl.when(block == 0)
+        def _():
+            acc_ref[...] = kept
+
+        @pl.when(block > 0)
+        def _():
+            acc_ref[...] += kept
+
+        @pl.when(block == blocks - 1)
+        def _():
+            total = acc_ref[:, :128]
+            for i in range(1, width // 128):
+                total = total + acc_ref[:, i * 128 : (i + 1) * 128]
+            out_ref[...] = total[:, :rank] + total[:, rank:]
+
+    return pl.pallas_call(
+        kernel,
+        out_shape=jax.ShapeDtypeStruct((rows, rank), jnp.float32),
+        grid=(blocks,),
+        in_specs=[
+            pl.BlockSpec((rows, depth), lambda b: (0, 0)),
+            pl.BlockSpec((rows, 1), lambda b: (0, 0)),
+            pl.BlockSpec((1, width, depth), lambda b: (b, 0, 0)),
+        ],
+        out_specs=pl.BlockSpec((rows, rank), lambda b: (0, 0)),
+        scratch_shapes=[pltpu.VMEM((rows, width), jnp.float32)],
+        compiler_params=pltpu.CompilerParams(vmem_limit_bytes=VMEM_LIMIT),
+        cost_estimate=pl.CostEstimate(
+            flops=2 * rows * depth * width * blocks,
+            bytes_accessed=2 * depth * (rows + width * blocks),
+            transcendentals=0,
+        ),
+        name="rank",
+    )(tokens, row_adapters, down)
+
+
+def finish_query(base, ranks, row_adapters, gathered_up, owners, per_block):
+    rows, columns = base.shape
+    halves = gathered_up.shape[0]
+    rank = gathered_up.shape[3]
+    blocks = halves * owners
+    width = per_block * rank
+    up = gathered_up.reshape(blocks, width, columns)
+
+    def kernel(base_ref, rank_ref, adapter_ref, up_ref, out_ref, acc_ref):
+        block = pl.program_id(0)
+        half, owner = block // owners, block % owners
+        start = owner * (halves * per_block) + half * per_block
+        column = lax.broadcasted_iota(jnp.int32, (rows, width), 1) // rank + start
+        own = rank_ref[...]
+        wide = jnp.concatenate([own] * per_block, axis=1)
+        kept = jnp.where(column == adapter_ref[...], wide, 0.0).astype(jnp.bfloat16)
+        product = jnp.dot(kept, up_ref[0], preferred_element_type=jnp.float32)
+
+        @pl.when(block == 0)
+        def _():
+            acc_ref[...] = product
+
+        @pl.when(block > 0)
+        def _():
+            acc_ref[...] += product
+
+        @pl.when(block == blocks - 1)
+        def _():
+            delta = acc_ref[...].astype(jnp.bfloat16).astype(jnp.float32)
+            out_ref[...] = (base_ref[...] + delta).astype(jnp.bfloat16)
+
+    return pl.pallas_call(
+        kernel,
+        out_shape=jax.ShapeDtypeStruct((rows, columns), jnp.bfloat16),
+        grid=(blocks,),
+        in_specs=[
+            pl.BlockSpec((rows, columns), lambda b: (0, 0)),
+            pl.BlockSpec((rows, rank), lambda b: (0, 0)),
+            pl.BlockSpec((rows, 1), lambda b: (0, 0)),
+            pl.BlockSpec((1, width, columns), lambda b: (b, 0, 0)),
+        ],
+        out_specs=pl.BlockSpec((rows, columns), lambda b: (0, 0)),
+        scratch_shapes=[pltpu.VMEM((rows, columns), jnp.float32)],
+        compiler_params=pltpu.CompilerParams(vmem_limit_bytes=VMEM_LIMIT),
+        cost_estimate=pl.CostEstimate(
+            flops=2 * rows * columns * width * blocks,
+            bytes_accessed=2 * columns * (3 * rows + width * blocks),
+            transcendentals=0,
+        ),
+        name="query",
+    )(base, ranks, row_adapters, up)
+
+
+def attend(block_ids, query, lengths, key_values, fresh_keys, fresh_values):
+    steps, rows, width = query.shape
+    head_size = fresh_keys.shape[2]
+    heads = width // head_size
+    blocks = len(key_values)
+    positions = key_values[0].shape[1] // rows
+    group = 8
+    bundle = 16
+    cached = blocks * group * positions
+    scale = head_size ** (-0.5)
+
+    def kernel(ids_ref, query_ref, length_ref, *refs):
+        key_refs = refs[:blocks]
+        fresh_key_ref, fresh_value_ref, out_ref = refs[blocks:]
+        column = lax.broadcasted_iota(jnp.int32, (group, group * positions), 1)
+        own_row = lax.broadcasted_iota(jnp.int32, (group, group * positions), 0)
+        on_row = column // positions == own_row
+        offset = column % positions
+        fresh_column = lax.broadcasted_iota(jnp.int32, (steps, group, steps * group), 2)
+        fresh_row = lax.broadcasted_iota(jnp.int32, (steps, group, steps * group), 1)
+        fresh_step = lax.broadcasted_iota(jnp.int32, (steps, group, steps * group), 0)
+        fresh_seen = (fresh_column % group == fresh_row) & (fresh_column // group <= fresh_step)
+        fresh_seen = jnp.broadcast_to(
+            fresh_seen[:, None], (steps, heads, group, steps * group)
+        ).reshape(steps * heads, group, steps * group)
+        query_all = query_ref[...].astype(jnp.float32)
+        fresh_key_all = fresh_key_ref[...].astype(jnp.float32)
+        fresh_value_all = fresh_value_ref[...].astype(jnp.float32)
+        outputs = []
+        for part in range(bundle // group):
+            here = slice(part * group, (part + 1) * group)
+            there = slice(part * group * positions, (part + 1) * group * positions)
+            queries = jnp.concatenate(
+                [
+                    query_all[s, here, h * head_size : (h + 1) * head_size]
+                    for s in range(steps)
+                    for h in range(heads)
+                ],
+                axis=0,
+            ).astype(jnp.bfloat16)
+            keys = jnp.concatenate([ref[0, there, :] for ref in key_refs], axis=0)
+            values = jnp.concatenate([ref[1, there, :] for ref in key_refs], axis=0)
+            new_keys = fresh_key_all[:, here].reshape(steps * group, head_size)
+            new_values = fresh_value_all[:, here].reshape(steps * group, head_size)
+            contract = (((1,), (1,)), ((), ()))
+            scores = lax.dot_general(
+                queries, keys, contract, preferred_element_type=jnp.float32
+            ).reshape(steps * heads, group, cached)
+            new_scores = lax.dot_general(
+                queries,
+                new_keys.astype(jnp.bfloat16),
+                contract,
+                preferred_element_type=jnp.float32,
+            ).reshape(steps * heads, group, steps * group)
+            seen = jnp.concatenate(
+                [
+                    (on_row & (offset + ids_ref[b] * positions < length_ref[here])).astype(
+                        jnp.float32
+                    )
+                    for b in range(blocks)
+                ],
+                axis=1,
+            )
+            scores = jnp.where(seen[None] > 0.0, scores * scale, -1e30)
+            new_scores = jnp.where(fresh_seen, new_scores * scale, -1e30)
+            top = jnp.maximum(
+                jnp.max(scores, axis=-1, keepdims=True), jnp.max(new_scores, axis=-1, keepdims=True)
+            )
+            raised = jnp.exp(scores - top)
+            new_raised = jnp.exp(new_scores - top)
+            total = jnp.sum(raised, axis=-1, keepdims=True) + jnp.sum(
+                new_raised, axis=-1, keepdims=True
+            )
+            numerator = jnp.dot(
+                raised.reshape(steps * heads * group, cached).astype(jnp.bfloat16),
+                values,
+                preferred_element_type=jnp.float32,
+            ) + jnp.dot(
+                new_raised.reshape(steps * heads * group, steps * group).astype(jnp.bfloat16),
+                new_values.astype(jnp.bfloat16),
+                preferred_element_type=jnp.float32,
+            )
+            outputs.append(numerator.reshape(steps * heads, group, head_size) / total)
+        for s in range(steps):
+            for h in range(heads):
+                out_ref[s, :, h * head_size : (h + 1) * head_size] = jnp.concatenate(
+                    [out[s * heads + h] for out in outputs], axis=0
+                ).astype(jnp.bfloat16)
+
+    key_spec = pl.BlockSpec((2, bundle * positions, head_size), lambda g, ids: (0, g, 0))
+    fresh_spec = pl.BlockSpec((steps, bundle, head_size), lambda g, ids: (0, g, 0))
+    wide_spec = pl.BlockSpec((steps, bundle, width), lambda g, ids: (0, g, 0))
+    return pl.pallas_call(
+        kernel,
+        out_shape=jax.ShapeDtypeStruct(query.shape, jnp.bfloat16),
+        grid_spec=pltpu.PrefetchScalarGridSpec(
+            num_scalar_prefetch=1,
+            grid=(rows // bundle,),
+            in_specs=[wide_spec, pl.BlockSpec((bundle, 1), lambda g, ids: (g, 0))]
+            + [key_spec] * blocks
+            + [fresh_spec] * 2,
+            out_specs=wide_spec,
+        ),
+        compiler_params=pltpu.CompilerParams(vmem_limit_bytes=VMEM_LIMIT),
+        cost_estimate=pl.CostEstimate(
+            flops=4 * steps * rows * width * group * (blocks * positions + steps),
+            bytes_accessed=4 * steps * rows * width + 4 * blocks * rows * positions * head_size,
+            transcendentals=steps * rows * heads * 512,
+        ),
+        name="attend",
+    )(block_ids, query, lengths, *key_values, fresh_keys, fresh_values)
+
+
+def body(
+    tokens,
+    query_weight,
+    adapter_down_weight,
+    adapter_up_weight,
+    cached_key_rows,
+    cached_value_rows,
+    incoming_key_rows,
+    incoming_value_rows,
+    cached_length_rows,
+    row_adapter_index,
+):
+    steps, rows, features = tokens.shape
+    width = query_weight.shape[1]
+    positions, head_size = cached_key_rows.shape[2:]
+    count = lax.axis_size("tensor")
+    owners = lax.axis_size("dp")
+    replicas = lax.axis_size("rep")
+    me = lax.axis_index("tensor")
+    ids = jnp.stack([me ^ j for j in range(count)]).astype(jnp.int32)
+    adapters = adapter_down_weight.shape[0]
+    per_block = adapters // replicas
+
+    start = lax.axis_index("rep") * per_block
+    own_down = lax.dynamic_slice_in_dim(
+        jnp.swapaxes(adapter_down_weight, 1, 2), start, per_block, axis=0
+    )
+    own_up = lax.dynamic_slice_in_dim(adapter_up_weight, start, per_block, axis=0)
+    all_down = lax.all_gather(own_down, ("rep", "dp"))
+    all_up = lax.all_gather(own_up, ("rep", "dp"))
+    all_down = all_down.reshape((replicas, owners) + own_down.shape)
+    all_up = all_up.reshape((replicas, owners) + own_up.shape)
+
+    near = swap(tokens, 1, count)
+    far = [swap(tokens[s], 2, count) for s in range(steps)]
+    far_near = [swap(part, 1, count) for part in far]
+    flat = (steps * rows, features)
+
+    key_heads = jnp.transpose(cached_key_rows, (1, 0, 2, 3)).reshape(KVH, rows * positions, head_size)
+    value_heads = jnp.transpose(cached_value_rows, (1, 0, 2, 3)).reshape(
+        KVH, rows * positions, head_size
+    )
+    both = jnp.stack([key_heads, value_heads], axis=1)
+    parcels = [lax.dynamic_index_in_dim(both, ids[j], 0, keepdims=False) for j in range(count)]
+    far_parcels = lax.optimization_barrier((parcels[2], parcels[3], far[steps - 1]))
+    key_values = [
+        parcels[0],
+        swap(parcels[1], 1, count),
+        swap(far_parcels[0], 2, count),
+        swap(far_parcels[1], 3, count),
+    ]
+
+    base = project_pair(ids[:2], tokens.reshape(flat), near.reshape(flat), query_weight)
+    base = project_pair(
+        ids[2:], jnp.stack(far).reshape(flat), jnp.stack(far_near).reshape(flat), query_weight, base
+    )
+
+    row_adapters = jnp.tile(row_adapter_index, steps).reshape(steps * rows, 1)
+    ranks = adapter_rank(tokens.reshape(flat), row_adapters, all_down, owners, per_block)
+    ranks = ranks + swap(ranks, 1, count)
+    ranks = ranks + swap(ranks, 2, count)
+    query = finish_query(base, ranks, row_adapters, all_up, owners, per_block)
+
+    fresh_keys = lax.dynamic_index_in_dim(incoming_key_rows, me, 2, keepdims=False)
+    fresh_values = lax.dynamic_index_in_dim(incoming_value_rows, me, 2, keepdims=False)
+    return attend(
+        ids,
+        query.reshape(steps, rows, width),
+        cached_length_rows.reshape(rows, 1),
+        key_values,
+        fresh_keys,
+        fresh_values,
+    )
+
+
 def solution(mesh):
     in_specs = (
         P(None, ("rep", "dp"), "tensor"),
@@ -144,4 +499,5 @@
         P(("rep", "dp")),
     )
     out_specs = P(None, ("rep", "dp"), "tensor")
-    return jax.shard_map(body, mesh=mesh, in_specs=in_specs, out_specs=out_specs, check_vma=False)
+    chosen = body if mesh.shape["tensor"] == KVH else general_body
+    return jax.shard_map(chosen, mesh=mesh, in_specs=in_specs, out_specs=out_specs, check_vma=False)

time: 527 us -> 243 us (0.46); the launches traced: 519 us -> 242 us
  matrix products: 110 us -> 0 us
  local copies, waits for them, and re-layouts: 110 us -> 19.3 us
  blocking collectives: 75.7 us -> 0 us
  Pallas kernels: 0 us -> 58.4 us
  other arithmetic: 32.7 us -> 9.46 us
  waiting for transfers between devices: 151 us -> 132 us
  starting transfers between devices: 25.2 us -> 8.85 us
    all_to_all x5 -> x0, waiting for transfers between devices: 114 us -> none  [the longest x1 66.9 us: body(): lax.all_to_all(block_numerator[None], 'tensor', split_axis=3, concat_axis...]
    dot_general x9 -> x0, matrix products: 110 us -> none  [the longest x1 36.9 us: body(): jnp.einsum('oskd,okdr->oskr', incoming, slot_down, preferred_element_type...]
    gather x4 -> x0, local copies, waits for them, and re-layouts: 66.6 us -> none  [the longest x1 37.5 us: body(): jnp.take(adapter_down_weight, slot_ids, axis=0)]
    pallas_call x0 -> x5, Pallas kernels: none -> 58.4 us  [the longest x2 22.9 us: project_pair(): pl.pallas_call(kernel, out_shape=jax.ShapeDtypeStruct((rows, columns), jn...]
    all_to_all x1 -> x0, blocking collectives: 56.4 us -> none  [body(): lax.all_to_all(corrections, 'dp', split_axis=0, concat_axis=0, tiled=True)]
    all_gather x2, waiting for transfers between devices: 36.6 us -> 86.6 us  [the longest x1 49.4 us: body(): all_down = lax.all_gather(own_down, ('rep', 'dp'))]
    ppermute x0 -> x12, waiting for transfers between devices: none -> 45.9 us  [swap(): return lax.ppermute(array, 'tensor', [(i, i ^ bit) for i in range(count)])]
    all_to_all x5 -> x0, starting transfers between devices: 25.2 us -> none  [the longest x1 6.32 us: body(): lax.all_to_all(slot_adapter, 'dp', split_axis=0, concat_axis=0, tiled=True)]
  transfers between devices with their start and end apart: 7 -> 14, of which waited for: 3 -> 5; matrix products, arithmetic and copies ran while one was open for 38% -> 10% of each run, Pallas kernels for 0% -> 18%
where the time goes in v1:
time: 243 us; the launch traced here: 242 us
  waiting for transfers between devices  132 us (54%)
  Pallas kernels  58.4 us (24%)
  local copies, waits for them, and re-layouts  19.3 us (8%)
  between operations  13.5 us (6%)
  other arithmetic  9.46 us (4%)
  starting transfers between devices  8.85 us (4%)
    all_gather x1, waiting for transfers between devices, body(): all_down = lax.all_gather(own_down, ('rep', 'dp'))  49.4 us
    ppermute x12, waiting for transfers between devices, swap(): return lax.ppermute(array, 'tensor', [(i, i ^ bit) for i in range(count)])  45.9 us
    all_gather x1, waiting for transfers between devices, body(): all_up = lax.all_gather(own_up, ('rep', 'dp'))  37.2 us
    pallas_call x2, Pallas kernels, project_pair(): pl.pallas_call(kernel, out_shape=jax.ShapeDtypeStruct((rows, columns), jn...  22.9 us
    pallas_call x1, Pallas kernels, attend(): pl.pallas_call(kernel, out_shape=jax.ShapeDtypeStruct(query.shape, jnp.bf...  14.1 us
    pallas_call x1, Pallas kernels, adapter_rank(): pl.pallas_call(kernel, out_shape=jax.ShapeDtypeStruct((rows, rank), jnp.f...  11.2 us
    pallas_call x1, Pallas kernels, finish_query(): pl.pallas_call(kernel, out_shape=jax.ShapeDtypeStruct((rows, columns), jn...  10.2 us
    ppermute x12, starting transfers between devices, swap(): return lax.ppermute(array, 'tensor', [(i, i ^ bit) for i in range(count)])  8.81 us
  transfers between devices with their start and end apart: 14, of which 5 were waited for; matrix products, arithmetic and copies ran while one was open for 10% of the time, Pallas kernels for 18%

profile of v1, /device:TPU:0, one launch (start us, length us, event | category | flops | bytes accessed | tf_op | source)
XLA Modules:
  0.0 242.0 jit_solution(2090390462862617857)
XLA Ops:
  6.5 1.6 copy-done
  8.1 1.1 dynamic-slice_bitcast_fusion.4
  9.2 0.0 all-gather.5.cloned.1.call-update
  9.2 0.0 all-gather.7.cloned.1.call-start
  9.3 0.8 constant_dynamic-slice_fusion.2
  10.1 0.0 all-gather.7.cloned.1.call-update
  10.2 0.9 copy-done.2
  11.1 0.5 collective-permute-start.6
  11.5 1.4 slice_bitcast_fusion.2
  12.9 2.5 %collective-permute-start.2 = (bf16[192,2048]{1,0:T(8,128)(2,1)}, bf16[192,2048]{1,0:T(8,128)(2,1)}, u32[]{:S(2)}, u32[]{:S(2)}) collective-permute-start(bf16[192,2048]{1,0:T(8,128)(2,1)} %get-tuple-element.14), channel_id=1, source_target_pairs={{0,2},{1,3},{2,0},{3,1},{4,6},{5,7},{6,4},{7,5},{8,10},{9,11},{10,... | collective-permute-start | bytes 2359304 | tf_op jit(solution)/shard_map/ppermute | solution.py:139
  15.4 0.0 collective-permute-start.1
  15.4 2.0 collective-permute-start
  17.4 1.7 copy_dynamic-update-slice_fusion.1
  19.1 0.9 copy-done.4
  20.0 1.8 copy_dynamic-update-slice_fusion
  21.8 12.3 %collective-permute-done.2 = bf16[192,2048]{1,0:T(8,128)(2,1)} collective-permute-done((bf16[192,2048]{1,0:T(8,128)(2,1)}, bf16[192,2048]{1,0:T(8,128)(2,1)}, u32[]{:S(2)}, u32[]{:S(2)}) %collective-permute-start.2) | collective-permute-done | bytes 786464 | tf_op jit(solution)/shard_map/ppermute | solution.py:139
  34.1 16.8 %collective-permute-done.1 = bf16[192,2048]{1,0:T(8,128)(2,1)} collective-permute-done((bf16[192,2048]{1,0:T(8,128)(2,1)}, bf16[192,2048]{1,0:T(8,128)(2,1)}, u32[]{:S(2)}, u32[]{:S(2)}) %collective-permute-start.1) | collective-permute-done | bytes 786464 | tf_op jit(solution)/shard_map/ppermute | solution.py:139
  51.0 0.0 collective-permute-start.4
  51.0 16.7 %collective-permute-done = bf16[192,2048]{1,0:T(8,128)(2,1)} collective-permute-done((bf16[192,2048]{1,0:T(8,128)(2,1)S(1)}, bf16[192,2048]{1,0:T(8,128)(2,1)}, u32[]{:S(2)}, u32[]{:S(2)}) %collective-permute-start) | collective-permute-done | bytes 786464 | tf_op jit(solution)/shard_map/ppermute | solution.py:139
  67.6 4.2 %dynamic-slice_bitcast_fusion = (bf16[2,2304,128]{2,1,0:T(8,128)(2,1)S(1)}, bf16[2,2304,128]{2,1,0:T(8,128)(2,1)}, bf16[2,2304,128]{2,1,0:T(8,128)(2,1)}, bf16[2,2304,128]{2,1,0:T(8,128)(2,1)}) fusion(bf16[4,2,2304,128]{3,2,1,0:T(8,128)(2,1)} %copy_dynamic-update-slice_fusion, s32[]{:T(128)S(6)} %select_n.24, s32[]{:T(128)S(6)} %select_n.23, ...), kind=kLoop, calls=%fused_computation.4 | loop fusion | bytes 9437200 | tf_op jit(solution)/shard_map/jit(dynamic_index_in_dim)/squeeze | solution.py:456
  71.9 0.5 collective-permute-start.9
  72.4 0.9 reshape_tile.4.adapter_ref
  73.3 0.8 copy.26.length_ref
  74.1 1.9 constant_dynamic-slice_fusion
  76.0 0.7 copy.34
  76.6 0.7 copy.33
  77.3 0.7 pad_add_fusion.1.ids_ref
  78.0 0.7 pad_add_fusion.ids_ref
  78.6 0.7 pad_add_fusion.2.ids_ref
  79.3 3.3 %pad_maximum_fusion = bf16[3,192,2048]{2,1,0:T(8,128)(2,1)} fusion(bf16[1,192,2048]{2,1,0:T(8,128)(2,1)} %bitcast.9, bf16[1,192,2048]{2,1,0:T(8,128)(2,1)} %bitcast.7, bf16[1,192,2048]{2,1,0:T(8,128)(2,1)} %bitcast.5), kind=kLoop, calls=%fused_computation | loop fusion | flops 2359296 | bytes 4718592 | tf_op jit(solution)/shard_map/stack | solution.py:467
  82.6 0.0 collective-permute-done.5
  82.6 1.7 collective-permute-start.10
  84.4 0.0 collective-permute-done.4
  84.4 0.0 collective-permute-start.11
  84.4 0.0 collective-permute-done.3
  84.4 3.4 %pad_maximum_fusion.1 = bf16[3,192,2048]{2,1,0:T(8,128)(2,1)} fusion(bf16[1,192,2048]{2,1,0:T(8,128)(2,1)} %bitcast.13, bf16[1,192,2048]{2,1,0:T(8,128)(2,1)} %bitcast.12, bf16[1,192,2048]{2,1,0:T(8,128)(2,1)} %bitcast.11), kind=kLoop, calls=%fused_computation.1 | loop fusion | flops 2359296 | bytes 4718592 | tf_op jit(solution)/shard_map/stack | solution.py:467
  87.8 49.4 %all-gather.5.cloned.1.call-done = bf16[32,64,2048]{2,1,0:T(8,128)(2,1)} async-done(((bf16[4,64,2048]{2,1,0:T(8,128)(2,1)}), bf16[32,64,2048]{2,1,0:T(8,128)(2,1)}) %all-gather.5.cloned.1.call-update) | async-done | bytes 8388624 | tf_op jit(solution)/shard_map/all_gather | solution.py:441
  137.1 11.2 %rank.1 = f32[576,64]{1,0:T(8,128)} custom-call(bf16[576,2048]{1,0:T(8,128)(2,1)} %bitcast.48, s32[576,1]{1,0:T(8,128)} %reshape_tile.4.adapter_ref, bf16[8,256,2048]{2,1,0:T(8,128)(2,1)} %bitcast.56), custom_call_target="tpu_custom_call" | custom-call | flops 4831838208 | bytes 10747904 | tf_op jit(solution)/shard_map/rank/pallas_call | solution.py:226
  148.3 0.0 collective-permute-start.7
  148.3 0.0 collective-permute-done.6
  148.3 11.0 %project.2.refs_4_ = f32[576,1024]{1,0:T(8,128)} custom-call(s32[2]{0:T(128)} %pad_add_fusion.2.ids_ref, bf16[576,2048]{1,0:T(8,128)(2,1)} %bitcast.49, bf16[8192,1024]{1,0:T(8,128)(2,1)} %refs_3_.3, bf16[576,2048]{1,0:T(8,128)(2,1)} %bitcast.16.refs_2_, bf16[8192,1024]{1,0:T(8,128)(2,1)} %refs_3_.3), custom_call_target="tpu_custom_call" | custom-call | flops 4831838208 | bytes 15466496 | tf_op jit(solution)/shard_map/project/pallas_call | solution.py:174
  159.4 1.6 collective-permute-start.8
  160.9 12.0 %project.3.base_ref = f32[576,1024]{1,0:T(8,128)} custom-call(s32[2]{0:T(128)} %pad_add_fusion.1.ids_ref, bf16[576,2048]{1,0:T(8,128)(2,1)} %bitcast.46, bf16[8192,1024]{1,0:T(8,128)(2,1)} %refs_3_.3, bf16[576,2048]{1,0:T(8,128)(2,1)} %bitcast.47, bf16[8192,1024]{1,0:T(8,128)(2,1)} %refs_3_.3, f32[576,1024]{1,0:T(8,128)} %project.2.refs_4_), custom_call_target="tpu_custom_call" | custom-call | flops 4831838208 | bytes 15466496 | tf_op jit(solution)/shard_map/project/pallas_call | solution.py:174
  172.9 0.7 add.28.rank_ref
  173.7 37.2 %all-gather.7.cloned.1.call-done = bf16[32,64,1024]{2,1,0:T(8,128)(2,1)} async-done(((bf16[4,64,1024]{2,1,0:T(8,128)(2,1)}), bf16[32,64,1024]{2,1,0:T(8,128)(2,1)}) %all-gather.7.cloned.1.call-update) | async-done | bytes 4194320 | tf_op jit(solution)/shard_map/all_gather | solution.py:442
  210.8 10.2 %query.1 = bf16[576,1024]{1,0:T(8,128)(2,1)} custom-call(f32[576,1024]{1,0:T(8,128)} %project.3.base_ref, f32[576,64]{1,0:T(8,128)} %add.28.rank_ref, s32[576,1]{1,0:T(8,128)} %reshape_tile.4.adapter_ref, bf16[8,256,1024]{2,1,0:T(8,128)(2,1)} %bitcast.57), custom_call_target="tpu_custom_call" | custom-call | flops 2415919104 | bytes 7733248 | tf_op jit(solution)/shard_map/query/pallas_call | solution.py:278
  221.1 0.0 copy-start.1
  221.1 14.1 %attend.1 = bf16[3,192,1024]{2,1,0:T(8,128)(2,1)} custom-call(s32[4]{0:T(128)} %pad_add_fusion.ids_ref, bf16[3,192,1024]{2,1,0:T(8,128)(2,1)} %bitcast.52, s32[192,1]{1,0:T(8,128)} %copy.26.length_ref, bf16[2,2304,128]{2,1,0:T(8,128)(2,1)} %get-tuple-element.12.refs_0_, bf16[2,2304,128]{2,1,0:T(8,128)(2,1)} %collective-permute-done.9.refs_1_, ...), custom_call_target="tpu_custom_call" | custom-call | flops 962592768 | bytes 7077888 | tf_op jit(solution)/shard_map/attend/pallas_call | solution.py:392
  (24 shorter events, 0.1 us)
Async XLA Ops:
  6.5 1.6 copy-start
  6.5 2.7 %copy-start.6 = (bf16[8,64,1024]{2,1,0:T(8,128)(2,1)S(1)}, bf16[8,64,1024]{2,1,0:T(8,128)(2,1)}, u32[]{:S(2)}) copy-start(bf16[8,64,1024]{2,1,0:T(8,128)(2,1)} %param.13) | copy-start | bytes 3145732
  6.5 130.6 %all-gather.5.cloned.1.call-start = ((), (), s32[]{:S(2)}) async-start(), calls=%async_computation | async-start | bytes 9437184 | tf_op jit(solution)/shard_map/all_gather | solution.py:441
  9.2 1.9 copy-start.2
  9.2 201.6 %all-gather.7.cloned.1.call-start = ((), (), s32[]{:S(2)}) async-start(), calls=%async_computation.1 | async-start | bytes 4718592 | tf_op jit(solution)/shard_map/all_gather | solution.py:442
  11.1 6.4 %copy-start.3 = (bf16[192,4,12,128]{3,1,2,0:T(4,128)(2,1)S(1)}, bf16[192,4,12,128]{3,1,2,0:T(4,128)(2,1)}, u32[]{:S(2)}) copy-start(bf16[192,4,12,128]{3,1,2,0:T(4,128)(2,1)} %param.14) | copy-start | bytes 7077892
  11.1 137.3 %collective-permute-start.6 = (bf16[3,192,2048]{2,1,0:T(8,128)(2,1)S(1)}, bf16[3,192,2048]{2,1,0:T(8,128)(2,1)}, u32[]{:S(2)}, u32[]{:S(2)}) collective-permute-start(bf16[3,192,2048]{2,1,0:T(8,128)(2,1)S(1)} %copy-done.2), channel_id=1, source_target_pairs={{0,1},{1,0},{2,3},{3,2},{4,5},{5,4},{6,7},{7,6},{8,9},{9,8},{10,11... | collective-permute-start | bytes 7077896 | tf_op jit(solution)/shard_map/ppermute | solution.py:139
  12.9 21.2 %collective-permute-start.2 = (bf16[192,2048]{1,0:T(8,128)(2,1)}, bf16[192,2048]{1,0:T(8,128)(2,1)}, u32[]{:S(2)}, u32[]{:S(2)}) collective-permute-start(bf16[192,2048]{1,0:T(8,128)(2,1)} %get-tuple-element.14), channel_id=1, source_target_pairs={{0,2},{1,3},{2,0},{3,1},{4,6},{5,7},{6,4},{7,5},{8,10},{9,11},{10,... | collective-permute-start | bytes 2359304 | tf_op jit(solution)/shard_map/ppermute | solution.py:139
  15.4 35.6 %collective-permute-start.1 = (bf16[192,2048]{1,0:T(8,128)(2,1)}, bf16[192,2048]{1,0:T(8,128)(2,1)}, u32[]{:S(2)}, u32[]{:S(2)}) collective-permute-start(bf16[192,2048]{1,0:T(8,128)(2,1)} %get-tuple-element.15), channel_id=1, source_target_pairs={{0,2},{1,3},{2,0},{3,1},{4,6},{5,7},{6,4},{7,5},{8,10},{9,11},{10,... | collective-permute-start | bytes 2359304 | tf_op jit(solution)/shard_map/ppermute | solution.py:139
  15.4 52.2 %collective-permute-start = (bf16[192,2048]{1,0:T(8,128)(2,1)S(1)}, bf16[192,2048]{1,0:T(8,128)(2,1)}, u32[]{:S(2)}, u32[]{:S(2)}) collective-permute-start(bf16[192,2048]{1,0:T(8,128)(2,1)S(1)} %get-tuple-element.13), channel_id=1, source_target_pairs={{0,2},{1,3},{2,0},{3,1},{4,6},{5,7},{6,4},{7,5},{8,10},{9,11},{10,... | collective-permute-start | bytes 2359304 | tf_op jit(solution)/shard_map/ppermute | solution.py:139
  17.4 2.6 %copy-start.4 = (bf16[192,4,12,128]{3,1,2,0:T(4,128)(2,1)S(1)}, bf16[192,4,12,128]{3,1,2,0:T(4,128)(2,1)}, u32[]{:S(2)}) copy-start(bf16[192,4,12,128]{3,1,2,0:T(4,128)(2,1)} %param.15) | copy-start | bytes 7077892
  21.8 50.6 %copy-start.8 = (s32[192]{0:T(256)S(1)}, s32[192]{0:T(256)}, u32[]{:S(2)}) copy-start(s32[192]{0:T(256)} %param.19) | copy-start | bytes 2308
  21.8 51.6 %copy-start.7 = (s32[192]{0:T(256)S(1)}, s32[192]{0:T(256)}, u32[]{:S(2)}) copy-start(s32[192]{0:T(256)} %param.18) | copy-start | bytes 2308
  34.1 48.5 %collective-permute-start.5 = (bf16[192,2048]{1,0:T(8,128)(2,1)}, bf16[192,2048]{1,0:T(8,128)(2,1)}, u32[]{:S(2)}, u32[]{:S(2)}) collective-permute-start(bf16[192,2048]{1,0:T(8,128)(2,1)} %collective-permute-done.2), channel_id=1, source_target_pairs={{0,1},{1,0},{2,3},{3,2},{4,5},{5,4},{6,7},{7,6},{8,9},{9,8},{10,11... | collective-permute-start | bytes 2359304 | tf_op jit(solution)/shard_map/ppermute | solution.py:139
  51.0 33.4 %collective-permute-start.4 = (bf16[192,2048]{1,0:T(8,128)(2,1)}, bf16[192,2048]{1,0:T(8,128)(2,1)}, u32[]{:S(2)}, u32[]{:S(2)}) collective-permute-start(bf16[192,2048]{1,0:T(8,128)(2,1)} %collective-permute-done.1), channel_id=1, source_target_pairs={{0,1},{1,0},{2,3},{3,2},{4,5},{5,4},{6,7},{7,6},{8,9},{9,8},{10,11... | collective-permute-start | bytes 2359304 | tf_op jit(solution)/shard_map/ppermute | solution.py:139
  67.6 16.8 %collective-permute-start.3 = (bf16[192,2048]{1,0:T(8,128)(2,1)}, bf16[192,2048]{1,0:T(8,128)(2,1)}, u32[]{:S(2)}, u32[]{:S(2)}) collective-permute-start(bf16[192,2048]{1,0:T(8,128)(2,1)} %collective-permute-done), channel_id=1, source_target_pairs={{0,1},{1,0},{2,3},{3,2},{4,5},{5,4},{6,7},{7,6},{8,9},{9,8},{10,11... | collective-permute-start | bytes 2359304 | tf_op jit(solution)/shard_map/ppermute | solution.py:139
  71.9 149.2 %collective-permute-start.9 = (bf16[2,2304,128]{2,1,0:T(8,128)(2,1)}, bf16[2,2304,128]{2,1,0:T(8,128)(2,1)}, u32[]{:S(2)}, u32[]{:S(2)}) collective-permute-start(bf16[2,2304,128]{2,1,0:T(8,128)(2,1)} %get-tuple-element.11), channel_id=1, source_target_pairs={{0,1},{1,0},{2,3},{3,2},{4,5},{5,4},{6,7},{7,6},{8,9},{9,8},{10,11... | collective-permute-start | bytes 3538952 | tf_op jit(solution)/shard_map/ppermute | solution.py:139
  82.6 138.4 %collective-permute-start.10 = (bf16[2,2304,128]{2,1,0:T(8,128)(2,1)}, bf16[2,2304,128]{2,1,0:T(8,128)(2,1)}, u32[]{:S(2)}, u32[]{:S(2)}) collective-permute-start(bf16[2,2304,128]{2,1,0:T(8,128)(2,1)} %get-tuple-element.7), channel_id=1, source_target_pairs={{0,2},{1,3},{2,0},{3,1},{4,6},{5,7},{6,4},{7,5},{8,10},{9,11},{10,... | collective-permute-start | bytes 3538952 | tf_op jit(solution)/shard_map/ppermute | solution.py:139
  84.4 136.7 %collective-permute-start.11 = (bf16[2,2304,128]{2,1,0:T(8,128)(2,1)S(1)}, bf16[2,2304,128]{2,1,0:T(8,128)(2,1)}, u32[]{:S(2)}, u32[]{:S(2)}) collective-permute-start(bf16[2,2304,128]{2,1,0:T(8,128)(2,1)S(1)} %get-tuple-element.8), channel_id=1, source_target_pairs={{0,3},{1,2},{2,1},{3,0},{4,7},{5,6},{6,5},{7,4},{8,11},{9,10},{10,... | collective-permute-start | bytes 3538952 | tf_op jit(solution)/shard_map/ppermute | solution.py:139
  148.3 11.0 %collective-permute-start.7 = (f32[576,64]{1,0:T(8,128)}, f32[576,64]{1,0:T(8,128)S(1)}, u32[]{:S(2)}, u32[]{:S(2)}) collective-permute-start(f32[576,64]{1,0:T(8,128)} %rank.1), channel_id=1, source_target_pairs={{0,1},{1,0},{2,3},{3,2},{4,5},{5,4},{6,7},{7,6},{8,9},{9,8},{10,11... | collective-permute-start | bytes 442376 | tf_op jit(solution)/shard_map/ppermute | solution.py:139
  148.3 11.0 %copy-start.5 = (f32[576,64]{1,0:T(8,128)S(1)}, f32[576,64]{1,0:T(8,128)}, u32[]{:S(2)}) copy-start(f32[576,64]{1,0:T(8,128)} %rank.1) | copy-start | bytes 442372
  159.4 13.6 %collective-permute-start.8 = (f32[576,64]{1,0:T(8,128)S(1)}, f32[576,64]{1,0:T(8,128)S(1)}, u32[]{:S(2)}, u32[]{:S(2)}) collective-permute-start(f32[576,64]{1,0:T(8,128)S(1)} %add.27), channel_id=1, source_target_pairs={{0,2},{1,3},{2,0},{3,1},{4,6},{5,7},{6,4},{7,5},{8,10},{9,11},{10,... | collective-permute-start | bytes 442376 | tf_op jit(solution)/shard_map/ppermute | solution.py:139
  221.1 14.1 %copy-start.1 = (bf16[8,2048,64]{1,2,0:T(8,128)(2,1)S(1)}, bf16[8,2048,64]{1,2,0:T(8,128)(2,1)}, u32[]{:S(2)}) copy-start(bf16[8,2048,64]{1,2,0:T(8,128)(2,1)} %param.12) | copy-start | bytes 6291460
Sparse Core Ops, SparseCore 0:
  9.5 127.6 all-gather.4
  139.2 71.5 all-gather.6

commit v2 on v0

v2 whole, which is shorter than its diff:
```python
import jax
import jax.numpy as jnp
from jax import lax
from jax.experimental import pallas as pl
from jax.experimental.pallas import tpu as pltpu
from jax.sharding import PartitionSpec as P

KVH = 4
VMEM_LIMIT = 56 * 1024 * 1024


def swap(array, bit, count):
    return lax.ppermute(array, "tensor", [(i, i ^ bit) for i in range(count)])


def project_pair(tensor_ids, first, second, weight, earlier=None):
    depth = first[0].shape[1]
    rows = sum(part.shape[0] for part in first)
    columns = weight.shape[1]
    chunk = 512
    chunks = depth // chunk
    parts = len(first)

    def kernel(ids_ref, *refs):
        first_weight, second_weight = refs[2 * parts : 2 * parts + 2]
        out_ref = refs[-1]
        left = jnp.concatenate([ref[...] for ref in refs[:parts]], axis=0)
        right = jnp.concatenate([ref[...] for ref in refs[parts : 2 * parts]], axis=0)
        product = jnp.dot(
            left, first_weight[...], preferred_element_type=jnp.float32
        ) + jnp.dot(right, second_weight[...], preferred_element_type=jnp.float32)

        @pl.when(pl.program_id(0) == 0)
        def _():
            out_ref[...] = product if earlier is None else product + refs[2 * parts + 2][...]

        @pl.when(pl.program_id(0) > 0)
        def _():
            out_ref[...] += product

    whole = pl.BlockSpec((rows, columns), lambda k, ids: (0, 0))
    in_specs = [
        pl.BlockSpec((part.shape[0], chunk), lambda k, ids: (0, k)) for part in first + second
    ] + [
        pl.BlockSpec((chunk, columns), lambda k, ids: (ids[0] * chunks + k, 0)),
        pl.BlockSpec((chunk, columns), lambda k, ids: (ids[1] * chunks + k, 0)),
    ]
    operands = first + second + [weight, weight]
    if earlier is not None:
        in_specs.append(whole)
        operands.append(earlier)
    return pl.pallas_call(
        kernel,
        out_shape=jax.ShapeDtypeStruct((rows, columns), jnp.float32),
        grid_spec=pltpu.PrefetchScalarGridSpec(
            num_scalar_prefetch=1, grid=(chunks,), in_specs=in_specs, out_specs=whole
        ),
        compiler_params=pltpu.CompilerParams(vmem_limit_bytes=VMEM_LIMIT),
        cost_estimate=pl.CostEstimate(
            flops=4 * rows * depth * columns,
            bytes_accessed=4 * depth * (rows + columns) + 4 * rows * columns,
            transcendentals=0,
        ),
        name="project",
    )(tensor_ids, *operands)


def all_ranks(starts, tokens, row_adapters, groups, rank):
    rows, depth = tokens.shape
    width = sum(part.shape[0] for part in groups[0])
    sizes = [len(group) for group in groups]
    flat = [part for group in groups for part in group]

    def kernel(starts_ref, tokens_ref, adapter_ref, *refs):
        down_refs, out_ref = refs[:-1], refs[-1]
        lane = lax.broadcasted_iota(jnp.int32, (rows, width), 1) // rank
        total = jnp.zeros((rows, width), jnp.float32)
        used = 0
        for i, size in enumerate(sizes):
            down = jnp.concatenate([ref[...] for ref in down_refs[used : used + size]], axis=0)
            used += size
            product = lax.dot_general(
                tokens_ref[...],
                down,
                (((1,), (1,)), ((), ())),
                preferred_element_type=jnp.float32,
            )
            total = total + jnp.where(lane + starts_ref[i] == adapter_ref[...], product, 0.0)
        folded = total[:, :128]
        for i in range(1, width // 128):
            folded = folded + total[:, i * 128 : (i + 1) * 128]
        out_ref[...] = folded[:, :rank] + folded[:, rank:]

    operands = [tokens, row_adapters] + flat
    return pl.pallas_call(
        kernel,
        out_shape=jax.ShapeDtypeStruct((rows, rank), jnp.float32),
        grid_spec=pltpu.PrefetchScalarGridSpec(
            num_scalar_prefetch=1,
            grid=(1,),
            in_specs=[pl.BlockSpec(op.shape, lambda g, starts: (0, 0)) for op in operands],
            out_specs=pl.BlockSpec((rows, rank), lambda g, starts: (0, 0)),
        ),
        compiler_params=pltpu.CompilerParams(vmem_limit_bytes=VMEM_LIMIT),
        cost_estimate=pl.CostEstimate(
            flops=2 * rows * depth * width * len(groups),
            bytes_accessed=2 * depth * (rows + width * len(groups)),
            transcendentals=0,
        ),
        name="rank",
    )(starts, *operands)


def part_delta(starts_ref, ranks, held, up_refs, sizes):
    rows, rank = ranks.shape
    width = sum(ref.shape[0] for ref in up_refs[: sizes[0]])
    lane = lax.broadcasted_iota(jnp.int32, (rows, width), 1) // rank
    wide = jnp.concatenate([ranks] * (width // rank), axis=1)
    kept = [
        jnp.where(lane + starts_ref[i] == held, wide, 0.0).astype(jnp.bfloat16)
        for i in range(len(sizes))
    ]
    return jnp.dot(
        jnp.concatenate(kept, axis=1),
        jnp.concatenate([ref[...] for ref in up_refs], axis=0),
        preferred_element_type=jnp.float32,
    )


def early_delta(starts, ranks, row_adapters, groups):
    rows = ranks.shape[0]
    columns = groups[0][0].shape[1]
    sizes = [len(group) for group in groups]
    flat = [part for group in groups for part in group]
    depth = sum(part.shape[0] for part in flat)

    def kernel(starts_ref, rank_ref, adapter_ref, *refs):
        refs[-1][...] = part_delta(starts_ref, rank_ref[...], adapter_ref[...], refs[:-1], sizes)

    operands = [ranks, row_adapters] + flat
    return pl.pallas_call(
        kernel,
        out_shape=jax.ShapeDtypeStruct((rows, columns), jnp.float32),
        grid_spec=pltpu.PrefetchScalarGridSpec(
            num_scalar_prefetch=1,
            grid=(1,),
            in_specs=[pl.BlockSpec(op.shape, lambda g, starts: (0, 0)) for op in operands],
            out_specs=pl.BlockSpec((rows, columns), lambda g, starts: (0, 0)),
        ),
        compiler_params=pltpu.CompilerParams(vmem_limit_bytes=VMEM_LIMIT),
        cost_estimate=pl.CostEstimate(
            flops=2 * rows * columns * depth,
            bytes_accessed=4 * columns * rows + 2 * columns * depth,
            transcendentals=0,
        ),
        name="delta",
    )(starts, *operands)


def attend(
    scalars,
    base,
    delta,
    ranks,
    row_adapters,
    groups,
    lengths,
    key_values,
    fresh_keys,
    fresh_values,
):
    steps, rows, head_size = fresh_keys.shape
    width = base.shape[1]
    heads = width // head_size
    blocks = len(key_values)
    sizes = [len(group) for group in groups]
    ups = [part for group in groups for part in group]
    positions = key_values[0].shape[1] // rows
    bundle = 16
    group = 8 if 8 * positions % 16 == 0 else 16
    cached = blocks * group * positions
    fresh = steps * group
    columns = -(-(cached + fresh) // 128) * 128
    scale = head_size ** (-0.5)

    def kernel(scalars_ref, *refs):
        base_ref, delta_ref, rank_ref, adapter_ref = refs[:4]
        up_refs = refs[4 : 4 + len(ups)]
        length_ref = refs[4 + len(ups)]
        cache_refs = refs[5 + len(ups) : 5 + len(ups) + blocks]
        fresh_key_ref, fresh_value_ref, out_ref, query_ref = refs[5 + len(ups) + blocks :]
        step = pl.program_id(0)

        @pl.when(step == 0)
        def _():
            whole_delta = delta_ref[...] + part_delta(
                scalars_ref, rank_ref[...], adapter_ref[...], up_refs, sizes
            )
            query_ref[...] = base_ref[...] + whole_delta.astype(jnp.bfloat16).astype(jnp.float32)

        column = lax.broadcasted_iota(jnp.int32, (group, group * positions), 1)
        own_row = lax.broadcasted_iota(jnp.int32, (group, group * positions), 0)
        on_row = column // positions == own_row
        place = column % positions
        fresh_column = lax.broadcasted_iota(jnp.int32, (group, columns - cached), 1)
        fresh_row = lax.broadcasted_iota(jnp.int32, (group, columns - cached), 0)
        fresh_own = fresh_column % group == fresh_row
        fresh_key_all = fresh_key_ref[...].astype(jnp.float32)
        fresh_value_all = fresh_value_ref[...].astype(jnp.float32)
        padding = jnp.zeros((columns - cached - fresh, head_size), jnp.float32)
        ones = jnp.ones((columns, head_size), jnp.bfloat16)
        for part in range(bundle // group):
            here = slice(part * group, (part + 1) * group)
            there = slice(part * group * positions, (part + 1) * group * positions)
            queries = jnp.concatenate(
                [
                    query_ref[
                        pl.ds(
                            pl.multiple_of(s * rows + step * bundle + part * group, group), group
                        ),
                        h * head_size : (h + 1) * head_size,
                    ]
                    for s in range(steps)
                    for h in range(heads)
                ],
                axis=0,
            ).astype(jnp.bfloat16)
            new_keys = jnp.concatenate(
                [fresh_key_all[t, here] for t in range(steps)] + [padding], axis=0
            ).astype(jnp.bfloat16)
            new_values = jnp.concatenate(
                [fresh_value_all[t, here] for t in range(steps)] + [padding], axis=0
            ).astype(jnp.bfloat16)
            keys = jnp.concatenate(
                [ref[0, there, :] for ref in cache_refs] + [new_keys], axis=0
            )
            values = jnp.concatenate(
                [ref[1, there, :] for ref in cache_refs] + [new_values], axis=0
            )
            values = jnp.concatenate([values, ones], axis=1)
            scores = lax.dot_general(
                queries, keys, (((1,), (1,)), ((), ())), preferred_element_type=jnp.float32
            ).reshape(steps, heads, group, columns)
            cached_bias = [
                jnp.where(
                    on_row & (place + scalars_ref[len(sizes) + b] * positions < length_ref[here]),
                    0.0,
                    -1e30,
                )
                for b in range(blocks)
            ]
            raised = []
            for s in range(steps):
                bias = jnp.concatenate(
                    cached_bias
                    + [jnp.where(fresh_own & (fresh_column // group <= s), 0.0, -1e30)],
                    axis=1,
                )
                shifted = scores[s] * scale + bias[None]
                shifted = shifted - jnp.max(shifted, axis=-1, keepdims=True)
                raised.append(jnp.exp(shifted).reshape(heads * group, columns))
            sums = jnp.dot(
                jnp.concatenate(raised, axis=0).astype(jnp.bfloat16),
                values,
                preferred_element_type=jnp.float32,
            )
            result = sums[:, :head_size] / sums[:, head_size:]
            for s in range(steps):
                for h in range(heads):
                    start = (s * heads + h) * group
                    out_ref[s, here, h * head_size : (h + 1) * head_size] = result[
                        start : start + group
                    ].astype(jnp.bfloat16)

    def whole(array):
        return pl.BlockSpec(array.shape, lambda g, scalars: (0,) * array.ndim)

    cache_spec = pl.BlockSpec((2, bundle * positions, head_size), lambda g, scalars: (0, g, 0))
    fresh_spec = pl.BlockSpec((steps, bundle, head_size), lambda g, scalars: (0, g, 0))
    wide_spec = pl.BlockSpec((steps, bundle, width), lambda g, scalars: (0, g, 0))
    first = [base, delta, ranks, row_adapters, *ups]
    return pl.pallas_call(
        kernel,
        out_shape=jax.ShapeDtypeStruct((steps, rows, width), jnp.bfloat16),
        grid_spec=pltpu.PrefetchScalarGridSpec(
            num_scalar_prefetch=1,
            grid=(rows // bundle,),
            in_specs=[whole(op) for op in first]
            + [pl.BlockSpec((bundle, 1), lambda g, scalars: (g, 0))]
            + [cache_spec] * blocks
            + [fresh_spec] * 2,
            out_specs=wide_spec,
            scratch_shapes=[pltpu.VMEM((steps * rows, width), jnp.float32)],
        ),
        compiler_params=pltpu.CompilerParams(vmem_limit_bytes=VMEM_LIMIT),
        cost_estimate=pl.CostEstimate(
            flops=4 * steps * rows * width * group * (blocks * positions + steps),
            bytes_accessed=4 * steps * rows * width + 4 * blocks * rows * positions * head_size,
            transcendentals=steps * rows * heads * columns,
        ),
        name="attend",
    )(scalars, *first, lengths, *key_values, fresh_keys, fresh_values)


def ring_hop(array, step, owners):
    size = 2 * owners
    device = [place if place < owners else 3 * owners - 1 - place for place in range(size)]
    pairs = [(device[place], device[(place + step) % size]) for place in range(size)]
    return lax.ppermute(array, ("rep", "dp"), pairs)


def ring_gather(own, owners, gates):
    before, after = own, own
    rows = own.shape[0] // 2
    arrivals = []
    for k in range(1, owners + 1):
        if k in gates:
            before, after, _ = lax.optimization_barrier((before, after, gates[k]))
        if k == owners:
            before, after = before[:rows], after[rows:]
        before, after = ring_hop(before, 1, owners), ring_hop(after, -1, owners)
        arrivals.append((before, after))
    return arrivals


def body(
    tokens,
    query_weight,
    adapter_down_weight,
    adapter_up_weight,
    cached_key_rows,
    cached_value_rows,
    incoming_key_rows,
    incoming_value_rows,
    cached_length_rows,
    row_adapter_index,
):
    steps, rows, features = tokens.shape
    width = query_weight.shape[1]
    positions, head_size = cached_key_rows.shape[2:]
    count = lax.axis_size("tensor")
    owners = lax.axis_size("dp")
    me = lax.axis_index("tensor")
    owner = lax.axis_index("dp")
    replica = lax.axis_index("rep")
    adapters, _, rank = adapter_down_weight.shape
    half = adapters // 2
    flat_tokens = tokens.reshape(steps * rows, features)

    key_heads = jnp.transpose(cached_key_rows, (1, 0, 2, 3)).reshape(KVH, rows * positions, head_size)
    value_heads = jnp.transpose(cached_value_rows, (1, 0, 2, 3)).reshape(
        KVH, rows * positions, head_size
    )
    both = jnp.stack([key_heads, value_heads], axis=1)
    if count == 4:
        ids = jnp.stack([me ^ j for j in range(count)]).astype(jnp.int32)
        near = swap(flat_tokens, 1, count)
        far = swap(flat_tokens, 2, count)
        far_near = swap(far, 1, count)
        base = project_pair(ids[:2], [flat_tokens], [near], query_weight)
        base = project_pair(ids[2:], [far], [far_near], query_weight, base)
        parcels = lax.optimization_barrier(
            [lax.dynamic_index_in_dim(both, ids[j], 0, keepdims=False) for j in range(count)]
        )
        parcel, _ = lax.optimization_barrier((parcels[2], (near, far)))
        second = swap(parcel, 2, count)
        parcel, _ = lax.optimization_barrier((parcels[3], (second, far_near)))
        third = swap(parcel, 3, count)
        key_values = [parcels[0], swap(parcels[1], 1, count), second, third]
        gates = [{2: near, owners: far}, {}, {}]
    else:
        all_tokens = lax.all_gather(flat_tokens, "tensor", axis=1, tiled=True)
        base = jnp.dot(all_tokens, query_weight, preferred_element_type=jnp.float32)
        ids = jnp.arange(count, dtype=jnp.int32)
        key_values = lax.all_to_all(
            jnp.repeat(both, count // KVH, axis=0),
            "tensor",
            split_axis=0,
            concat_axis=0,
            tiled=True,
        )
        key_values = [key_values[b] for b in range(count)]
        gates = [{}, {}, {}]

    down_rows = jnp.swapaxes(adapter_down_weight, 1, 2).reshape(adapters * rank, features)
    up_rows = adapter_up_weight.reshape(adapters * rank, width)
    own_down = lax.dynamic_slice_in_dim(down_rows, replica * half * rank, half * rank, axis=0)
    own_up = lax.dynamic_slice_in_dim(up_rows, replica * half * rank, half * rank, axis=0)
    chunk = half * rank // 2
    down_chunks = [own_down[:chunk], own_down[chunk:]]
    down = [ring_gather(down_chunks[c], owners, gates[c]) for c in range(2)]
    own_up, _ = lax.optimization_barrier((own_up, down[0][owners - 2]))
    up = ring_gather(own_up, owners, gates[2])

    size = 2 * owners
    place = jnp.where(replica == 0, owner, size - 1 - owner)
    steps_round = [d for k in range(1, owners) for d in (-k, k)] + [owners]
    start = []
    for step in [0] + steps_round:
        other = lax.rem(place + step + size, size)
        start.append(
            jnp.where(other < owners, other * adapters, (size - 1 - other) * adapters + half)
        )
    starts = jnp.stack(start).astype(jnp.int32)

    row_adapters = jnp.tile(row_adapter_index, steps).reshape(steps * rows, 1)
    groups = [[own_down]]
    for k in range(owners - 1):
        groups += [[down[c][k][side] for c in range(2)] for side in range(2)]
    groups.append([down[c][owners - 1][side] for c in range(2) for side in range(2)])
    ranks = all_ranks(starts, flat_tokens, row_adapters, groups, rank)
    bit = 1
    while bit < count:
        ranks = ranks + swap(ranks, bit, count)
        bit *= 2
    groups = [[own_up]] + [[part] for pair in up[:-1] for part in pair] + [list(up[-1])]
    early = 2 * (owners - 2) + 1
    delta = early_delta(starts[:early], ranks, row_adapters, groups[:early])

    kv_head = me * KVH // count
    fresh_keys = lax.dynamic_index_in_dim(incoming_key_rows, kv_head, 2, keepdims=False)
    fresh_values = lax.dynamic_index_in_dim(incoming_value_rows, kv_head, 2, keepdims=False)
    return attend(
        jnp.concatenate([starts[early:], ids]),
        base,
        delta,
        ranks,
        row_adapters,
        groups[early:],
        cached_length_rows.reshape(rows, 1),
        key_values,
        fresh_keys,
        fresh_values,
    )


def solution(mesh):
    in_specs = (
        P(None, ("rep", "dp"), "tensor"),
        P(None, "tensor"),
        P("dp", "tensor", None),
        P("dp", None, "tensor"),
        P(("rep", "dp"), None, "tensor", None),
        P(("rep", "dp"), None, "tensor", None),
        P(None, ("rep", "dp"), None, None),
        P(None, ("rep", "dp"), None, None),
        P(("rep", "dp")),
        P(("rep", "dp")),
    )
    out_specs = P(None, ("rep", "dp"), "tensor")
    return jax.shard_map(body, mesh=mesh, in_specs=in_specs, out_specs=out_specs, check_vma=False)
```

time: 527 us -> 195 us (0.37); the launches traced: 519 us -> 194 us
  matrix products: 110 us -> 0 us
  local copies, waits for them, and re-layouts: 110 us -> 27.8 us
  waiting for transfers between devices: 151 us -> 74.3 us
  blocking collectives: 75.7 us -> 0 us
  Pallas kernels: 0 us -> 55.6 us
  other arithmetic: 32.7 us -> 2.93 us
  between operations: 14 us -> 0.41 us
  starting transfers between devices: 25.2 us -> 33.4 us
    all_to_all x5 -> x0, waiting for transfers between devices: 114 us -> none  [the longest x1 66.9 us: body(): lax.all_to_all(block_numerator[None], 'tensor', split_axis=3, concat_axis...]
    dot_general x9 -> x0, matrix products: 110 us -> none  [the longest x1 36.9 us: body(): jnp.einsum('oskd,okdr->oskr', incoming, slot_down, preferred_element_type...]
    ppermute x0 -> x32, waiting for transfers between devices: none -> 74.3 us  [the longest x24 53 us: ring_hop(): return lax.ppermute(array, ('rep', 'dp'), pairs)]
    gather x4 -> x0, local copies, waits for them, and re-layouts: 66.6 us -> none  [the longest x1 37.5 us: body(): jnp.take(adapter_down_weight, slot_ids, axis=0)]
    all_to_all x1 -> x0, blocking collectives: 56.4 us -> none  [body(): lax.all_to_all(corrections, 'dp', split_axis=0, concat_axis=0, tiled=True)]
    pallas_call x0 -> x5, Pallas kernels: none -> 55.6 us  [the longest x2 22.8 us: project_pair(): pl.pallas_call(kernel, out_shape=jax.ShapeDtypeStruct((rows, columns), jn...]
    all_gather x2 -> x0, waiting for transfers between devices: 36.6 us -> none  [the longest x1 36.6 us: body(): full_query = lax.all_gather(query_rows, 'tensor', axis=2, tiled=True)]
    ppermute x0 -> x32, starting transfers between devices: none -> 33.4 us  [the longest x24 27.8 us: ring_hop(): return lax.ppermute(array, ('rep', 'dp'), pairs)]
  transfers between devices with their start and end apart: 7 -> 32, of which waited for: 3 -> 12; matrix products, arithmetic and copies ran while one was open for 38% -> 15% of each run, Pallas kernels for 0% -> 20%
where the time goes in v2:
time: 195 us; the launch traced here: 194 us
  waiting for transfers between devices  74.3 us (38%)
  Pallas kernels  55.6 us (29%)
  starting transfers between devices  33.4 us (17%)
  local copies, waits for them, and re-layouts  27.8 us (14%)
  other arithmetic  2.93 us (2%)
    ppermute x24, waiting for transfers between devices, ring_hop(): return lax.ppermute(array, ('rep', 'dp'), pairs)  53 us
    ppermute x24, starting transfers between devices, ring_hop(): return lax.ppermute(array, ('rep', 'dp'), pairs)  27.8 us
    pallas_call x2, Pallas kernels, project_pair(): pl.pallas_call(kernel, out_shape=jax.ShapeDtypeStruct((rows, columns), jn...  22.8 us
    ppermute x8, waiting for transfers between devices, swap(): return lax.ppermute(array, 'tensor', [(i, i ^ bit) for i in range(count)])  21.3 us
    pallas_call x1, Pallas kernels, attend(): pl.pallas_call(kernel, out_shape=jax.ShapeDtypeStruct((steps, rows, width...  16.5 us
    pallas_call x1, Pallas kernels, all_ranks(): pl.pallas_call(kernel, out_shape=jax.ShapeDtypeStruct((rows, rank), jnp.f...  10.6 us
    unnamed x37, local copies, waits for them, and re-layouts  6.75 us
    pallas_call x1, Pallas kernels, early_delta(): pl.pallas_call(kernel, out_shape=jax.ShapeDtypeStruct((rows, columns), jn...  5.66 us
  transfers between devices with their start and end apart: 32, of which 12 were waited for; matrix products, arithmetic and copies ran while one was open for 15% of the time, Pallas kernels for 20%

profile of v2, /device:TPU:0, one launch (start us, length us, event | category | flops | bytes accessed | tf_op | source)
XLA Modules:
  0.0 194.4 jit_solution(3711742944578779738)
XLA Ops:
  0.5 2.6 %collective-permute-start = (bf16[576,2048]{1,0:T(8,128)(2,1)}, bf16[576,2048]{1,0:T(8,128)(2,1)S(1)}, u32[]{:S(2)}, u32[]{:S(2)}) collective-permute-start(bf16[576,2048]{1,0:T(8,128)(2,1)} %bitcast.42), channel_id=1, source_target_pairs={{0,2},{1,3},{2,0},{3,1},{4,6},{5,7},{6,4},{7,5},{8,10},{9,11},{10,... | collective-permute-start | bytes 7077896 | tf_op jit(solution)/shard_map/ppermute | solution.py:13
  3.0 1.3 constant_dynamic-slice_fusion
  4.3 1.6 collective-permute-start.3
  5.9 1.6 collective-permute-start.4
  7.9 11.2 %collective-permute-done.3.refs_1_ = bf16[128,2048]{1,0:T(8,128)(2,1)S(1)} collective-permute-done((bf16[128,2048]{1,0:T(8,128)(2,1)S(1)}, bf16[128,2048]{1,0:T(8,128)(2,1)S(1)}, u32[]{:S(2)}, u32[]{:S(2)}) %collective-permute-start.3) | collective-permute-done | bytes 524320 | tf_op jit(solution)/shard_map/ppermute | solution.py:309
  19.1 1.5 collective-permute-start.5
  20.7 8.9 %collective-permute-done.4.refs_2_ = bf16[128,2048]{1,0:T(8,128)(2,1)S(1)} collective-permute-done((bf16[128,2048]{1,0:T(8,128)(2,1)S(1)}, bf16[128,2048]{1,0:T(8,128)(2,1)S(1)}, u32[]{:S(2)}, u32[]{:S(2)}) %collective-permute-start.4) | collective-permute-done | bytes 524320 | tf_op jit(solution)/shard_map/ppermute | solution.py:309
  29.6 1.6 collective-permute-start.8
  32.3 1.6 collective-permute-start.7
  33.8 3.5 %copy_dynamic-update-slice_fusion.1 = bf16[4,2,2304,128]{3,2,1,0:T(8,128)(2,1)} fusion(bf16[4,1,2304,128]{3,0,2,1:T(4,128)(2,1)} %bitcast.39), kind=kLoop, calls=%fused_computation.1 | loop fusion | bytes 4718592
  37.4 7.1 %collective-permute-done.8.refs_6_ = bf16[128,2048]{1,0:T(8,128)(2,1)} collective-permute-done((bf16[128,2048]{1,0:T(8,128)(2,1)S(1)}, bf16[128,2048]{1,0:T(8,128)(2,1)}, u32[]{:S(2)}, u32[]{:S(2)}) %collective-permute-start.8) | collective-permute-done | bytes 524320 | tf_op jit(solution)/shard_map/ppermute | solution.py:309
  44.5 1.6 collective-permute-start.12
  46.6 1.5 collective-permute-start.9
  48.1 7.0 %collective-permute-done.refs_0_ = bf16[576,2048]{1,0:T(8,128)(2,1)S(1)} collective-permute-done((bf16[576,2048]{1,0:T(8,128)(2,1)}, bf16[576,2048]{1,0:T(8,128)(2,1)S(1)}, u32[]{:S(2)}, u32[]{:S(2)}) %collective-permute-start) | collective-permute-done | bytes 2359328 | tf_op jit(solution)/shard_map/ppermute | solution.py:13
  55.1 0.7 collective-permute-done.7.refs_5_
  55.8 1.6 collective-permute-start.11
  57.3 1.7 copy_dynamic-update-slice_fusion
  59.1 7.9 %collective-permute-done.12.refs_10_ = bf16[128,2048]{1,0:T(8,128)(2,1)} collective-permute-done((bf16[128,2048]{1,0:T(8,128)(2,1)}, bf16[128,2048]{1,0:T(8,128)(2,1)}, u32[]{:S(2)}, u32[]{:S(2)}) %collective-permute-start.12) | collective-permute-done | bytes 524320 | tf_op jit(solution)/shard_map/ppermute | solution.py:309
  67.0 1.0 slice.40
  68.0 1.6 collective-permute-start.17
  69.6 1.0 slice.41
  71.1 1.5 collective-permute-start.13
  72.6 4.6 %dynamic-slice_bitcast_fusion = (bf16[2,2304,128]{2,1,0:T(8,128)(2,1)}, bf16[2,2304,128]{2,1,0:T(8,128)(2,1)}, bf16[2,2304,128]{2,1,0:T(8,128)(2,1)}, bf16[2,2304,128]{2,1,0:T(8,128)(2,1)}) fusion(bf16[4,2,2304,128]{3,2,1,0:T(8,128)(2,1)} %copy_dynamic-update-slice_fusion, s32[]{:T(128)S(6)} %select_n.67, s32[]{:T(128)S(6)} %select_n.66, s32[]{:T(128)S(6)} %select_n.65, ...), kind=kLoop, calls=%fused_computation.2 | loop fusion | bytes 9437200 | tf_op jit(solution)/shard_map/jit(dynamic_index_in_dim)/squeeze | solution.py:363
  77.2 1.0 collective-permute-done.11.refs_9_
  78.5 8.2 %collective-permute-done.13.refs_11_ = bf16[128,2048]{1,0:T(8,128)(2,1)S(1)} collective-permute-done((bf16[128,2048]{1,0:T(8,128)(2,1)}, bf16[128,2048]{1,0:T(8,128)(2,1)S(1)}, u32[]{:S(2)}, u32[]{:S(2)}) %collective-permute-start.13) | collective-permute-done | bytes 524320 | tf_op jit(solution)/shard_map/ppermute | solution.py:309
  86.7 1.9 slice.34
  88.6 1.6 collective-permute-start.15
  90.1 0.8 constant_dynamic-slice_fusion.4.refs_0_
  91.0 1.6 collective-permute-start.21
  93.7 1.0 slice.35
  94.7 3.5 %collective-permute-done.15.refs_13_ = bf16[64,2048]{1,0:T(8,128)(2,1)} collective-permute-done((bf16[64,2048]{1,0:T(8,128)(2,1)}, bf16[64,2048]{1,0:T(8,128)(2,1)}, u32[]{:S(2)}, u32[]{:S(2)}) %collective-permute-start.15) | collective-permute-done | bytes 262176 | tf_op jit(solution)/shard_map/ppermute | solution.py:309
  98.6 1.9 constant_dynamic-slice_fusion.2
  100.5 1.0 reshape_tile.4.adapter_ref.refs_3_
  102.1 2.3 %constant_dynamic-slice_fusion.5.refs_0_ = bf16[256,2048]{1,0:T(8,128)(2,1)} fusion(bf16[512,2048]{1,0:T(8,128)(2,1)} %bitcast.46, s32[]{:T(128)S(6)} %select_n.63), kind=kLoop, calls=%fused_computation.13 | loop fusion | bytes 2097156 | tf_op jit(solution)/shard_map/dynamic_slice | solution.py:387
  104.4 3.9 %collective-permute-done.16.refs_14_ = bf16[64,2048]{1,0:T(8,128)(2,1)} collective-permute-done((bf16[64,2048]{1,0:T(8,128)(2,1)S(1)}, bf16[64,2048]{1,0:T(8,128)(2,1)}, u32[]{:S(2)}, u32[]{:S(2)}) %collective-permute-start.16) | collective-permute-done | bytes 262176 | tf_op jit(solution)/shard_map/ppermute | solution.py:309
  108.3 1.5 collective-permute-start.23
  110.3 10.6 %rank.1 = f32[576,64]{1,0:T(8,128)} custom-call(s32[8]{0:T(128)} %stack.64.starts_ref, bf16[576,2048]{1,0:T(8,128)(2,1)} %bitcast.43, s32[576,1]{1,0:T(8,128)} %reshape_tile.4.adapter_ref.refs_3_, bf16[256,2048]{1,0:T(8,128)(2,1)} %constant_dynamic-slice_fusion.5.refs_0_, bf16[128,2048]{1,0:T(8,128)(2,1)} %copy-done.12, bf16[128,2048]{1,0:T(8,128)(2,1)} %copy-done.13, ...), custom_call_target="tpu_custom_call" | custom-call | flops 4831838208 | bytes 10747904 | tf_op jit(solution)/shard_map/rank/pallas_call | solution.py:95
  124.3 0.8 copy.20.refs_8_
  126.2 1.0 add.115
  127.2 1.6 collective-permute-start.20
  128.8 1.5 collective-permute-start.25
  130.8 10.8 %project.2.refs_4_ = f32[576,1024]{1,0:T(8,128)} custom-call(s32[2]{0:T(128)} %pad_add_fusion.1.ids_ref, bf16[576,2048]{1,0:T(8,128)(2,1)} %bitcast.44, bf16[576,2048]{1,0:T(8,128)(2,1)} %collective-permute-done.2.refs_1_, bf16[8192,1024]{1,0:T(8,128)(2,1)} %refs_3_.3, bf16[8192,1024]{1,0:T(8,128)(2,1)} %refs_3_.3), custom_call_target="tpu_custom_call" | custom-call | flops 4831838208 | bytes 15466496 | tf_op jit(solution)/shard_map/project/pallas_call | solution.py:52
  141.6 14.3 %collective-permute-done.20 = f32[576,64]{1,0:T(8,128)S(1)} collective-permute-done((f32[576,64]{1,0:T(8,128)S(1)}, f32[576,64]{1,0:T(8,128)S(1)}, u32[]{:S(2)}, u32[]{:S(2)}) %collective-permute-start.20) | collective-permute-done | bytes 147488 | tf_op jit(solution)/shard_map/ppermute | solution.py:13
  155.9 0.7 add.116.rank_ref.refs_2_
  156.7 5.7 %delta.1.refs_1_ = f32[576,1024]{1,0:T(8,128)} custom-call(s32[5]{0:T(128)} %stack.63.starts_ref, f32[576,64]{1,0:T(8,128)} %add.116.rank_ref.refs_2_, s32[576,1]{1,0:T(8,128)} %reshape_tile.4.adapter_ref.refs_3_, bf16[256,1024]{1,0:T(8,128)(2,1)} %constant_dynamic-slice_fusion.4.refs_0_, bf16[256,1024]{1,0:T(8,128)(2,1)} %collective-permute-done.21.refs_1_, ...), custom_call_target="tpu_custom_call" | custom-call | flops 1509949440 | bytes 4980736 | tf_op jit(solution)/shard_map/delta/pallas_call | solution.py:141
  162.4 1.6 collective-permute-start.27
  164.5 12.0 %project.3.refs_0_ = f32[576,1024]{1,0:T(8,128)} custom-call(s32[2]{0:T(128)} %pad_add_fusion.ids_ref, bf16[576,2048]{1,0:T(8,128)(2,1)} %copy-done.2, bf16[576,2048]{1,0:T(8,128)(2,1)} %collective-permute-done.1.refs_1_, bf16[8192,1024]{1,0:T(8,128)(2,1)} %refs_3_.3, bf16[8192,1024]{1,0:T(8,128)(2,1)} %refs_3_.3, f32[576,1024]{1,0:T(8,128)} %project.2.refs_4_), custom_call_target="tpu_custom_call" | custom-call | flops 4831838208 | bytes 15466496 | tf_op jit(solution)/shard_map/project/pallas_call | solution.py:52
  177.8 16.5 %attend.1 = bf16[3,192,1024]{2,1,0:T(8,128)(2,1)} custom-call(s32[7]{0:T(128)} %concatenate.9.scalars_ref, f32[576,1024]{1,0:T(8,128)} %project.3.refs_0_, f32[576,1024]{1,0:T(8,128)} %delta.1.refs_1_, f32[576,64]{1,0:T(8,128)} %add.116.rank_ref.refs_2_, s32[576,1]{1,0:T(8,128)} %reshape_tile.4.adapter_ref.refs_3_, bf16[256,1024]{1,0:T(8,128)(2,1)} %copy-done.5, ...), custom_call_target="tpu_custom_call" | custom-call | flops 962592768 | bytes 7077888 | tf_op jit(solution)/shard_map/attend/pallas_call | solution.py:282
  (80 shorter events, 12.8 us)
Async XLA Ops:
  0.0 90.1 %copy-start = (bf16[8,64,1024]{2,1,0:T(8,128)(2,1)S(1)}, bf16[8,64,1024]{2,1,0:T(8,128)(2,1)}, u32[]{:S(2)}) copy-start(bf16[8,64,1024]{2,1,0:T(8,128)(2,1)} %param.13) | copy-start | bytes 3145732
  0.0 32.3 %collective-permute-start.2 = (bf16[576,2048]{1,0:T(8,128)(2,1)}, bf16[576,2048]{1,0:T(8,128)(2,1)}, u32[]{:S(2)}, u32[]{:S(2)}) collective-permute-start(bf16[576,2048]{1,0:T(8,128)(2,1)} %bitcast.41), channel_id=1, source_target_pairs={{0,1},{1,0},{2,3},{3,2},{4,5},{5,4},{6,7},{7,6},{8,9},{9,8},{10,11... | collective-permute-start | bytes 7077896 | tf_op jit(solution)/shard_map/ppermute | solution.py:13
  0.5 54.6 %collective-permute-start = (bf16[576,2048]{1,0:T(8,128)(2,1)}, bf16[576,2048]{1,0:T(8,128)(2,1)S(1)}, u32[]{:S(2)}, u32[]{:S(2)}) collective-permute-start(bf16[576,2048]{1,0:T(8,128)(2,1)} %bitcast.42), channel_id=1, source_target_pairs={{0,2},{1,3},{2,0},{3,1},{4,6},{5,7},{6,4},{7,5},{8,10},{9,11},{10,... | collective-permute-start | bytes 7077896 | tf_op jit(solution)/shard_map/ppermute | solution.py:13
  4.3 14.8 %collective-permute-start.3 = (bf16[128,2048]{1,0:T(8,128)(2,1)S(1)}, bf16[128,2048]{1,0:T(8,128)(2,1)S(1)}, u32[]{:S(2)}, u32[]{:S(2)}) collective-permute-start(bf16[128,2048]{1,0:T(8,128)(2,1)S(1)} %get-tuple-element.32), channel_id=1, source_target_pairs={{0,4},{4,8},{8,12},{12,28},{28,24},{24,20},{20,16},{16,0},{1,5},{5... | collective-permute-start | bytes 1572872 | tf_op jit(solution)/shard_map/ppermute | solution.py:309
  5.9 23.6 %collective-permute-start.4 = (bf16[128,2048]{1,0:T(8,128)(2,1)S(1)}, bf16[128,2048]{1,0:T(8,128)(2,1)S(1)}, u32[]{:S(2)}, u32[]{:S(2)}) collective-permute-start(bf16[128,2048]{1,0:T(8,128)(2,1)S(1)} %get-tuple-element.31), channel_id=1, source_target_pairs={{0,4},{4,8},{8,12},{12,28},{28,24},{24,20},{20,16},{16,0},{1,5},{5... | collective-permute-start | bytes 1572872 | tf_op jit(solution)/shard_map/ppermute | solution.py:309
  7.5 23.7 %collective-permute-start.6 = (bf16[128,2048]{1,0:T(8,128)(2,1)S(1)}, bf16[128,2048]{1,0:T(8,128)(2,1)S(1)}, u32[]{:S(2)}, u32[]{:S(2)}) collective-permute-start(bf16[128,2048]{1,0:T(8,128)(2,1)S(1)} %get-tuple-element.31), channel_id=1, source_target_pairs={{0,16},{4,0},{8,4},{12,8},{28,12},{24,28},{20,24},{16,20},{1,17},{... | collective-permute-start | bytes 1572872 | tf_op jit(solution)/shard_map/ppermute | solution.py:309
  19.1 18.3 %copy-start.12 = (bf16[128,2048]{1,0:T(8,128)(2,1)}, bf16[128,2048]{1,0:T(8,128)(2,1)S(1)}, u32[]{:S(2)}) copy-start(bf16[128,2048]{1,0:T(8,128)(2,1)S(1)} %collective-permute-done.3.refs_1_) | copy-start | bytes 1572868
  19.1 13.2 %collective-permute-start.5 = (bf16[128,2048]{1,0:T(8,128)(2,1)S(1)}, bf16[128,2048]{1,0:T(8,128)(2,1)}, u32[]{:S(2)}, u32[]{:S(2)}) collective-permute-start(bf16[128,2048]{1,0:T(8,128)(2,1)S(1)} %get-tuple-element.32), channel_id=1, source_target_pairs={{0,16},{4,0},{8,4},{12,8},{28,12},{24,28},{20,24},{16,20},{1,17},{... | collective-permute-start | bytes 1572872 | tf_op jit(solution)/shard_map/ppermute | solution.py:309
  29.6 7.8 %copy-start.13 = (bf16[128,2048]{1,0:T(8,128)(2,1)}, bf16[128,2048]{1,0:T(8,128)(2,1)S(1)}, u32[]{:S(2)}) copy-start(bf16[128,2048]{1,0:T(8,128)(2,1)S(1)} %collective-permute-done.4.refs_2_) | copy-start | bytes 1572868
  29.6 15.0 %collective-permute-start.8 = (bf16[128,2048]{1,0:T(8,128)(2,1)S(1)}, bf16[128,2048]{1,0:T(8,128)(2,1)}, u32[]{:S(2)}, u32[]{:S(2)}) collective-permute-start(bf16[128,2048]{1,0:T(8,128)(2,1)S(1)} %collective-permute-done.4.refs_2_), channel_id=1, source_target_pairs={{0,4},{4,8},{8,12},{12,28},{28,24},{24,20},{20,16},{16,0},{1,5},{5... | collective-permute-start | bytes 1572872 | tf_op jit(solution)/shard_map/ppermute | solution.py:309
  31.1 6.2 %copy-start.14 = (bf16[128,2048]{1,0:T(8,128)(2,1)}, bf16[128,2048]{1,0:T(8,128)(2,1)S(1)}, u32[]{:S(2)}) copy-start(bf16[128,2048]{1,0:T(8,128)(2,1)S(1)} %collective-permute-done.6.refs_4_) | copy-start | bytes 1572868
  31.1 15.0 %collective-permute-start.10 = (bf16[128,2048]{1,0:T(8,128)(2,1)S(1)}, bf16[128,2048]{1,0:T(8,128)(2,1)}, u32[]{:S(2)}, u32[]{:S(2)}) collective-permute-start(bf16[128,2048]{1,0:T(8,128)(2,1)S(1)} %collective-permute-done.6.refs_4_), channel_id=1, source_target_pairs={{0,16},{4,0},{8,4},{12,8},{28,12},{24,28},{20,24},{16,20},{1,17},{... | collective-permute-start | bytes 1572872 | tf_op jit(solution)/shard_map/ppermute | solution.py:309
  32.3 23.5 %collective-permute-start.7 = (bf16[128,2048]{1,0:T(8,128)(2,1)S(1)}, bf16[128,2048]{1,0:T(8,128)(2,1)}, u32[]{:S(2)}, u32[]{:S(2)}) collective-permute-start(bf16[128,2048]{1,0:T(8,128)(2,1)S(1)} %collective-permute-done.3.refs_1_), channel_id=1, source_target_pairs={{0,4},{4,8},{8,12},{12,28},{28,24},{24,20},{20,16},{16,0},{1,5},{5... | collective-permute-start | bytes 1572872 | tf_op jit(solution)/shard_map/ppermute | solution.py:309
  33.8 23.5 %copy-start.3 = (bf16[192,4,12,128]{3,1,2,0:T(4,128)(2,1)S(1)}, bf16[192,4,12,128]{3,1,2,0:T(4,128)(2,1)}, u32[]{:S(2)}) copy-start(bf16[192,4,12,128]{3,1,2,0:T(4,128)(2,1)} %param.15) | copy-start | bytes 7077892
  44.5 22.5 %collective-permute-start.12 = (bf16[128,2048]{1,0:T(8,128)(2,1)}, bf16[128,2048]{1,0:T(8,128)(2,1)}, u32[]{:S(2)}, u32[]{:S(2)}) collective-permute-start(bf16[128,2048]{1,0:T(8,128)(2,1)} %collective-permute-done.8.refs_6_), channel_id=1, source_target_pairs={{0,4},{4,8},{8,12},{12,28},{28,24},{24,20},{20,16},{16,0},{1,5},{5... | collective-permute-start | bytes 1572872 | tf_op jit(solution)/shard_map/ppermute | solution.py:309
  46.1 23.5 %collective-permute-start.14 = (bf16[128,2048]{1,0:T(8,128)(2,1)}, bf16[128,2048]{1,0:T(8,128)(2,1)}, u32[]{:S(2)}, u32[]{:S(2)}) collective-permute-start(bf16[128,2048]{1,0:T(8,128)(2,1)} %collective-permute-done.10.refs_8_), channel_id=1, source_target_pairs={{0,16},{4,0},{8,4},{12,8},{28,12},{24,28},{20,24},{16,20},{1,17},{... | collective-permute-start | bytes 1572872 | tf_op jit(solution)/shard_map/ppermute | solution.py:309
  46.6 24.5 %collective-permute-start.9 = (bf16[128,2048]{1,0:T(8,128)(2,1)}, bf16[128,2048]{1,0:T(8,128)(2,1)}, u32[]{:S(2)}, u32[]{:S(2)}) collective-permute-start(bf16[128,2048]{1,0:T(8,128)(2,1)} %collective-permute-done.5.refs_3_), channel_id=1, source_target_pairs={{0,16},{4,0},{8,4},{12,8},{28,12},{24,28},{20,24},{16,20},{1,17},{... | collective-permute-start | bytes 1572872 | tf_op jit(solution)/shard_map/ppermute | solution.py:309
  55.1 4.0 %copy-start.2 = (bf16[576,2048]{1,0:T(8,128)(2,1)}, bf16[576,2048]{1,0:T(8,128)(2,1)S(1)}, u32[]{:S(2)}) copy-start(bf16[576,2048]{1,0:T(8,128)(2,1)S(1)} %collective-permute-done.refs_0_) | copy-start | bytes 7077892
  55.1 66.0 %collective-permute-start.1 = (bf16[576,2048]{1,0:T(8,128)(2,1)S(1)}, bf16[576,2048]{1,0:T(8,128)(2,1)}, u32[]{:S(2)}, u32[]{:S(2)}) collective-permute-start(bf16[576,2048]{1,0:T(8,128)(2,1)S(1)} %collective-permute-done.refs_0_), channel_id=1, source_target_pairs={{0,1},{1,0},{2,3},{3,2},{4,5},{5,4},{6,7},{7,6},{8,9},{9,8},{10,11... | collective-permute-start | bytes 7077896 | tf_op jit(solution)/shard_map/ppermute | solution.py:13
  55.8 22.5 %collective-permute-start.11 = (bf16[128,2048]{1,0:T(8,128)(2,1)}, bf16[128,2048]{1,0:T(8,128)(2,1)}, u32[]{:S(2)}, u32[]{:S(2)}) collective-permute-start(bf16[128,2048]{1,0:T(8,128)(2,1)} %collective-permute-done.7.refs_5_), channel_id=1, source_target_pairs={{0,4},{4,8},{8,12},{12,28},{28,24},{24,20},{20,16},{16,0},{1,5},{5... | collective-permute-start | bytes 1572872 | tf_op jit(solution)/shard_map/ppermute | solution.py:309
  68.0 23.0 %collective-permute-start.17 = (bf16[64,2048]{1,0:T(8,128)(2,1)S(1)}, bf16[64,2048]{1,0:T(8,128)(2,1)S(1)}, u32[]{:S(2)}, u32[]{:S(2)}) collective-permute-start(bf16[64,2048]{1,0:T(8,128)(2,1)S(1)} %slice.40), channel_id=1, source_target_pairs={{0,4},{4,8},{8,12},{12,28},{28,24},{24,20},{20,16},{16,0},{1,5},{5... | collective-permute-start | bytes 786440 | tf_op jit(solution)/shard_map/ppermute | solution.py:309
  70.6 22.0 %collective-permute-start.18 = (bf16[64,2048]{1,0:T(8,128)(2,1)S(1)}, bf16[64,2048]{1,0:T(8,128)(2,1)S(1)}, u32[]{:S(2)}, u32[]{:S(2)}) collective-permute-start(bf16[64,2048]{1,0:T(8,128)(2,1)S(1)} %slice.41), channel_id=1, source_target_pairs={{0,16},{4,0},{8,4},{12,8},{28,12},{24,28},{20,24},{16,20},{1,17},{... | collective-permute-start | bytes 786440 | tf_op jit(solution)/shard_map/ppermute | solution.py:309
  71.1 15.6 %collective-permute-start.13 = (bf16[128,2048]{1,0:T(8,128)(2,1)}, bf16[128,2048]{1,0:T(8,128)(2,1)S(1)}, u32[]{:S(2)}, u32[]{:S(2)}) collective-permute-start(bf16[128,2048]{1,0:T(8,128)(2,1)} %collective-permute-done.9.refs_7_), channel_id=1, source_target_pairs={{0,16},{4,0},{8,4},{12,8},{28,12},{24,28},{20,24},{16,20},{1,17},{... | collective-permute-start | bytes 1572872 | tf_op jit(solution)/shard_map/ppermute | solution.py:309
  77.2 23.3 %copy-start.11 = (s32[192]{0:T(256)S(1)}, s32[192]{0:T(256)}, u32[]{:S(2)}) copy-start(s32[192]{0:T(256)} %param.19) | copy-start | bytes 2308
  78.2 42.7 %collective-permute-start.30 = (bf16[2,2304,128]{2,1,0:T(8,128)(2,1)}, bf16[2,2304,128]{2,1,0:T(8,128)(2,1)}, u32[]{:S(2)}, u32[]{:S(2)}) collective-permute-start(bf16[2,2304,128]{2,1,0:T(8,128)(2,1)} %get-tuple-element.24), channel_id=1, source_target_pairs={{0,2},{1,3},{2,0},{3,1},{4,6},{5,7},{6,4},{7,5},{8,10},{9,11},{10,... | collective-permute-start | bytes 3538952 | tf_op jit(solution)/shard_map/ppermute | solution.py:13
  86.7 5.8 %copy-start.9 = (bf16[128,2048]{1,0:T(8,128)(2,1)}, bf16[128,2048]{1,0:T(8,128)(2,1)S(1)}, u32[]{:S(2)}) copy-start(bf16[128,2048]{1,0:T(8,128)(2,1)S(1)} %collective-permute-done.13.refs_11_) | copy-start | bytes 1572868
  88.6 9.6 %collective-permute-start.15 = (bf16[64,2048]{1,0:T(8,128)(2,1)}, bf16[64,2048]{1,0:T(8,128)(2,1)}, u32[]{:S(2)}, u32[]{:S(2)}) collective-permute-start(bf16[64,2048]{1,0:T(8,128)(2,1)} %slice.34), channel_id=1, source_target_pairs={{0,4},{4,8},{8,12},{12,28},{28,24},{24,20},{20,16},{16,0},{1,5},{5... | collective-permute-start | bytes 786440 | tf_op jit(solution)/shard_map/ppermute | solution.py:309
  91.0 1.6 copy-start.15
  91.0 17.3 %collective-permute-start.21 = (bf16[256,1024]{1,0:T(8,128)(2,1)}, bf16[256,1024]{1,0:T(8,128)(2,1)}, u32[]{:S(2)}, u32[]{:S(2)}) collective-permute-start(bf16[256,1024]{1,0:T(8,128)(2,1)} %constant_dynamic-slice_fusion.4.refs_0_), channel_id=1, source_target_pairs={{0,4},{4,8},{8,12},{12,28},{28,24},{24,20},{20,16},{16,0},{1,5},{5... | collective-permute-start | bytes 1572872 | tf_op jit(solution)/shard_map/ppermute | solution.py:309
  93.3 16.6 %collective-permute-start.22 = (bf16[256,1024]{1,0:T(8,128)(2,1)}, bf16[256,1024]{1,0:T(8,128)(2,1)}, u32[]{:S(2)}, u32[]{:S(2)}) collective-permute-start(bf16[256,1024]{1,0:T(8,128)(2,1)} %constant_dynamic-slice_fusion.4.refs_0_), channel_id=1, source_target_pairs={{0,16},{4,0},{8,4},{12,8},{28,12},{24,28},{20,24},{16,20},{1,17},{... | collective-permute-start | bytes 1572872 | tf_op jit(solution)/shard_map/ppermute | solution.py:309
  98.1 10.2 %collective-permute-start.16 = (bf16[64,2048]{1,0:T(8,128)(2,1)S(1)}, bf16[64,2048]{1,0:T(8,128)(2,1)}, u32[]{:S(2)}, u32[]{:S(2)}) collective-permute-start(bf16[64,2048]{1,0:T(8,128)(2,1)S(1)} %slice.35), channel_id=1, source_target_pairs={{0,16},{4,0},{8,4},{12,8},{28,12},{24,28},{20,24},{16,20},{1,17},{... | collective-permute-start | bytes 786440 | tf_op jit(solution)/shard_map/ppermute | solution.py:309
  104.4 19.9 %copy-start.10 = (s32[192]{0:T(256)S(1)}, s32[192]{0:T(256)}, u32[]{:S(2)}) copy-start(s32[192]{0:T(256)} %param.18) | copy-start | bytes 2308
  108.3 68.3 %collective-permute-start.29 = (bf16[2,2304,128]{2,1,0:T(8,128)(2,1)}, bf16[2,2304,128]{2,1,0:T(8,128)(2,1)}, u32[]{:S(2)}, u32[]{:S(2)}) collective-permute-start(bf16[2,2304,128]{2,1,0:T(8,128)(2,1)} %get-tuple-element.22), channel_id=1, source_target_pairs={{0,1},{1,0},{2,3},{3,2},{4,5},{5,4},{6,7},{7,6},{8,9},{9,8},{10,11... | collective-permute-start | bytes 3538952 | tf_op jit(solution)/shard_map/ppermute | solution.py:13
  108.3 20.5 %collective-permute-start.23 = (bf16[256,1024]{1,0:T(8,128)(2,1)}, bf16[256,1024]{1,0:T(8,128)(2,1)}, u32[]{:S(2)}, u32[]{:S(2)}) collective-permute-start(bf16[256,1024]{1,0:T(8,128)(2,1)} %collective-permute-done.21.refs_1_), channel_id=1, source_target_pairs={{0,4},{4,8},{8,12},{12,28},{28,24},{24,20},{20,16},{16,0},{1,5},{5... | collective-permute-start | bytes 1572872 | tf_op jit(solution)/shard_map/ppermute | solution.py:309
  109.8 20.5 %collective-permute-start.24 = (bf16[256,1024]{1,0:T(8,128)(2,1)}, bf16[256,1024]{1,0:T(8,128)(2,1)}, u32[]{:S(2)}, u32[]{:S(2)}) collective-permute-start(bf16[256,1024]{1,0:T(8,128)(2,1)} %collective-permute-done.22.refs_2_), channel_id=1, source_target_pairs={{0,16},{4,0},{8,4},{12,8},{28,12},{24,28},{20,24},{16,20},{1,17},{... | collective-permute-start | bytes 1572872 | tf_op jit(solution)/shard_map/ppermute | solution.py:309
  121.0 5.3 %collective-permute-start.19 = (f32[576,64]{1,0:T(8,128)}, f32[576,64]{1,0:T(8,128)S(1)}, u32[]{:S(2)}, u32[]{:S(2)}) collective-permute-start(f32[576,64]{1,0:T(8,128)} %rank.1), channel_id=1, source_target_pairs={{0,1},{1,0},{2,3},{3,2},{4,5},{5,4},{6,7},{7,6},{8,9},{9,8},{10,11... | collective-permute-start | bytes 442376 | tf_op jit(solution)/shard_map/ppermute | solution.py:13
  121.1 55.6 %collective-permute-start.31 = (bf16[2,2304,128]{2,1,0:T(8,128)(2,1)}, bf16[2,2304,128]{2,1,0:T(8,128)(2,1)S(1)}, u32[]{:S(2)}, u32[]{:S(2)}) collective-permute-start(bf16[2,2304,128]{2,1,0:T(8,128)(2,1)} %get-tuple-element.26), channel_id=1, source_target_pairs={{0,3},{1,2},{2,1},{3,0},{4,7},{5,6},{6,5},{7,4},{8,11},{9,10},{10,... | collective-permute-start | bytes 3538952 | tf_op jit(solution)/shard_map/ppermute | solution.py:13
  127.2 28.7 %collective-permute-start.20 = (f32[576,64]{1,0:T(8,128)S(1)}, f32[576,64]{1,0:T(8,128)S(1)}, u32[]{:S(2)}, u32[]{:S(2)}) collective-permute-start(f32[576,64]{1,0:T(8,128)S(1)} %add.115), channel_id=1, source_target_pairs={{0,2},{1,3},{2,0},{3,1},{4,6},{5,7},{6,4},{7,5},{8,10},{9,11},{10,... | collective-permute-start | bytes 442376 | tf_op jit(solution)/shard_map/ppermute | solution.py:13
  128.8 33.5 %collective-permute-start.25 = (bf16[256,1024]{1,0:T(8,128)(2,1)}, bf16[256,1024]{1,0:T(8,128)(2,1)S(1)}, u32[]{:S(2)}, u32[]{:S(2)}) collective-permute-start(bf16[256,1024]{1,0:T(8,128)(2,1)} %collective-permute-done.23.refs_3_), channel_id=1, source_target_pairs={{0,4},{4,8},{8,12},{12,28},{28,24},{24,20},{20,16},{16,0},{1,5},{5... | collective-permute-start | bytes 1572872 | tf_op jit(solution)/shard_map/ppermute | solution.py:309
  130.3 33.6 %collective-permute-start.26 = (bf16[256,1024]{1,0:T(8,128)(2,1)}, bf16[256,1024]{1,0:T(8,128)(2,1)S(1)}, u32[]{:S(2)}, u32[]{:S(2)}) collective-permute-start(bf16[256,1024]{1,0:T(8,128)(2,1)} %collective-permute-done.24.refs_4_), channel_id=1, source_target_pairs={{0,16},{4,0},{8,4},{12,8},{28,12},{24,28},{20,24},{16,20},{1,17},{... | collective-permute-start | bytes 1572872 | tf_op jit(solution)/shard_map/ppermute | solution.py:309
  162.3 14.2 %copy-start.5 = (bf16[256,1024]{1,0:T(8,128)(2,1)}, bf16[256,1024]{1,0:T(8,128)(2,1)S(1)}, u32[]{:S(2)}) copy-start(bf16[256,1024]{1,0:T(8,128)(2,1)S(1)} %collective-permute-done.25.refs_4_) | copy-start | bytes 1572868
  162.4 14.2 %collective-permute-start.27 = (bf16[128,1024]{1,0:T(8,128)(2,1)S(1)}, bf16[128,1024]{1,0:T(8,128)(2,1)S(1)}, u32[]{:S(2)}, u32[]{:S(2)}) collective-permute-start(bf16[128,1024]{1,0:T(8,128)(2,1)S(1)} %slice.42), channel_id=1, source_target_pairs={{0,4},{4,8},{8,12},{12,28},{28,24},{24,20},{20,16},{16,0},{1,5},{5... | collective-permute-start | bytes 786440 | tf_op jit(solution)/shard_map/ppermute | solution.py:309
  163.9 12.6 %copy-start.6 = (bf16[256,1024]{1,0:T(8,128)(2,1)}, bf16[256,1024]{1,0:T(8,128)(2,1)S(1)}, u32[]{:S(2)}) copy-start(bf16[256,1024]{1,0:T(8,128)(2,1)S(1)} %collective-permute-done.26.refs_5_) | copy-start | bytes 1572868
  164.0 12.6 %collective-permute-start.28 = (bf16[128,1024]{1,0:T(8,128)(2,1)S(1)}, bf16[128,1024]{1,0:T(8,128)(2,1)S(1)}, u32[]{:S(2)}, u32[]{:S(2)}) collective-permute-start(bf16[128,1024]{1,0:T(8,128)(2,1)S(1)} %slice.43), channel_id=1, source_target_pairs={{0,16},{4,0},{8,4},{12,8},{28,12},{24,28},{20,24},{16,20},{1,17},{... | collective-permute-start | bytes 786440 | tf_op jit(solution)/shard_map/ppermute | solution.py:309
  176.6 0.7 copy-start.7
  176.6 0.8 copy-start.8
  176.6 1.1 copy-start.4
  177.8 16.5 %copy-start.1 = (bf16[8,64,1024]{2,1,0:T(8,128)(2,1)S(1)}, bf16[8,64,1024]{2,1,0:T(8,128)(2,1)}, u32[]{:S(2)}) copy-start(bf16[8,64,1024]{2,1,0:T(8,128)(2,1)} %param.13) | copy-start | bytes 3145732
  (1 other events, 0.7 us)

commit v3 on v2

v3 whole, which is shorter than its diff:
```python
import jax
import jax.numpy as jnp
from jax import lax
from jax.experimental import pallas as pl
from jax.experimental.pallas import tpu as pltpu
from jax.sharding import PartitionSpec as P

KVH = 4
VMEM_LIMIT = 56 * 1024 * 1024


def swap(array, bit, count):
    return lax.ppermute(array, "tensor", [(i, i ^ bit) for i in range(count)])


def project_pair(tensor_ids, first, second, weight, earlier=None):
    depth = first[0].shape[1]
    rows = sum(part.shape[0] for part in first)
    columns = weight.shape[1]
    chunk = 512
    chunks = depth // chunk
    parts = len(first)

    def kernel(ids_ref, *refs):
        first_weight, second_weight = refs[2 * parts : 2 * parts + 2]
        out_ref = refs[-1]
        left = jnp.concatenate([ref[...] for ref in refs[:parts]], axis=0)
        right = jnp.concatenate([ref[...] for ref in refs[parts : 2 * parts]], axis=0)
        product = jnp.dot(
            left, first_weight[...], preferred_element_type=jnp.float32
        ) + jnp.dot(right, second_weight[...], preferred_element_type=jnp.float32)

        @pl.when(pl.program_id(0) == 0)
        def _():
            out_ref[...] = product if earlier is None else product + refs[2 * parts + 2][...]

        @pl.when(pl.program_id(0) > 0)
        def _():
            out_ref[...] += product

    whole = pl.BlockSpec((rows, columns), lambda k, ids: (0, 0))
    in_specs = [
        pl.BlockSpec((part.shape[0], chunk), lambda k, ids: (0, k)) for part in first + second
    ] + [
        pl.BlockSpec((chunk, columns), lambda k, ids: (ids[0] * chunks + k, 0)),
        pl.BlockSpec((chunk, columns), lambda k, ids: (ids[1] * chunks + k, 0)),
    ]
    operands = first + second + [weight, weight]
    if earlier is not None:
        in_specs.append(whole)
        operands.append(earlier)
    return pl.pallas_call(
        kernel,
        out_shape=jax.ShapeDtypeStruct((rows, columns), jnp.float32),
        grid_spec=pltpu.PrefetchScalarGridSpec(
            num_scalar_prefetch=1, grid=(chunks,), in_specs=in_specs, out_specs=whole
        ),
        compiler_params=pltpu.CompilerParams(vmem_limit_bytes=VMEM_LIMIT),
        cost_estimate=pl.CostEstimate(
            flops=4 * rows * depth * columns,
            bytes_accessed=4 * depth * (rows + columns) + 4 * rows * columns,
            transcendentals=0,
        ),
        name="project",
    )(tensor_ids, *operands)


def add_ranks(starts, tokens, row_adapters, groups, rank, earlier=None, last=False):
    rows, depth = tokens.shape
    width = sum(part.shape[0] for part in groups[0])
    sizes = [len(group) for group in groups]
    flat = [part for group in groups for part in group]

    def kernel(starts_ref, tokens_ref, adapter_ref, *refs):
        out_ref = refs[-1]
        lane = lax.broadcasted_iota(jnp.int32, (rows, width), 1) // rank
        total = jnp.zeros((rows, width), jnp.float32) if earlier is None else refs[-2][...]
        used = 0
        for i, size in enumerate(sizes):
            down = jnp.concatenate([ref[...] for ref in refs[used : used + size]], axis=0)
            used += size
            product = lax.dot_general(
                tokens_ref[...],
                down,
                (((1,), (1,)), ((), ())),
                preferred_element_type=jnp.float32,
            )
            total = total + jnp.where(lane + starts_ref[i] == adapter_ref[...], product, 0.0)
        if last:
            folded = total[:, :128]
            for i in range(1, width // 128):
                folded = folded + total[:, i * 128 : (i + 1) * 128]
            out_ref[...] = folded[:, :rank] + folded[:, rank:]
        else:
            out_ref[...] = total

    out_width = rank if last else width
    operands = [tokens, row_adapters] + flat + ([] if earlier is None else [earlier])
    return pl.pallas_call(
        kernel,
        out_shape=jax.ShapeDtypeStruct((rows, out_width), jnp.float32),
        grid_spec=pltpu.PrefetchScalarGridSpec(
            num_scalar_prefetch=1,
            grid=(1,),
            in_specs=[pl.BlockSpec(op.shape, lambda g, starts: (0, 0)) for op in operands],
            out_specs=pl.BlockSpec((rows, out_width), lambda g, starts: (0, 0)),
        ),
        compiler_params=pltpu.CompilerParams(vmem_limit_bytes=VMEM_LIMIT),
        cost_estimate=pl.CostEstimate(
            flops=2 * rows * depth * width * len(groups),
            bytes_accessed=2 * depth * (rows + width * len(groups)),
            transcendentals=0,
        ),
        name="rank",
    )(starts, *operands)


def part_delta(starts_ref, ranks, held, up_refs, sizes):
    rows, rank = ranks.shape
    width = sum(ref.shape[0] for ref in up_refs[: sizes[0]])
    lane = lax.broadcasted_iota(jnp.int32, (rows, width), 1) // rank
    wide = jnp.concatenate([ranks] * (width // rank), axis=1)
    kept = [
        jnp.where(lane + starts_ref[i] == held, wide, 0.0).astype(jnp.bfloat16)
        for i in range(len(sizes))
    ]
    return jnp.dot(
        jnp.concatenate(kept, axis=1),
        jnp.concatenate([ref[...] for ref in up_refs], axis=0),
        preferred_element_type=jnp.float32,
    )


def early_query(starts, base, ranks, row_adapters, groups):
    rows, columns = base.shape
    sizes = [len(group) for group in groups]
    flat = [part for group in groups for part in group]
    depth = sum(part.shape[0] for part in flat)

    def kernel(starts_ref, base_ref, rank_ref, adapter_ref, *refs):
        delta = part_delta(starts_ref, rank_ref[...], adapter_ref[...], refs[:-1], sizes)
        refs[-1][...] = base_ref[...] + delta.astype(jnp.bfloat16).astype(jnp.float32)

    operands = [base, ranks, row_adapters] + flat
    return pl.pallas_call(
        kernel,
        out_shape=jax.ShapeDtypeStruct((rows, columns), jnp.float32),
        grid_spec=pltpu.PrefetchScalarGridSpec(
            num_scalar_prefetch=1,
            grid=(1,),
            in_specs=[pl.BlockSpec(op.shape, lambda g, starts: (0, 0)) for op in operands],
            out_specs=pl.BlockSpec((rows, columns), lambda g, starts: (0, 0)),
        ),
        compiler_params=pltpu.CompilerParams(vmem_limit_bytes=VMEM_LIMIT),
        cost_estimate=pl.CostEstimate(
            flops=2 * rows * columns * depth,
            bytes_accessed=8 * columns * rows + 2 * columns * depth,
            transcendentals=0,
        ),
        name="delta",
    )(starts, *operands)


def attend(
    scalars, query, ranks, row_adapters, groups, lengths, key_values, fresh_keys, fresh_values
):
    steps, rows, head_size = fresh_keys.shape
    width = query.shape[1]
    heads = width // head_size
    blocks = len(key_values)
    sizes = [len(group) for group in groups]
    ups = [part for group in groups for part in group]
    positions = key_values[0].shape[1] // rows
    bundle = 32
    sub = 4 if 4 * positions % 16 == 0 and heads % 2 == 0 else 16
    slab = max(sub, 8)
    pack = slab // sub
    span = sub * positions
    cached = blocks * span
    fresh = steps * slab
    columns = -(-(cached + fresh) // 128) * 128
    scale = head_size ** (-0.5)

    def kernel(scalars_ref, *refs):
        given_ref, rank_ref, adapter_ref = refs[:3]
        up_refs = refs[3 : 3 + len(ups)]
        length_ref = refs[3 + len(ups)]
        cache_refs = refs[4 + len(ups) : 4 + len(ups) + blocks]
        fresh_key_ref, fresh_value_ref, out_ref, query_ref = refs[4 + len(ups) + blocks :]
        step = pl.program_id(0)

        @pl.when(step == 0)
        def _():
            delta = part_delta(scalars_ref, rank_ref[...], adapter_ref[...], up_refs, sizes)
            rounded = (given_ref[...] + delta.astype(jnp.bfloat16).astype(jnp.float32)).astype(
                jnp.bfloat16
            )
            query_ref[...] = rounded.astype(jnp.float32)

        column = lax.broadcasted_iota(jnp.int32, (slab, columns), 1)
        own = lax.broadcasted_iota(jnp.int32, (slab, columns), 0) % sub
        on_row = (column % span) // positions == own
        place = jnp.full((slab, columns), 1 << 20, jnp.int32)
        for b in range(blocks):
            here = (column >= b * span) & (column < (b + 1) * span)
            place = jnp.where(
                here & on_row, column % positions + scalars_ref[len(sizes) + b] * positions, place
            )
        fresh_step = (column - cached) // slab
        fresh_row = (column - cached) % slab
        is_fresh = (column >= cached) & (column < cached + fresh)
        padding = jnp.zeros((columns - cached - fresh, head_size), jnp.bfloat16)
        ones = jnp.ones((columns, head_size), jnp.bfloat16)
        fresh_key_all = fresh_key_ref[...].astype(jnp.float32)
        fresh_value_all = fresh_value_ref[...].astype(jnp.float32)
        outputs = []
        for first in range(0, bundle, slab):
            begin = pl.multiple_of(step * bundle + first, slab)
            slabs = [
                [
                    query_ref[pl.ds(s * rows + begin, slab), h * head_size : (h + 1) * head_size]
                    for h in range(heads)
                ]
                for s in range(steps)
            ]
            new = slice(first, first + slab)
            new_keys = jnp.concatenate(
                [fresh_key_all[t, new] for t in range(steps)], axis=0
            ).astype(jnp.bfloat16)
            new_values = jnp.concatenate(
                [fresh_value_all[t, new] for t in range(steps)], axis=0
            ).astype(jnp.bfloat16)
            length_all = length_ref[new]
            for part in range(pack):
                mine = slice(part * sub, (part + 1) * sub)
                there = slice((first + part * sub) * positions, (first + (part + 1) * sub) * positions)
                queries = jnp.concatenate(
                    [slabs[s][h][mine] for s in range(steps) for h in range(heads)], axis=0
                ).astype(jnp.bfloat16)
                keys = jnp.concatenate(
                    [ref[0, there, :] for ref in cache_refs] + [new_keys, padding], axis=0
                )
                values = jnp.concatenate(
                    [ref[1, there, :] for ref in cache_refs] + [new_values, padding], axis=0
                )
                values = jnp.concatenate([values, ones], axis=1)
                scores = lax.dot_general(
                    queries, keys, (((1,), (1,)), ((), ())), preferred_element_type=jnp.float32
                ).reshape(steps, heads // pack, slab, columns)
                length = jnp.concatenate([length_all[mine]] * pack, axis=0)
                cached_seen = place < length
                fresh_seen = is_fresh & (fresh_row == own + part * sub)
                raised = []
                for s in range(steps):
                    seen = cached_seen | (fresh_seen & (fresh_step <= s))
                    bias = jnp.where(seen, 0.0, -1e30)
                    shifted = scores[s] * scale + bias[None]
                    shifted = shifted - jnp.max(shifted, axis=-1, keepdims=True)
                    raised.append(jnp.exp(shifted).reshape(heads // pack * slab, columns))
                sums = jnp.dot(
                    jnp.concatenate(raised, axis=0).astype(jnp.bfloat16),
                    values,
                    preferred_element_type=jnp.float32,
                )
                outputs.append(sums[:, :head_size] / sums[:, head_size:])
        for s in range(steps):
            for h in range(heads):
                start = (s * heads + h) * sub
                out_ref[s, :, h * head_size : (h + 1) * head_size] = jnp.concatenate(
                    [out[start : start + sub] for out in outputs], axis=0
                ).astype(jnp.bfloat16)

    def whole(array):
        return pl.BlockSpec(array.shape, lambda g, scalars: (0,) * array.ndim)

    cache_spec = pl.BlockSpec((2, bundle * positions, head_size), lambda g, scalars: (0, g, 0))
    fresh_spec = pl.BlockSpec((steps, bundle, head_size), lambda g, scalars: (0, g, 0))
    wide_spec = pl.BlockSpec((steps, bundle, width), lambda g, scalars: (0, g, 0))
    first = [query, ranks, row_adapters, *ups]
    return pl.pallas_call(
        kernel,
        out_shape=jax.ShapeDtypeStruct((steps, rows, width), jnp.bfloat16),
        grid_spec=pltpu.PrefetchScalarGridSpec(
            num_scalar_prefetch=1,
            grid=(rows // bundle,),
            in_specs=[whole(op) for op in first]
            + [pl.BlockSpec((bundle, 1), lambda g, scalars: (g, 0))]
            + [cache_spec] * blocks
            + [fresh_spec] * 2,
            out_specs=wide_spec,
            scratch_shapes=[pltpu.VMEM((steps * rows, width), jnp.float32)],
        ),
        compiler_params=pltpu.CompilerParams(vmem_limit_bytes=VMEM_LIMIT),
        cost_estimate=pl.CostEstimate(
            flops=4 * steps * rows * width * sub * (blocks * positions + steps),
            bytes_accessed=4 * steps * rows * width + 4 * blocks * rows * positions * head_size,
            transcendentals=steps * rows * heads * columns,
        ),
        name="attend",
    )(scalars, *first, lengths, *key_values, fresh_keys, fresh_values)


def ring_hop(array, step, owners):
    size = 2 * owners
    device = [place if place < owners else 3 * owners - 1 - place for place in range(size)]
    pairs = [(device[place], device[(place + step) % size]) for place in range(size)]
    return lax.ppermute(array, ("rep", "dp"), pairs)


def gate(array, *others):
    return lax.optimization_barrier((array, others))[0]


def ring_step(k, before, after, owners):
    if k == owners:
        rows = before.shape[0] // 2
        before, after = before[:rows], after[rows:]
    return ring_hop(before, 1, owners), ring_hop(after, -1, owners)


def body(
    tokens,
    query_weight,
    adapter_down_weight,
    adapter_up_weight,
    cached_key_rows,
    cached_value_rows,
    incoming_key_rows,
    incoming_value_rows,
    cached_length_rows,
    row_adapter_index,
):
    steps, rows, features = tokens.shape
    width = query_weight.shape[1]
    positions, head_size = cached_key_rows.shape[2:]
    count = lax.axis_size("tensor")
    owners = lax.axis_size("dp")
    me = lax.axis_index("tensor")
    owner = lax.axis_index("dp")
    replica = lax.axis_index("rep")
    adapters, _, rank = adapter_down_weight.shape
    half = adapters // 2
    flat_tokens = tokens.reshape(steps * rows, features)

    row_adapters = jnp.tile(row_adapter_index, steps).reshape(steps * rows, 1)

    down_rows = jnp.swapaxes(adapter_down_weight, 1, 2).reshape(adapters * rank, features)
    up_rows = adapter_up_weight.reshape(adapters * rank, width)
    own_down = lax.dynamic_slice_in_dim(down_rows, replica * half * rank, half * rank, axis=0)
    own_up = lax.dynamic_slice_in_dim(up_rows, replica * half * rank, half * rank, axis=0)

    size = 2 * owners
    place = jnp.where(replica == 0, owner, size - 1 - owner)
    start = []
    for step in [0] + [d for k in range(1, owners) for d in (-k, k)] + [owners]:
        other = lax.rem(place + step + size, size)
        start.append(
            jnp.where(other < owners, other * adapters, (size - 1 - other) * adapters + half)
        )
    starts = jnp.stack(start).astype(jnp.int32)

    key_heads = jnp.transpose(cached_key_rows, (1, 0, 2, 3)).reshape(KVH, rows * positions, head_size)
    value_heads = jnp.transpose(cached_value_rows, (1, 0, 2, 3)).reshape(
        KVH, rows * positions, head_size
    )
    both = jnp.stack([key_heads, value_heads], axis=1)

    paired = count == 4
    down = [ring_step(1, own_down, own_down, owners)]
    if paired:
        ids = jnp.stack([me ^ j for j in range(count)]).astype(jnp.int32)
        far = swap(flat_tokens, 2, count)
        near = swap(flat_tokens, 1, count)
        parcels = lax.optimization_barrier(
            [lax.dynamic_index_in_dim(both, ids[j], 0, keepdims=False) for j in range(count)]
        )
        base = project_pair(ids[:2], [flat_tokens], [near], query_weight)
        second = swap(gate(parcels[2], near, down[0]), 2, count)
        waits = {2: [near, parcels], 3: [base]}
    else:
        all_tokens = lax.all_gather(flat_tokens, "tensor", axis=1, tiled=True)
        base = jnp.dot(all_tokens, query_weight, preferred_element_type=jnp.float32)
        ids = jnp.arange(count, dtype=jnp.int32)
        gathered = lax.all_to_all(
            jnp.repeat(both, count // KVH, axis=0),
            "tensor",
            split_axis=0,
            concat_axis=0,
            tiled=True,
        )
        key_values = [gathered[b] for b in range(count)]
        waits = {}
    early = 1 + 2 * (owners - 2)
    for k in range(2, owners + 1):
        before, after = down[-1]
        if k == owners:
            groups = [[own_down]] + [[part] for pair in down[: owners - 2] for part in pair]
            ranks = add_ranks(starts[:early], flat_tokens, row_adapters, groups, rank)
        if k in waits:
            before, after = gate((before, after), *waits[k])
        down.append(ring_step(k, before, after, owners))
    if paired:
        far = gate(far, down[owners - 2])
        far_near = swap(far, 1, count)
        third = swap(gate(parcels[3], far), 3, count)
        first = swap(gate(parcels[1], far_near), 1, count)
        key_values = [parcels[0], first, second, third]
        base = project_pair(ids[2:], [far], [far_near], query_weight, base)

    groups = [[part] for part in down[owners - 2]] + [list(down[owners - 1])]
    ranks = add_ranks(
        starts[early:], flat_tokens, row_adapters, groups, rank, earlier=ranks, last=True
    )

    own_up = gate(own_up, down[owners - 2])
    up = [ring_step(1, own_up, own_up, owners)]
    waits = {2: [ranks] + ([second] if paired else [])}
    bit = 1
    while bit < count:
        ranks = ranks + swap(ranks, bit, count)
        bit *= 2
    waits[3] = [ranks, base]
    for k in range(2, owners + 1):
        up.append(ring_step(k, *gate(up[-1], *waits.get(k, [])), owners))

    groups = [[own_up]] + [[part] for pair in up[: owners - 2] for part in pair]
    query = early_query(starts[:early], base, ranks, row_adapters, groups)
    groups = [[part] for part in up[owners - 2]] + [list(up[owners - 1])]

    kv_head = me * KVH // count
    fresh_keys = lax.dynamic_index_in_dim(incoming_key_rows, kv_head, 2, keepdims=False)
    fresh_values = lax.dynamic_index_in_dim(incoming_value_rows, kv_head, 2, keepdims=False)
    return attend(
        jnp.concatenate([starts[early:], ids]),
        query,
        ranks,
        row_adapters,
        groups,
        cached_length_rows.reshape(rows, 1),
        key_values,
        fresh_keys,
        fresh_values,
    )


def solution(mesh):
    in_specs = (
        P(None, ("rep", "dp"), "tensor"),
        P(None, "tensor"),
        P("dp", "tensor", None),
        P("dp", None, "tensor"),
        P(("rep", "dp"), None, "tensor", None),
        P(("rep", "dp"), None, "tensor", None),
        P(None, ("rep", "dp"), None, None),
        P(None, ("rep", "dp"), None, None),
        P(("rep", "dp")),
        P(("rep", "dp")),
    )
    out_specs = P(None, ("rep", "dp"), "tensor")
    return jax.shard_map(body, mesh=mesh, in_specs=in_specs, out_specs=out_specs, check_vma=False)
```

time: 195 us -> 184 us (0.944)
  starting transfers between devices: 33.4 us -> 22.3 us
  local copies, waits for them, and re-layouts: 27.8 us -> 17.9 us
  Pallas kernels: 55.6 us -> 63.1 us
    ppermute x24 -> x16, waiting for transfers between devices: 53 us -> 65.9 us  [ring_hop(): return lax.ppermute(array, ('rep', 'dp'), pairs)]
    ppermute x8, waiting for transfers between devices: 21.3 us -> 9.9 us  [swap(): return lax.ppermute(array, 'tensor', [(i, i ^ bit) for i in range(count)])]
    ppermute x24 -> x16, starting transfers between devices: 27.8 us -> 17.4 us  [ring_hop(): return lax.ppermute(array, ('rep', 'dp'), pairs)]
    pallas_call x2 -> x3, Pallas kernels: 16.3 us -> 20.7 us  [the longest x2 14.3 us: add_ranks(): pl.pallas_call(kernel, out_shape=jax.ShapeDtypeStruct((rows, out_width),...]
    slice x7 -> x4, local copies, waits for them, and re-layouts: 6.06 us -> 1.96 us  [ring_step(): before, after = (before[:rows], after[rows:])]
    pallas_call x1, Pallas kernels: 16.5 us -> 19.4 us  [attend(): pl.pallas_call(kernel, out_shape=jax.ShapeDtypeStruct((steps, rows, width...]
    squeeze x1, local copies, waits for them, and re-layouts: 4.63 us -> 2.29 us  [body(): lax.dynamic_index_in_dim(both, ids[j], 0, keepdims=False)]
    dynamic_slice x1, local copies, waits for them, and re-layouts: 2.31 us -> 0.07 us  [body(): lax.dynamic_slice_in_dim(down_rows, replica * half * rank, half * rank, a...]
  transfers between devices with their start and end apart: 32 -> 24, of which waited for: 12 -> 12; matrix products, arithmetic and copies ran while one was open for 15% -> 10% of each run, Pallas kernels for 20% -> 24%
where the time goes in v3:
time: 184 us; the launch traced here: 183 us
  waiting for transfers between devices  75.7 us (41%)
  Pallas kernels  63.1 us (34%)
  starting transfers between devices  22.3 us (12%)
  local copies, waits for them, and re-layouts  17.9 us (10%)
  other arithmetic  3.69 us (2%)
    ppermute x16, waiting for transfers between devices, ring_hop(): return lax.ppermute(array, ('rep', 'dp'), pairs)  65.9 us
    pallas_call x2, Pallas kernels, project_pair(): pl.pallas_call(kernel, out_shape=jax.ShapeDtypeStruct((rows, columns), jn...  23 us
    pallas_call x1, Pallas kernels, attend(): pl.pallas_call(kernel, out_shape=jax.ShapeDtypeStruct((steps, rows, width...  19.4 us
    ppermute x16, starting transfers between devices, ring_hop(): return lax.ppermute(array, ('rep', 'dp'), pairs)  17.4 us
    pallas_call x2, Pallas kernels, add_ranks(): pl.pallas_call(kernel, out_shape=jax.ShapeDtypeStruct((rows, out_width),...  14.3 us
    ppermute x8, waiting for transfers between devices, swap(): return lax.ppermute(array, 'tensor', [(i, i ^ bit) for i in range(count)])  9.9 us
    unnamed x43, local copies, waits for them, and re-layouts  7.23 us
    pallas_call x1, Pallas kernels, early_query(): pl.pallas_call(kernel, out_shape=jax.ShapeDtypeStruct((rows, columns), jn...  6.41 us
  transfers between devices with their start and end apart: 24, of which 12 were waited for; matrix products, arithmetic and copies ran while one was open for 10% of the time, Pallas kernels for 24%

profile of v3, /device:TPU:0, one launch (start us, length us, event | category | flops | bytes accessed | tf_op | source)
XLA Modules:
  0.0 183.2 jit_solution(8404541632975759755)
XLA Ops:
  0.5 1.1 copy-done
  1.7 3.0 %collective-permute-start.2 = (bf16[256,2048]{1,0:T(8,128)(2,1)S(1)}, bf16[256,2048]{1,0:T(8,128)(2,1)}, u32[]{:S(2)}, u32[]{:S(2)}) collective-permute-start(bf16[256,2048]{1,0:T(8,128)(2,1)S(1)} %constant_dynamic-slice_fusion.3.refs_0_), channel_id=1, source_target_pairs={{0,16},{4,0},{8,4},{12,8},{28,12},{24,28},{20,24},{16,20},{1,17},{... | collective-permute-start | bytes 3145736 | tf_op jit(solution)/shard_map/ppermute | solution.py:307
  4.8 1.9 %collective-permute-start = (bf16[576,2048]{1,0:T(8,128)(2,1)}, bf16[576,2048]{1,0:T(8,128)(2,1)S(1)}, u32[]{:S(2)}, u32[]{:S(2)}) collective-permute-start(bf16[576,2048]{1,0:T(8,128)(2,1)} %bitcast.42), channel_id=1, source_target_pairs={{0,2},{1,3},{2,0},{3,1},{4,6},{5,7},{6,4},{7,5},{8,10},{9,11},{10,... | collective-permute-start | bytes 7077896 | tf_op jit(solution)/shard_map/ppermute | solution.py:13
  6.7 2.1 %copy_dynamic-update-slice_fusion.1 = bf16[4,2,2304,128]{3,2,1,0:T(8,128)(2,1)S(1)} fusion(bf16[4,1,2304,128]{3,0,2,1:T(4,128)(2,1)} %bitcast.39), kind=kLoop, calls=%fused_computation.1 | loop fusion | bytes 4718592
  9.6 2.3 %dynamic-slice_bitcast_fusion = (bf16[2,2304,128]{2,1,0:T(8,128)(2,1)}, bf16[2,2304,128]{2,1,0:T(8,128)(2,1)}, bf16[2,2304,128]{2,1,0:T(8,128)(2,1)}, bf16[2,2304,128]{2,1,0:T(8,128)(2,1)}) fusion(bf16[4,2,2304,128]{3,2,1,0:T(8,128)(2,1)S(1)} %copy_dynamic-update-slice_fusion, s32[]{:T(128)S(6)} %select_n.67, s32[]{:T(128)S(6)} %select_n.66, ...), kind=kLoop, calls=%fused_computation.2 | loop fusion | bytes 9437200 | tf_op jit(solution)/shard_map/jit(dynamic_index_in_dim)/squeeze | solution.py:375
  11.9 16.1 %collective-permute-done.2.refs_2_ = bf16[256,2048]{1,0:T(8,128)(2,1)} collective-permute-done((bf16[256,2048]{1,0:T(8,128)(2,1)S(1)}, bf16[256,2048]{1,0:T(8,128)(2,1)}, u32[]{:S(2)}, u32[]{:S(2)}) %collective-permute-start.2) | collective-permute-done | bytes 1048608 | tf_op jit(solution)/shard_map/ppermute | solution.py:307
  28.0 1.4 collective-permute-done.1.refs_1_
  29.8 1.6 collective-permute-start.5
  31.4 0.7 pad_add_fusion.1.ids_ref
  32.1 11.0 %project.2.refs_4_ = f32[576,1024]{1,0:T(8,128)} custom-call(s32[2]{0:T(128)} %pad_add_fusion.1.ids_ref, bf16[576,2048]{1,0:T(8,128)(2,1)} %bitcast.43, bf16[576,2048]{1,0:T(8,128)(2,1)} %collective-permute-done.3.refs_1_, bf16[8192,1024]{1,0:T(8,128)(2,1)} %refs_3_.3, bf16[8192,1024]{1,0:T(8,128)(2,1)} %refs_3_.3), custom_call_target="tpu_custom_call" | custom-call | flops 4831838208 | bytes 15466496 | tf_op jit(solution)/shard_map/project/pallas_call | solution.py:52
  43.1 10.3 %collective-permute-done.4.refs_3_ = bf16[256,2048]{1,0:T(8,128)(2,1)S(1)} collective-permute-done((bf16[256,2048]{1,0:T(8,128)(2,1)}, bf16[256,2048]{1,0:T(8,128)(2,1)S(1)}, u32[]{:S(2)}, u32[]{:S(2)}) %collective-permute-start.4) | collective-permute-done | bytes 1048608 | tf_op jit(solution)/shard_map/ppermute | solution.py:307
  53.8 1.5 collective-permute-start.6
  55.8 1.9 %collective-permute-done.refs_0_ = bf16[576,2048]{1,0:T(8,128)(2,1)S(1)} collective-permute-done((bf16[576,2048]{1,0:T(8,128)(2,1)}, bf16[576,2048]{1,0:T(8,128)(2,1)S(1)}, u32[]{:S(2)}, u32[]{:S(2)}) %collective-permute-start) | collective-permute-done | bytes 2359328 | tf_op jit(solution)/shard_map/ppermute | solution.py:13
  57.7 18.9 %collective-permute-done.6.refs_0_ = bf16[256,2048]{1,0:T(8,128)(2,1)S(1)} collective-permute-done((bf16[256,2048]{1,0:T(8,128)(2,1)S(1)}, bf16[256,2048]{1,0:T(8,128)(2,1)S(1)}, u32[]{:S(2)}, u32[]{:S(2)}) %collective-permute-start.6) | collective-permute-done | bytes 1048608 | tf_op jit(solution)/shard_map/ppermute | solution.py:307
  76.6 1.1 collective-permute-done.7.refs_1_
  77.7 1.0 copy-done.14
  78.7 1.5 collective-permute-start.15
  80.2 1.6 collective-permute-start.9
  81.9 1.9 %slice.27 = bf16[128,2048]{1,0:T(8,128)(2,1)} slice(bf16[256,2048]{1,0:T(8,128)(2,1)} %copy-done.14), slice={[128:256], [0:2048]} | slice | bytes 1048576 | tf_op jit(solution)/shard_map/slice | solution.py:317
  84.2 0.9 reshape_tile.4.adapter_ref.refs_2_
  85.2 0.6 stack.61.starts_ref
  85.7 0.7 pad_add_fusion.2.starts_ref
  86.4 1.1 constant_dynamic-slice_fusion.2.refs_0_
  88.0 5.4 %collective-permute-done.9.refs_2_ = bf16[128,2048]{1,0:T(8,128)(2,1)S(1)} collective-permute-done((bf16[128,2048]{1,0:T(8,128)(2,1)S(1)}, bf16[128,2048]{1,0:T(8,128)(2,1)S(1)}, u32[]{:S(2)}, u32[]{:S(2)}) %collective-permute-start.9) | collective-permute-done | bytes 524320 | tf_op jit(solution)/shard_map/ppermute | solution.py:307
  93.4 1.6 collective-permute-start.13
  94.9 8.0 %rank.2.refs_4_ = f32[576,256]{1,0:T(8,128)} custom-call(s32[5]{0:T(128)} %stack.61.starts_ref, bf16[576,2048]{1,0:T(8,128)(2,1)} %bitcast.44, s32[576,1]{1,0:T(8,128)} %reshape_tile.4.adapter_ref.refs_2_, bf16[256,2048]{1,0:T(8,128)(2,1)} %copy-done.8, bf16[256,2048]{1,0:T(8,128)(2,1)} %collective-permute-done.1.refs_1_, ...), custom_call_target="tpu_custom_call" | custom-call | flops 3019898880 | bytes 7602176 | tf_op jit(solution)/shard_map/rank/pallas_call | solution.py:99
  103.0 6.3 %rank.3 = f32[576,64]{1,0:T(8,128)} custom-call(s32[3]{0:T(128)} %pad_add_fusion.2.starts_ref, bf16[576,2048]{1,0:T(8,128)(2,1)} %bitcast.45, s32[576,1]{1,0:T(8,128)} %reshape_tile.4.adapter_ref.refs_2_, bf16[256,2048]{1,0:T(8,128)(2,1)} %copy-done.13, bf16[256,2048]{1,0:T(8,128)(2,1)} %copy-done.14, bf16[128,2048]{1,0:T(8,128)(2,1)} %copy-done.19, ...), custom_call_target="tpu_custom_call" | custom-call | flops 1811939328 | bytes 5505024 | tf_op jit(solution)/shard_map/rank/pallas_call | solution.py:99
  109.3 1.8 collective-permute-done.11
  111.1 1.0 add.119
  112.1 0.6 collective-permute-start.12
  112.7 1.5 collective-permute-start.16
  114.8 0.6 pad_add_fusion.ids_ref
  115.8 6.2 %collective-permute-done.12 = f32[576,64]{1,0:T(8,128)S(1)} collective-permute-done((f32[576,64]{1,0:T(8,128)S(1)}, f32[576,64]{1,0:T(8,128)S(1)}, u32[]{:S(2)}, u32[]{:S(2)}) %collective-permute-start.12) | collective-permute-done | bytes 147488 | tf_op jit(solution)/shard_map/ppermute | solution.py:13
  122.0 0.7 add.120.rank_ref.refs_1_
  122.7 12.0 %project.3.base_ref = f32[576,1024]{1,0:T(8,128)} custom-call(s32[2]{0:T(128)} %pad_add_fusion.ids_ref, bf16[576,2048]{1,0:T(8,128)(2,1)} %copy-done.2, bf16[576,2048]{1,0:T(8,128)(2,1)} %collective-permute-done.8.refs_1_, bf16[8192,1024]{1,0:T(8,128)(2,1)} %refs_3_.3, bf16[8192,1024]{1,0:T(8,128)(2,1)} %refs_3_.3, f32[576,1024]{1,0:T(8,128)} %project.2.refs_4_), custom_call_target="tpu_custom_call" | custom-call | flops 4831838208 | bytes 15466496 | tf_op jit(solution)/shard_map/project/pallas_call | solution.py:52
  134.8 1.5 collective-permute-start.18
  136.9 0.7 concatenate.9.scalars_ref
  137.5 0.8 copy.21.refs_7_
  138.3 11.1 %collective-permute-done.18.refs_3_ = bf16[256,1024]{1,0:T(8,128)(2,1)S(1)} collective-permute-done((bf16[256,1024]{1,0:T(8,128)(2,1)}, bf16[256,1024]{1,0:T(8,128)(2,1)S(1)}, u32[]{:S(2)}, u32[]{:S(2)}) %collective-permute-start.18) | collective-permute-done | bytes 524320 | tf_op jit(solution)/shard_map/ppermute | solution.py:307
  149.4 1.2 collective-permute-done.19.refs_4_
  150.6 0.6 collective-permute-start.21
  151.4 1.3 collective-permute-start.20
  152.7 1.9 %constant_dynamic-slice_fusion = (bf16[3,192,1,128]{3,2,1,0:T(2,128)(2,1)S(1)}, bf16[3,192,1,128]{3,2,1,0:T(2,128)(2,1)S(1)}) fusion(bf16[3,192,4,128]{3,2,1,0:T(4,128)(2,1)} %param.17, s32[]{:T(128)S(6)} %select_n.69, bf16[3,192,4,128]{3,2,1,0:T(4,128)(2,1)} %param.16), kind=kLoop, calls=%fused_computation.8 | loop fusion | bytes 589828 | tf_op jit(solution)/shard_map/jit(dynamic_index_in_dim)/dynamic_slice | solution.py:432
  154.6 0.7 copy.28
  155.2 0.7 copy.29
  155.9 6.4 %delta.1.refs_0_ = f32[576,1024]{1,0:T(8,128)} custom-call(s32[5]{0:T(128)} %stack.61.starts_ref, f32[576,1024]{1,0:T(8,128)} %project.3.base_ref, f32[576,64]{1,0:T(8,128)} %add.120.rank_ref.refs_1_, s32[576,1]{1,0:T(8,128)} %reshape_tile.4.adapter_ref.refs_2_, bf16[256,1024]{1,0:T(8,128)(2,1)} %copy-done.4, bf16[256,1024]{1,0:T(8,128)(2,1)} %copy-done.10, ...), custom_call_target="tpu_custom_call" | custom-call | flops 1509949440 | bytes 7340032 | tf_op jit(solution)/shard_map/delta/pallas_call | solution.py:145
  162.4 1.0 copy-done.5
  163.6 19.4 %attend.1 = bf16[3,192,1024]{2,1,0:T(8,128)(2,1)} custom-call(s32[7]{0:T(128)} %concatenate.9.scalars_ref, f32[576,1024]{1,0:T(8,128)} %delta.1.refs_0_, f32[576,64]{1,0:T(8,128)} %add.120.rank_ref.refs_1_, s32[576,1]{1,0:T(8,128)} %reshape_tile.4.adapter_ref.refs_2_, bf16[256,1024]{1,0:T(8,128)(2,1)} %copy-done.6, bf16[256,1024]{1,0:T(8,128)(2,1)} %copy-done.7, ...), custom_call_target="tpu_custom_call" | custom-call | flops 481296384 | bytes 7077888 | tf_op jit(solution)/shard_map/attend/pallas_call | solution.py:280
  (68 shorter events, 5.7 us)
Async XLA Ops:
  0.0 1.6 copy-start
  0.0 29.4 %collective-permute-start.3 = (bf16[576,2048]{1,0:T(8,128)(2,1)}, bf16[576,2048]{1,0:T(8,128)(2,1)}, u32[]{:S(2)}, u32[]{:S(2)}) collective-permute-start(bf16[576,2048]{1,0:T(8,128)(2,1)} %bitcast.41), channel_id=1, source_target_pairs={{0,1},{1,0},{2,3},{3,2},{4,5},{5,4},{6,7},{7,6},{8,9},{9,8},{10,11... | collective-permute-start | bytes 7077896 | tf_op jit(solution)/shard_map/ppermute | solution.py:13
  1.7 7.2 %copy-start.8 = (bf16[256,2048]{1,0:T(8,128)(2,1)}, bf16[256,2048]{1,0:T(8,128)(2,1)S(1)}, u32[]{:S(2)}) copy-start(bf16[256,2048]{1,0:T(8,128)(2,1)S(1)} %constant_dynamic-slice_fusion.3.refs_0_) | copy-start | bytes 3145732
  1.7 26.3 %collective-permute-start.2 = (bf16[256,2048]{1,0:T(8,128)(2,1)S(1)}, bf16[256,2048]{1,0:T(8,128)(2,1)}, u32[]{:S(2)}, u32[]{:S(2)}) collective-permute-start(bf16[256,2048]{1,0:T(8,128)(2,1)S(1)} %constant_dynamic-slice_fusion.3.refs_0_), channel_id=1, source_target_pairs={{0,16},{4,0},{8,4},{12,8},{28,12},{24,28},{20,24},{16,20},{1,17},{... | collective-permute-start | bytes 3145736 | tf_op jit(solution)/shard_map/ppermute | solution.py:307
  4.7 24.7 %collective-permute-start.1 = (bf16[256,2048]{1,0:T(8,128)(2,1)S(1)}, bf16[256,2048]{1,0:T(8,128)(2,1)}, u32[]{:S(2)}, u32[]{:S(2)}) collective-permute-start(bf16[256,2048]{1,0:T(8,128)(2,1)S(1)} %constant_dynamic-slice_fusion.3.refs_0_), channel_id=1, source_target_pairs={{0,4},{4,8},{8,12},{12,28},{28,24},{24,20},{20,16},{16,0},{1,5},{5... | collective-permute-start | bytes 3145736 | tf_op jit(solution)/shard_map/ppermute | solution.py:307
  4.8 52.9 %collective-permute-start = (bf16[576,2048]{1,0:T(8,128)(2,1)}, bf16[576,2048]{1,0:T(8,128)(2,1)S(1)}, u32[]{:S(2)}, u32[]{:S(2)}) collective-permute-start(bf16[576,2048]{1,0:T(8,128)(2,1)} %bitcast.42), channel_id=1, source_target_pairs={{0,2},{1,3},{2,0},{3,1},{4,6},{5,7},{6,4},{7,5},{8,10},{9,11},{10,... | collective-permute-start | bytes 7077896 | tf_op jit(solution)/shard_map/ppermute | solution.py:13
  6.7 2.4 %copy-start.3 = (bf16[192,4,12,128]{3,1,2,0:T(4,128)(2,1)S(1)}, bf16[192,4,12,128]{3,1,2,0:T(4,128)(2,1)}, u32[]{:S(2)}) copy-start(bf16[192,4,12,128]{3,1,2,0:T(4,128)(2,1)} %param.15) | copy-start | bytes 7077892
  29.4 23.9 %collective-permute-start.4 = (bf16[256,2048]{1,0:T(8,128)(2,1)}, bf16[256,2048]{1,0:T(8,128)(2,1)S(1)}, u32[]{:S(2)}, u32[]{:S(2)}) collective-permute-start(bf16[256,2048]{1,0:T(8,128)(2,1)} %collective-permute-done.1.refs_1_), channel_id=1, source_target_pairs={{0,4},{4,8},{8,12},{12,28},{28,24},{24,20},{20,16},{16,0},{1,5},{5... | collective-permute-start | bytes 3145736 | tf_op jit(solution)/shard_map/ppermute | solution.py:307
  29.8 24.0 %collective-permute-start.5 = (bf16[256,2048]{1,0:T(8,128)(2,1)}, bf16[256,2048]{1,0:T(8,128)(2,1)S(1)}, u32[]{:S(2)}, u32[]{:S(2)}) collective-permute-start(bf16[256,2048]{1,0:T(8,128)(2,1)} %collective-permute-done.2.refs_2_), channel_id=1, source_target_pairs={{0,16},{4,0},{8,4},{12,8},{28,12},{24,28},{20,24},{16,20},{1,17},{... | collective-permute-start | bytes 3145736 | tf_op jit(solution)/shard_map/ppermute | solution.py:307
  32.1 52.1 %copy-start.16 = (s32[192]{0:T(256)S(1)}, s32[192]{0:T(256)}, u32[]{:S(2)}) copy-start(s32[192]{0:T(256)} %param.19) | copy-start | bytes 2308
  53.3 26.9 %copy-start.17 = (bf16[256,2048]{1,0:T(8,128)(2,1)}, bf16[256,2048]{1,0:T(8,128)(2,1)S(1)}, u32[]{:S(2)}) copy-start(bf16[256,2048]{1,0:T(8,128)(2,1)S(1)} %collective-permute-done.4.refs_3_) | copy-start | bytes 3145732
  53.8 26.5 %copy-start.18 = (bf16[256,2048]{1,0:T(8,128)(2,1)}, bf16[256,2048]{1,0:T(8,128)(2,1)S(1)}, u32[]{:S(2)}) copy-start(bf16[256,2048]{1,0:T(8,128)(2,1)S(1)} %collective-permute-done.5.refs_4_) | copy-start | bytes 3145732
  53.8 22.8 %collective-permute-start.6 = (bf16[256,2048]{1,0:T(8,128)(2,1)S(1)}, bf16[256,2048]{1,0:T(8,128)(2,1)S(1)}, u32[]{:S(2)}, u32[]{:S(2)}) collective-permute-start(bf16[256,2048]{1,0:T(8,128)(2,1)S(1)} %collective-permute-done.4.refs_3_), channel_id=1, source_target_pairs={{0,4},{4,8},{8,12},{12,28},{28,24},{24,20},{20,16},{16,0},{1,5},{5... | collective-permute-start | bytes 3145736 | tf_op jit(solution)/shard_map/ppermute | solution.py:307
  55.3 22.4 %collective-permute-start.7 = (bf16[256,2048]{1,0:T(8,128)(2,1)S(1)}, bf16[256,2048]{1,0:T(8,128)(2,1)S(1)}, u32[]{:S(2)}, u32[]{:S(2)}) collective-permute-start(bf16[256,2048]{1,0:T(8,128)(2,1)S(1)} %collective-permute-done.5.refs_4_), channel_id=1, source_target_pairs={{0,16},{4,0},{8,4},{12,8},{28,12},{24,28},{20,24},{16,20},{1,17},{... | collective-permute-start | bytes 3145736 | tf_op jit(solution)/shard_map/ppermute | solution.py:307
  57.7 45.2 %copy-start.2 = (bf16[576,2048]{1,0:T(8,128)(2,1)}, bf16[576,2048]{1,0:T(8,128)(2,1)S(1)}, u32[]{:S(2)}) copy-start(bf16[576,2048]{1,0:T(8,128)(2,1)S(1)} %collective-permute-done.refs_0_) | copy-start | bytes 7077892
  76.6 3.6 %copy-start.13 = (bf16[256,2048]{1,0:T(8,128)(2,1)}, bf16[256,2048]{1,0:T(8,128)(2,1)S(1)}, u32[]{:S(2)}) copy-start(bf16[256,2048]{1,0:T(8,128)(2,1)S(1)} %collective-permute-done.6.refs_0_) | copy-start | bytes 3145732
  77.7 1.0 copy-start.14
  77.7 45.1 %collective-permute-start.8 = (bf16[576,2048]{1,0:T(8,128)(2,1)S(1)}, bf16[576,2048]{1,0:T(8,128)(2,1)}, u32[]{:S(2)}, u32[]{:S(2)}) collective-permute-start(bf16[576,2048]{1,0:T(8,128)(2,1)S(1)} %collective-permute-done.refs_0_), channel_id=1, source_target_pairs={{0,1},{1,0},{2,3},{3,2},{4,5},{5,4},{6,7},{7,6},{8,9},{9,8},{10,11... | collective-permute-start | bytes 7077896 | tf_op jit(solution)/shard_map/ppermute | solution.py:13
  78.7 34.0 %collective-permute-start.15 = (bf16[2,2304,128]{2,1,0:T(8,128)(2,1)}, bf16[2,2304,128]{2,1,0:T(8,128)(2,1)}, u32[]{:S(2)}, u32[]{:S(2)}) collective-permute-start(bf16[2,2304,128]{2,1,0:T(8,128)(2,1)} %get-tuple-element.34), channel_id=1, source_target_pairs={{0,2},{1,3},{2,0},{3,1},{4,6},{5,7},{6,4},{7,5},{8,10},{9,11},{10,... | collective-permute-start | bytes 3538952 | tf_op jit(solution)/shard_map/ppermute | solution.py:13
  80.2 13.1 %collective-permute-start.9 = (bf16[128,2048]{1,0:T(8,128)(2,1)S(1)}, bf16[128,2048]{1,0:T(8,128)(2,1)S(1)}, u32[]{:S(2)}, u32[]{:S(2)}) collective-permute-start(bf16[128,2048]{1,0:T(8,128)(2,1)S(1)} %slice.26), channel_id=1, source_target_pairs={{0,4},{4,8},{8,12},{12,28},{28,24},{24,20},{20,16},{16,0},{1,5},{5... | collective-permute-start | bytes 1572872 | tf_op jit(solution)/shard_map/ppermute | solution.py:307
  83.8 19.2 %collective-permute-start.10 = (bf16[128,2048]{1,0:T(8,128)(2,1)}, bf16[128,2048]{1,0:T(8,128)(2,1)}, u32[]{:S(2)}, u32[]{:S(2)}) collective-permute-start(bf16[128,2048]{1,0:T(8,128)(2,1)} %slice.27), channel_id=1, source_target_pairs={{0,16},{4,0},{8,4},{12,8},{28,12},{24,28},{20,24},{16,20},{1,17},{... | collective-permute-start | bytes 1572872 | tf_op jit(solution)/shard_map/ppermute | solution.py:307
  87.5 15.5 %copy-start.4 = (bf16[256,1024]{1,0:T(8,128)(2,1)}, bf16[256,1024]{1,0:T(8,128)(2,1)S(1)}, u32[]{:S(2)}) copy-start(bf16[256,1024]{1,0:T(8,128)(2,1)S(1)} %constant_dynamic-slice_fusion.2.refs_0_) | copy-start | bytes 1572868
  87.5 25.2 %collective-permute-start.14 = (bf16[256,1024]{1,0:T(8,128)(2,1)S(1)}, bf16[256,1024]{1,0:T(8,128)(2,1)S(1)}, u32[]{:S(2)}, u32[]{:S(2)}) collective-permute-start(bf16[256,1024]{1,0:T(8,128)(2,1)S(1)} %constant_dynamic-slice_fusion.2.refs_0_), channel_id=1, source_target_pairs={{0,16},{4,0},{8,4},{12,8},{28,12},{24,28},{20,24},{16,20},{1,17},{... | collective-permute-start | bytes 1572872 | tf_op jit(solution)/shard_map/ppermute | solution.py:307
  93.4 9.6 %copy-start.19 = (bf16[128,2048]{1,0:T(8,128)(2,1)}, bf16[128,2048]{1,0:T(8,128)(2,1)S(1)}, u32[]{:S(2)}) copy-start(bf16[128,2048]{1,0:T(8,128)(2,1)S(1)} %collective-permute-done.9.refs_2_) | copy-start | bytes 1572868
  93.4 19.3 %collective-permute-start.13 = (bf16[256,1024]{1,0:T(8,128)(2,1)S(1)}, bf16[256,1024]{1,0:T(8,128)(2,1)S(1)}, u32[]{:S(2)}, u32[]{:S(2)}) collective-permute-start(bf16[256,1024]{1,0:T(8,128)(2,1)S(1)} %constant_dynamic-slice_fusion.2.refs_0_), channel_id=1, source_target_pairs={{0,4},{4,8},{8,12},{12,28},{28,24},{24,20},{20,16},{16,0},{1,5},{5... | collective-permute-start | bytes 1572872 | tf_op jit(solution)/shard_map/ppermute | solution.py:307
  109.3 1.8 collective-permute-start.11
  112.1 9.9 %collective-permute-start.12 = (f32[576,64]{1,0:T(8,128)S(1)}, f32[576,64]{1,0:T(8,128)S(1)}, u32[]{:S(2)}, u32[]{:S(2)}) collective-permute-start(f32[576,64]{1,0:T(8,128)S(1)} %add.119), channel_id=1, source_target_pairs={{0,2},{1,3},{2,0},{3,1},{4,6},{5,7},{6,4},{7,5},{8,10},{9,11},{10,... | collective-permute-start | bytes 442376 | tf_op jit(solution)/shard_map/ppermute | solution.py:13
  112.7 22.1 %copy-start.9 = (bf16[256,1024]{1,0:T(8,128)(2,1)}, bf16[256,1024]{1,0:T(8,128)(2,1)S(1)}, u32[]{:S(2)}) copy-start(bf16[256,1024]{1,0:T(8,128)(2,1)S(1)} %collective-permute-done.14.refs_2_) | copy-start | bytes 1572868
  112.7 22.1 %copy-start.10 = (bf16[256,1024]{1,0:T(8,128)(2,1)}, bf16[256,1024]{1,0:T(8,128)(2,1)S(1)}, u32[]{:S(2)}) copy-start(bf16[256,1024]{1,0:T(8,128)(2,1)S(1)} %collective-permute-done.13.refs_1_) | copy-start | bytes 1572868
  112.7 22.1 %collective-permute-start.16 = (bf16[256,1024]{1,0:T(8,128)(2,1)S(1)}, bf16[256,1024]{1,0:T(8,128)(2,1)}, u32[]{:S(2)}, u32[]{:S(2)}) collective-permute-start(bf16[256,1024]{1,0:T(8,128)(2,1)S(1)} %collective-permute-done.13.refs_1_), channel_id=1, source_target_pairs={{0,4},{4,8},{8,12},{12,28},{28,24},{24,20},{20,16},{16,0},{1,5},{5... | collective-permute-start | bytes 1572872 | tf_op jit(solution)/shard_map/ppermute | solution.py:307
  114.2 20.6 %collective-permute-start.17 = (bf16[256,1024]{1,0:T(8,128)(2,1)S(1)}, bf16[256,1024]{1,0:T(8,128)(2,1)}, u32[]{:S(2)}, u32[]{:S(2)}) collective-permute-start(bf16[256,1024]{1,0:T(8,128)(2,1)S(1)} %collective-permute-done.14.refs_2_), channel_id=1, source_target_pairs={{0,16},{4,0},{8,4},{12,8},{28,12},{24,28},{20,24},{16,20},{1,17},{... | collective-permute-start | bytes 1572872 | tf_op jit(solution)/shard_map/ppermute | solution.py:307
  115.4 46.9 %collective-permute-start.23 = (bf16[2,2304,128]{2,1,0:T(8,128)(2,1)}, bf16[2,2304,128]{2,1,0:T(8,128)(2,1)S(1)}, u32[]{:S(2)}, u32[]{:S(2)}) collective-permute-start(bf16[2,2304,128]{2,1,0:T(8,128)(2,1)} %get-tuple-element.42), channel_id=1, source_target_pairs={{0,3},{1,2},{2,1},{3,0},{4,7},{5,6},{6,5},{7,4},{8,11},{9,10},{10,... | collective-permute-start | bytes 3538952 | tf_op jit(solution)/shard_map/ppermute | solution.py:13
  122.7 14.8 %copy-start.15 = (s32[192]{0:T(256)S(1)}, s32[192]{0:T(256)}, u32[]{:S(2)}) copy-start(s32[192]{0:T(256)} %param.18) | copy-start | bytes 2308
  122.7 39.6 %collective-permute-start.22 = (bf16[2,2304,128]{2,1,0:T(8,128)(2,1)}, bf16[2,2304,128]{2,1,0:T(8,128)(2,1)}, u32[]{:S(2)}, u32[]{:S(2)}) collective-permute-start(bf16[2,2304,128]{2,1,0:T(8,128)(2,1)} %get-tuple-element.41), channel_id=1, source_target_pairs={{0,1},{1,0},{2,3},{3,2},{4,5},{5,4},{6,7},{7,6},{8,9},{9,8},{10,11... | collective-permute-start | bytes 3538952 | tf_op jit(solution)/shard_map/ppermute | solution.py:13
  134.8 14.6 %collective-permute-start.18 = (bf16[256,1024]{1,0:T(8,128)(2,1)}, bf16[256,1024]{1,0:T(8,128)(2,1)S(1)}, u32[]{:S(2)}, u32[]{:S(2)}) collective-permute-start(bf16[256,1024]{1,0:T(8,128)(2,1)} %collective-permute-done.16.refs_3_), channel_id=1, source_target_pairs={{0,4},{4,8},{8,12},{12,28},{28,24},{24,20},{20,16},{16,0},{1,5},{5... | collective-permute-start | bytes 1572872 | tf_op jit(solution)/shard_map/ppermute | solution.py:307
  136.3 14.3 %collective-permute-start.19 = (bf16[256,1024]{1,0:T(8,128)(2,1)}, bf16[256,1024]{1,0:T(8,128)(2,1)S(1)}, u32[]{:S(2)}, u32[]{:S(2)}) collective-permute-start(bf16[256,1024]{1,0:T(8,128)(2,1)} %collective-permute-done.17.refs_4_), channel_id=1, source_target_pairs={{0,16},{4,0},{8,4},{12,8},{28,12},{24,28},{20,24},{16,20},{1,17},{... | collective-permute-start | bytes 1572872 | tf_op jit(solution)/shard_map/ppermute | solution.py:307
  149.4 1.9 %copy-start.6 = (bf16[256,1024]{1,0:T(8,128)(2,1)}, bf16[256,1024]{1,0:T(8,128)(2,1)S(1)}, u32[]{:S(2)}) copy-start(bf16[256,1024]{1,0:T(8,128)(2,1)S(1)} %collective-permute-done.18.refs_3_) | copy-start | bytes 1572868
  150.6 0.8 copy-start.7
  150.6 11.7 %collective-permute-start.21 = (bf16[128,1024]{1,0:T(8,128)(2,1)S(1)}, bf16[128,1024]{1,0:T(8,128)(2,1)S(1)}, u32[]{:S(2)}, u32[]{:S(2)}) collective-permute-start(bf16[128,1024]{1,0:T(8,128)(2,1)S(1)} %slice.25), channel_id=1, source_target_pairs={{0,16},{4,0},{8,4},{12,8},{28,12},{24,28},{20,24},{16,20},{1,17},{... | collective-permute-start | bytes 786440 | tf_op jit(solution)/shard_map/ppermute | solution.py:307
  151.4 11.0 %collective-permute-start.20 = (bf16[128,1024]{1,0:T(8,128)(2,1)S(1)}, bf16[128,1024]{1,0:T(8,128)(2,1)S(1)}, u32[]{:S(2)}, u32[]{:S(2)}) collective-permute-start(bf16[128,1024]{1,0:T(8,128)(2,1)S(1)} %slice.24), channel_id=1, source_target_pairs={{0,4},{4,8},{8,12},{12,28},{28,24},{24,20},{20,16},{16,0},{1,5},{5... | collective-permute-start | bytes 786440 | tf_op jit(solution)/shard_map/ppermute | solution.py:307
  162.3 1.0 copy-start.5
  162.3 1.1 copy-start.11
  162.4 1.2 copy-start.12
  163.6 19.4 %copy-start.1 = (bf16[8,2048,64]{1,2,0:T(8,128)(2,1)S(1)}, bf16[8,2048,64]{1,2,0:T(8,128)(2,1)}, u32[]{:S(2)}) copy-start(bf16[8,2048,64]{1,2,0:T(8,128)(2,1)} %param.12) | copy-start | bytes 6291460

commit v4 on v3

--- a/solution.py
+++ b/solution.py
@@ -213,7 +213,7 @@
         ones = jnp.ones((columns, head_size), jnp.bfloat16)
         fresh_key_all = fresh_key_ref[...].astype(jnp.float32)
         fresh_value_all = fresh_value_ref[...].astype(jnp.float32)
-        outputs = []
+        scores, values, seen = [], [], []
         for first in range(0, bundle, slab):
             begin = pl.multiple_of(step * bundle + first, slab)
             slabs = [
@@ -240,29 +240,44 @@
                 keys = jnp.concatenate(
                     [ref[0, there, :] for ref in cache_refs] + [new_keys, padding], axis=0
                 )
-                values = jnp.concatenate(
+                own_values = jnp.concatenate(
                     [ref[1, there, :] for ref in cache_refs] + [new_values, padding], axis=0
                 )
-                values = jnp.concatenate([values, ones], axis=1)
-                scores = lax.dot_general(
-                    queries, keys, (((1,), (1,)), ((), ())), preferred_element_type=jnp.float32
-                ).reshape(steps, heads // pack, slab, columns)
+                values.append(jnp.concatenate([own_values, ones], axis=1))
+                scores.append(
+                    lax.dot_general(
+                        queries, keys, (((1,), (1,)), ((), ())), preferred_element_type=jnp.float32
+                    ).reshape(steps, heads // pack, slab, columns)
+                )
                 length = jnp.concatenate([length_all[mine]] * pack, axis=0)
                 cached_seen = place < length
                 fresh_seen = is_fresh & (fresh_row == own + part * sub)
-                raised = []
-                for s in range(steps):
-                    seen = cached_seen | (fresh_seen & (fresh_step <= s))
-                    bias = jnp.where(seen, 0.0, -1e30)
-                    shifted = scores[s] * scale + bias[None]
-                    shifted = shifted - jnp.max(shifted, axis=-1, keepdims=True)
-                    raised.append(jnp.exp(shifted).reshape(heads // pack * slab, columns))
-                sums = jnp.dot(
-                    jnp.concatenate(raised, axis=0).astype(jnp.bfloat16),
-                    values,
-                    preferred_element_type=jnp.float32,
+                seen.append(
+                    [
+                        jnp.where(cached_seen | (fresh_seen & (fresh_step <= s)), 0.0, -1e30)
+                        for s in range(steps)
+                    ]
                 )
-                outputs.append(sums[:, :head_size] / sums[:, head_size:])
+        shifted = [
+            [score[s] * scale + bias[s][None] for s in range(steps)]
+            for score, bias in zip(scores, seen)
+        ]
+        top = [[jnp.max(part, axis=-1, keepdims=True) for part in parts] for parts in shifted]
+        raised = [
+            jnp.concatenate(
+                [
+                    jnp.exp(part - most).reshape(heads // pack * slab, columns)
+                    for part, most in zip(parts, tops)
+                ],
+                axis=0,
+            ).astype(jnp.bfloat16)
+            for parts, tops in zip(shifted, top)
+        ]
+        sums = [
+            jnp.dot(weights, value, preferred_element_type=jnp.float32)
+            for weights, value in zip(raised, values)
+        ]
+        outputs = [both[:, :head_size] / both[:, head_size:] for both in sums]
         for s in range(steps):
             for h in range(heads):
                 start = (s * heads + h) * sub
@@ -375,8 +390,7 @@
             [lax.dynamic_index_in_dim(both, ids[j], 0, keepdims=False) for j in range(count)]
         )
         base = project_pair(ids[:2], [flat_tokens], [near], query_weight)
-        second = swap(gate(parcels[2], near, down[0]), 2, count)
-        waits = {2: [near, parcels], 3: [base]}
+        waits = {2: [near, parcels, base]}
     else:
         all_tokens = lax.all_gather(flat_tokens, "tensor", axis=1, tiled=True)
         base = jnp.dot(all_tokens, query_weight, preferred_element_type=jnp.float32)
@@ -396,30 +410,36 @@
         if k == owners:
             groups = [[own_down]] + [[part] for pair in down[: owners - 2] for part in pair]
             ranks = add_ranks(starts[:early], flat_tokens, row_adapters, groups, rank)
+            if paired:
+                far = gate(far, down[1])
+                far_near = swap(far, 1, count)
+                second = swap(gate(parcels[2], far), 2, count)
+                both_far = gate((far, far_near), ranks)
+                base = project_pair(ids[2:], [both_far[0]], [both_far[1]], query_weight, base)
+                waits[owners] = [base]
         if k in waits:
             before, after = gate((before, after), *waits[k])
         down.append(ring_step(k, before, after, owners))
     if paired:
-        far = gate(far, down[owners - 2])
-        far_near = swap(far, 1, count)
-        third = swap(gate(parcels[3], far), 3, count)
         first = swap(gate(parcels[1], far_near), 1, count)
+        third = swap(gate(parcels[3], second, first), 3, count)
         key_values = [parcels[0], first, second, third]
-        base = project_pair(ids[2:], [far], [far_near], query_weight, base)
 
     groups = [[part] for part in down[owners - 2]] + [list(down[owners - 1])]
     ranks = add_ranks(
         starts[early:], flat_tokens, row_adapters, groups, rank, earlier=ranks, last=True
     )
 
-    own_up = gate(own_up, down[owners - 2])
+    own_up = gate(own_up, down[owners - 2], base)
     up = [ring_step(1, own_up, own_up, owners)]
-    waits = {2: [ranks] + ([second] if paired else [])}
+    waits = {2: [ranks]}
     bit = 1
     while bit < count:
         ranks = ranks + swap(ranks, bit, count)
         bit *= 2
-    waits[3] = [ranks, base]
+    waits[3] = [ranks]
+    if paired:
+        waits[owners] = [third]
     for k in range(2, owners + 1):
         up.append(ring_step(k, *gate(up[-1], *waits.get(k, [])), owners))
 

time: 184 us -> 167 us (0.908)
  waiting for transfers between devices: 75.7 us -> 66.2 us
  Pallas kernels: 63.1 us -> 54.4 us
  local copies, waits for them, and re-layouts: 17.9 us -> 21.3 us
  starting transfers between devices: 22.3 us -> 20.3 us
    ppermute x16, waiting for transfers between devices: 65.9 us -> 34 us  [ring_hop(): return lax.ppermute(array, ('rep', 'dp'), pairs)]
    ppermute x8, waiting for transfers between devices: 9.9 us -> 32.2 us  [swap(): return lax.ppermute(array, 'tensor', [(i, i ^ bit) for i in range(count)])]
    pallas_call x1, Pallas kernels: 19.4 us -> 10.7 us  [attend(): pl.pallas_call(kernel, out_shape=jax.ShapeDtypeStruct((steps, rows, width...]
    squeeze x1, local copies, waits for them, and re-layouts: 2.29 us -> 4.19 us  [body(): lax.dynamic_index_in_dim(both, ids[j], 0, keepdims=False)]
    slice x4, local copies, waits for them, and re-layouts: 1.96 us -> 3.81 us  [ring_step(): before, after = (before[:rows], after[rows:])]
    unnamed x43 -> x35, local copies, waits for them, and re-layouts: 7.23 us -> 5.69 us
  transfers between devices with their start and end apart: 24 -> 24, of which waited for: 12 -> 15; matrix products, arithmetic and copies ran while one was open for 10% -> 14% of each run, Pallas kernels for 24% -> 26%
where the time goes in v4:
time: 167 us; the launch traced here: 166 us
  waiting for transfers between devices  66.2 us (40%)
  Pallas kernels  54.4 us (33%)
  local copies, waits for them, and re-layouts  21.3 us (13%)
  starting transfers between devices  20.3 us (12%)
  other arithmetic  3.55 us (2%)
    ppermute x16, waiting for transfers between devices, ring_hop(): return lax.ppermute(array, ('rep', 'dp'), pairs)  34 us
    ppermute x8, waiting for transfers between devices, swap(): return lax.ppermute(array, 'tensor', [(i, i ^ bit) for i in range(count)])  32.2 us
    pallas_call x2, Pallas kernels, project_pair(): pl.pallas_call(kernel, out_shape=jax.ShapeDtypeStruct((rows, columns), jn...  22.9 us
    ppermute x16, starting transfers between devices, ring_hop(): return lax.ppermute(array, ('rep', 'dp'), pairs)  16.6 us
    pallas_call x2, Pallas kernels, add_ranks(): pl.pallas_call(kernel, out_shape=jax.ShapeDtypeStruct((rows, out_width),...  14.3 us
    pallas_call x1, Pallas kernels, attend(): pl.pallas_call(kernel, out_shape=jax.ShapeDtypeStruct((steps, rows, width...  10.7 us
    pallas_call x1, Pallas kernels, early_query(): pl.pallas_call(kernel, out_shape=jax.ShapeDtypeStruct((rows, columns), jn...  6.38 us
    unnamed x35, local copies, waits for them, and re-layouts  5.69 us
  transfers between devices with their start and end apart: 24, of which 15 were waited for; matrix products, arithmetic and copies ran while one was open for 14% of the time, Pallas kernels for 26%

profile of v4, /device:TPU:0, one launch (start us, length us, event | category | flops | bytes accessed | tf_op | source)
XLA Modules:
  0.0 166.1 jit_solution(8342375389557051200)
XLA Ops:
  0.0 2.9 %collective-permute-start = (bf16[576,2048]{1,0:T(8,128)(2,1)}, bf16[576,2048]{1,0:T(8,128)(2,1)}, u32[]{:S(2)}, u32[]{:S(2)}) collective-permute-start(bf16[576,2048]{1,0:T(8,128)(2,1)} %bitcast.41), channel_id=1, source_target_pairs={{0,2},{1,3},{2,0},{3,1},{4,6},{5,7},{6,4},{7,5},{8,10},{9,11},{10,... | collective-permute-start | bytes 7077896 | tf_op jit(solution)/shard_map/ppermute | solution.py:13
  2.9 1.0 constant_dynamic-slice_fusion.3.refs_0_
  4.0 1.7 %collective-permute-start.1 = (bf16[256,2048]{1,0:T(8,128)(2,1)}, bf16[256,2048]{1,0:T(8,128)(2,1)S(1)}, u32[]{:S(2)}, u32[]{:S(2)}) collective-permute-start(bf16[256,2048]{1,0:T(8,128)(2,1)} %constant_dynamic-slice_fusion.3.refs_0_), channel_id=1, source_target_pairs={{0,4},{4,8},{8,12},{12,28},{28,24},{24,20},{20,16},{16,0},{1,5},{5... | collective-permute-start | bytes 3145736 | tf_op jit(solution)/shard_map/ppermute | solution.py:322
  6.0 3.5 %copy_dynamic-update-slice_fusion.1 = bf16[4,2,2304,128]{3,2,1,0:T(8,128)(2,1)} fusion(bf16[4,1,2304,128]{3,0,2,1:T(4,128)(2,1)} %bitcast.39), kind=kLoop, calls=%fused_computation.1 | loop fusion | bytes 4718592
  9.6 1.7 %copy_dynamic-update-slice_fusion = bf16[4,2,2304,128]{3,2,1,0:T(8,128)(2,1)} fusion(bf16[4,2,2304,128]{3,2,1,0:T(8,128)(2,1)} %copy_dynamic-update-slice_fusion.1, bf16[4,1,2304,128]{3,0,2,1:T(4,128)(2,1)S(1)} %bitcast.40), kind=kLoop, calls=%fused_computation | loop fusion | bytes 4718592 | tf_op jit(solution)/shard_map/stack | solution.py:381
  11.3 4.2 %dynamic-slice_bitcast_fusion = (bf16[2,2304,128]{2,1,0:T(8,128)(2,1)S(1)}, bf16[2,2304,128]{2,1,0:T(8,128)(2,1)}, bf16[2,2304,128]{2,1,0:T(8,128)(2,1)}, bf16[2,2304,128]{2,1,0:T(8,128)(2,1)}) fusion(bf16[4,2,2304,128]{3,2,1,0:T(8,128)(2,1)} %copy_dynamic-update-slice_fusion, s32[]{:T(128)S(6)} %select_n.67, s32[]{:T(128)S(6)} %select_n.66, ...), kind=kLoop, calls=%fused_computation.2 | loop fusion | bytes 9437200 | tf_op jit(solution)/shard_map/jit(dynamic_index_in_dim)/squeeze | solution.py:390
  15.5 0.7 pad_add_fusion.1.ids_ref
  16.1 10.9 %project.2.refs_4_ = f32[576,1024]{1,0:T(8,128)} custom-call(s32[2]{0:T(128)} %pad_add_fusion.1.ids_ref, bf16[576,2048]{1,0:T(8,128)(2,1)} %bitcast.43, bf16[576,2048]{1,0:T(8,128)(2,1)} %collective-permute-done.3.refs_1_, bf16[8192,1024]{1,0:T(8,128)(2,1)} %refs_3_.3, bf16[8192,1024]{1,0:T(8,128)(2,1)} %refs_3_.3), custom_call_target="tpu_custom_call" | custom-call | flops 4831838208 | bytes 15466496 | tf_op jit(solution)/shard_map/project/pallas_call | solution.py:52
  27.0 2.7 %collective-permute-done.1.refs_1_ = bf16[256,2048]{1,0:T(8,128)(2,1)S(1)} collective-permute-done((bf16[256,2048]{1,0:T(8,128)(2,1)}, bf16[256,2048]{1,0:T(8,128)(2,1)S(1)}, u32[]{:S(2)}, u32[]{:S(2)}) %collective-permute-start.1) | collective-permute-done | bytes 1048608 | tf_op jit(solution)/shard_map/ppermute | solution.py:322
  29.8 1.3 collective-permute-done.2.refs_2_
  31.1 1.6 collective-permute-start.4
  33.1 21.4 %collective-permute-done.refs_0_ = bf16[576,2048]{1,0:T(8,128)(2,1)} collective-permute-done((bf16[576,2048]{1,0:T(8,128)(2,1)}, bf16[576,2048]{1,0:T(8,128)(2,1)}, u32[]{:S(2)}, u32[]{:S(2)}) %collective-permute-start) | collective-permute-done | bytes 2359328 | tf_op jit(solution)/shard_map/ppermute | solution.py:13
  54.5 1.2 collective-permute-done.4.refs_3_
  55.7 1.3 collective-permute-done.5.refs_4_
  57.0 1.6 collective-permute-start.7
  59.2 1.0 reshape_tile.4.adapter_ref.refs_2_
  60.2 0.7 stack.61.starts_ref
  61.9 8.0 %rank.2.refs_4_ = f32[576,256]{1,0:T(8,128)} custom-call(s32[5]{0:T(128)} %stack.61.starts_ref, bf16[576,2048]{1,0:T(8,128)(2,1)} %bitcast.44, s32[576,1]{1,0:T(8,128)} %reshape_tile.4.adapter_ref.refs_2_, bf16[256,2048]{1,0:T(8,128)(2,1)} %constant_dynamic-slice_fusion.3.refs_0_, bf16[256,2048]{1,0:T(8,128)(2,1)} %copy-done.14, ...), custom_call_target="tpu_custom_call" | custom-call | flops 3019898880 | bytes 7602176 | tf_op jit(solution)/shard_map/rank/pallas_call | solution.py:99
  69.9 12.0 %project.3.base_ref = f32[576,1024]{1,0:T(8,128)} custom-call(s32[2]{0:T(128)} %pad_add_fusion.ids_ref, bf16[576,2048]{1,0:T(8,128)(2,1)} %collective-permute-done.refs_0_, bf16[576,2048]{1,0:T(8,128)(2,1)} %copy-done.2, bf16[8192,1024]{1,0:T(8,128)(2,1)} %refs_3_.3, bf16[8192,1024]{1,0:T(8,128)(2,1)} %refs_3_.3, f32[576,1024]{1,0:T(8,128)} %project.2.refs_4_), custom_call_target="tpu_custom_call" | custom-call | flops 4831838208 | bytes 15466496 | tf_op jit(solution)/shard_map/project/pallas_call | solution.py:52
  81.9 1.0 collective-permute-done.7.refs_0_
  82.9 1.3 collective-permute-done.8.refs_1_
  84.2 1.9 %slice.22 = bf16[128,2048]{1,0:T(8,128)(2,1)} slice(bf16[256,2048]{1,0:T(8,128)(2,1)} %collective-permute-done.7.refs_0_), slice={[0:128], [0:2048]} | slice | bytes 1048576 | tf_op jit(solution)/shard_map/slice | solution.py:332
  86.0 1.5 collective-permute-start.9
  87.6 1.9 %slice.23 = bf16[128,2048]{1,0:T(8,128)(2,1)} slice(bf16[256,2048]{1,0:T(8,128)(2,1)} %collective-permute-done.8.refs_1_), slice={[128:256], [0:2048]} | slice | bytes 1048576 | tf_op jit(solution)/shard_map/slice | solution.py:332
  90.0 1.6 collective-permute-start.13
  92.7 8.5 %collective-permute-done.9.refs_2_ = bf16[128,2048]{1,0:T(8,128)(2,1)} collective-permute-done((bf16[128,2048]{1,0:T(8,128)(2,1)}, bf16[128,2048]{1,0:T(8,128)(2,1)}, u32[]{:S(2)}, u32[]{:S(2)}) %collective-permute-start.9) | collective-permute-done | bytes 524320 | tf_op jit(solution)/shard_map/ppermute | solution.py:322
  101.2 3.4 %collective-permute-done.10.refs_3_ = bf16[128,2048]{1,0:T(8,128)(2,1)} collective-permute-done((bf16[128,2048]{1,0:T(8,128)(2,1)}, bf16[128,2048]{1,0:T(8,128)(2,1)}, u32[]{:S(2)}, u32[]{:S(2)}) %collective-permute-start.10) | collective-permute-done | bytes 524320 | tf_op jit(solution)/shard_map/ppermute | solution.py:322
  104.6 6.3 %rank.3 = f32[576,64]{1,0:T(8,128)} custom-call(s32[3]{0:T(128)} %pad_add_fusion.2.starts_ref, bf16[576,2048]{1,0:T(8,128)(2,1)} %bitcast.45, s32[576,1]{1,0:T(8,128)} %reshape_tile.4.adapter_ref.refs_2_, bf16[256,2048]{1,0:T(8,128)(2,1)} %collective-permute-done.7.refs_0_, bf16[256,2048]{1,0:T(8,128)(2,1)} %collective-permute-done.8.refs_1_, ...), custom_call_target="tpu_custom_call" | custom-call | flops 1811939328 | bytes 5505024 | tf_op jit(solution)/shard_map/rank/pallas_call | solution.py:99
  110.9 3.0 %collective-permute-done.14.refs_2_ = bf16[256,1024]{1,0:T(8,128)(2,1)} collective-permute-done((bf16[256,1024]{1,0:T(8,128)(2,1)S(1)}, bf16[256,1024]{1,0:T(8,128)(2,1)}, u32[]{:S(2)}, u32[]{:S(2)}) %collective-permute-start.14) | collective-permute-done | bytes 524320 | tf_op jit(solution)/shard_map/ppermute | solution.py:322
  114.0 0.7 collective-permute-start.15
  114.6 1.4 collective-permute-start.16
  116.0 1.8 %collective-permute-done.11 = f32[576,64]{1,0:T(8,128)S(1)} collective-permute-done((f32[576,64]{1,0:T(8,128)}, f32[576,64]{1,0:T(8,128)S(1)}, u32[]{:S(2)}, u32[]{:S(2)}) %collective-permute-start.11) | collective-permute-done | bytes 147488 | tf_op jit(solution)/shard_map/ppermute | solution.py:13
  117.8 1.0 add.119
  119.2 8.7 %collective-permute-done.12 = f32[576,64]{1,0:T(8,128)S(1)} collective-permute-done((f32[576,64]{1,0:T(8,128)S(1)}, f32[576,64]{1,0:T(8,128)S(1)}, u32[]{:S(2)}, u32[]{:S(2)}) %collective-permute-start.12) | collective-permute-done | bytes 147488 | tf_op jit(solution)/shard_map/ppermute | solution.py:13
  127.9 0.7 add.120.rank_ref.refs_1_
  128.7 0.7 collective-permute-start.17
  129.4 1.4 collective-permute-start.18
  130.7 0.6 concatenate.9.scalars_ref
  131.4 0.8 copy.21.refs_7_
  132.1 9.9 %collective-permute-done.17.refs_3_ = bf16[256,1024]{1,0:T(8,128)(2,1)S(1)} collective-permute-done((bf16[256,1024]{1,0:T(8,128)(2,1)}, bf16[256,1024]{1,0:T(8,128)(2,1)S(1)}, u32[]{:S(2)}, u32[]{:S(2)}) %collective-permute-start.17) | collective-permute-done | bytes 524320 | tf_op jit(solution)/shard_map/ppermute | solution.py:322
  142.5 0.8 collective-permute-start.22
  143.2 1.6 collective-permute-start.23
  144.8 1.9 %constant_dynamic-slice_fusion = (bf16[3,192,1,128]{3,2,1,0:T(2,128)(2,1)S(1)}, bf16[3,192,1,128]{3,2,1,0:T(2,128)(2,1)S(1)}) fusion(bf16[3,192,4,128]{3,2,1,0:T(4,128)(2,1)} %param.17, s32[]{:T(128)S(6)} %select_n.69, bf16[3,192,4,128]{3,2,1,0:T(4,128)(2,1)} %param.16), kind=kLoop, calls=%fused_computation.8 | loop fusion | bytes 589828 | tf_op jit(solution)/shard_map/jit(dynamic_index_in_dim)/dynamic_slice | solution.py:452
  146.6 0.7 copy.29
  147.3 0.7 copy.28
  148.0 6.4 %delta.1.refs_0_ = f32[576,1024]{1,0:T(8,128)} custom-call(s32[5]{0:T(128)} %stack.61.starts_ref, f32[576,1024]{1,0:T(8,128)} %project.3.base_ref, f32[576,64]{1,0:T(8,128)} %add.120.rank_ref.refs_1_, s32[576,1]{1,0:T(8,128)} %reshape_tile.4.adapter_ref.refs_2_, bf16[256,1024]{1,0:T(8,128)(2,1)} %copy-done.4, bf16[256,1024]{1,0:T(8,128)(2,1)} %copy-done.8, ...), custom_call_target="tpu_custom_call" | custom-call | flops 1509949440 | bytes 7340032 | tf_op jit(solution)/shard_map/delta/pallas_call | solution.py:145
  154.4 0.7 copy-done.9
  155.2 10.7 %attend.1 = bf16[3,192,1024]{2,1,0:T(8,128)(2,1)} custom-call(s32[7]{0:T(128)} %concatenate.9.scalars_ref, f32[576,1024]{1,0:T(8,128)} %delta.1.refs_0_, f32[576,64]{1,0:T(8,128)} %add.120.rank_ref.refs_1_, s32[576,1]{1,0:T(8,128)} %reshape_tile.4.adapter_ref.refs_2_, bf16[256,1024]{1,0:T(8,128)(2,1)} %copy-done.6, bf16[256,1024]{1,0:T(8,128)(2,1)} %copy-done.7, ...), custom_call_target="tpu_custom_call" | custom-call | flops 481296384 | bytes 7077888 | tf_op jit(solution)/shard_map/attend/pallas_call | solution.py:295
  (60 shorter events, 5.1 us)
Async XLA Ops:
  0.0 2.9 %copy-start = (bf16[8,2048,64]{1,2,0:T(8,128)(2,1)S(1)}, bf16[8,2048,64]{1,2,0:T(8,128)(2,1)}, u32[]{:S(2)}) copy-start(bf16[8,2048,64]{1,2,0:T(8,128)(2,1)} %param.12) | copy-start | bytes 6291460
  0.0 54.5 %collective-permute-start = (bf16[576,2048]{1,0:T(8,128)(2,1)}, bf16[576,2048]{1,0:T(8,128)(2,1)}, u32[]{:S(2)}, u32[]{:S(2)}) collective-permute-start(bf16[576,2048]{1,0:T(8,128)(2,1)} %bitcast.41), channel_id=1, source_target_pairs={{0,2},{1,3},{2,0},{3,1},{4,6},{5,7},{6,4},{7,5},{8,10},{9,11},{10,... | collective-permute-start | bytes 7077896 | tf_op jit(solution)/shard_map/ppermute | solution.py:13
  2.9 13.2 %collective-permute-start.3 = (bf16[576,2048]{1,0:T(8,128)(2,1)}, bf16[576,2048]{1,0:T(8,128)(2,1)}, u32[]{:S(2)}, u32[]{:S(2)}) collective-permute-start(bf16[576,2048]{1,0:T(8,128)(2,1)} %bitcast.42), channel_id=1, source_target_pairs={{0,1},{1,0},{2,3},{3,2},{4,5},{5,4},{6,7},{7,6},{8,9},{9,8},{10,11... | collective-permute-start | bytes 7077896 | tf_op jit(solution)/shard_map/ppermute | solution.py:13
  4.0 25.8 %collective-permute-start.1 = (bf16[256,2048]{1,0:T(8,128)(2,1)}, bf16[256,2048]{1,0:T(8,128)(2,1)S(1)}, u32[]{:S(2)}, u32[]{:S(2)}) collective-permute-start(bf16[256,2048]{1,0:T(8,128)(2,1)} %constant_dynamic-slice_fusion.3.refs_0_), channel_id=1, source_target_pairs={{0,4},{4,8},{8,12},{12,28},{28,24},{24,20},{20,16},{16,0},{1,5},{5... | collective-permute-start | bytes 3145736 | tf_op jit(solution)/shard_map/ppermute | solution.py:322
  5.7 25.4 %collective-permute-start.2 = (bf16[256,2048]{1,0:T(8,128)(2,1)}, bf16[256,2048]{1,0:T(8,128)(2,1)S(1)}, u32[]{:S(2)}, u32[]{:S(2)}) collective-permute-start(bf16[256,2048]{1,0:T(8,128)(2,1)} %constant_dynamic-slice_fusion.3.refs_0_), channel_id=1, source_target_pairs={{0,16},{4,0},{8,4},{12,8},{28,12},{24,28},{20,24},{16,20},{1,17},{... | collective-permute-start | bytes 3145736 | tf_op jit(solution)/shard_map/ppermute | solution.py:322
  6.0 3.6 %copy-start.3 = (bf16[192,4,12,128]{3,1,2,0:T(4,128)(2,1)S(1)}, bf16[192,4,12,128]{3,1,2,0:T(4,128)(2,1)}, u32[]{:S(2)}) copy-start(bf16[192,4,12,128]{3,1,2,0:T(4,128)(2,1)} %param.15) | copy-start | bytes 7077892
  16.1 43.1 %copy-start.13 = (s32[192]{0:T(256)S(1)}, s32[192]{0:T(256)}, u32[]{:S(2)}) copy-start(s32[192]{0:T(256)} %param.19) | copy-start | bytes 2308
  29.8 25.9 %copy-start.14 = (bf16[256,2048]{1,0:T(8,128)(2,1)}, bf16[256,2048]{1,0:T(8,128)(2,1)S(1)}, u32[]{:S(2)}) copy-start(bf16[256,2048]{1,0:T(8,128)(2,1)S(1)} %collective-permute-done.1.refs_1_) | copy-start | bytes 3145732
  31.1 24.6 %copy-start.15 = (bf16[256,2048]{1,0:T(8,128)(2,1)}, bf16[256,2048]{1,0:T(8,128)(2,1)S(1)}, u32[]{:S(2)}) copy-start(bf16[256,2048]{1,0:T(8,128)(2,1)S(1)} %collective-permute-done.2.refs_2_) | copy-start | bytes 3145732
  31.1 24.6 %collective-permute-start.4 = (bf16[256,2048]{1,0:T(8,128)(2,1)S(1)}, bf16[256,2048]{1,0:T(8,128)(2,1)}, u32[]{:S(2)}, u32[]{:S(2)}) collective-permute-start(bf16[256,2048]{1,0:T(8,128)(2,1)S(1)} %collective-permute-done.1.refs_1_), channel_id=1, source_target_pairs={{0,4},{4,8},{8,12},{12,28},{28,24},{24,20},{20,16},{16,0},{1,5},{5... | collective-permute-start | bytes 3145736 | tf_op jit(solution)/shard_map/ppermute | solution.py:322
  32.7 24.3 %collective-permute-start.5 = (bf16[256,2048]{1,0:T(8,128)(2,1)S(1)}, bf16[256,2048]{1,0:T(8,128)(2,1)}, u32[]{:S(2)}, u32[]{:S(2)}) collective-permute-start(bf16[256,2048]{1,0:T(8,128)(2,1)S(1)} %collective-permute-done.2.refs_2_), channel_id=1, source_target_pairs={{0,16},{4,0},{8,4},{12,8},{28,12},{24,28},{20,24},{16,20},{1,17},{... | collective-permute-start | bytes 3145736 | tf_op jit(solution)/shard_map/ppermute | solution.py:322
  57.0 4.7 %collective-permute-start.6 = (bf16[576,2048]{1,0:T(8,128)(2,1)}, bf16[576,2048]{1,0:T(8,128)(2,1)S(1)}, u32[]{:S(2)}, u32[]{:S(2)}) collective-permute-start(bf16[576,2048]{1,0:T(8,128)(2,1)} %collective-permute-done.refs_0_), channel_id=1, source_target_pairs={{0,1},{1,0},{2,3},{3,2},{4,5},{5,4},{6,7},{7,6},{8,9},{9,8},{10,11... | collective-permute-start | bytes 7077896 | tf_op jit(solution)/shard_map/ppermute | solution.py:13
  57.0 25.9 %collective-permute-start.7 = (bf16[256,2048]{1,0:T(8,128)(2,1)}, bf16[256,2048]{1,0:T(8,128)(2,1)}, u32[]{:S(2)}, u32[]{:S(2)}) collective-permute-start(bf16[256,2048]{1,0:T(8,128)(2,1)} %collective-permute-done.4.refs_3_), channel_id=1, source_target_pairs={{0,4},{4,8},{8,12},{12,28},{28,24},{24,20},{20,16},{16,0},{1,5},{5... | collective-permute-start | bytes 3145736 | tf_op jit(solution)/shard_map/ppermute | solution.py:322
  58.6 25.6 %collective-permute-start.8 = (bf16[256,2048]{1,0:T(8,128)(2,1)}, bf16[256,2048]{1,0:T(8,128)(2,1)}, u32[]{:S(2)}, u32[]{:S(2)}) collective-permute-start(bf16[256,2048]{1,0:T(8,128)(2,1)} %collective-permute-done.5.refs_4_), channel_id=1, source_target_pairs={{0,16},{4,0},{8,4},{12,8},{28,12},{24,28},{20,24},{16,20},{1,17},{... | collective-permute-start | bytes 3145736 | tf_op jit(solution)/shard_map/ppermute | solution.py:322
  59.0 32.6 %collective-permute-start.19 = (bf16[2,2304,128]{2,1,0:T(8,128)(2,1)}, bf16[2,2304,128]{2,1,0:T(8,128)(2,1)}, u32[]{:S(2)}, u32[]{:S(2)}) collective-permute-start(bf16[2,2304,128]{2,1,0:T(8,128)(2,1)} %get-tuple-element.42), channel_id=1, source_target_pairs={{0,2},{1,3},{2,0},{3,1},{4,6},{5,7},{6,4},{7,5},{8,10},{9,11},{10,... | collective-permute-start | bytes 3538952 | tf_op jit(solution)/shard_map/ppermute | solution.py:13
  61.7 8.2 %copy-start.2 = (bf16[576,2048]{1,0:T(8,128)(2,1)}, bf16[576,2048]{1,0:T(8,128)(2,1)S(1)}, u32[]{:S(2)}) copy-start(bf16[576,2048]{1,0:T(8,128)(2,1)S(1)} %collective-permute-done.6.refs_1_) | copy-start | bytes 7077892
  61.7 31.0 %collective-permute-start.20 = (bf16[2,2304,128]{2,1,0:T(8,128)(2,1)}, bf16[2,2304,128]{2,1,0:T(8,128)(2,1)}, u32[]{:S(2)}, u32[]{:S(2)}) collective-permute-start(bf16[2,2304,128]{2,1,0:T(8,128)(2,1)} %get-tuple-element.43), channel_id=1, source_target_pairs={{0,1},{1,0},{2,3},{3,2},{4,5},{5,4},{6,7},{7,6},{8,9},{9,8},{10,11... | collective-permute-start | bytes 3538952 | tf_op jit(solution)/shard_map/ppermute | solution.py:13
  81.9 8.1 %copy-start.11 = (bf16[8,64,1024]{2,1,0:T(8,128)(2,1)S(1)}, bf16[8,64,1024]{2,1,0:T(8,128)(2,1)}, u32[]{:S(2)}) copy-start(bf16[8,64,1024]{2,1,0:T(8,128)(2,1)} %param.13) | copy-start | bytes 3145732
  86.0 15.2 %collective-permute-start.9 = (bf16[128,2048]{1,0:T(8,128)(2,1)}, bf16[128,2048]{1,0:T(8,128)(2,1)}, u32[]{:S(2)}, u32[]{:S(2)}) collective-permute-start(bf16[128,2048]{1,0:T(8,128)(2,1)} %slice.22), channel_id=1, source_target_pairs={{0,4},{4,8},{8,12},{12,28},{28,24},{24,20},{20,16},{16,0},{1,5},{5... | collective-permute-start | bytes 1572872 | tf_op jit(solution)/shard_map/ppermute | solution.py:322
  89.5 15.2 %collective-permute-start.10 = (bf16[128,2048]{1,0:T(8,128)(2,1)}, bf16[128,2048]{1,0:T(8,128)(2,1)}, u32[]{:S(2)}, u32[]{:S(2)}) collective-permute-start(bf16[128,2048]{1,0:T(8,128)(2,1)} %slice.23), channel_id=1, source_target_pairs={{0,16},{4,0},{8,4},{12,8},{28,12},{24,28},{20,24},{16,20},{1,17},{... | collective-permute-start | bytes 1572872 | tf_op jit(solution)/shard_map/ppermute | solution.py:322
  90.0 20.9 %copy-start.4 = (bf16[256,1024]{1,0:T(8,128)(2,1)}, bf16[256,1024]{1,0:T(8,128)(2,1)S(1)}, u32[]{:S(2)}) copy-start(bf16[256,1024]{1,0:T(8,128)(2,1)S(1)} %constant_dynamic-slice_fusion.2.refs_0_) | copy-start | bytes 1572868
  90.0 20.9 %collective-permute-start.13 = (bf16[256,1024]{1,0:T(8,128)(2,1)S(1)}, bf16[256,1024]{1,0:T(8,128)(2,1)S(1)}, u32[]{:S(2)}, u32[]{:S(2)}) collective-permute-start(bf16[256,1024]{1,0:T(8,128)(2,1)S(1)} %constant_dynamic-slice_fusion.2.refs_0_), channel_id=1, source_target_pairs={{0,4},{4,8},{8,12},{12,28},{28,24},{24,20},{20,16},{16,0},{1,5},{5... | collective-permute-start | bytes 1572872 | tf_op jit(solution)/shard_map/ppermute | solution.py:322
  91.6 22.4 %collective-permute-start.14 = (bf16[256,1024]{1,0:T(8,128)(2,1)S(1)}, bf16[256,1024]{1,0:T(8,128)(2,1)}, u32[]{:S(2)}, u32[]{:S(2)}) collective-permute-start(bf16[256,1024]{1,0:T(8,128)(2,1)S(1)} %constant_dynamic-slice_fusion.2.refs_0_), channel_id=1, source_target_pairs={{0,16},{4,0},{8,4},{12,8},{28,12},{24,28},{20,24},{16,20},{1,17},{... | collective-permute-start | bytes 1572872 | tf_op jit(solution)/shard_map/ppermute | solution.py:322
  92.7 38.7 %copy-start.12 = (s32[192]{0:T(256)S(1)}, s32[192]{0:T(256)}, u32[]{:S(2)}) copy-start(s32[192]{0:T(256)} %param.18) | copy-start | bytes 2308
  92.7 49.7 %collective-permute-start.21 = (bf16[2,2304,128]{2,1,0:T(8,128)(2,1)S(1)}, bf16[2,2304,128]{2,1,0:T(8,128)(2,1)S(1)}, u32[]{:S(2)}, u32[]{:S(2)}) collective-permute-start(bf16[2,2304,128]{2,1,0:T(8,128)(2,1)S(1)} %get-tuple-element.44), channel_id=1, source_target_pairs={{0,3},{1,2},{2,1},{3,0},{4,7},{5,6},{6,5},{7,4},{8,11},{9,10},{10,... | collective-permute-start | bytes 3538952 | tf_op jit(solution)/shard_map/ppermute | solution.py:13
  110.9 17.7 %copy-start.8 = (bf16[256,1024]{1,0:T(8,128)(2,1)}, bf16[256,1024]{1,0:T(8,128)(2,1)S(1)}, u32[]{:S(2)}) copy-start(bf16[256,1024]{1,0:T(8,128)(2,1)S(1)} %collective-permute-done.13.refs_1_) | copy-start | bytes 1572868
  114.0 14.7 %collective-permute-start.15 = (bf16[256,1024]{1,0:T(8,128)(2,1)S(1)}, bf16[256,1024]{1,0:T(8,128)(2,1)}, u32[]{:S(2)}, u32[]{:S(2)}) collective-permute-start(bf16[256,1024]{1,0:T(8,128)(2,1)S(1)} %collective-permute-done.13.refs_1_), channel_id=1, source_target_pairs={{0,4},{4,8},{8,12},{12,28},{28,24},{24,20},{20,16},{16,0},{1,5},{5... | collective-permute-start | bytes 1572872 | tf_op jit(solution)/shard_map/ppermute | solution.py:322
  114.6 14.0 %collective-permute-start.16 = (bf16[256,1024]{1,0:T(8,128)(2,1)}, bf16[256,1024]{1,0:T(8,128)(2,1)}, u32[]{:S(2)}, u32[]{:S(2)}) collective-permute-start(bf16[256,1024]{1,0:T(8,128)(2,1)} %collective-permute-done.14.refs_2_), channel_id=1, source_target_pairs={{0,16},{4,0},{8,4},{12,8},{28,12},{24,28},{20,24},{16,20},{1,17},{... | collective-permute-start | bytes 1572872 | tf_op jit(solution)/shard_map/ppermute | solution.py:322
  116.0 1.8 %collective-permute-start.11 = (f32[576,64]{1,0:T(8,128)}, f32[576,64]{1,0:T(8,128)S(1)}, u32[]{:S(2)}, u32[]{:S(2)}) collective-permute-start(f32[576,64]{1,0:T(8,128)} %rank.3), channel_id=1, source_target_pairs={{0,1},{1,0},{2,3},{3,2},{4,5},{5,4},{6,7},{7,6},{8,9},{9,8},{10,11... | collective-permute-start | bytes 442376 | tf_op jit(solution)/shard_map/ppermute | solution.py:13
  118.8 9.1 %collective-permute-start.12 = (f32[576,64]{1,0:T(8,128)S(1)}, f32[576,64]{1,0:T(8,128)S(1)}, u32[]{:S(2)}, u32[]{:S(2)}) collective-permute-start(f32[576,64]{1,0:T(8,128)S(1)} %add.119), channel_id=1, source_target_pairs={{0,2},{1,3},{2,0},{3,1},{4,6},{5,7},{6,4},{7,5},{8,10},{9,11},{10,... | collective-permute-start | bytes 442376 | tf_op jit(solution)/shard_map/ppermute | solution.py:13
  128.7 13.4 %collective-permute-start.17 = (bf16[256,1024]{1,0:T(8,128)(2,1)}, bf16[256,1024]{1,0:T(8,128)(2,1)S(1)}, u32[]{:S(2)}, u32[]{:S(2)}) collective-permute-start(bf16[256,1024]{1,0:T(8,128)(2,1)} %collective-permute-done.15.refs_3_), channel_id=1, source_target_pairs={{0,4},{4,8},{8,12},{12,28},{28,24},{24,20},{20,16},{16,0},{1,5},{5... | collective-permute-start | bytes 1572872 | tf_op jit(solution)/shard_map/ppermute | solution.py:322
  129.4 13.1 %collective-permute-start.18 = (bf16[256,1024]{1,0:T(8,128)(2,1)}, bf16[256,1024]{1,0:T(8,128)(2,1)S(1)}, u32[]{:S(2)}, u32[]{:S(2)}) collective-permute-start(bf16[256,1024]{1,0:T(8,128)(2,1)} %collective-permute-done.16.refs_4_), channel_id=1, source_target_pairs={{0,16},{4,0},{8,4},{12,8},{28,12},{24,28},{20,24},{16,20},{1,17},{... | collective-permute-start | bytes 1572872 | tf_op jit(solution)/shard_map/ppermute | solution.py:322
  142.1 12.3 %copy-start.6 = (bf16[256,1024]{1,0:T(8,128)(2,1)}, bf16[256,1024]{1,0:T(8,128)(2,1)S(1)}, u32[]{:S(2)}) copy-start(bf16[256,1024]{1,0:T(8,128)(2,1)S(1)} %collective-permute-done.17.refs_3_) | copy-start | bytes 1572868
  142.4 11.9 %copy-start.7 = (bf16[256,1024]{1,0:T(8,128)(2,1)}, bf16[256,1024]{1,0:T(8,128)(2,1)S(1)}, u32[]{:S(2)}) copy-start(bf16[256,1024]{1,0:T(8,128)(2,1)S(1)} %collective-permute-done.18.refs_4_) | copy-start | bytes 1572868
  142.4 11.9 %copy-start.5 = (bf16[2,2304,128]{2,1,0:T(8,128)(2,1)}, bf16[2,2304,128]{2,1,0:T(8,128)(2,1)S(1)}, u32[]{:S(2)}) copy-start(bf16[2,2304,128]{2,1,0:T(8,128)(2,1)S(1)} %collective-permute-done.21.refs_11_) | copy-start | bytes 3538948
  142.5 11.9 %collective-permute-start.22 = (bf16[128,1024]{1,0:T(8,128)(2,1)S(1)}, bf16[128,1024]{1,0:T(8,128)(2,1)S(1)}, u32[]{:S(2)}, u32[]{:S(2)}) collective-permute-start(bf16[128,1024]{1,0:T(8,128)(2,1)S(1)} %slice.24), channel_id=1, source_target_pairs={{0,4},{4,8},{8,12},{12,28},{28,24},{24,20},{20,16},{16,0},{1,5},{5... | collective-permute-start | bytes 786440 | tf_op jit(solution)/shard_map/ppermute | solution.py:322
  143.2 11.2 %collective-permute-start.23 = (bf16[128,1024]{1,0:T(8,128)(2,1)S(1)}, bf16[128,1024]{1,0:T(8,128)(2,1)S(1)}, u32[]{:S(2)}, u32[]{:S(2)}) collective-permute-start(bf16[128,1024]{1,0:T(8,128)(2,1)S(1)} %slice.25), channel_id=1, source_target_pairs={{0,16},{4,0},{8,4},{12,8},{28,12},{24,28},{20,24},{16,20},{1,17},{... | collective-permute-start | bytes 786440 | tf_op jit(solution)/shard_map/ppermute | solution.py:322
  154.4 0.7 copy-start.9
  154.4 0.8 copy-start.10
  155.2 10.7 %copy-start.1 = (bf16[8,2048,64]{1,2,0:T(8,128)(2,1)S(1)}, bf16[8,2048,64]{1,2,0:T(8,128)(2,1)}, u32[]{:S(2)}) copy-start(bf16[8,2048,64]{1,2,0:T(8,128)(2,1)} %param.12) | copy-start | bytes 6291460

commit v5 on v4

--- a/solution.py
+++ b/solution.py
@@ -326,10 +326,7 @@
     return lax.optimization_barrier((array, others))[0]
 
 
-def ring_step(k, before, after, owners):
-    if k == owners:
-        rows = before.shape[0] // 2
-        before, after = before[:rows], after[rows:]
+def ring_step(before, after, owners):
     return ring_hop(before, 1, owners), ring_hop(after, -1, owners)
 
 
@@ -381,7 +378,7 @@
     both = jnp.stack([key_heads, value_heads], axis=1)
 
     paired = count == 4
-    down = [ring_step(1, own_down, own_down, owners)]
+    down = [ring_step(own_down, own_down, owners)]
     if paired:
         ids = jnp.stack([me ^ j for j in range(count)]).astype(jnp.int32)
         far = swap(flat_tokens, 2, count)
@@ -405,47 +402,53 @@
         key_values = [gathered[b] for b in range(count)]
         waits = {}
     early = 1 + 2 * (owners - 2)
+    for k in range(2, owners):
+        down.append(ring_step(*gate(down[-1], *waits.get(k, [])), owners))
+    groups = [[own_down]] + [[part] for pair in down[: owners - 2] for part in pair]
+    ranks = add_ranks(starts[:early], flat_tokens, row_adapters, groups, rank)
+    before, after = gate(down[-1], ranks)
+    down.append([ring_hop(before, 1, owners)])
+    waits = {1: down[owners - 3]}
+    if paired:
+        far = gate(far, down[owners - 3])
+        far_near = swap(far, 1, count)
+        second = swap(gate(parcels[2], far), 2, count)
+        third = swap(gate(parcels[3], second), 3, count)
+        base = project_pair(ids[2:], [far], [far_near], query_weight, base)
+        waits = {1: [down[owners - 3], far]}
+
+    from_after = [ring_hop(gate(own_up, *waits[1]), -1, owners)]
+    from_before = [ring_hop(gate(own_up, before, from_after[0], base), 1, owners)]
+    if paired:
+        first = swap(gate(parcels[1], from_after[0]), 1, count)
+        key_values = [parcels[0], first, second, third]
+    groups = [[part] for part in down[owners - 2]]
+    ranks = add_ranks(
+        starts[early : early + 2], flat_tokens, row_adapters, groups, rank, earlier=ranks
+    )
+    ranks = add_ranks(
+        starts[early + 2 :],
+        flat_tokens,
+        row_adapters,
+        [down[owners - 1]],
+        rank,
+        earlier=ranks,
+        last=True,
+    )
     for k in range(2, owners + 1):
-        before, after = down[-1]
-        if k == owners:
-            groups = [[own_down]] + [[part] for pair in down[: owners - 2] for part in pair]
-            ranks = add_ranks(starts[:early], flat_tokens, row_adapters, groups, rank)
-            if paired:
-                far = gate(far, down[1])
-                far_near = swap(far, 1, count)
-                second = swap(gate(parcels[2], far), 2, count)
-                both_far = gate((far, far_near), ranks)
-                base = project_pair(ids[2:], [both_far[0]], [both_far[1]], query_weight, base)
-                waits[owners] = [base]
-        if k in waits:
-            before, after = gate((before, after), *waits[k])
-        down.append(ring_step(k, before, after, owners))
-    if paired:
-        first = swap(gate(parcels[1], far_near), 1, count)
-        third = swap(gate(parcels[3], second, first), 3, count)
-        key_values = [parcels[0], first, second, third]
-
-    groups = [[part] for part in down[owners - 2]] + [list(down[owners - 1])]
-    ranks = add_ranks(
-        starts[early:], flat_tokens, row_adapters, groups, rank, earlier=ranks, last=True
-    )
-
-    own_up = gate(own_up, down[owners - 2], base)
-    up = [ring_step(1, own_up, own_up, owners)]
-    waits = {2: [ranks]}
-    bit = 1
-    while bit < count:
+        from_after.append(ring_hop(gate(from_after[-1], *waits.get(k, [])), -1, owners))
+    bits = [1 << i for i in range((count - 1).bit_length())]
+    for k in range(2, owners):
+        for bit in bits[k - 2 : k - 1]:
+            ranks = ranks + swap(ranks, bit, count)
+        wait = [third] if paired and k == owners - 1 else []
+        from_before.append(ring_hop(gate(from_before[-1], ranks, *wait), 1, owners))
+    for bit in bits[owners - 2 :]:
         ranks = ranks + swap(ranks, bit, count)
-        bit *= 2
-    waits[3] = [ranks]
-    if paired:
-        waits[owners] = [third]
-    for k in range(2, owners + 1):
-        up.append(ring_step(k, *gate(up[-1], *waits.get(k, [])), owners))
-
-    groups = [[own_up]] + [[part] for pair in up[: owners - 2] for part in pair]
+    up = [part for pair in zip(from_before, from_after) for part in pair] + [from_after[-1]]
+    groups = [[own_up]] + [[part] for part in up[: early - 1]]
     query = early_query(starts[:early], base, ranks, row_adapters, groups)
-    groups = [[part] for part in up[owners - 2]] + [list(up[owners - 1])]
+    groups = [[part] for part in up[early - 1 :]]
 
     kv_head = me * KVH // count
     fresh_keys = lax.dynamic_index_in_dim(incoming_key_rows, kv_head, 2, keepdims=False)

time: 167 us -> 164 us (0.982)
  waiting for transfers between devices: 66.2 us -> 61.7 us
  Pallas kernels: 54.4 us -> 57.3 us
  local copies, waits for them, and re-layouts: 21.3 us -> 18.7 us
  starting transfers between devices: 20.3 us -> 22.4 us
    ppermute x8, waiting for transfers between devices: 32.2 us -> 27.6 us  [swap(): return lax.ppermute(array, 'tensor', [(i, i ^ bit) for i in range(count)])]
    slice x4 -> x0, local copies, waits for them, and re-layouts: 3.81 us -> none  [ring_step(): before, after = (before[:rows], after[rows:])]
    pallas_call x2 -> x3, Pallas kernels: 14.3 us -> 17.2 us  [add_ranks(): pl.pallas_call(kernel, out_shape=jax.ShapeDtypeStruct((rows, out_width),...]
    ppermute x8, starting transfers between devices: 3.74 us -> 5.99 us  [swap(): return lax.ppermute(array, 'tensor', [(i, i ^ bit) for i in range(count)])]
    unnamed x35 -> x25, local copies, waits for them, and re-layouts: 5.69 us -> 6.85 us
    ppermute x16 -> x14, starting transfers between devices: 16.6 us -> 16.4 us  [ring_hop(): return lax.ppermute(array, ('rep', 'dp'), pairs)]
    ppermute x16 -> x14, waiting for transfers between devices: 34 us -> 34.1 us  [ring_hop(): return lax.ppermute(array, ('rep', 'dp'), pairs)]
  transfers between devices with their start and end apart: 24 -> 22, of which waited for: 15 -> 10; matrix products, arithmetic and copies ran while one was open for 14% -> 12% of each run, Pallas kernels for 26% -> 28%
where the time goes in v5:
time: 164 us
  waiting for transfers between devices  61.7 us (38%)
  Pallas kernels  57.3 us (35%)
  starting transfers between devices  22.4 us (14%)
  local copies, waits for them, and re-layouts  18.7 us (11%)
  other arithmetic  3.63 us (2%)
    ppermute x14, waiting for transfers between devices, ring_hop(): return lax.ppermute(array, ('rep', 'dp'), pairs)  34.1 us
    ppermute x8, waiting for transfers between devices, swap(): return lax.ppermute(array, 'tensor', [(i, i ^ bit) for i in range(count)])  27.6 us
    pallas_call x2, Pallas kernels, project_pair(): pl.pallas_call(kernel, out_shape=jax.ShapeDtypeStruct((rows, columns), jn...  23 us
    pallas_call x3, Pallas kernels, add_ranks(): pl.pallas_call(kernel, out_shape=jax.ShapeDtypeStruct((rows, out_width),...  17.2 us
    ppermute x14, starting transfers between devices, ring_hop(): return lax.ppermute(array, ('rep', 'dp'), pairs)  16.4 us
    pallas_call x1, Pallas kernels, attend(): pl.pallas_call(kernel, out_shape=jax.ShapeDtypeStruct((steps, rows, width...  10.8 us
    unnamed x25, local copies, waits for them, and re-layouts  6.85 us
    pallas_call x1, Pallas kernels, early_query(): pl.pallas_call(kernel, out_shape=jax.ShapeDtypeStruct((rows, columns), jn...  6.4 us
  transfers between devices with their start and end apart: 22, of which 10 were waited for; matrix products, arithmetic and copies ran while one was open for 12% of the time, Pallas kernels for 28%

profile of v5, /device:TPU:0, one launch (start us, length us, event | category | flops | bytes accessed | tf_op | source)
XLA Modules:
  0.0 163.9 jit_solution(11274072651718617665)
XLA Ops:
  0.0 0.5 collective-permute-start.3
  0.5 1.1 copy-done
  1.7 3.1 %collective-permute-start.1 = (bf16[256,2048]{1,0:T(8,128)(2,1)S(1)}, bf16[256,2048]{1,0:T(8,128)(2,1)}, u32[]{:S(2)}, u32[]{:S(2)}) collective-permute-start(bf16[256,2048]{1,0:T(8,128)(2,1)S(1)} %constant_dynamic-slice_fusion.3.refs_0_), channel_id=1, source_target_pairs={{0,4},{4,8},{8,12},{12,28},{28,24},{24,20},{20,16},{16,0},{1,5},{5... | collective-permute-start | bytes 3145736 | tf_op jit(solution)/shard_map/ppermute | solution.py:322
  4.8 1.9 %collective-permute-start = (bf16[576,2048]{1,0:T(8,128)(2,1)}, bf16[576,2048]{1,0:T(8,128)(2,1)}, u32[]{:S(2)}, u32[]{:S(2)}) collective-permute-start(bf16[576,2048]{1,0:T(8,128)(2,1)} %bitcast.40), channel_id=1, source_target_pairs={{0,2},{1,3},{2,0},{3,1},{4,6},{5,7},{6,4},{7,5},{8,10},{9,11},{10,... | collective-permute-start | bytes 7077896 | tf_op jit(solution)/shard_map/ppermute | solution.py:13
  6.7 3.5 %copy_dynamic-update-slice_fusion.1 = bf16[4,2,2304,128]{3,2,1,0:T(8,128)(2,1)} fusion(bf16[4,1,2304,128]{3,0,2,1:T(4,128)(2,1)} %bitcast.45), kind=kLoop, calls=%fused_computation.1 | loop fusion | bytes 4718592
  10.2 1.7 %copy_dynamic-update-slice_fusion = bf16[4,2,2304,128]{3,2,1,0:T(8,128)(2,1)} fusion(bf16[4,2,2304,128]{3,2,1,0:T(8,128)(2,1)} %copy_dynamic-update-slice_fusion.1, bf16[4,1,2304,128]{3,0,2,1:T(4,128)(2,1)S(1)} %bitcast.46), kind=kLoop, calls=%fused_computation | loop fusion | bytes 4718592 | tf_op jit(solution)/shard_map/stack | solution.py:378
  12.0 4.1 %dynamic-slice_bitcast_fusion = (bf16[2,2304,128]{2,1,0:T(8,128)(2,1)S(1)}, bf16[2,2304,128]{2,1,0:T(8,128)(2,1)}, bf16[2,2304,128]{2,1,0:T(8,128)(2,1)S(1)}, bf16[2,2304,128]{2,1,0:T(8,128)(2,1)}) fusion(bf16[4,2,2304,128]{3,2,1,0:T(8,128)(2,1)} %copy_dynamic-update-slice_fusion, s32[]{:T(128)S(6)} %select_n.67, s32[]{:T(128)S(6)} %select_n.66, ...), kind=kLoop, calls=%fused_computation.2 | loop fusion | bytes 9437200 | tf_op jit(solution)/shard_map/jit(dynamic_index_in_dim)/squeeze | solution.py:387
  16.0 0.6 pad_add_fusion.1.ids_ref
  16.7 10.9 %project.2.refs_4_ = f32[576,1024]{1,0:T(8,128)} custom-call(s32[2]{0:T(128)} %pad_add_fusion.1.ids_ref, bf16[576,2048]{1,0:T(8,128)(2,1)} %bitcast.41, bf16[576,2048]{1,0:T(8,128)(2,1)} %collective-permute-done.3.refs_1_, bf16[8192,1024]{1,0:T(8,128)(2,1)} %refs_3_.3, bf16[8192,1024]{1,0:T(8,128)(2,1)} %refs_3_.3), custom_call_target="tpu_custom_call" | custom-call | flops 4831838208 | bytes 15466496 | tf_op jit(solution)/shard_map/project/pallas_call | solution.py:52
  28.0 1.5 collective-permute-done.2.refs_2_
  29.5 1.6 collective-permute-start.4
  31.5 26.3 %collective-permute-done.refs_0_ = bf16[576,2048]{1,0:T(8,128)(2,1)} collective-permute-done((bf16[576,2048]{1,0:T(8,128)(2,1)}, bf16[576,2048]{1,0:T(8,128)(2,1)}, u32[]{:S(2)}, u32[]{:S(2)}) %collective-permute-start) | collective-permute-done | bytes 2359328 | tf_op jit(solution)/shard_map/ppermute | solution.py:13
  57.8 1.8 %collective-permute-start.7 = (bf16[256,2048]{1,0:T(8,128)(2,1)}, bf16[256,2048]{1,0:T(8,128)(2,1)}, u32[]{:S(2)}, u32[]{:S(2)}) collective-permute-start(bf16[256,2048]{1,0:T(8,128)(2,1)} %collective-permute-done.4.refs_3_), channel_id=1, source_target_pairs={{0,4},{4,8},{8,12},{12,28},{28,24},{24,20},{20,16},{16,0},{1,5},{5... | collective-permute-start | bytes 3145736 | tf_op jit(solution)/shard_map/ppermute | solution.py:322
  59.9 1.7 %collective-permute-start.16 = (bf16[2,2304,128]{2,1,0:T(8,128)(2,1)}, bf16[2,2304,128]{2,1,0:T(8,128)(2,1)}, u32[]{:S(2)}, u32[]{:S(2)}) collective-permute-start(bf16[2,2304,128]{2,1,0:T(8,128)(2,1)} %get-tuple-element.35), channel_id=1, source_target_pairs={{0,2},{1,3},{2,0},{3,1},{4,6},{5,7},{6,4},{7,5},{8,10},{9,11},{10,... | collective-permute-start | bytes 3538952 | tf_op jit(solution)/shard_map/ppermute | solution.py:13
  61.5 1.0 reshape_tile.4.adapter_ref.refs_2_
  62.5 0.7 stack.61.starts_ref
  63.2 1.1 constant_dynamic-slice_fusion.2.refs_0_
  64.3 1.6 collective-permute-start.12
  65.8 8.0 %rank.3.refs_2_ = f32[576,256]{1,0:T(8,128)} custom-call(s32[5]{0:T(128)} %stack.61.starts_ref, bf16[576,2048]{1,0:T(8,128)(2,1)} %bitcast.42, s32[576,1]{1,0:T(8,128)} %reshape_tile.4.adapter_ref.refs_2_, bf16[256,2048]{1,0:T(8,128)(2,1)} %copy-done.4, bf16[256,2048]{1,0:T(8,128)(2,1)} %collective-permute-done.1.refs_1_, ...), custom_call_target="tpu_custom_call" | custom-call | flops 3019898880 | bytes 7602176 | tf_op jit(solution)/shard_map/rank/pallas_call | solution.py:99
  73.9 9.8 %collective-permute-done.7.refs_0_ = bf16[256,2048]{1,0:T(8,128)(2,1)} collective-permute-done((bf16[256,2048]{1,0:T(8,128)(2,1)}, bf16[256,2048]{1,0:T(8,128)(2,1)}, u32[]{:S(2)}, u32[]{:S(2)}) %collective-permute-start.7) | collective-permute-done | bytes 1048608 | tf_op jit(solution)/shard_map/ppermute | solution.py:322
  83.7 2.2 %collective-permute-done.8.refs_1_ = bf16[256,2048]{1,0:T(8,128)(2,1)} collective-permute-done((bf16[256,2048]{1,0:T(8,128)(2,1)}, bf16[256,2048]{1,0:T(8,128)(2,1)}, u32[]{:S(2)}, u32[]{:S(2)}) %collective-permute-start.8) | collective-permute-done | bytes 1048608 | tf_op jit(solution)/shard_map/ppermute | solution.py:322
  85.9 1.6 collective-permute-start.9
  87.5 0.6 pad_add_fusion.ids_ref
  88.1 8.2 %collective-permute-done.12.refs_2_ = bf16[256,1024]{1,0:T(8,128)(2,1)S(1)} collective-permute-done((bf16[256,1024]{1,0:T(8,128)(2,1)S(1)}, bf16[256,1024]{1,0:T(8,128)(2,1)S(1)}, u32[]{:S(2)}, u32[]{:S(2)}) %collective-permute-start.12) | collective-permute-done | bytes 524320 | tf_op jit(solution)/shard_map/ppermute | solution.py:322
  97.0 12.0 %project.3.base_ref = f32[576,1024]{1,0:T(8,128)} custom-call(s32[2]{0:T(128)} %pad_add_fusion.ids_ref, bf16[576,2048]{1,0:T(8,128)(2,1)} %collective-permute-done.refs_0_, bf16[576,2048]{1,0:T(8,128)(2,1)} %collective-permute-done.6.refs_1_, bf16[8192,1024]{1,0:T(8,128)(2,1)} %refs_3_.3, bf16[8192,1024]{1,0:T(8,128)(2,1)} %refs_3_.3, ...), custom_call_target="tpu_custom_call" | custom-call | flops 4831838208 | bytes 15466496 | tf_op jit(solution)/shard_map/project/pallas_call | solution.py:52
  109.0 1.6 collective-permute-start.13
  110.7 0.6 pad_add_fusion.2.starts_ref
  111.3 5.4 %rank.4.refs_1_ = f32[576,256]{1,0:T(8,128)} custom-call(s32[2]{0:T(128)} %pad_add_fusion.2.starts_ref, bf16[576,2048]{1,0:T(8,128)(2,1)} %bitcast.43, s32[576,1]{1,0:T(8,128)} %reshape_tile.4.adapter_ref.refs_2_, bf16[256,2048]{1,0:T(8,128)(2,1)} %collective-permute-done.7.refs_0_, bf16[256,2048]{1,0:T(8,128)(2,1)} %collective-permute-done.8.refs_1_, ...), custom_call_target="tpu_custom_call" | custom-call | flops 1207959552 | bytes 4456448 | tf_op jit(solution)/shard_map/rank/pallas_call | solution.py:99
  116.7 3.8 %rank.5 = f32[576,64]{1,0:T(8,128)} custom-call(s32[1]{0:T(128)} %bitcast.2.starts_ref, bf16[576,2048]{1,0:T(8,128)(2,1)} %bitcast.44, s32[576,1]{1,0:T(8,128)} %reshape_tile.4.adapter_ref.refs_2_, bf16[256,2048]{1,0:T(8,128)(2,1)} %collective-permute-done.9.refs_0_, f32[576,256]{1,0:T(8,128)} %rank.4.refs_1_), custom_call_target="tpu_custom_call" | custom-call | flops 603979776 | bytes 3407872 | tf_op jit(solution)/shard_map/rank/pallas_call | solution.py:99
  120.5 1.1 collective-permute-start.10
  121.5 0.5 collective-permute-start.19
  122.0 1.4 collective-permute-done.10
  123.3 1.0 add.119
  124.4 1.6 %collective-permute-start.14 = (bf16[256,1024]{1,0:T(8,128)(2,1)}, bf16[256,1024]{1,0:T(8,128)(2,1)S(1)}, u32[]{:S(2)}, u32[]{:S(2)}) collective-permute-start(bf16[256,1024]{1,0:T(8,128)(2,1)} %collective-permute-done.13.refs_1_), channel_id=1, source_target_pairs={{0,4},{4,8},{8,12},{12,28},{28,24},{24,20},{20,16},{16,0},{1,5},{5... | collective-permute-start | bytes 1572872 | tf_op jit(solution)/shard_map/ppermute | solution.py:322
  126.0 0.5 collective-permute-start.11
  126.5 9.6 %collective-permute-done.19.refs_4_ = bf16[256,1024]{1,0:T(8,128)(2,1)S(1)} collective-permute-done((bf16[256,1024]{1,0:T(8,128)(2,1)}, bf16[256,1024]{1,0:T(8,128)(2,1)S(1)}, u32[]{:S(2)}, u32[]{:S(2)}) %collective-permute-start.19) | collective-permute-done | bytes 524320 | tf_op jit(solution)/shard_map/ppermute | solution.py:322
  136.5 0.8 add.120.rank_ref.refs_1_
  137.3 1.5 collective-permute-done.14.refs_3_
  138.8 1.6 collective-permute-start.18
  140.4 0.6 concatenate.10.scalars_ref
  141.0 1.9 %constant_dynamic-slice_fusion = (bf16[3,192,1,128]{3,2,1,0:T(2,128)(2,1)S(1)}, bf16[3,192,1,128]{3,2,1,0:T(2,128)(2,1)S(1)}) fusion(bf16[3,192,4,128]{3,2,1,0:T(4,128)(2,1)} %param.17, s32[]{:T(128)S(6)} %select_n.69, bf16[3,192,4,128]{3,2,1,0:T(4,128)(2,1)} %param.16), kind=kLoop, calls=%fused_computation.8 | loop fusion | bytes 589828 | tf_op jit(solution)/shard_map/jit(dynamic_index_in_dim)/dynamic_slice | solution.py:455
  142.8 0.7 copy.29
  143.5 0.7 copy.30
  144.2 0.8 copy.22.refs_6_
  145.0 6.4 %delta.1.refs_0_ = f32[576,1024]{1,0:T(8,128)} custom-call(s32[5]{0:T(128)} %stack.61.starts_ref, f32[576,1024]{1,0:T(8,128)} %project.3.base_ref, f32[576,64]{1,0:T(8,128)} %add.120.rank_ref.refs_1_, s32[576,1]{1,0:T(8,128)} %reshape_tile.4.adapter_ref.refs_2_, bf16[256,1024]{1,0:T(8,128)(2,1)} %copy-done.3, ...), custom_call_target="tpu_custom_call" | custom-call | flops 1509949440 | bytes 7340032 | tf_op jit(solution)/shard_map/delta/pallas_call | solution.py:145
  151.4 0.8 collective-permute-done.18.refs_3_
  152.2 0.8 copy-done.8
  153.0 10.8 %attend.1 = bf16[3,192,1024]{2,1,0:T(8,128)(2,1)} custom-call(s32[7]{0:T(128)} %concatenate.10.scalars_ref, f32[576,1024]{1,0:T(8,128)} %delta.1.refs_0_, f32[576,64]{1,0:T(8,128)} %add.120.rank_ref.refs_1_, s32[576,1]{1,0:T(8,128)} %reshape_tile.4.adapter_ref.refs_2_, bf16[256,1024]{1,0:T(8,128)(2,1)} %copy-done.8, bf16[256,1024]{1,0:T(8,128)(2,1)} %copy-done.7, ...), custom_call_target="tpu_custom_call" | custom-call | flops 481296384 | bytes 7077888 | tf_op jit(solution)/shard_map/attend/pallas_call | solution.py:295
  (43 shorter events, 2.4 us)
Async XLA Ops:
  0.0 1.6 copy-start
  0.0 16.7 %collective-permute-start.3 = (bf16[576,2048]{1,0:T(8,128)(2,1)}, bf16[576,2048]{1,0:T(8,128)(2,1)}, u32[]{:S(2)}, u32[]{:S(2)}) collective-permute-start(bf16[576,2048]{1,0:T(8,128)(2,1)} %bitcast.39), channel_id=1, source_target_pairs={{0,1},{1,0},{2,3},{3,2},{4,5},{5,4},{6,7},{7,6},{8,9},{9,8},{10,11... | collective-permute-start | bytes 7077896 | tf_op jit(solution)/shard_map/ppermute | solution.py:13
  1.7 8.6 %copy-start.4 = (bf16[256,2048]{1,0:T(8,128)(2,1)}, bf16[256,2048]{1,0:T(8,128)(2,1)S(1)}, u32[]{:S(2)}) copy-start(bf16[256,2048]{1,0:T(8,128)(2,1)S(1)} %constant_dynamic-slice_fusion.3.refs_0_) | copy-start | bytes 3145732
  1.7 26.3 %collective-permute-start.1 = (bf16[256,2048]{1,0:T(8,128)(2,1)S(1)}, bf16[256,2048]{1,0:T(8,128)(2,1)}, u32[]{:S(2)}, u32[]{:S(2)}) collective-permute-start(bf16[256,2048]{1,0:T(8,128)(2,1)S(1)} %constant_dynamic-slice_fusion.3.refs_0_), channel_id=1, source_target_pairs={{0,4},{4,8},{8,12},{12,28},{28,24},{24,20},{20,16},{16,0},{1,5},{5... | collective-permute-start | bytes 3145736 | tf_op jit(solution)/shard_map/ppermute | solution.py:322
  4.8 24.7 %collective-permute-start.2 = (bf16[256,2048]{1,0:T(8,128)(2,1)S(1)}, bf16[256,2048]{1,0:T(8,128)(2,1)}, u32[]{:S(2)}, u32[]{:S(2)}) collective-permute-start(bf16[256,2048]{1,0:T(8,128)(2,1)S(1)} %constant_dynamic-slice_fusion.3.refs_0_), channel_id=1, source_target_pairs={{0,16},{4,0},{8,4},{12,8},{28,12},{24,28},{20,24},{16,20},{1,17},{... | collective-permute-start | bytes 3145736 | tf_op jit(solution)/shard_map/ppermute | solution.py:322
  4.8 53.0 %collective-permute-start = (bf16[576,2048]{1,0:T(8,128)(2,1)}, bf16[576,2048]{1,0:T(8,128)(2,1)}, u32[]{:S(2)}, u32[]{:S(2)}) collective-permute-start(bf16[576,2048]{1,0:T(8,128)(2,1)} %bitcast.40), channel_id=1, source_target_pairs={{0,2},{1,3},{2,0},{3,1},{4,6},{5,7},{6,4},{7,5},{8,10},{9,11},{10,... | collective-permute-start | bytes 7077896 | tf_op jit(solution)/shard_map/ppermute | solution.py:13
  6.7 3.5 %copy-start.2 = (bf16[192,4,12,128]{3,1,2,0:T(4,128)(2,1)S(1)}, bf16[192,4,12,128]{3,1,2,0:T(4,128)(2,1)}, u32[]{:S(2)}) copy-start(bf16[192,4,12,128]{3,1,2,0:T(4,128)(2,1)} %param.15) | copy-start | bytes 7077892
  16.7 44.9 %copy-start.10 = (s32[192]{0:T(256)S(1)}, s32[192]{0:T(256)}, u32[]{:S(2)}) copy-start(s32[192]{0:T(256)} %param.19) | copy-start | bytes 2308
  29.5 28.3 %collective-permute-start.4 = (bf16[256,2048]{1,0:T(8,128)(2,1)}, bf16[256,2048]{1,0:T(8,128)(2,1)}, u32[]{:S(2)}, u32[]{:S(2)}) collective-permute-start(bf16[256,2048]{1,0:T(8,128)(2,1)} %collective-permute-done.1.refs_1_), channel_id=1, source_target_pairs={{0,4},{4,8},{8,12},{12,28},{28,24},{24,20},{20,16},{16,0},{1,5},{5... | collective-permute-start | bytes 3145736 | tf_op jit(solution)/shard_map/ppermute | solution.py:322
  31.1 26.7 %collective-permute-start.5 = (bf16[256,2048]{1,0:T(8,128)(2,1)}, bf16[256,2048]{1,0:T(8,128)(2,1)}, u32[]{:S(2)}, u32[]{:S(2)}) collective-permute-start(bf16[256,2048]{1,0:T(8,128)(2,1)} %collective-permute-done.2.refs_2_), channel_id=1, source_target_pairs={{0,16},{4,0},{8,4},{12,8},{28,12},{24,28},{20,24},{16,20},{1,17},{... | collective-permute-start | bytes 3145736 | tf_op jit(solution)/shard_map/ppermute | solution.py:322
  57.8 39.2 %collective-permute-start.6 = (bf16[576,2048]{1,0:T(8,128)(2,1)}, bf16[576,2048]{1,0:T(8,128)(2,1)}, u32[]{:S(2)}, u32[]{:S(2)}) collective-permute-start(bf16[576,2048]{1,0:T(8,128)(2,1)} %collective-permute-done.refs_0_), channel_id=1, source_target_pairs={{0,1},{1,0},{2,3},{3,2},{4,5},{5,4},{6,7},{7,6},{8,9},{9,8},{10,11... | collective-permute-start | bytes 7077896 | tf_op jit(solution)/shard_map/ppermute | solution.py:13
  57.8 25.9 %collective-permute-start.7 = (bf16[256,2048]{1,0:T(8,128)(2,1)}, bf16[256,2048]{1,0:T(8,128)(2,1)}, u32[]{:S(2)}, u32[]{:S(2)}) collective-permute-start(bf16[256,2048]{1,0:T(8,128)(2,1)} %collective-permute-done.4.refs_3_), channel_id=1, source_target_pairs={{0,4},{4,8},{8,12},{12,28},{28,24},{24,20},{20,16},{16,0},{1,5},{5... | collective-permute-start | bytes 3145736 | tf_op jit(solution)/shard_map/ppermute | solution.py:322
  59.6 26.3 %collective-permute-start.8 = (bf16[256,2048]{1,0:T(8,128)(2,1)}, bf16[256,2048]{1,0:T(8,128)(2,1)}, u32[]{:S(2)}, u32[]{:S(2)}) collective-permute-start(bf16[256,2048]{1,0:T(8,128)(2,1)} %collective-permute-done.5.refs_4_), channel_id=1, source_target_pairs={{0,16},{4,0},{8,4},{12,8},{28,12},{24,28},{20,24},{16,20},{1,17},{... | collective-permute-start | bytes 3145736 | tf_op jit(solution)/shard_map/ppermute | solution.py:322
  59.9 36.7 %collective-permute-start.16 = (bf16[2,2304,128]{2,1,0:T(8,128)(2,1)}, bf16[2,2304,128]{2,1,0:T(8,128)(2,1)}, u32[]{:S(2)}, u32[]{:S(2)}) collective-permute-start(bf16[2,2304,128]{2,1,0:T(8,128)(2,1)} %get-tuple-element.35), channel_id=1, source_target_pairs={{0,2},{1,3},{2,0},{3,1},{4,6},{5,7},{6,4},{7,5},{8,10},{9,11},{10,... | collective-permute-start | bytes 3538952 | tf_op jit(solution)/shard_map/ppermute | solution.py:13
  64.3 44.8 %copy-start.3 = (bf16[256,1024]{1,0:T(8,128)(2,1)}, bf16[256,1024]{1,0:T(8,128)(2,1)S(1)}, u32[]{:S(2)}) copy-start(bf16[256,1024]{1,0:T(8,128)(2,1)S(1)} %constant_dynamic-slice_fusion.2.refs_0_) | copy-start | bytes 1572868
  64.3 32.0 %collective-permute-start.12 = (bf16[256,1024]{1,0:T(8,128)(2,1)S(1)}, bf16[256,1024]{1,0:T(8,128)(2,1)S(1)}, u32[]{:S(2)}, u32[]{:S(2)}) collective-permute-start(bf16[256,1024]{1,0:T(8,128)(2,1)S(1)} %constant_dynamic-slice_fusion.2.refs_0_), channel_id=1, source_target_pairs={{0,16},{4,0},{8,4},{12,8},{28,12},{24,28},{20,24},{16,20},{1,17},{... | collective-permute-start | bytes 1572872 | tf_op jit(solution)/shard_map/ppermute | solution.py:322
  85.9 30.8 %collective-permute-start.9 = (bf16[256,2048]{1,0:T(8,128)(2,1)}, bf16[256,2048]{1,0:T(8,128)(2,1)}, u32[]{:S(2)}, u32[]{:S(2)}) collective-permute-start(bf16[256,2048]{1,0:T(8,128)(2,1)} %collective-permute-done.7.refs_0_), channel_id=1, source_target_pairs={{0,4},{4,8},{8,12},{12,28},{28,24},{24,20},{20,16},{16,0},{1,5},{5... | collective-permute-start | bytes 3145736 | tf_op jit(solution)/shard_map/ppermute | solution.py:322
  96.3 12.8 %copy-start.5 = (bf16[256,1024]{1,0:T(8,128)(2,1)}, bf16[256,1024]{1,0:T(8,128)(2,1)S(1)}, u32[]{:S(2)}) copy-start(bf16[256,1024]{1,0:T(8,128)(2,1)S(1)} %collective-permute-done.12.refs_2_) | copy-start | bytes 1572868
  96.3 25.3 %collective-permute-start.15 = (bf16[256,1024]{1,0:T(8,128)(2,1)S(1)}, bf16[256,1024]{1,0:T(8,128)(2,1)}, u32[]{:S(2)}, u32[]{:S(2)}) collective-permute-start(bf16[256,1024]{1,0:T(8,128)(2,1)S(1)} %collective-permute-done.12.refs_2_), channel_id=1, source_target_pairs={{0,16},{4,0},{8,4},{12,8},{28,12},{24,28},{20,24},{16,20},{1,17},{... | collective-permute-start | bytes 1572872 | tf_op jit(solution)/shard_map/ppermute | solution.py:322
  96.6 40.7 %collective-permute-start.17 = (bf16[2,2304,128]{2,1,0:T(8,128)(2,1)S(1)}, bf16[2,2304,128]{2,1,0:T(8,128)(2,1)}, u32[]{:S(2)}, u32[]{:S(2)}) collective-permute-start(bf16[2,2304,128]{2,1,0:T(8,128)(2,1)S(1)} %get-tuple-element.36), channel_id=1, source_target_pairs={{0,3},{1,2},{2,1},{3,0},{4,7},{5,6},{6,5},{7,4},{8,11},{9,10},{10,... | collective-permute-start | bytes 3538952 | tf_op jit(solution)/shard_map/ppermute | solution.py:13
  109.0 15.3 %collective-permute-start.13 = (bf16[256,1024]{1,0:T(8,128)(2,1)S(1)}, bf16[256,1024]{1,0:T(8,128)(2,1)}, u32[]{:S(2)}, u32[]{:S(2)}) collective-permute-start(bf16[256,1024]{1,0:T(8,128)(2,1)S(1)} %constant_dynamic-slice_fusion.2.refs_0_), channel_id=1, source_target_pairs={{0,4},{4,8},{8,12},{12,28},{28,24},{24,20},{20,16},{16,0},{1,5},{5... | collective-permute-start | bytes 1572872 | tf_op jit(solution)/shard_map/ppermute | solution.py:322
  120.5 23.7 %copy-start.9 = (s32[192]{0:T(256)S(1)}, s32[192]{0:T(256)}, u32[]{:S(2)}) copy-start(s32[192]{0:T(256)} %param.18) | copy-start | bytes 2308
  120.5 2.9 %collective-permute-start.10 = (f32[576,64]{1,0:T(8,128)}, f32[576,64]{1,0:T(8,128)S(1)}, u32[]{:S(2)}, u32[]{:S(2)}) collective-permute-start(f32[576,64]{1,0:T(8,128)} %rank.5), channel_id=1, source_target_pairs={{0,1},{1,0},{2,3},{3,2},{4,5},{5,4},{6,7},{7,6},{8,9},{9,8},{10,11... | collective-permute-start | bytes 442376 | tf_op jit(solution)/shard_map/ppermute | solution.py:13
  121.5 29.8 %collective-permute-start.21 = (bf16[2,2304,128]{2,1,0:T(8,128)(2,1)S(1)}, bf16[2,2304,128]{2,1,0:T(8,128)(2,1)}, u32[]{:S(2)}, u32[]{:S(2)}) collective-permute-start(bf16[2,2304,128]{2,1,0:T(8,128)(2,1)S(1)} %get-tuple-element.38), channel_id=1, source_target_pairs={{0,1},{1,0},{2,3},{3,2},{4,5},{5,4},{6,7},{7,6},{8,9},{9,8},{10,11... | collective-permute-start | bytes 3538952 | tf_op jit(solution)/shard_map/ppermute | solution.py:13
  121.5 14.5 %collective-permute-start.19 = (bf16[256,1024]{1,0:T(8,128)(2,1)}, bf16[256,1024]{1,0:T(8,128)(2,1)S(1)}, u32[]{:S(2)}, u32[]{:S(2)}) collective-permute-start(bf16[256,1024]{1,0:T(8,128)(2,1)} %collective-permute-done.15.refs_4_), channel_id=1, source_target_pairs={{0,16},{4,0},{8,4},{12,8},{28,12},{24,28},{20,24},{16,20},{1,17},{... | collective-permute-start | bytes 1572872 | tf_op jit(solution)/shard_map/ppermute | solution.py:322
  124.4 14.5 %collective-permute-start.14 = (bf16[256,1024]{1,0:T(8,128)(2,1)}, bf16[256,1024]{1,0:T(8,128)(2,1)S(1)}, u32[]{:S(2)}, u32[]{:S(2)}) collective-permute-start(bf16[256,1024]{1,0:T(8,128)(2,1)} %collective-permute-done.13.refs_1_), channel_id=1, source_target_pairs={{0,4},{4,8},{8,12},{12,28},{28,24},{24,20},{20,16},{16,0},{1,5},{5... | collective-permute-start | bytes 1572872 | tf_op jit(solution)/shard_map/ppermute | solution.py:322
  126.0 10.5 %collective-permute-start.11 = (f32[576,64]{1,0:T(8,128)S(1)}, f32[576,64]{1,0:T(8,128)S(1)}, u32[]{:S(2)}, u32[]{:S(2)}) collective-permute-start(f32[576,64]{1,0:T(8,128)S(1)} %add.119), channel_id=1, source_target_pairs={{0,2},{1,3},{2,0},{3,1},{4,6},{5,7},{6,4},{7,5},{8,10},{9,11},{10,... | collective-permute-start | bytes 442376 | tf_op jit(solution)/shard_map/ppermute | solution.py:13
  136.1 15.3 %copy-start.7 = (bf16[256,1024]{1,0:T(8,128)(2,1)}, bf16[256,1024]{1,0:T(8,128)(2,1)S(1)}, u32[]{:S(2)}) copy-start(bf16[256,1024]{1,0:T(8,128)(2,1)S(1)} %collective-permute-done.19.refs_4_) | copy-start | bytes 1572868
  136.1 15.3 %collective-permute-start.20 = (bf16[256,1024]{1,0:T(8,128)(2,1)S(1)}, bf16[256,1024]{1,0:T(8,128)(2,1)}, u32[]{:S(2)}, u32[]{:S(2)}) collective-permute-start(bf16[256,1024]{1,0:T(8,128)(2,1)S(1)} %collective-permute-done.19.refs_4_), channel_id=1, source_target_pairs={{0,16},{4,0},{8,4},{12,8},{28,12},{24,28},{20,24},{16,20},{1,17},{... | collective-permute-start | bytes 1572872 | tf_op jit(solution)/shard_map/ppermute | solution.py:322
  138.8 6.1 %copy-start.6 = (bf16[256,1024]{1,0:T(8,128)(2,1)}, bf16[256,1024]{1,0:T(8,128)(2,1)S(1)}, u32[]{:S(2)}) copy-start(bf16[256,1024]{1,0:T(8,128)(2,1)S(1)} %collective-permute-done.14.refs_3_) | copy-start | bytes 1572868
  138.8 13.4 %collective-permute-start.18 = (bf16[256,1024]{1,0:T(8,128)(2,1)S(1)}, bf16[256,1024]{1,0:T(8,128)(2,1)S(1)}, u32[]{:S(2)}, u32[]{:S(2)}) collective-permute-start(bf16[256,1024]{1,0:T(8,128)(2,1)S(1)} %collective-permute-done.14.refs_3_), channel_id=1, source_target_pairs={{0,4},{4,8},{8,12},{12,28},{28,24},{24,20},{20,16},{16,0},{1,5},{5... | collective-permute-start | bytes 1572872 | tf_op jit(solution)/shard_map/ppermute | solution.py:322
  152.2 0.8 copy-start.8
  153.0 10.8 %copy-start.1 = (bf16[8,2048,64]{1,2,0:T(8,128)(2,1)S(1)}, bf16[8,2048,64]{1,2,0:T(8,128)(2,1)}, u32[]{:S(2)}) copy-start(bf16[8,2048,64]{1,2,0:T(8,128)(2,1)} %param.12) | copy-start | bytes 6291460

commit v6 on v5

--- a/solution.py
+++ b/solution.py
@@ -330,6 +330,36 @@
     return ring_hop(before, 1, owners), ring_hop(after, -1, owners)
 
 
+def split_rows(before, after):
+    rows, columns = before.shape
+    cut = rows * 3 // 4
+
+    def kernel(before_ref, after_ref, first_ref, last_ref, sems):
+        copies = [
+            pltpu.make_async_copy(before_ref.at[pl.ds(0, cut)], first_ref, sems.at[0]),
+            pltpu.make_async_copy(after_ref.at[pl.ds(cut, rows - cut)], last_ref, sems.at[1]),
+        ]
+        for copy in copies:
+            copy.start()
+        for copy in copies:
+            copy.wait()
+
+    return pl.pallas_call(
+        kernel,
+        out_shape=[
+            jax.ShapeDtypeStruct((cut, columns), before.dtype),
+            jax.ShapeDtypeStruct((rows - cut, columns), before.dtype),
+        ],
+        in_specs=[pl.BlockSpec(memory_space=pl.ANY)] * 2,
+        out_specs=[pl.BlockSpec(memory_space=pl.ANY)] * 2,
+        scratch_shapes=[pltpu.SemaphoreType.DMA((2,))],
+        cost_estimate=pl.CostEstimate(
+            flops=0, bytes_accessed=4 * rows * columns, transcendentals=0
+        ),
+        name="split",
+    )(before, after)
+
+
 def body(
     tokens,
     query_weight,
@@ -406,44 +436,33 @@
         down.append(ring_step(*gate(down[-1], *waits.get(k, [])), owners))
     groups = [[own_down]] + [[part] for pair in down[: owners - 2] for part in pair]
     ranks = add_ranks(starts[:early], flat_tokens, row_adapters, groups, rank)
-    before, after = gate(down[-1], ranks)
-    down.append([ring_hop(before, 1, owners)])
-    waits = {1: down[owners - 3]}
     if paired:
         far = gate(far, down[owners - 3])
         far_near = swap(far, 1, count)
         second = swap(gate(parcels[2], far), 2, count)
         third = swap(gate(parcels[3], second), 3, count)
         base = project_pair(ids[2:], [far], [far_near], query_weight, base)
-        waits = {1: [down[owners - 3], far]}
-
-    from_after = [ring_hop(gate(own_up, *waits[1]), -1, owners)]
-    from_before = [ring_hop(gate(own_up, before, from_after[0], base), 1, owners)]
+    before, after = gate(down[-1], ranks)
+    parts = split_rows(before, after)
+    down.append(ring_step(*parts, owners))
+
+    from_after = [ring_hop(gate(own_up, *(down[owners - 3] + (far,) if paired else [])), -1, owners)]
+    from_before = [ring_hop(gate(own_up, *parts), 1, owners)]
     if paired:
         first = swap(gate(parcels[1], from_after[0]), 1, count)
         key_values = [parcels[0], first, second, third]
-    groups = [[part] for part in down[owners - 2]]
+    groups = [[part] for part in down[owners - 2]] + [list(down[owners - 1])]
     ranks = add_ranks(
-        starts[early : early + 2], flat_tokens, row_adapters, groups, rank, earlier=ranks
-    )
-    ranks = add_ranks(
-        starts[early + 2 :],
-        flat_tokens,
-        row_adapters,
-        [down[owners - 1]],
-        rank,
-        earlier=ranks,
-        last=True,
+        starts[early:], flat_tokens, row_adapters, groups, rank, earlier=ranks, last=True
     )
     for k in range(2, owners + 1):
-        from_after.append(ring_hop(gate(from_after[-1], *waits.get(k, [])), -1, owners))
+        from_after.append(ring_hop(gate(from_after[-1], *(down[-1] if k == 2 else [])), -1, owners))
     bits = [1 << i for i in range((count - 1).bit_length())]
+    ranks = ranks + swap(ranks, bits[0], count)
     for k in range(2, owners):
-        for bit in bits[k - 2 : k - 1]:
-            ranks = ranks + swap(ranks, bit, count)
-        wait = [third] if paired and k == owners - 1 else []
-        from_before.append(ring_hop(gate(from_before[-1], ranks, *wait), 1, owners))
-    for bit in bits[owners - 2 :]:
+        wait = [ranks] + ([third, base] if paired else []) if k == owners - 1 else []
+        from_before.append(ring_hop(gate(from_before[-1], *wait), 1, owners))
+    for bit in bits[1:]:
         ranks = ranks + swap(ranks, bit, count)
     up = [part for pair in zip(from_before, from_after) for part in pair] + [from_after[-1]]
     groups = [[own_up]] + [[part] for part in up[: early - 1]]

time: 164 us -> 187 us (1.14)
  Pallas kernels: 57.3 us -> 87.3 us
  waiting for transfers between devices: 61.7 us -> 52.5 us
  local copies, waits for them, and re-layouts: 18.7 us -> 20.6 us
    pallas_call x0 -> x1, Pallas kernels: none -> 32.9 us  [split_rows(): pl.pallas_call(kernel, out_shape=[jax.ShapeDtypeStruct((cut, columns), be...]
    ppermute x8, waiting for transfers between devices: 27.6 us -> 1.45 us  [swap(): return lax.ppermute(array, 'tensor', [(i, i ^ bit) for i in range(count)])]
    ppermute x14 -> x15, waiting for transfers between devices: 34.1 us -> 51.1 us  [ring_hop(): return lax.ppermute(array, ('rep', 'dp'), pairs)]
    pallas_call x3 -> x2, Pallas kernels: 17.2 us -> 14.3 us  [add_ranks(): pl.pallas_call(kernel, out_shape=jax.ShapeDtypeStruct((rows, out_width),...]
    unnamed x25 -> x31, local copies, waits for them, and re-layouts: 6.85 us -> 8.31 us
    ppermute x14 -> x15, starting transfers between devices: 16.4 us -> 15.8 us  [ring_hop(): return lax.ppermute(array, ('rep', 'dp'), pairs)]
  transfers between devices with their start and end apart: 22 -> 23, of which waited for: 10 -> 11; matrix products, arithmetic and copies ran while one was open for 12% -> 11% of each run, Pallas kernels for 28% -> 41%
where the time goes in v6:
time: 187 us; the launch traced here: 186 us
  Pallas kernels  87.3 us (47%)
  waiting for transfers between devices  52.5 us (28%)
  starting transfers between devices  21.8 us (12%)
  local copies, waits for them, and re-layouts  20.6 us (11%)
  other arithmetic  3.56 us (2%)
    ppermute x15, waiting for transfers between devices, ring_hop(): return lax.ppermute(array, ('rep', 'dp'), pairs)  51.1 us
    pallas_call x1, Pallas kernels, split_rows(): pl.pallas_call(kernel, out_shape=[jax.ShapeDtypeStruct((cut, columns), be...  32.9 us
    pallas_call x2, Pallas kernels, project_pair(): pl.pallas_call(kernel, out_shape=jax.ShapeDtypeStruct((rows, columns), jn...  23 us
    ppermute x15, starting transfers between devices, ring_hop(): return lax.ppermute(array, ('rep', 'dp'), pairs)  15.8 us
    pallas_call x2, Pallas kernels, add_ranks(): pl.pallas_call(kernel, out_shape=jax.ShapeDtypeStruct((rows, out_width),...  14.3 us
    pallas_call x1, Pallas kernels, attend(): pl.pallas_call(kernel, out_shape=jax.ShapeDtypeStruct((steps, rows, width...  10.8 us
    unnamed x31, local copies, waits for them, and re-layouts  8.31 us
    pallas_call x1, Pallas kernels, early_query(): pl.pallas_call(kernel, out_shape=jax.ShapeDtypeStruct((rows, columns), jn...  6.38 us
  transfers between devices with their start and end apart: 23, of which 11 were waited for; matrix products, arithmetic and copies ran while one was open for 11% of the time, Pallas kernels for 41%

profile of v6, /device:TPU:0, one launch (start us, length us, event | category | flops | bytes accessed | tf_op | source)
XLA Modules:
  0.0 186.1 jit_solution(9851886333426494839)
XLA Ops:
  0.5 1.1 copy-done
  1.7 3.1 %collective-permute-start.1 = (bf16[256,2048]{1,0:T(8,128)(2,1)S(1)}, bf16[256,2048]{1,0:T(8,128)(2,1)}, u32[]{:S(2)}, u32[]{:S(2)}) collective-permute-start(bf16[256,2048]{1,0:T(8,128)(2,1)S(1)} %constant_dynamic-slice_fusion.3.refs_0_), channel_id=1, source_target_pairs={{0,4},{4,8},{8,12},{12,28},{28,24},{24,20},{20,16},{16,0},{1,5},{5... | collective-permute-start | bytes 3145736 | tf_op jit(solution)/shard_map/ppermute | solution.py:322
  4.8 1.9 %collective-permute-start = (bf16[576,2048]{1,0:T(8,128)(2,1)}, bf16[576,2048]{1,0:T(8,128)(2,1)S(1)}, u32[]{:S(2)}, u32[]{:S(2)}) collective-permute-start(bf16[576,2048]{1,0:T(8,128)(2,1)} %bitcast.42), channel_id=1, source_target_pairs={{0,2},{1,3},{2,0},{3,1},{4,6},{5,7},{6,4},{7,5},{8,10},{9,11},{10,... | collective-permute-start | bytes 7077896 | tf_op jit(solution)/shard_map/ppermute | solution.py:13
  6.7 3.5 %copy_dynamic-update-slice_fusion.1 = bf16[4,2,2304,128]{3,2,1,0:T(8,128)(2,1)} fusion(bf16[4,1,2304,128]{3,0,2,1:T(4,128)(2,1)} %bitcast.39), kind=kLoop, calls=%fused_computation.1 | loop fusion | bytes 4718592
  10.2 1.7 copy_dynamic-update-slice_fusion
  11.9 4.6 %dynamic-slice_bitcast_fusion = (bf16[2,2304,128]{2,1,0:T(8,128)(2,1)}, bf16[2,2304,128]{2,1,0:T(8,128)(2,1)}, bf16[2,2304,128]{2,1,0:T(8,128)(2,1)}, bf16[2,2304,128]{2,1,0:T(8,128)(2,1)}) fusion(bf16[4,2,2304,128]{3,2,1,0:T(8,128)(2,1)} %copy_dynamic-update-slice_fusion, s32[]{:T(128)S(6)} %select_n.67, s32[]{:T(128)S(6)} %select_n.66, s32[]{:T(128)S(6)} %select_n.65, ...), kind=kLoop, calls=%fused_computation.2 | loop fusion | bytes 9437200 | tf_op jit(solution)/shard_map/jit(dynamic_index_in_dim)/squeeze | solution.py:417
  16.5 0.6 pad_add_fusion.1.ids_ref
  17.1 10.9 %project.2.refs_4_ = f32[576,1024]{1,0:T(8,128)} custom-call(s32[2]{0:T(128)} %pad_add_fusion.1.ids_ref, bf16[576,2048]{1,0:T(8,128)(2,1)} %bitcast.43, bf16[576,2048]{1,0:T(8,128)(2,1)} %collective-permute-done.3.refs_1_, bf16[8192,1024]{1,0:T(8,128)(2,1)} %refs_3_.3, bf16[8192,1024]{1,0:T(8,128)(2,1)} %refs_3_.3), custom_call_target="tpu_custom_call" | custom-call | flops 4831838208 | bytes 15466496 | tf_op jit(solution)/shard_map/project/pallas_call | solution.py:52
  28.1 1.4 collective-permute-done.2.refs_2_
  29.5 1.6 collective-permute-start.4
  31.5 22.0 %collective-permute-done.4.refs_3_ = bf16[256,2048]{1,0:T(8,128)(2,1)} collective-permute-done((bf16[256,2048]{1,0:T(8,128)(2,1)}, bf16[256,2048]{1,0:T(8,128)(2,1)}, u32[]{:S(2)}, u32[]{:S(2)}) %collective-permute-start.4) | collective-permute-done | bytes 1048608 | tf_op jit(solution)/shard_map/ppermute | solution.py:322
  53.5 1.3 collective-permute-done.5.refs_4_
  54.8 1.6 collective-permute-start.7
  56.8 0.9 collective-permute-done.refs_0_
  57.7 1.7 collective-permute-start.17
  59.3 0.9 reshape_tile.4.adapter_ref.refs_2_
  60.3 0.6 stack.61.starts_ref
  60.9 8.0 %rank.2.refs_4_ = f32[576,256]{1,0:T(8,128)} custom-call(s32[5]{0:T(128)} %stack.61.starts_ref, bf16[576,2048]{1,0:T(8,128)(2,1)} %bitcast.44, s32[576,1]{1,0:T(8,128)} %reshape_tile.4.adapter_ref.refs_2_, bf16[256,2048]{1,0:T(8,128)(2,1)} %copy-done.5, bf16[256,2048]{1,0:T(8,128)(2,1)} %collective-permute-done.1.refs_1_, ...), custom_call_target="tpu_custom_call" | custom-call | flops 3019898880 | bytes 7602176 | tf_op jit(solution)/shard_map/rank/pallas_call | solution.py:99
  68.9 8.6 %collective-permute-done.7.before_ref.refs_0_ = bf16[256,2048]{1,0:T(8,128)(2,1)S(1)} collective-permute-done((bf16[256,2048]{1,0:T(8,128)(2,1)}, bf16[256,2048]{1,0:T(8,128)(2,1)S(1)}, u32[]{:S(2)}, u32[]{:S(2)}) %collective-permute-start.7) | collective-permute-done | bytes 1048608 | tf_op jit(solution)/shard_map/ppermute | solution.py:322
  77.5 1.4 collective-permute-done.8.after_ref.refs_1_
  78.9 32.9 %split.1 = (bf16[192,2048]{1,0:T(8,128)(2,1)}, bf16[64,2048]{1,0:T(8,128)(2,1)}) custom-call(bf16[256,2048]{1,0:T(8,128)(2,1)} %copy-done.6, bf16[256,2048]{1,0:T(8,128)(2,1)} %collective-permute-done.8.after_ref.refs_1_), custom_call_target="tpu_custom_call" | custom-call | bytes 2097152 | tf_op jit(solution)/shard_map/split/pallas_call | solution.py:347
  111.8 1.6 collective-permute-start.9
  113.4 1.1 constant_dynamic-slice_fusion.2.refs_0_
  114.5 0.6 collective-permute-start.14
  115.5 11.7 %collective-permute-done.14.refs_2_ = bf16[256,1024]{1,0:T(8,128)(2,1)S(1)} collective-permute-done((bf16[256,1024]{1,0:T(8,128)(2,1)S(1)}, bf16[256,1024]{1,0:T(8,128)(2,1)S(1)}, u32[]{:S(2)}, u32[]{:S(2)}) %collective-permute-start.14) | collective-permute-done | bytes 524320 | tf_op jit(solution)/shard_map/ppermute | solution.py:322
  127.2 1.5 collective-permute-start.13
  128.7 2.6 %collective-permute-done.10.refs_3_ = bf16[64,2048]{1,0:T(8,128)(2,1)S(1)} collective-permute-done((bf16[64,2048]{1,0:T(8,128)(2,1)}, bf16[64,2048]{1,0:T(8,128)(2,1)S(1)}, u32[]{:S(2)}, u32[]{:S(2)}) %collective-permute-start.10) | collective-permute-done | bytes 262176 | tf_op jit(solution)/shard_map/ppermute | solution.py:322
  131.3 0.7 copy-done.13
  132.0 0.7 collective-permute-done.9.refs_2_
  133.1 0.7 pad_add_fusion.2.starts_ref
  133.8 6.3 %rank.3 = f32[576,64]{1,0:T(8,128)} custom-call(s32[3]{0:T(128)} %pad_add_fusion.2.starts_ref, bf16[576,2048]{1,0:T(8,128)(2,1)} %bitcast.45, s32[576,1]{1,0:T(8,128)} %reshape_tile.4.adapter_ref.refs_2_, bf16[256,2048]{1,0:T(8,128)(2,1)} %copy-done.6, bf16[256,2048]{1,0:T(8,128)(2,1)} %collective-permute-done.8.after_ref.refs_1_, ...), custom_call_target="tpu_custom_call" | custom-call | flops 1811939328 | bytes 5505024 | tf_op jit(solution)/shard_map/rank/pallas_call | solution.py:99
  140.6 1.4 collective-permute-done.16.refs_4_
  141.9 1.5 collective-permute-start.15
  144.5 1.0 add.119
  145.6 12.1 %project.3.base_ref = f32[576,1024]{1,0:T(8,128)} custom-call(s32[2]{0:T(128)} %pad_add_fusion.ids_ref, bf16[576,2048]{1,0:T(8,128)(2,1)} %copy-done.2, bf16[576,2048]{1,0:T(8,128)(2,1)} %collective-permute-done.6.refs_1_, bf16[8192,1024]{1,0:T(8,128)(2,1)} %refs_3_.3, bf16[8192,1024]{1,0:T(8,128)(2,1)} %refs_3_.3, f32[576,1024]{1,0:T(8,128)} %project.2.refs_4_), custom_call_target="tpu_custom_call" | custom-call | flops 4831838208 | bytes 15466496 | tf_op jit(solution)/shard_map/project/pallas_call | solution.py:52
  157.7 1.6 collective-permute-start.19
  159.7 1.5 collective-permute-start.12
  161.2 0.7 concatenate.9.scalars_ref
  161.9 1.9 constant_dynamic-slice_fusion
  163.8 0.7 copy.28
  164.4 0.7 copy.29
  165.1 0.8 copy.21.refs_6_
  165.9 0.6 collective-permute-done.12
  166.5 0.7 add.120.rank_ref.refs_1_
  167.2 6.4 %delta.1.refs_0_ = f32[576,1024]{1,0:T(8,128)} custom-call(s32[5]{0:T(128)} %stack.61.starts_ref, f32[576,1024]{1,0:T(8,128)} %project.3.base_ref, f32[576,64]{1,0:T(8,128)} %add.120.rank_ref.refs_1_, s32[576,1]{1,0:T(8,128)} %reshape_tile.4.adapter_ref.refs_2_, bf16[256,1024]{1,0:T(8,128)(2,1)} %copy-done.4, ...), custom_call_target="tpu_custom_call" | custom-call | flops 1509949440 | bytes 7340032 | tf_op jit(solution)/shard_map/delta/pallas_call | solution.py:145
  173.6 0.8 copy-done.9
  174.4 0.8 copy-done.10
  175.2 10.8 %attend.1 = bf16[3,192,1024]{2,1,0:T(8,128)(2,1)} custom-call(s32[7]{0:T(128)} %concatenate.9.scalars_ref, f32[576,1024]{1,0:T(8,128)} %delta.1.refs_0_, f32[576,64]{1,0:T(8,128)} %add.120.rank_ref.refs_1_, s32[576,1]{1,0:T(8,128)} %reshape_tile.4.adapter_ref.refs_2_, bf16[256,1024]{1,0:T(8,128)(2,1)} %copy-done.9, ...), custom_call_target="tpu_custom_call" | custom-call | flops 481296384 | bytes 7077888 | tf_op jit(solution)/shard_map/attend/pallas_call | solution.py:295
  (51 shorter events, 4.5 us)
Async XLA Ops:
  0.0 1.6 copy-start
  0.0 17.1 %collective-permute-start.3 = (bf16[576,2048]{1,0:T(8,128)(2,1)}, bf16[576,2048]{1,0:T(8,128)(2,1)}, u32[]{:S(2)}, u32[]{:S(2)}) collective-permute-start(bf16[576,2048]{1,0:T(8,128)(2,1)} %bitcast.41), channel_id=1, source_target_pairs={{0,1},{1,0},{2,3},{3,2},{4,5},{5,4},{6,7},{7,6},{8,9},{9,8},{10,11... | collective-permute-start | bytes 7077896 | tf_op jit(solution)/shard_map/ppermute | solution.py:13
  1.7 8.5 %copy-start.5 = (bf16[256,2048]{1,0:T(8,128)(2,1)}, bf16[256,2048]{1,0:T(8,128)(2,1)S(1)}, u32[]{:S(2)}) copy-start(bf16[256,2048]{1,0:T(8,128)(2,1)S(1)} %constant_dynamic-slice_fusion.3.refs_0_) | copy-start | bytes 3145732
  1.7 26.4 %collective-permute-start.1 = (bf16[256,2048]{1,0:T(8,128)(2,1)S(1)}, bf16[256,2048]{1,0:T(8,128)(2,1)}, u32[]{:S(2)}, u32[]{:S(2)}) collective-permute-start(bf16[256,2048]{1,0:T(8,128)(2,1)S(1)} %constant_dynamic-slice_fusion.3.refs_0_), channel_id=1, source_target_pairs={{0,4},{4,8},{8,12},{12,28},{28,24},{24,20},{20,16},{16,0},{1,5},{5... | collective-permute-start | bytes 3145736 | tf_op jit(solution)/shard_map/ppermute | solution.py:322
  4.8 24.7 %collective-permute-start.2 = (bf16[256,2048]{1,0:T(8,128)(2,1)S(1)}, bf16[256,2048]{1,0:T(8,128)(2,1)}, u32[]{:S(2)}, u32[]{:S(2)}) collective-permute-start(bf16[256,2048]{1,0:T(8,128)(2,1)S(1)} %constant_dynamic-slice_fusion.3.refs_0_), channel_id=1, source_target_pairs={{0,16},{4,0},{8,4},{12,8},{28,12},{24,28},{20,24},{16,20},{1,17},{... | collective-permute-start | bytes 3145736 | tf_op jit(solution)/shard_map/ppermute | solution.py:322
  4.8 52.9 %collective-permute-start = (bf16[576,2048]{1,0:T(8,128)(2,1)}, bf16[576,2048]{1,0:T(8,128)(2,1)S(1)}, u32[]{:S(2)}, u32[]{:S(2)}) collective-permute-start(bf16[576,2048]{1,0:T(8,128)(2,1)} %bitcast.42), channel_id=1, source_target_pairs={{0,2},{1,3},{2,0},{3,1},{4,6},{5,7},{6,4},{7,5},{8,10},{9,11},{10,... | collective-permute-start | bytes 7077896 | tf_op jit(solution)/shard_map/ppermute | solution.py:13
  6.7 3.5 %copy-start.3 = (bf16[192,4,12,128]{3,1,2,0:T(4,128)(2,1)S(1)}, bf16[192,4,12,128]{3,1,2,0:T(4,128)(2,1)}, u32[]{:S(2)}) copy-start(bf16[192,4,12,128]{3,1,2,0:T(4,128)(2,1)} %param.15) | copy-start | bytes 7077892
  17.1 42.2 %copy-start.12 = (s32[192]{0:T(256)S(1)}, s32[192]{0:T(256)}, u32[]{:S(2)}) copy-start(s32[192]{0:T(256)} %param.19) | copy-start | bytes 2308
  29.5 24.0 %collective-permute-start.4 = (bf16[256,2048]{1,0:T(8,128)(2,1)}, bf16[256,2048]{1,0:T(8,128)(2,1)}, u32[]{:S(2)}, u32[]{:S(2)}) collective-permute-start(bf16[256,2048]{1,0:T(8,128)(2,1)} %collective-permute-done.1.refs_1_), channel_id=1, source_target_pairs={{0,4},{4,8},{8,12},{12,28},{28,24},{24,20},{20,16},{16,0},{1,5},{5... | collective-permute-start | bytes 3145736 | tf_op jit(solution)/shard_map/ppermute | solution.py:322
  31.1 23.7 %collective-permute-start.5 = (bf16[256,2048]{1,0:T(8,128)(2,1)}, bf16[256,2048]{1,0:T(8,128)(2,1)}, u32[]{:S(2)}, u32[]{:S(2)}) collective-permute-start(bf16[256,2048]{1,0:T(8,128)(2,1)} %collective-permute-done.2.refs_2_), channel_id=1, source_target_pairs={{0,16},{4,0},{8,4},{12,8},{28,12},{24,28},{20,24},{16,20},{1,17},{... | collective-permute-start | bytes 3145736 | tf_op jit(solution)/shard_map/ppermute | solution.py:322
  54.8 22.7 %collective-permute-start.7 = (bf16[256,2048]{1,0:T(8,128)(2,1)}, bf16[256,2048]{1,0:T(8,128)(2,1)S(1)}, u32[]{:S(2)}, u32[]{:S(2)}) collective-permute-start(bf16[256,2048]{1,0:T(8,128)(2,1)} %collective-permute-done.4.refs_3_), channel_id=1, source_target_pairs={{0,4},{4,8},{8,12},{12,28},{28,24},{24,20},{20,16},{16,0},{1,5},{5... | collective-permute-start | bytes 3145736 | tf_op jit(solution)/shard_map/ppermute | solution.py:322
  56.4 22.5 %collective-permute-start.8 = (bf16[256,2048]{1,0:T(8,128)(2,1)}, bf16[256,2048]{1,0:T(8,128)(2,1)}, u32[]{:S(2)}, u32[]{:S(2)}) collective-permute-start(bf16[256,2048]{1,0:T(8,128)(2,1)} %collective-permute-done.5.refs_4_), channel_id=1, source_target_pairs={{0,16},{4,0},{8,4},{12,8},{28,12},{24,28},{20,24},{16,20},{1,17},{... | collective-permute-start | bytes 3145736 | tf_op jit(solution)/shard_map/ppermute | solution.py:322
  57.7 11.2 %copy-start.2 = (bf16[576,2048]{1,0:T(8,128)(2,1)}, bf16[576,2048]{1,0:T(8,128)(2,1)S(1)}, u32[]{:S(2)}) copy-start(bf16[576,2048]{1,0:T(8,128)(2,1)S(1)} %collective-permute-done.refs_0_) | copy-start | bytes 7077892
  57.7 87.9 %collective-permute-start.6 = (bf16[576,2048]{1,0:T(8,128)(2,1)S(1)}, bf16[576,2048]{1,0:T(8,128)(2,1)}, u32[]{:S(2)}, u32[]{:S(2)}) collective-permute-start(bf16[576,2048]{1,0:T(8,128)(2,1)S(1)} %collective-permute-done.refs_0_), channel_id=1, source_target_pairs={{0,1},{1,0},{2,3},{3,2},{4,5},{5,4},{6,7},{7,6},{8,9},{9,8},{10,11... | collective-permute-start | bytes 7077896 | tf_op jit(solution)/shard_map/ppermute | solution.py:13
  57.7 57.8 %collective-permute-start.17 = (bf16[2,2304,128]{2,1,0:T(8,128)(2,1)}, bf16[2,2304,128]{2,1,0:T(8,128)(2,1)}, u32[]{:S(2)}, u32[]{:S(2)}) collective-permute-start(bf16[2,2304,128]{2,1,0:T(8,128)(2,1)} %get-tuple-element.41), channel_id=1, source_target_pairs={{0,2},{1,3},{2,0},{3,1},{4,6},{5,7},{6,4},{7,5},{8,10},{9,11},{10,... | collective-permute-start | bytes 3538952 | tf_op jit(solution)/shard_map/ppermute | solution.py:13
  77.5 1.4 copy-start.6
  111.8 20.8 %collective-permute-start.9 = (bf16[192,2048]{1,0:T(8,128)(2,1)}, bf16[192,2048]{1,0:T(8,128)(2,1)}, u32[]{:S(2)}, u32[]{:S(2)}) collective-permute-start(bf16[192,2048]{1,0:T(8,128)(2,1)} %get-tuple-element.36), channel_id=1, source_target_pairs={{0,4},{4,8},{8,12},{12,28},{28,24},{24,20},{20,16},{16,0},{1,5},{5... | collective-permute-start | bytes 2359304 | tf_op jit(solution)/shard_map/ppermute | solution.py:322
  114.5 25.6 %copy-start.4 = (bf16[256,1024]{1,0:T(8,128)(2,1)}, bf16[256,1024]{1,0:T(8,128)(2,1)S(1)}, u32[]{:S(2)}) copy-start(bf16[256,1024]{1,0:T(8,128)(2,1)S(1)} %constant_dynamic-slice_fusion.2.refs_0_) | copy-start | bytes 1572868
  114.5 12.7 %collective-permute-start.14 = (bf16[256,1024]{1,0:T(8,128)(2,1)S(1)}, bf16[256,1024]{1,0:T(8,128)(2,1)S(1)}, u32[]{:S(2)}, u32[]{:S(2)}) collective-permute-start(bf16[256,1024]{1,0:T(8,128)(2,1)S(1)} %constant_dynamic-slice_fusion.2.refs_0_), channel_id=1, source_target_pairs={{0,16},{4,0},{8,4},{12,8},{28,12},{24,28},{20,24},{16,20},{1,17},{... | collective-permute-start | bytes 1572872 | tf_op jit(solution)/shard_map/ppermute | solution.py:322
  115.0 16.3 %collective-permute-start.10 = (bf16[64,2048]{1,0:T(8,128)(2,1)}, bf16[64,2048]{1,0:T(8,128)(2,1)S(1)}, u32[]{:S(2)}, u32[]{:S(2)}) collective-permute-start(bf16[64,2048]{1,0:T(8,128)(2,1)} %get-tuple-element.37), channel_id=1, source_target_pairs={{0,16},{4,0},{8,4},{12,8},{28,12},{24,28},{20,24},{16,20},{1,17},{... | collective-permute-start | bytes 786440 | tf_op jit(solution)/shard_map/ppermute | solution.py:322
  115.5 42.2 %collective-permute-start.18 = (bf16[2,2304,128]{2,1,0:T(8,128)(2,1)}, bf16[2,2304,128]{2,1,0:T(8,128)(2,1)}, u32[]{:S(2)}, u32[]{:S(2)}) collective-permute-start(bf16[2,2304,128]{2,1,0:T(8,128)(2,1)} %get-tuple-element.42), channel_id=1, source_target_pairs={{0,3},{1,2},{2,1},{3,0},{4,7},{5,6},{6,5},{7,4},{8,11},{9,10},{10,... | collective-permute-start | bytes 3538952 | tf_op jit(solution)/shard_map/ppermute | solution.py:13
  127.2 12.9 %copy-start.7 = (bf16[256,1024]{1,0:T(8,128)(2,1)}, bf16[256,1024]{1,0:T(8,128)(2,1)S(1)}, u32[]{:S(2)}) copy-start(bf16[256,1024]{1,0:T(8,128)(2,1)S(1)} %collective-permute-done.14.refs_2_) | copy-start | bytes 1572868
  127.2 12.9 %collective-permute-start.13 = (bf16[256,1024]{1,0:T(8,128)(2,1)S(1)}, bf16[256,1024]{1,0:T(8,128)(2,1)}, u32[]{:S(2)}, u32[]{:S(2)}) collective-permute-start(bf16[256,1024]{1,0:T(8,128)(2,1)S(1)} %constant_dynamic-slice_fusion.2.refs_0_), channel_id=1, source_target_pairs={{0,4},{4,8},{8,12},{12,28},{28,24},{24,20},{20,16},{16,0},{1,5},{5... | collective-permute-start | bytes 1572872 | tf_op jit(solution)/shard_map/ppermute | solution.py:322
  131.3 0.7 copy-start.13
  132.7 9.3 %collective-permute-start.16 = (bf16[256,1024]{1,0:T(8,128)(2,1)S(1)}, bf16[256,1024]{1,0:T(8,128)(2,1)}, u32[]{:S(2)}, u32[]{:S(2)}) collective-permute-start(bf16[256,1024]{1,0:T(8,128)(2,1)S(1)} %collective-permute-done.14.refs_2_), channel_id=1, source_target_pairs={{0,16},{4,0},{8,4},{12,8},{28,12},{24,28},{20,24},{16,20},{1,17},{... | collective-permute-start | bytes 1572872 | tf_op jit(solution)/shard_map/ppermute | solution.py:322
  140.1 3.4 %collective-permute-start.11 = (f32[576,64]{1,0:T(8,128)}, f32[576,64]{1,0:T(8,128)S(1)}, u32[]{:S(2)}, u32[]{:S(2)}) collective-permute-start(f32[576,64]{1,0:T(8,128)} %rank.3), channel_id=1, source_target_pairs={{0,1},{1,0},{2,3},{3,2},{4,5},{5,4},{6,7},{7,6},{8,9},{9,8},{10,11... | collective-permute-start | bytes 442376 | tf_op jit(solution)/shard_map/ppermute | solution.py:13
  140.1 33.5 %collective-permute-start.22 = (bf16[2,2304,128]{2,1,0:T(8,128)(2,1)}, bf16[2,2304,128]{2,1,0:T(8,128)(2,1)}, u32[]{:S(2)}, u32[]{:S(2)}) collective-permute-start(bf16[2,2304,128]{2,1,0:T(8,128)(2,1)} %get-tuple-element.44), channel_id=1, source_target_pairs={{0,1},{1,0},{2,3},{3,2},{4,5},{5,4},{6,7},{7,6},{8,9},{9,8},{10,11... | collective-permute-start | bytes 3538952 | tf_op jit(solution)/shard_map/ppermute | solution.py:13
  141.9 15.7 %collective-permute-start.15 = (bf16[256,1024]{1,0:T(8,128)(2,1)}, bf16[256,1024]{1,0:T(8,128)(2,1)S(1)}, u32[]{:S(2)}, u32[]{:S(2)}) collective-permute-start(bf16[256,1024]{1,0:T(8,128)(2,1)} %collective-permute-done.13.refs_1_), channel_id=1, source_target_pairs={{0,4},{4,8},{8,12},{12,28},{28,24},{24,20},{20,16},{16,0},{1,5},{5... | collective-permute-start | bytes 1572872 | tf_op jit(solution)/shard_map/ppermute | solution.py:322
  143.5 15.8 %collective-permute-start.20 = (bf16[256,1024]{1,0:T(8,128)(2,1)}, bf16[256,1024]{1,0:T(8,128)(2,1)}, u32[]{:S(2)}, u32[]{:S(2)}) collective-permute-start(bf16[256,1024]{1,0:T(8,128)(2,1)} %collective-permute-done.16.refs_4_), channel_id=1, source_target_pairs={{0,16},{4,0},{8,4},{12,8},{28,12},{24,28},{20,24},{16,20},{1,17},{... | collective-permute-start | bytes 1572872 | tf_op jit(solution)/shard_map/ppermute | solution.py:322
  145.5 19.6 %copy-start.11 = (s32[192]{0:T(256)S(1)}, s32[192]{0:T(256)}, u32[]{:S(2)}) copy-start(s32[192]{0:T(256)} %param.18) | copy-start | bytes 2308
  157.6 9.6 %copy-start.8 = (bf16[256,1024]{1,0:T(8,128)(2,1)}, bf16[256,1024]{1,0:T(8,128)(2,1)S(1)}, u32[]{:S(2)}) copy-start(bf16[256,1024]{1,0:T(8,128)(2,1)S(1)} %collective-permute-done.15.refs_3_) | copy-start | bytes 1572868
  157.7 15.9 %collective-permute-start.19 = (bf16[256,1024]{1,0:T(8,128)(2,1)S(1)}, bf16[256,1024]{1,0:T(8,128)(2,1)S(1)}, u32[]{:S(2)}, u32[]{:S(2)}) collective-permute-start(bf16[256,1024]{1,0:T(8,128)(2,1)S(1)} %collective-permute-done.15.refs_3_), channel_id=1, source_target_pairs={{0,4},{4,8},{8,12},{12,28},{28,24},{24,20},{20,16},{16,0},{1,5},{5... | collective-permute-start | bytes 1572872 | tf_op jit(solution)/shard_map/ppermute | solution.py:322
  159.2 15.2 %collective-permute-start.21 = (bf16[256,1024]{1,0:T(8,128)(2,1)}, bf16[256,1024]{1,0:T(8,128)(2,1)S(1)}, u32[]{:S(2)}, u32[]{:S(2)}) collective-permute-start(bf16[256,1024]{1,0:T(8,128)(2,1)} %collective-permute-done.20.refs_4_), channel_id=1, source_target_pairs={{0,16},{4,0},{8,4},{12,8},{28,12},{24,28},{20,24},{16,20},{1,17},{... | collective-permute-start | bytes 1572872 | tf_op jit(solution)/shard_map/ppermute | solution.py:322
  159.7 6.7 %collective-permute-start.12 = (f32[576,64]{1,0:T(8,128)S(1)}, f32[576,64]{1,0:T(8,128)S(1)}, u32[]{:S(2)}, u32[]{:S(2)}) collective-permute-start(f32[576,64]{1,0:T(8,128)S(1)} %add.119), channel_id=1, source_target_pairs={{0,2},{1,3},{2,0},{3,1},{4,6},{5,7},{6,4},{7,5},{8,10},{9,11},{10,... | collective-permute-start | bytes 442376 | tf_op jit(solution)/shard_map/ppermute | solution.py:13
  173.6 0.8 copy-start.9
  174.4 0.8 copy-start.10
  175.2 10.8 %copy-start.1 = (bf16[8,2048,64]{1,2,0:T(8,128)(2,1)S(1)}, bf16[8,2048,64]{1,2,0:T(8,128)(2,1)}, u32[]{:S(2)}) copy-start(bf16[8,2048,64]{1,2,0:T(8,128)(2,1)} %param.12) | copy-start | bytes 6291460

commit v7 on v6

--- a/solution.py
+++ b/solution.py
@@ -334,15 +334,9 @@
     rows, columns = before.shape
     cut = rows * 3 // 4
 
-    def kernel(before_ref, after_ref, first_ref, last_ref, sems):
-        copies = [
-            pltpu.make_async_copy(before_ref.at[pl.ds(0, cut)], first_ref, sems.at[0]),
-            pltpu.make_async_copy(after_ref.at[pl.ds(cut, rows - cut)], last_ref, sems.at[1]),
-        ]
-        for copy in copies:
-            copy.start()
-        for copy in copies:
-            copy.wait()
+    def kernel(before_ref, after_ref, first_ref, last_ref):
+        first_ref[...] = before_ref[...]
+        last_ref[...] = after_ref[...]
 
     return pl.pallas_call(
         kernel,
@@ -350,9 +344,16 @@
             jax.ShapeDtypeStruct((cut, columns), before.dtype),
             jax.ShapeDtypeStruct((rows - cut, columns), before.dtype),
         ],
-        in_specs=[pl.BlockSpec(memory_space=pl.ANY)] * 2,
-        out_specs=[pl.BlockSpec(memory_space=pl.ANY)] * 2,
-        scratch_shapes=[pltpu.SemaphoreType.DMA((2,))],
+        grid=(1,),
+        in_specs=[
+            pl.BlockSpec((cut, columns), lambda g: (0, 0)),
+            pl.BlockSpec((rows - cut, columns), lambda g: (3, 0)),
+        ],
+        out_specs=[
+            pl.BlockSpec((cut, columns), lambda g: (0, 0)),
+            pl.BlockSpec((rows - cut, columns), lambda g: (0, 0)),
+        ],
+        compiler_params=pltpu.CompilerParams(vmem_limit_bytes=VMEM_LIMIT),
         cost_estimate=pl.CostEstimate(
             flops=0, bytes_accessed=4 * rows * columns, transcendentals=0
         ),

time: 187 us -> 156 us (0.83)
  Pallas kernels: 87.3 us -> 56.7 us
    pallas_call x1, Pallas kernels: 32.9 us -> 2.22 us  [split_rows(): pl.pallas_call(kernel, out_shape=[jax.ShapeDtypeStruct((cut, columns), be...]
    ppermute x8, waiting for transfers between devices: 1.45 us -> 4.13 us  [swap(): return lax.ppermute(array, 'tensor', [(i, i ^ bit) for i in range(count)])]
    ppermute x15, waiting for transfers between devices: 51.1 us -> 48.5 us  [ring_hop(): return lax.ppermute(array, ('rep', 'dp'), pairs)]
    unnamed x31 -> x33, local copies, waits for them, and re-layouts: 8.31 us -> 8.34 us
  transfers between devices with their start and end apart: 23 -> 23, of which waited for: 11 -> 12; matrix products, arithmetic and copies ran while one was open for 11% -> 13% of each run, Pallas kernels for 41% -> 30%
where the time goes in v7:
time: 156 us; the launch traced here: 155 us
  Pallas kernels  56.7 us (36%)
  waiting for transfers between devices  52.6 us (34%)
  starting transfers between devices  22.7 us (15%)
  local copies, waits for them, and re-layouts  19.5 us (12%)
  other arithmetic  3.65 us (2%)
    ppermute x15, waiting for transfers between devices, ring_hop(): return lax.ppermute(array, ('rep', 'dp'), pairs)  48.5 us
    pallas_call x2, Pallas kernels, project_pair(): pl.pallas_call(kernel, out_shape=jax.ShapeDtypeStruct((rows, columns), jn...  23 us
    ppermute x15, starting transfers between devices, ring_hop(): return lax.ppermute(array, ('rep', 'dp'), pairs)  15.7 us
    pallas_call x2, Pallas kernels, add_ranks(): pl.pallas_call(kernel, out_shape=jax.ShapeDtypeStruct((rows, out_width),...  14.3 us
    pallas_call x1, Pallas kernels, attend(): pl.pallas_call(kernel, out_shape=jax.ShapeDtypeStruct((steps, rows, width...  10.8 us
    unnamed x33, local copies, waits for them, and re-layouts  8.34 us
    ppermute x8, starting transfers between devices, swap(): return lax.ppermute(array, 'tensor', [(i, i ^ bit) for i in range(count)])  7.01 us
    pallas_call x1, Pallas kernels, early_query(): pl.pallas_call(kernel, out_shape=jax.ShapeDtypeStruct((rows, columns), jn...  6.39 us
  transfers between devices with their start and end apart: 23, of which 12 were waited for; matrix products, arithmetic and copies ran while one was open for 13% of the time, Pallas kernels for 30%

profile of v7, /device:TPU:0, one launch (start us, length us, event | category | flops | bytes accessed | tf_op | source)
XLA Modules:
  0.0 155.4 jit_solution(7627467718263841724)
XLA Ops:
  0.5 1.1 copy-done
  1.7 3.1 %collective-permute-start.1 = (bf16[256,2048]{1,0:T(8,128)(2,1)S(1)}, bf16[256,2048]{1,0:T(8,128)(2,1)}, u32[]{:S(2)}, u32[]{:S(2)}) collective-permute-start(bf16[256,2048]{1,0:T(8,128)(2,1)S(1)} %constant_dynamic-slice_fusion.3.refs_0_), channel_id=1, source_target_pairs={{0,4},{4,8},{8,12},{12,28},{28,24},{24,20},{20,16},{16,0},{1,5},{5... | collective-permute-start | bytes 3145736 | tf_op jit(solution)/shard_map/ppermute | solution.py:322
  4.8 1.9 %collective-permute-start = (bf16[576,2048]{1,0:T(8,128)(2,1)}, bf16[576,2048]{1,0:T(8,128)(2,1)S(1)}, u32[]{:S(2)}, u32[]{:S(2)}) collective-permute-start(bf16[576,2048]{1,0:T(8,128)(2,1)} %bitcast.42), channel_id=1, source_target_pairs={{0,2},{1,3},{2,0},{3,1},{4,6},{5,7},{6,4},{7,5},{8,10},{9,11},{10,... | collective-permute-start | bytes 7077896 | tf_op jit(solution)/shard_map/ppermute | solution.py:13
  6.7 3.5 %copy_dynamic-update-slice_fusion.1 = bf16[4,2,2304,128]{3,2,1,0:T(8,128)(2,1)} fusion(bf16[4,1,2304,128]{3,0,2,1:T(4,128)(2,1)} %bitcast.39), kind=kLoop, calls=%fused_computation.1 | loop fusion | bytes 4718592
  10.2 1.7 %copy_dynamic-update-slice_fusion = bf16[4,2,2304,128]{3,2,1,0:T(8,128)(2,1)} fusion(bf16[4,2,2304,128]{3,2,1,0:T(8,128)(2,1)} %copy_dynamic-update-slice_fusion.1, bf16[4,1,2304,128]{3,0,2,1:T(4,128)(2,1)S(1)} %bitcast.40), kind=kLoop, calls=%fused_computation | loop fusion | bytes 4718592 | tf_op jit(solution)/shard_map/stack | solution.py:409
  11.9 4.6 %dynamic-slice_bitcast_fusion = (bf16[2,2304,128]{2,1,0:T(8,128)(2,1)}, bf16[2,2304,128]{2,1,0:T(8,128)(2,1)}, bf16[2,2304,128]{2,1,0:T(8,128)(2,1)}, bf16[2,2304,128]{2,1,0:T(8,128)(2,1)}) fusion(bf16[4,2,2304,128]{3,2,1,0:T(8,128)(2,1)} %copy_dynamic-update-slice_fusion, s32[]{:T(128)S(6)} %select_n.67, s32[]{:T(128)S(6)} %select_n.66, s32[]{:T(128)S(6)} %select_n.65, ...), kind=kLoop, calls=%fused_computation.2 | loop fusion | bytes 9437200 | tf_op jit(solution)/shard_map/jit(dynamic_index_in_dim)/squeeze | solution.py:418
  16.5 0.6 pad_add_fusion.1.ids_ref
  17.2 10.9 %project.2.refs_4_ = f32[576,1024]{1,0:T(8,128)} custom-call(s32[2]{0:T(128)} %pad_add_fusion.1.ids_ref, bf16[576,2048]{1,0:T(8,128)(2,1)} %bitcast.43, bf16[576,2048]{1,0:T(8,128)(2,1)} %collective-permute-done.3.refs_1_, bf16[8192,1024]{1,0:T(8,128)(2,1)} %refs_3_.3, bf16[8192,1024]{1,0:T(8,128)(2,1)} %refs_3_.3), custom_call_target="tpu_custom_call" | custom-call | flops 4831838208 | bytes 15466496 | tf_op jit(solution)/shard_map/project/pallas_call | solution.py:52
  28.1 1.4 collective-permute-done.2.refs_2_
  29.5 1.6 %collective-permute-start.4 = (bf16[256,2048]{1,0:T(8,128)(2,1)}, bf16[256,2048]{1,0:T(8,128)(2,1)}, u32[]{:S(2)}, u32[]{:S(2)}) collective-permute-start(bf16[256,2048]{1,0:T(8,128)(2,1)} %collective-permute-done.1.refs_1_), channel_id=1, source_target_pairs={{0,4},{4,8},{8,12},{12,28},{28,24},{24,20},{20,16},{16,0},{1,5},{5... | collective-permute-start | bytes 3145736 | tf_op jit(solution)/shard_map/ppermute | solution.py:322
  31.5 22.0 %collective-permute-done.4.refs_3_ = bf16[256,2048]{1,0:T(8,128)(2,1)} collective-permute-done((bf16[256,2048]{1,0:T(8,128)(2,1)}, bf16[256,2048]{1,0:T(8,128)(2,1)}, u32[]{:S(2)}, u32[]{:S(2)}) %collective-permute-start.4) | collective-permute-done | bytes 1048608 | tf_op jit(solution)/shard_map/ppermute | solution.py:322
  53.5 1.3 collective-permute-done.5.refs_4_
  54.8 1.6 %collective-permute-start.7 = (bf16[256,2048]{1,0:T(8,128)(2,1)}, bf16[256,2048]{1,0:T(8,128)(2,1)S(1)}, u32[]{:S(2)}, u32[]{:S(2)}) collective-permute-start(bf16[256,2048]{1,0:T(8,128)(2,1)} %collective-permute-done.4.refs_3_), channel_id=1, source_target_pairs={{0,4},{4,8},{8,12},{12,28},{28,24},{24,20},{20,16},{16,0},{1,5},{5... | collective-permute-start | bytes 3145736 | tf_op jit(solution)/shard_map/ppermute | solution.py:322
  56.8 0.9 collective-permute-done.refs_0_
  57.7 1.7 %collective-permute-start.17 = (bf16[2,2304,128]{2,1,0:T(8,128)(2,1)}, bf16[2,2304,128]{2,1,0:T(8,128)(2,1)}, u32[]{:S(2)}, u32[]{:S(2)}) collective-permute-start(bf16[2,2304,128]{2,1,0:T(8,128)(2,1)} %get-tuple-element.41), channel_id=1, source_target_pairs={{0,2},{1,3},{2,0},{3,1},{4,6},{5,7},{6,4},{7,5},{8,10},{9,11},{10,... | collective-permute-start | bytes 3538952 | tf_op jit(solution)/shard_map/ppermute | solution.py:13
  59.3 0.9 reshape_tile.4.adapter_ref.refs_2_
  60.8 8.0 %rank.2.refs_4_ = f32[576,256]{1,0:T(8,128)} custom-call(s32[5]{0:T(128)} %stack.61.starts_ref, bf16[576,2048]{1,0:T(8,128)(2,1)} %bitcast.44, s32[576,1]{1,0:T(8,128)} %reshape_tile.4.adapter_ref.refs_2_, bf16[256,2048]{1,0:T(8,128)(2,1)} %copy-done.5, bf16[256,2048]{1,0:T(8,128)(2,1)} %collective-permute-done.1.refs_1_, ...), custom_call_target="tpu_custom_call" | custom-call | flops 3019898880 | bytes 7602176 | tf_op jit(solution)/shard_map/rank/pallas_call | solution.py:99
  68.9 8.7 %collective-permute-done.7.before_ref.refs_0_ = bf16[256,2048]{1,0:T(8,128)(2,1)S(1)} collective-permute-done((bf16[256,2048]{1,0:T(8,128)(2,1)}, bf16[256,2048]{1,0:T(8,128)(2,1)S(1)}, u32[]{:S(2)}, u32[]{:S(2)}) %collective-permute-start.7) | collective-permute-done | bytes 1048608 | tf_op jit(solution)/shard_map/ppermute | solution.py:322
  77.5 1.4 collective-permute-done.8.after_ref.refs_1_
  78.9 2.2 %split.1 = (bf16[192,2048]{1,0:T(8,128)(2,1)}, bf16[64,2048]{1,0:T(8,128)(2,1)}) custom-call(bf16[256,2048]{1,0:T(8,128)(2,1)} %copy-done.6, bf16[256,2048]{1,0:T(8,128)(2,1)} %collective-permute-done.8.after_ref.refs_1_), custom_call_target="tpu_custom_call" | custom-call | bytes 2097152 | tf_op jit(solution)/shard_map/split/pallas_call | solution.py:341
  81.1 1.5 collective-permute-start.9
  83.7 2.7 %collective-permute-done.17.refs_9_ = bf16[2,2304,128]{2,1,0:T(8,128)(2,1)} collective-permute-done((bf16[2,2304,128]{2,1,0:T(8,128)(2,1)}, bf16[2,2304,128]{2,1,0:T(8,128)(2,1)}, u32[]{:S(2)}, u32[]{:S(2)}) %collective-permute-start.17) | collective-permute-done | bytes 1179680 | tf_op jit(solution)/shard_map/ppermute | solution.py:13
  86.4 1.0 collective-permute-start.18
  87.4 8.0 %collective-permute-done.14.refs_2_ = bf16[256,1024]{1,0:T(8,128)(2,1)S(1)} collective-permute-done((bf16[256,1024]{1,0:T(8,128)(2,1)S(1)}, bf16[256,1024]{1,0:T(8,128)(2,1)S(1)}, u32[]{:S(2)}, u32[]{:S(2)}) %collective-permute-start.14) | collective-permute-done | bytes 524320 | tf_op jit(solution)/shard_map/ppermute | solution.py:322
  95.4 1.5 collective-permute-start.13
  96.9 2.6 %collective-permute-done.10.refs_3_ = bf16[64,2048]{1,0:T(8,128)(2,1)S(1)} collective-permute-done((bf16[64,2048]{1,0:T(8,128)(2,1)}, bf16[64,2048]{1,0:T(8,128)(2,1)S(1)}, u32[]{:S(2)}, u32[]{:S(2)}) %collective-permute-start.10) | collective-permute-done | bytes 262176 | tf_op jit(solution)/shard_map/ppermute | solution.py:322
  99.5 0.7 copy-done.14
  100.2 1.7 %collective-permute-done.9.refs_2_ = bf16[192,2048]{1,0:T(8,128)(2,1)} collective-permute-done((bf16[192,2048]{1,0:T(8,128)(2,1)}, bf16[192,2048]{1,0:T(8,128)(2,1)}, u32[]{:S(2)}, u32[]{:S(2)}) %collective-permute-start.9) | collective-permute-done | bytes 786464 | tf_op jit(solution)/shard_map/ppermute | solution.py:322
  102.4 0.7 pad_add_fusion.2.starts_ref
  103.1 6.3 %rank.3 = f32[576,64]{1,0:T(8,128)} custom-call(s32[3]{0:T(128)} %pad_add_fusion.2.starts_ref, bf16[576,2048]{1,0:T(8,128)(2,1)} %bitcast.45, s32[576,1]{1,0:T(8,128)} %reshape_tile.4.adapter_ref.refs_2_, bf16[256,2048]{1,0:T(8,128)(2,1)} %copy-done.6, bf16[256,2048]{1,0:T(8,128)(2,1)} %collective-permute-done.8.after_ref.refs_1_, ...), custom_call_target="tpu_custom_call" | custom-call | flops 1811939328 | bytes 5505024 | tf_op jit(solution)/shard_map/rank/pallas_call | solution.py:99
  109.9 1.4 collective-permute-done.16.refs_4_
  111.2 1.5 collective-permute-start.15
  113.3 0.6 pad_add_fusion.ids_ref
  113.8 1.0 add.119
  114.9 12.1 %project.3.base_ref = f32[576,1024]{1,0:T(8,128)} custom-call(s32[2]{0:T(128)} %pad_add_fusion.ids_ref, bf16[576,2048]{1,0:T(8,128)(2,1)} %copy-done.2, bf16[576,2048]{1,0:T(8,128)(2,1)} %collective-permute-done.6.refs_1_, bf16[8192,1024]{1,0:T(8,128)(2,1)} %refs_3_.3, bf16[8192,1024]{1,0:T(8,128)(2,1)} %refs_3_.3, f32[576,1024]{1,0:T(8,128)} %project.2.refs_4_), custom_call_target="tpu_custom_call" | custom-call | flops 4831838208 | bytes 15466496 | tf_op jit(solution)/shard_map/project/pallas_call | solution.py:52
  127.0 1.6 %collective-permute-start.19 = (bf16[256,1024]{1,0:T(8,128)(2,1)S(1)}, bf16[256,1024]{1,0:T(8,128)(2,1)S(1)}, u32[]{:S(2)}, u32[]{:S(2)}) collective-permute-start(bf16[256,1024]{1,0:T(8,128)(2,1)S(1)} %collective-permute-done.15.refs_3_), channel_id=1, source_target_pairs={{0,4},{4,8},{8,12},{12,28},{28,24},{24,20},{20,16},{16,0},{1,5},{5... | collective-permute-start | bytes 1572872 | tf_op jit(solution)/shard_map/ppermute | solution.py:322
  129.1 1.5 collective-permute-start.12
  130.5 0.7 concatenate.9.scalars_ref
  131.2 1.9 %constant_dynamic-slice_fusion = (bf16[3,192,1,128]{3,2,1,0:T(2,128)(2,1)S(1)}, bf16[3,192,1,128]{3,2,1,0:T(2,128)(2,1)S(1)}) fusion(bf16[3,192,4,128]{3,2,1,0:T(4,128)(2,1)} %param.17, s32[]{:T(128)S(6)} %select_n.69, bf16[3,192,4,128]{3,2,1,0:T(4,128)(2,1)} %param.16), kind=kLoop, calls=%fused_computation.8 | loop fusion | bytes 589828 | tf_op jit(solution)/shard_map/jit(dynamic_index_in_dim)/dynamic_slice | solution.py:475
  133.1 0.7 copy.28
  133.7 0.7 copy.29
  134.4 0.8 copy.21.refs_6_
  135.2 0.6 collective-permute-done.12
  135.8 0.7 add.120.rank_ref.refs_1_
  136.5 6.4 %delta.1.refs_0_ = f32[576,1024]{1,0:T(8,128)} custom-call(s32[5]{0:T(128)} %stack.61.starts_ref, f32[576,1024]{1,0:T(8,128)} %project.3.base_ref, f32[576,64]{1,0:T(8,128)} %add.120.rank_ref.refs_1_, s32[576,1]{1,0:T(8,128)} %reshape_tile.4.adapter_ref.refs_2_, bf16[256,1024]{1,0:T(8,128)(2,1)} %copy-done.4, ...), custom_call_target="tpu_custom_call" | custom-call | flops 1509949440 | bytes 7340032 | tf_op jit(solution)/shard_map/delta/pallas_call | solution.py:145
  142.9 0.8 copy-done.9
  143.7 0.8 copy-done.10
  144.5 10.8 %attend.1 = bf16[3,192,1024]{2,1,0:T(8,128)(2,1)} custom-call(s32[7]{0:T(128)} %concatenate.9.scalars_ref, f32[576,1024]{1,0:T(8,128)} %delta.1.refs_0_, f32[576,64]{1,0:T(8,128)} %add.120.rank_ref.refs_1_, s32[576,1]{1,0:T(8,128)} %reshape_tile.4.adapter_ref.refs_2_, bf16[256,1024]{1,0:T(8,128)(2,1)} %copy-done.9, ...), custom_call_target="tpu_custom_call" | custom-call | flops 481296384 | bytes 7077888 | tf_op jit(solution)/shard_map/attend/pallas_call | solution.py:295
  (53 shorter events, 5.1 us)
Async XLA Ops:
  0.0 1.6 %copy-start = (bf16[8,2048,64]{1,2,0:T(8,128)(2,1)S(1)}, bf16[8,2048,64]{1,2,0:T(8,128)(2,1)}, u32[]{:S(2)}) copy-start(bf16[8,2048,64]{1,2,0:T(8,128)(2,1)} %param.12) | copy-start | bytes 6291460
  0.0 17.2 %collective-permute-start.3 = (bf16[576,2048]{1,0:T(8,128)(2,1)}, bf16[576,2048]{1,0:T(8,128)(2,1)}, u32[]{:S(2)}, u32[]{:S(2)}) collective-permute-start(bf16[576,2048]{1,0:T(8,128)(2,1)} %bitcast.41), channel_id=1, source_target_pairs={{0,1},{1,0},{2,3},{3,2},{4,5},{5,4},{6,7},{7,6},{8,9},{9,8},{10,11... | collective-permute-start | bytes 7077896 | tf_op jit(solution)/shard_map/ppermute | solution.py:13
  1.7 8.6 %copy-start.5 = (bf16[256,2048]{1,0:T(8,128)(2,1)}, bf16[256,2048]{1,0:T(8,128)(2,1)S(1)}, u32[]{:S(2)}) copy-start(bf16[256,2048]{1,0:T(8,128)(2,1)S(1)} %constant_dynamic-slice_fusion.3.refs_0_) | copy-start | bytes 3145732
  1.7 26.4 %collective-permute-start.1 = (bf16[256,2048]{1,0:T(8,128)(2,1)S(1)}, bf16[256,2048]{1,0:T(8,128)(2,1)}, u32[]{:S(2)}, u32[]{:S(2)}) collective-permute-start(bf16[256,2048]{1,0:T(8,128)(2,1)S(1)} %constant_dynamic-slice_fusion.3.refs_0_), channel_id=1, source_target_pairs={{0,4},{4,8},{8,12},{12,28},{28,24},{24,20},{20,16},{16,0},{1,5},{5... | collective-permute-start | bytes 3145736 | tf_op jit(solution)/shard_map/ppermute | solution.py:322
  4.8 24.7 %collective-permute-start.2 = (bf16[256,2048]{1,0:T(8,128)(2,1)S(1)}, bf16[256,2048]{1,0:T(8,128)(2,1)}, u32[]{:S(2)}, u32[]{:S(2)}) collective-permute-start(bf16[256,2048]{1,0:T(8,128)(2,1)S(1)} %constant_dynamic-slice_fusion.3.refs_0_), channel_id=1, source_target_pairs={{0,16},{4,0},{8,4},{12,8},{28,12},{24,28},{20,24},{16,20},{1,17},{... | collective-permute-start | bytes 3145736 | tf_op jit(solution)/shard_map/ppermute | solution.py:322
  4.8 52.9 %collective-permute-start = (bf16[576,2048]{1,0:T(8,128)(2,1)}, bf16[576,2048]{1,0:T(8,128)(2,1)S(1)}, u32[]{:S(2)}, u32[]{:S(2)}) collective-permute-start(bf16[576,2048]{1,0:T(8,128)(2,1)} %bitcast.42), channel_id=1, source_target_pairs={{0,2},{1,3},{2,0},{3,1},{4,6},{5,7},{6,4},{7,5},{8,10},{9,11},{10,... | collective-permute-start | bytes 7077896 | tf_op jit(solution)/shard_map/ppermute | solution.py:13
  6.7 3.5 %copy-start.3 = (bf16[192,4,12,128]{3,1,2,0:T(4,128)(2,1)S(1)}, bf16[192,4,12,128]{3,1,2,0:T(4,128)(2,1)}, u32[]{:S(2)}) copy-start(bf16[192,4,12,128]{3,1,2,0:T(4,128)(2,1)} %param.15) | copy-start | bytes 7077892
  17.2 42.2 %copy-start.13 = (s32[192]{0:T(256)S(1)}, s32[192]{0:T(256)}, u32[]{:S(2)}) copy-start(s32[192]{0:T(256)} %param.19) | copy-start | bytes 2308
  29.5 24.0 %collective-permute-start.4 = (bf16[256,2048]{1,0:T(8,128)(2,1)}, bf16[256,2048]{1,0:T(8,128)(2,1)}, u32[]{:S(2)}, u32[]{:S(2)}) collective-permute-start(bf16[256,2048]{1,0:T(8,128)(2,1)} %collective-permute-done.1.refs_1_), channel_id=1, source_target_pairs={{0,4},{4,8},{8,12},{12,28},{28,24},{24,20},{20,16},{16,0},{1,5},{5... | collective-permute-start | bytes 3145736 | tf_op jit(solution)/shard_map/ppermute | solution.py:322
  31.1 23.7 %collective-permute-start.5 = (bf16[256,2048]{1,0:T(8,128)(2,1)}, bf16[256,2048]{1,0:T(8,128)(2,1)}, u32[]{:S(2)}, u32[]{:S(2)}) collective-permute-start(bf16[256,2048]{1,0:T(8,128)(2,1)} %collective-permute-done.2.refs_2_), channel_id=1, source_target_pairs={{0,16},{4,0},{8,4},{12,8},{28,12},{24,28},{20,24},{16,20},{1,17},{... | collective-permute-start | bytes 3145736 | tf_op jit(solution)/shard_map/ppermute | solution.py:322
  54.8 22.7 %collective-permute-start.7 = (bf16[256,2048]{1,0:T(8,128)(2,1)}, bf16[256,2048]{1,0:T(8,128)(2,1)S(1)}, u32[]{:S(2)}, u32[]{:S(2)}) collective-permute-start(bf16[256,2048]{1,0:T(8,128)(2,1)} %collective-permute-done.4.refs_3_), channel_id=1, source_target_pairs={{0,4},{4,8},{8,12},{12,28},{28,24},{24,20},{20,16},{16,0},{1,5},{5... | collective-permute-start | bytes 3145736 | tf_op jit(solution)/shard_map/ppermute | solution.py:322
  56.4 22.5 %collective-permute-start.8 = (bf16[256,2048]{1,0:T(8,128)(2,1)}, bf16[256,2048]{1,0:T(8,128)(2,1)}, u32[]{:S(2)}, u32[]{:S(2)}) collective-permute-start(bf16[256,2048]{1,0:T(8,128)(2,1)} %collective-permute-done.5.refs_4_), channel_id=1, source_target_pairs={{0,16},{4,0},{8,4},{12,8},{28,12},{24,28},{20,24},{16,20},{1,17},{... | collective-permute-start | bytes 3145736 | tf_op jit(solution)/shard_map/ppermute | solution.py:322
  57.7 11.2 %copy-start.2 = (bf16[576,2048]{1,0:T(8,128)(2,1)}, bf16[576,2048]{1,0:T(8,128)(2,1)S(1)}, u32[]{:S(2)}) copy-start(bf16[576,2048]{1,0:T(8,128)(2,1)S(1)} %collective-permute-done.refs_0_) | copy-start | bytes 7077892
  57.7 57.2 %collective-permute-start.6 = (bf16[576,2048]{1,0:T(8,128)(2,1)S(1)}, bf16[576,2048]{1,0:T(8,128)(2,1)}, u32[]{:S(2)}, u32[]{:S(2)}) collective-permute-start(bf16[576,2048]{1,0:T(8,128)(2,1)S(1)} %collective-permute-done.refs_0_), channel_id=1, source_target_pairs={{0,1},{1,0},{2,3},{3,2},{4,5},{5,4},{6,7},{7,6},{8,9},{9,8},{10,11... | collective-permute-start | bytes 7077896 | tf_op jit(solution)/shard_map/ppermute | solution.py:13
  57.7 28.7 %collective-permute-start.17 = (bf16[2,2304,128]{2,1,0:T(8,128)(2,1)}, bf16[2,2304,128]{2,1,0:T(8,128)(2,1)}, u32[]{:S(2)}, u32[]{:S(2)}) collective-permute-start(bf16[2,2304,128]{2,1,0:T(8,128)(2,1)} %get-tuple-element.41), channel_id=1, source_target_pairs={{0,2},{1,3},{2,0},{3,1},{4,6},{5,7},{6,4},{7,5},{8,10},{9,11},{10,... | collective-permute-start | bytes 3538952 | tf_op jit(solution)/shard_map/ppermute | solution.py:13
  68.8 13.8 %copy-start.11 = (bf16[8,64,1024]{2,1,0:T(8,128)(2,1)S(1)}, bf16[8,64,1024]{2,1,0:T(8,128)(2,1)}, u32[]{:S(2)}) copy-start(bf16[8,64,1024]{2,1,0:T(8,128)(2,1)} %param.13) | copy-start | bytes 3145732
  77.5 1.4 copy-start.6
  81.1 20.8 %collective-permute-start.9 = (bf16[192,2048]{1,0:T(8,128)(2,1)}, bf16[192,2048]{1,0:T(8,128)(2,1)}, u32[]{:S(2)}, u32[]{:S(2)}) collective-permute-start(bf16[192,2048]{1,0:T(8,128)(2,1)} %get-tuple-element.36), channel_id=1, source_target_pairs={{0,4},{4,8},{8,12},{12,28},{28,24},{24,20},{20,16},{16,0},{1,5},{5... | collective-permute-start | bytes 2359304 | tf_op jit(solution)/shard_map/ppermute | solution.py:322
  82.7 26.6 %copy-start.4 = (bf16[256,1024]{1,0:T(8,128)(2,1)}, bf16[256,1024]{1,0:T(8,128)(2,1)S(1)}, u32[]{:S(2)}) copy-start(bf16[256,1024]{1,0:T(8,128)(2,1)S(1)} %constant_dynamic-slice_fusion.2.refs_0_) | copy-start | bytes 1572868
  82.7 12.7 %collective-permute-start.14 = (bf16[256,1024]{1,0:T(8,128)(2,1)S(1)}, bf16[256,1024]{1,0:T(8,128)(2,1)S(1)}, u32[]{:S(2)}, u32[]{:S(2)}) collective-permute-start(bf16[256,1024]{1,0:T(8,128)(2,1)S(1)} %constant_dynamic-slice_fusion.2.refs_0_), channel_id=1, source_target_pairs={{0,16},{4,0},{8,4},{12,8},{28,12},{24,28},{20,24},{16,20},{1,17},{... | collective-permute-start | bytes 1572872 | tf_op jit(solution)/shard_map/ppermute | solution.py:322
  83.3 16.3 %collective-permute-start.10 = (bf16[64,2048]{1,0:T(8,128)(2,1)}, bf16[64,2048]{1,0:T(8,128)(2,1)S(1)}, u32[]{:S(2)}, u32[]{:S(2)}) collective-permute-start(bf16[64,2048]{1,0:T(8,128)(2,1)} %get-tuple-element.37), channel_id=1, source_target_pairs={{0,16},{4,0},{8,4},{12,8},{28,12},{24,28},{20,24},{16,20},{1,17},{... | collective-permute-start | bytes 786440 | tf_op jit(solution)/shard_map/ppermute | solution.py:322
  86.4 40.6 %collective-permute-start.18 = (bf16[2,2304,128]{2,1,0:T(8,128)(2,1)}, bf16[2,2304,128]{2,1,0:T(8,128)(2,1)}, u32[]{:S(2)}, u32[]{:S(2)}) collective-permute-start(bf16[2,2304,128]{2,1,0:T(8,128)(2,1)} %get-tuple-element.42), channel_id=1, source_target_pairs={{0,3},{1,2},{2,1},{3,0},{4,7},{5,6},{6,5},{7,4},{8,11},{9,10},{10,... | collective-permute-start | bytes 3538952 | tf_op jit(solution)/shard_map/ppermute | solution.py:13
  95.4 14.0 %copy-start.7 = (bf16[256,1024]{1,0:T(8,128)(2,1)}, bf16[256,1024]{1,0:T(8,128)(2,1)S(1)}, u32[]{:S(2)}) copy-start(bf16[256,1024]{1,0:T(8,128)(2,1)S(1)} %collective-permute-done.14.refs_2_) | copy-start | bytes 1572868
  95.4 14.0 %collective-permute-start.13 = (bf16[256,1024]{1,0:T(8,128)(2,1)S(1)}, bf16[256,1024]{1,0:T(8,128)(2,1)}, u32[]{:S(2)}, u32[]{:S(2)}) collective-permute-start(bf16[256,1024]{1,0:T(8,128)(2,1)S(1)} %constant_dynamic-slice_fusion.2.refs_0_), channel_id=1, source_target_pairs={{0,4},{4,8},{8,12},{12,28},{28,24},{24,20},{20,16},{16,0},{1,5},{5... | collective-permute-start | bytes 1572872 | tf_op jit(solution)/shard_map/ppermute | solution.py:322
  99.5 0.7 copy-start.14
  101.9 9.3 %collective-permute-start.16 = (bf16[256,1024]{1,0:T(8,128)(2,1)S(1)}, bf16[256,1024]{1,0:T(8,128)(2,1)}, u32[]{:S(2)}, u32[]{:S(2)}) collective-permute-start(bf16[256,1024]{1,0:T(8,128)(2,1)S(1)} %collective-permute-done.14.refs_2_), channel_id=1, source_target_pairs={{0,16},{4,0},{8,4},{12,8},{28,12},{24,28},{20,24},{16,20},{1,17},{... | collective-permute-start | bytes 1572872 | tf_op jit(solution)/shard_map/ppermute | solution.py:322
  109.3 3.4 %collective-permute-start.11 = (f32[576,64]{1,0:T(8,128)}, f32[576,64]{1,0:T(8,128)S(1)}, u32[]{:S(2)}, u32[]{:S(2)}) collective-permute-start(f32[576,64]{1,0:T(8,128)} %rank.3), channel_id=1, source_target_pairs={{0,1},{1,0},{2,3},{3,2},{4,5},{5,4},{6,7},{7,6},{8,9},{9,8},{10,11... | collective-permute-start | bytes 442376 | tf_op jit(solution)/shard_map/ppermute | solution.py:13
  109.4 33.6 %collective-permute-start.22 = (bf16[2,2304,128]{2,1,0:T(8,128)(2,1)}, bf16[2,2304,128]{2,1,0:T(8,128)(2,1)}, u32[]{:S(2)}, u32[]{:S(2)}) collective-permute-start(bf16[2,2304,128]{2,1,0:T(8,128)(2,1)} %get-tuple-element.44), channel_id=1, source_target_pairs={{0,1},{1,0},{2,3},{3,2},{4,5},{5,4},{6,7},{7,6},{8,9},{9,8},{10,11... | collective-permute-start | bytes 3538952 | tf_op jit(solution)/shard_map/ppermute | solution.py:13
  111.2 15.7 %collective-permute-start.15 = (bf16[256,1024]{1,0:T(8,128)(2,1)}, bf16[256,1024]{1,0:T(8,128)(2,1)S(1)}, u32[]{:S(2)}, u32[]{:S(2)}) collective-permute-start(bf16[256,1024]{1,0:T(8,128)(2,1)} %collective-permute-done.13.refs_1_), channel_id=1, source_target_pairs={{0,4},{4,8},{8,12},{12,28},{28,24},{24,20},{20,16},{16,0},{1,5},{5... | collective-permute-start | bytes 1572872 | tf_op jit(solution)/shard_map/ppermute | solution.py:322
  112.7 15.8 %collective-permute-start.20 = (bf16[256,1024]{1,0:T(8,128)(2,1)}, bf16[256,1024]{1,0:T(8,128)(2,1)}, u32[]{:S(2)}, u32[]{:S(2)}) collective-permute-start(bf16[256,1024]{1,0:T(8,128)(2,1)} %collective-permute-done.16.refs_4_), channel_id=1, source_target_pairs={{0,16},{4,0},{8,4},{12,8},{28,12},{24,28},{20,24},{16,20},{1,17},{... | collective-permute-start | bytes 1572872 | tf_op jit(solution)/shard_map/ppermute | solution.py:322
  114.9 19.6 %copy-start.12 = (s32[192]{0:T(256)S(1)}, s32[192]{0:T(256)}, u32[]{:S(2)}) copy-start(s32[192]{0:T(256)} %param.18) | copy-start | bytes 2308
  127.0 9.6 %copy-start.8 = (bf16[256,1024]{1,0:T(8,128)(2,1)}, bf16[256,1024]{1,0:T(8,128)(2,1)S(1)}, u32[]{:S(2)}) copy-start(bf16[256,1024]{1,0:T(8,128)(2,1)S(1)} %collective-permute-done.15.refs_3_) | copy-start | bytes 1572868
  127.0 16.0 %collective-permute-start.19 = (bf16[256,1024]{1,0:T(8,128)(2,1)S(1)}, bf16[256,1024]{1,0:T(8,128)(2,1)S(1)}, u32[]{:S(2)}, u32[]{:S(2)}) collective-permute-start(bf16[256,1024]{1,0:T(8,128)(2,1)S(1)} %collective-permute-done.15.refs_3_), channel_id=1, source_target_pairs={{0,4},{4,8},{8,12},{12,28},{28,24},{24,20},{20,16},{16,0},{1,5},{5... | collective-permute-start | bytes 1572872 | tf_op jit(solution)/shard_map/ppermute | solution.py:322
  128.5 15.2 %collective-permute-start.21 = (bf16[256,1024]{1,0:T(8,128)(2,1)}, bf16[256,1024]{1,0:T(8,128)(2,1)S(1)}, u32[]{:S(2)}, u32[]{:S(2)}) collective-permute-start(bf16[256,1024]{1,0:T(8,128)(2,1)} %collective-permute-done.20.refs_4_), channel_id=1, source_target_pairs={{0,16},{4,0},{8,4},{12,8},{28,12},{24,28},{20,24},{16,20},{1,17},{... | collective-permute-start | bytes 1572872 | tf_op jit(solution)/shard_map/ppermute | solution.py:322
  129.1 6.7 %collective-permute-start.12 = (f32[576,64]{1,0:T(8,128)S(1)}, f32[576,64]{1,0:T(8,128)S(1)}, u32[]{:S(2)}, u32[]{:S(2)}) collective-permute-start(f32[576,64]{1,0:T(8,128)S(1)} %add.119), channel_id=1, source_target_pairs={{0,2},{1,3},{2,0},{3,1},{4,6},{5,7},{6,4},{7,5},{8,10},{9,11},{10,... | collective-permute-start | bytes 442376 | tf_op jit(solution)/shard_map/ppermute | solution.py:13
  142.9 0.8 copy-start.9
  143.7 0.8 copy-start.10
  144.5 10.8 %copy-start.1 = (bf16[8,2048,64]{1,2,0:T(8,128)(2,1)S(1)}, bf16[8,2048,64]{1,2,0:T(8,128)(2,1)}, u32[]{:S(2)}) copy-start(bf16[8,2048,64]{1,2,0:T(8,128)(2,1)} %param.12) | copy-start | bytes 6291460

commit v8 on v7

--- a/solution.py
+++ b/solution.py
@@ -27,8 +27,10 @@
         left = jnp.concatenate([ref[...] for ref in refs[:parts]], axis=0)
         right = jnp.concatenate([ref[...] for ref in refs[parts : 2 * parts]], axis=0)
         product = jnp.dot(
-            left, first_weight[...], preferred_element_type=jnp.float32
-        ) + jnp.dot(right, second_weight[...], preferred_element_type=jnp.float32)
+            jnp.concatenate([left, right], axis=1),
+            jnp.concatenate([first_weight[...], second_weight[...]], axis=0),
+            preferred_element_type=jnp.float32,
+        )
 
         @pl.when(pl.program_id(0) == 0)
         def _():

time: 156 us -> 156 us (level)
  transfers between devices with their start and end apart: 23 -> 23, of which waited for: 12 -> 12; matrix products, arithmetic and copies ran while one was open for 13% -> 13% of each run, Pallas kernels for 30% -> 29%
where the time goes in v8:
time: 156 us; the launch traced here: 155 us
  Pallas kernels  56.6 us (36%)
  waiting for transfers between devices  52.7 us (34%)
  starting transfers between devices  22.7 us (15%)
  local copies, waits for them, and re-layouts  19.5 us (12%)
  other arithmetic  3.65 us (2%)
    ppermute x15, waiting for transfers between devices, ring_hop(): return lax.ppermute(array, ('rep', 'dp'), pairs)  48.5 us
    pallas_call x2, Pallas kernels, project_pair(): pl.pallas_call(kernel, out_shape=jax.ShapeDtypeStruct((rows, columns), jn...  22.9 us
    ppermute x15, starting transfers between devices, ring_hop(): return lax.ppermute(array, ('rep', 'dp'), pairs)  15.7 us
    pallas_call x2, Pallas kernels, add_ranks(): pl.pallas_call(kernel, out_shape=jax.ShapeDtypeStruct((rows, out_width),...  14.3 us
    pallas_call x1, Pallas kernels, attend(): pl.pallas_call(kernel, out_shape=jax.ShapeDtypeStruct((steps, rows, width...  10.8 us
    unnamed x33, local copies, waits for them, and re-layouts  8.34 us
    ppermute x8, starting transfers between devices, swap(): return lax.ppermute(array, 'tensor', [(i, i ^ bit) for i in range(count)])  7.01 us
    pallas_call x1, Pallas kernels, early_query(): pl.pallas_call(kernel, out_shape=jax.ShapeDtypeStruct((rows, columns), jn...  6.39 us
  transfers between devices with their start and end apart: 23, of which 12 were waited for; matrix products, arithmetic and copies ran while one was open for 13% of the time, Pallas kernels for 29%

profile of v8, /device:TPU:0, one launch (start us, length us, event | category | flops | bytes accessed | tf_op | source)
XLA Modules:
  0.0 155.4 jit_solution(2935221820511116315)
XLA Ops:
  0.5 1.1 copy-done
  1.7 3.1 %collective-permute-start.1 = (bf16[256,2048]{1,0:T(8,128)(2,1)S(1)}, bf16[256,2048]{1,0:T(8,128)(2,1)}, u32[]{:S(2)}, u32[]{:S(2)}) collective-permute-start(bf16[256,2048]{1,0:T(8,128)(2,1)S(1)} %constant_dynamic-slice_fusion.3.refs_0_), channel_id=1, source_target_pairs={{0,4},{4,8},{8,12},{12,28},{28,24},{24,20},{20,16},{16,0},{1,5},{5... | collective-permute-start | bytes 3145736 | tf_op jit(solution)/shard_map/ppermute | solution.py:324
  4.8 1.9 %collective-permute-start = (bf16[576,2048]{1,0:T(8,128)(2,1)}, bf16[576,2048]{1,0:T(8,128)(2,1)S(1)}, u32[]{:S(2)}, u32[]{:S(2)}) collective-permute-start(bf16[576,2048]{1,0:T(8,128)(2,1)} %bitcast.42), channel_id=1, source_target_pairs={{0,2},{1,3},{2,0},{3,1},{4,6},{5,7},{6,4},{7,5},{8,10},{9,11},{10,... | collective-permute-start | bytes 7077896 | tf_op jit(solution)/shard_map/ppermute | solution.py:13
  6.7 3.5 %copy_dynamic-update-slice_fusion.1 = bf16[4,2,2304,128]{3,2,1,0:T(8,128)(2,1)} fusion(bf16[4,1,2304,128]{3,0,2,1:T(4,128)(2,1)} %bitcast.39), kind=kLoop, calls=%fused_computation.1 | loop fusion | bytes 4718592
  10.2 1.7 %copy_dynamic-update-slice_fusion = bf16[4,2,2304,128]{3,2,1,0:T(8,128)(2,1)} fusion(bf16[4,2,2304,128]{3,2,1,0:T(8,128)(2,1)} %copy_dynamic-update-slice_fusion.1, bf16[4,1,2304,128]{3,0,2,1:T(4,128)(2,1)S(1)} %bitcast.40), kind=kLoop, calls=%fused_computation | loop fusion | bytes 4718592 | tf_op jit(solution)/shard_map/stack | solution.py:411
  11.9 4.6 %dynamic-slice_bitcast_fusion = (bf16[2,2304,128]{2,1,0:T(8,128)(2,1)}, bf16[2,2304,128]{2,1,0:T(8,128)(2,1)}, bf16[2,2304,128]{2,1,0:T(8,128)(2,1)}, bf16[2,2304,128]{2,1,0:T(8,128)(2,1)}) fusion(bf16[4,2,2304,128]{3,2,1,0:T(8,128)(2,1)} %copy_dynamic-update-slice_fusion, s32[]{:T(128)S(6)} %select_n.67, s32[]{:T(128)S(6)} %select_n.66, s32[]{:T(128)S(6)} %select_n.65, ...), kind=kLoop, calls=%fused_computation.2 | loop fusion | bytes 9437200 | tf_op jit(solution)/shard_map/jit(dynamic_index_in_dim)/squeeze | solution.py:420
  16.5 0.6 pad_add_fusion.1.ids_ref
  17.2 10.9 %project.2.refs_4_ = f32[576,1024]{1,0:T(8,128)} custom-call(s32[2]{0:T(128)} %pad_add_fusion.1.ids_ref, bf16[576,2048]{1,0:T(8,128)(2,1)} %bitcast.43, bf16[576,2048]{1,0:T(8,128)(2,1)} %collective-permute-done.3.refs_1_, bf16[8192,1024]{1,0:T(8,128)(2,1)} %refs_3_.3, bf16[8192,1024]{1,0:T(8,128)(2,1)} %refs_3_.3), custom_call_target="tpu_custom_call" | custom-call | flops 4831838208 | bytes 15466496 | tf_op jit(solution)/shard_map/project/pallas_call | solution.py:54
  28.0 1.4 collective-permute-done.2.refs_2_
  29.5 1.6 %collective-permute-start.4 = (bf16[256,2048]{1,0:T(8,128)(2,1)}, bf16[256,2048]{1,0:T(8,128)(2,1)}, u32[]{:S(2)}, u32[]{:S(2)}) collective-permute-start(bf16[256,2048]{1,0:T(8,128)(2,1)} %collective-permute-done.1.refs_1_), channel_id=1, source_target_pairs={{0,4},{4,8},{8,12},{12,28},{28,24},{24,20},{20,16},{16,0},{1,5},{5... | collective-permute-start | bytes 3145736 | tf_op jit(solution)/shard_map/ppermute | solution.py:324
  31.5 22.0 %collective-permute-done.4.refs_3_ = bf16[256,2048]{1,0:T(8,128)(2,1)} collective-permute-done((bf16[256,2048]{1,0:T(8,128)(2,1)}, bf16[256,2048]{1,0:T(8,128)(2,1)}, u32[]{:S(2)}, u32[]{:S(2)}) %collective-permute-start.4) | collective-permute-done | bytes 1048608 | tf_op jit(solution)/shard_map/ppermute | solution.py:324
  53.5 1.3 collective-permute-done.5.refs_4_
  54.8 1.6 %collective-permute-start.7 = (bf16[256,2048]{1,0:T(8,128)(2,1)}, bf16[256,2048]{1,0:T(8,128)(2,1)S(1)}, u32[]{:S(2)}, u32[]{:S(2)}) collective-permute-start(bf16[256,2048]{1,0:T(8,128)(2,1)} %collective-permute-done.4.refs_3_), channel_id=1, source_target_pairs={{0,4},{4,8},{8,12},{12,28},{28,24},{24,20},{20,16},{16,0},{1,5},{5... | collective-permute-start | bytes 3145736 | tf_op jit(solution)/shard_map/ppermute | solution.py:324
  56.8 0.9 collective-permute-done.refs_0_
  57.7 1.7 %collective-permute-start.17 = (bf16[2,2304,128]{2,1,0:T(8,128)(2,1)}, bf16[2,2304,128]{2,1,0:T(8,128)(2,1)}, u32[]{:S(2)}, u32[]{:S(2)}) collective-permute-start(bf16[2,2304,128]{2,1,0:T(8,128)(2,1)} %get-tuple-element.41), channel_id=1, source_target_pairs={{0,2},{1,3},{2,0},{3,1},{4,6},{5,7},{6,4},{7,5},{8,10},{9,11},{10,... | collective-permute-start | bytes 3538952 | tf_op jit(solution)/shard_map/ppermute | solution.py:13
  59.3 0.9 reshape_tile.4.adapter_ref.refs_2_
  60.8 8.0 %rank.2.refs_4_ = f32[576,256]{1,0:T(8,128)} custom-call(s32[5]{0:T(128)} %stack.61.starts_ref, bf16[576,2048]{1,0:T(8,128)(2,1)} %bitcast.44, s32[576,1]{1,0:T(8,128)} %reshape_tile.4.adapter_ref.refs_2_, bf16[256,2048]{1,0:T(8,128)(2,1)} %copy-done.5, bf16[256,2048]{1,0:T(8,128)(2,1)} %collective-permute-done.1.refs_1_, ...), custom_call_target="tpu_custom_call" | custom-call | flops 3019898880 | bytes 7602176 | tf_op jit(solution)/shard_map/rank/pallas_call | solution.py:101
  68.9 8.7 %collective-permute-done.7.before_ref.refs_0_ = bf16[256,2048]{1,0:T(8,128)(2,1)S(1)} collective-permute-done((bf16[256,2048]{1,0:T(8,128)(2,1)}, bf16[256,2048]{1,0:T(8,128)(2,1)S(1)}, u32[]{:S(2)}, u32[]{:S(2)}) %collective-permute-start.7) | collective-permute-done | bytes 1048608 | tf_op jit(solution)/shard_map/ppermute | solution.py:324
  77.5 1.4 collective-permute-done.8.after_ref.refs_1_
  78.9 2.2 %split.1 = (bf16[192,2048]{1,0:T(8,128)(2,1)}, bf16[64,2048]{1,0:T(8,128)(2,1)}) custom-call(bf16[256,2048]{1,0:T(8,128)(2,1)} %copy-done.6, bf16[256,2048]{1,0:T(8,128)(2,1)} %collective-permute-done.8.after_ref.refs_1_), custom_call_target="tpu_custom_call" | custom-call | bytes 2097152 | tf_op jit(solution)/shard_map/split/pallas_call | solution.py:343
  81.1 1.5 collective-permute-start.9
  83.7 2.7 %collective-permute-done.17.refs_9_ = bf16[2,2304,128]{2,1,0:T(8,128)(2,1)} collective-permute-done((bf16[2,2304,128]{2,1,0:T(8,128)(2,1)}, bf16[2,2304,128]{2,1,0:T(8,128)(2,1)}, u32[]{:S(2)}, u32[]{:S(2)}) %collective-permute-start.17) | collective-permute-done | bytes 1179680 | tf_op jit(solution)/shard_map/ppermute | solution.py:13
  86.4 1.0 collective-permute-start.18
  87.4 8.0 %collective-permute-done.14.refs_2_ = bf16[256,1024]{1,0:T(8,128)(2,1)S(1)} collective-permute-done((bf16[256,1024]{1,0:T(8,128)(2,1)S(1)}, bf16[256,1024]{1,0:T(8,128)(2,1)S(1)}, u32[]{:S(2)}, u32[]{:S(2)}) %collective-permute-start.14) | collective-permute-done | bytes 524320 | tf_op jit(solution)/shard_map/ppermute | solution.py:324
  95.4 1.5 collective-permute-start.13
  96.9 2.6 %collective-permute-done.10.refs_3_ = bf16[64,2048]{1,0:T(8,128)(2,1)S(1)} collective-permute-done((bf16[64,2048]{1,0:T(8,128)(2,1)}, bf16[64,2048]{1,0:T(8,128)(2,1)S(1)}, u32[]{:S(2)}, u32[]{:S(2)}) %collective-permute-start.10) | collective-permute-done | bytes 262176 | tf_op jit(solution)/shard_map/ppermute | solution.py:324
  99.5 0.7 copy-done.14
  100.2 1.7 %collective-permute-done.9.refs_2_ = bf16[192,2048]{1,0:T(8,128)(2,1)} collective-permute-done((bf16[192,2048]{1,0:T(8,128)(2,1)}, bf16[192,2048]{1,0:T(8,128)(2,1)}, u32[]{:S(2)}, u32[]{:S(2)}) %collective-permute-start.9) | collective-permute-done | bytes 786464 | tf_op jit(solution)/shard_map/ppermute | solution.py:324
  102.4 0.7 pad_add_fusion.2.starts_ref
  103.1 6.3 %rank.3 = f32[576,64]{1,0:T(8,128)} custom-call(s32[3]{0:T(128)} %pad_add_fusion.2.starts_ref, bf16[576,2048]{1,0:T(8,128)(2,1)} %bitcast.45, s32[576,1]{1,0:T(8,128)} %reshape_tile.4.adapter_ref.refs_2_, bf16[256,2048]{1,0:T(8,128)(2,1)} %copy-done.6, bf16[256,2048]{1,0:T(8,128)(2,1)} %collective-permute-done.8.after_ref.refs_1_, ...), custom_call_target="tpu_custom_call" | custom-call | flops 1811939328 | bytes 5505024 | tf_op jit(solution)/shard_map/rank/pallas_call | solution.py:101
  109.9 1.4 collective-permute-done.16.refs_4_
  111.2 1.5 collective-permute-start.15
  113.3 0.6 pad_add_fusion.ids_ref
  113.8 1.0 add.119
  114.9 12.1 %project.3.base_ref = f32[576,1024]{1,0:T(8,128)} custom-call(s32[2]{0:T(128)} %pad_add_fusion.ids_ref, bf16[576,2048]{1,0:T(8,128)(2,1)} %copy-done.2, bf16[576,2048]{1,0:T(8,128)(2,1)} %collective-permute-done.6.refs_1_, bf16[8192,1024]{1,0:T(8,128)(2,1)} %refs_3_.3, bf16[8192,1024]{1,0:T(8,128)(2,1)} %refs_3_.3, f32[576,1024]{1,0:T(8,128)} %project.2.refs_4_), custom_call_target="tpu_custom_call" | custom-call | flops 4831838208 | bytes 15466496 | tf_op jit(solution)/shard_map/project/pallas_call | solution.py:54
  127.0 1.6 %collective-permute-start.19 = (bf16[256,1024]{1,0:T(8,128)(2,1)S(1)}, bf16[256,1024]{1,0:T(8,128)(2,1)S(1)}, u32[]{:S(2)}, u32[]{:S(2)}) collective-permute-start(bf16[256,1024]{1,0:T(8,128)(2,1)S(1)} %collective-permute-done.15.refs_3_), channel_id=1, source_target_pairs={{0,4},{4,8},{8,12},{12,28},{28,24},{24,20},{20,16},{16,0},{1,5},{5... | collective-permute-start | bytes 1572872 | tf_op jit(solution)/shard_map/ppermute | solution.py:324
  129.0 1.5 collective-permute-start.12
  130.5 0.7 concatenate.9.scalars_ref
  131.2 1.9 %constant_dynamic-slice_fusion = (bf16[3,192,1,128]{3,2,1,0:T(2,128)(2,1)S(1)}, bf16[3,192,1,128]{3,2,1,0:T(2,128)(2,1)S(1)}) fusion(bf16[3,192,4,128]{3,2,1,0:T(4,128)(2,1)} %param.17, s32[]{:T(128)S(6)} %select_n.69, bf16[3,192,4,128]{3,2,1,0:T(4,128)(2,1)} %param.16), kind=kLoop, calls=%fused_computation.8 | loop fusion | bytes 589828 | tf_op jit(solution)/shard_map/jit(dynamic_index_in_dim)/dynamic_slice | solution.py:477
  133.0 0.7 copy.28
  133.7 0.7 copy.29
  134.4 0.8 copy.21.refs_6_
  135.2 0.6 collective-permute-done.12
  135.8 0.7 add.120.rank_ref.refs_1_
  136.5 6.4 %delta.1.refs_0_ = f32[576,1024]{1,0:T(8,128)} custom-call(s32[5]{0:T(128)} %stack.61.starts_ref, f32[576,1024]{1,0:T(8,128)} %project.3.base_ref, f32[576,64]{1,0:T(8,128)} %add.120.rank_ref.refs_1_, s32[576,1]{1,0:T(8,128)} %reshape_tile.4.adapter_ref.refs_2_, bf16[256,1024]{1,0:T(8,128)(2,1)} %copy-done.4, ...), custom_call_target="tpu_custom_call" | custom-call | flops 1509949440 | bytes 7340032 | tf_op jit(solution)/shard_map/delta/pallas_call | solution.py:147
  142.9 0.8 copy-done.9
  143.7 0.8 copy-done.10
  144.5 10.8 %attend.1 = bf16[3,192,1024]{2,1,0:T(8,128)(2,1)} custom-call(s32[7]{0:T(128)} %concatenate.9.scalars_ref, f32[576,1024]{1,0:T(8,128)} %delta.1.refs_0_, f32[576,64]{1,0:T(8,128)} %add.120.rank_ref.refs_1_, s32[576,1]{1,0:T(8,128)} %reshape_tile.4.adapter_ref.refs_2_, bf16[256,1024]{1,0:T(8,128)(2,1)} %copy-done.9, ...), custom_call_target="tpu_custom_call" | custom-call | flops 481296384 | bytes 7077888 | tf_op jit(solution)/shard_map/attend/pallas_call | solution.py:297
  (53 shorter events, 5.1 us)
Async XLA Ops:
  0.0 1.6 %copy-start = (bf16[8,2048,64]{1,2,0:T(8,128)(2,1)S(1)}, bf16[8,2048,64]{1,2,0:T(8,128)(2,1)}, u32[]{:S(2)}) copy-start(bf16[8,2048,64]{1,2,0:T(8,128)(2,1)} %param.12) | copy-start | bytes 6291460
  0.0 17.2 %collective-permute-start.3 = (bf16[576,2048]{1,0:T(8,128)(2,1)}, bf16[576,2048]{1,0:T(8,128)(2,1)}, u32[]{:S(2)}, u32[]{:S(2)}) collective-permute-start(bf16[576,2048]{1,0:T(8,128)(2,1)} %bitcast.41), channel_id=1, source_target_pairs={{0,1},{1,0},{2,3},{3,2},{4,5},{5,4},{6,7},{7,6},{8,9},{9,8},{10,11... | collective-permute-start | bytes 7077896 | tf_op jit(solution)/shard_map/ppermute | solution.py:13
  1.7 8.6 %copy-start.5 = (bf16[256,2048]{1,0:T(8,128)(2,1)}, bf16[256,2048]{1,0:T(8,128)(2,1)S(1)}, u32[]{:S(2)}) copy-start(bf16[256,2048]{1,0:T(8,128)(2,1)S(1)} %constant_dynamic-slice_fusion.3.refs_0_) | copy-start | bytes 3145732
  1.7 26.4 %collective-permute-start.1 = (bf16[256,2048]{1,0:T(8,128)(2,1)S(1)}, bf16[256,2048]{1,0:T(8,128)(2,1)}, u32[]{:S(2)}, u32[]{:S(2)}) collective-permute-start(bf16[256,2048]{1,0:T(8,128)(2,1)S(1)} %constant_dynamic-slice_fusion.3.refs_0_), channel_id=1, source_target_pairs={{0,4},{4,8},{8,12},{12,28},{28,24},{24,20},{20,16},{16,0},{1,5},{5... | collective-permute-start | bytes 3145736 | tf_op jit(solution)/shard_map/ppermute | solution.py:324
  4.8 24.7 %collective-permute-start.2 = (bf16[256,2048]{1,0:T(8,128)(2,1)S(1)}, bf16[256,2048]{1,0:T(8,128)(2,1)}, u32[]{:S(2)}, u32[]{:S(2)}) collective-permute-start(bf16[256,2048]{1,0:T(8,128)(2,1)S(1)} %constant_dynamic-slice_fusion.3.refs_0_), channel_id=1, source_target_pairs={{0,16},{4,0},{8,4},{12,8},{28,12},{24,28},{20,24},{16,20},{1,17},{... | collective-permute-start | bytes 3145736 | tf_op jit(solution)/shard_map/ppermute | solution.py:324
  4.8 52.9 %collective-permute-start = (bf16[576,2048]{1,0:T(8,128)(2,1)}, bf16[576,2048]{1,0:T(8,128)(2,1)S(1)}, u32[]{:S(2)}, u32[]{:S(2)}) collective-permute-start(bf16[576,2048]{1,0:T(8,128)(2,1)} %bitcast.42), channel_id=1, source_target_pairs={{0,2},{1,3},{2,0},{3,1},{4,6},{5,7},{6,4},{7,5},{8,10},{9,11},{10,... | collective-permute-start | bytes 7077896 | tf_op jit(solution)/shard_map/ppermute | solution.py:13
  6.7 3.5 %copy-start.3 = (bf16[192,4,12,128]{3,1,2,0:T(4,128)(2,1)S(1)}, bf16[192,4,12,128]{3,1,2,0:T(4,128)(2,1)}, u32[]{:S(2)}) copy-start(bf16[192,4,12,128]{3,1,2,0:T(4,128)(2,1)} %param.15) | copy-start | bytes 7077892
  17.2 42.2 %copy-start.13 = (s32[192]{0:T(256)S(1)}, s32[192]{0:T(256)}, u32[]{:S(2)}) copy-start(s32[192]{0:T(256)} %param.19) | copy-start | bytes 2308
  29.5 24.0 %collective-permute-start.4 = (bf16[256,2048]{1,0:T(8,128)(2,1)}, bf16[256,2048]{1,0:T(8,128)(2,1)}, u32[]{:S(2)}, u32[]{:S(2)}) collective-permute-start(bf16[256,2048]{1,0:T(8,128)(2,1)} %collective-permute-done.1.refs_1_), channel_id=1, source_target_pairs={{0,4},{4,8},{8,12},{12,28},{28,24},{24,20},{20,16},{16,0},{1,5},{5... | collective-permute-start | bytes 3145736 | tf_op jit(solution)/shard_map/ppermute | solution.py:324
  31.1 23.7 %collective-permute-start.5 = (bf16[256,2048]{1,0:T(8,128)(2,1)}, bf16[256,2048]{1,0:T(8,128)(2,1)}, u32[]{:S(2)}, u32[]{:S(2)}) collective-permute-start(bf16[256,2048]{1,0:T(8,128)(2,1)} %collective-permute-done.2.refs_2_), channel_id=1, source_target_pairs={{0,16},{4,0},{8,4},{12,8},{28,12},{24,28},{20,24},{16,20},{1,17},{... | collective-permute-start | bytes 3145736 | tf_op jit(solution)/shard_map/ppermute | solution.py:324
  54.8 22.7 %collective-permute-start.7 = (bf16[256,2048]{1,0:T(8,128)(2,1)}, bf16[256,2048]{1,0:T(8,128)(2,1)S(1)}, u32[]{:S(2)}, u32[]{:S(2)}) collective-permute-start(bf16[256,2048]{1,0:T(8,128)(2,1)} %collective-permute-done.4.refs_3_), channel_id=1, source_target_pairs={{0,4},{4,8},{8,12},{12,28},{28,24},{24,20},{20,16},{16,0},{1,5},{5... | collective-permute-start | bytes 3145736 | tf_op jit(solution)/shard_map/ppermute | solution.py:324
  56.4 22.5 %collective-permute-start.8 = (bf16[256,2048]{1,0:T(8,128)(2,1)}, bf16[256,2048]{1,0:T(8,128)(2,1)}, u32[]{:S(2)}, u32[]{:S(2)}) collective-permute-start(bf16[256,2048]{1,0:T(8,128)(2,1)} %collective-permute-done.5.refs_4_), channel_id=1, source_target_pairs={{0,16},{4,0},{8,4},{12,8},{28,12},{24,28},{20,24},{16,20},{1,17},{... | collective-permute-start | bytes 3145736 | tf_op jit(solution)/shard_map/ppermute | solution.py:324
  57.7 11.2 %copy-start.2 = (bf16[576,2048]{1,0:T(8,128)(2,1)}, bf16[576,2048]{1,0:T(8,128)(2,1)S(1)}, u32[]{:S(2)}) copy-start(bf16[576,2048]{1,0:T(8,128)(2,1)S(1)} %collective-permute-done.refs_0_) | copy-start | bytes 7077892
  57.7 57.2 %collective-permute-start.6 = (bf16[576,2048]{1,0:T(8,128)(2,1)S(1)}, bf16[576,2048]{1,0:T(8,128)(2,1)}, u32[]{:S(2)}, u32[]{:S(2)}) collective-permute-start(bf16[576,2048]{1,0:T(8,128)(2,1)S(1)} %collective-permute-done.refs_0_), channel_id=1, source_target_pairs={{0,1},{1,0},{2,3},{3,2},{4,5},{5,4},{6,7},{7,6},{8,9},{9,8},{10,11... | collective-permute-start | bytes 7077896 | tf_op jit(solution)/shard_map/ppermute | solution.py:13
  57.7 28.7 %collective-permute-start.17 = (bf16[2,2304,128]{2,1,0:T(8,128)(2,1)}, bf16[2,2304,128]{2,1,0:T(8,128)(2,1)}, u32[]{:S(2)}, u32[]{:S(2)}) collective-permute-start(bf16[2,2304,128]{2,1,0:T(8,128)(2,1)} %get-tuple-element.41), channel_id=1, source_target_pairs={{0,2},{1,3},{2,0},{3,1},{4,6},{5,7},{6,4},{7,5},{8,10},{9,11},{10,... | collective-permute-start | bytes 3538952 | tf_op jit(solution)/shard_map/ppermute | solution.py:13
  68.8 13.8 %copy-start.11 = (bf16[8,64,1024]{2,1,0:T(8,128)(2,1)S(1)}, bf16[8,64,1024]{2,1,0:T(8,128)(2,1)}, u32[]{:S(2)}) copy-start(bf16[8,64,1024]{2,1,0:T(8,128)(2,1)} %param.13) | copy-start | bytes 3145732
  77.5 1.4 copy-start.6
  81.1 20.8 %collective-permute-start.9 = (bf16[192,2048]{1,0:T(8,128)(2,1)}, bf16[192,2048]{1,0:T(8,128)(2,1)}, u32[]{:S(2)}, u32[]{:S(2)}) collective-permute-start(bf16[192,2048]{1,0:T(8,128)(2,1)} %get-tuple-element.36), channel_id=1, source_target_pairs={{0,4},{4,8},{8,12},{12,28},{28,24},{24,20},{20,16},{16,0},{1,5},{5... | collective-permute-start | bytes 2359304 | tf_op jit(solution)/shard_map/ppermute | solution.py:324
  82.7 26.6 %copy-start.4 = (bf16[256,1024]{1,0:T(8,128)(2,1)}, bf16[256,1024]{1,0:T(8,128)(2,1)S(1)}, u32[]{:S(2)}) copy-start(bf16[256,1024]{1,0:T(8,128)(2,1)S(1)} %constant_dynamic-slice_fusion.2.refs_0_) | copy-start | bytes 1572868
  82.7 12.7 %collective-permute-start.14 = (bf16[256,1024]{1,0:T(8,128)(2,1)S(1)}, bf16[256,1024]{1,0:T(8,128)(2,1)S(1)}, u32[]{:S(2)}, u32[]{:S(2)}) collective-permute-start(bf16[256,1024]{1,0:T(8,128)(2,1)S(1)} %constant_dynamic-slice_fusion.2.refs_0_), channel_id=1, source_target_pairs={{0,16},{4,0},{8,4},{12,8},{28,12},{24,28},{20,24},{16,20},{1,17},{... | collective-permute-start | bytes 1572872 | tf_op jit(solution)/shard_map/ppermute | solution.py:324
  83.3 16.3 %collective-permute-start.10 = (bf16[64,2048]{1,0:T(8,128)(2,1)}, bf16[64,2048]{1,0:T(8,128)(2,1)S(1)}, u32[]{:S(2)}, u32[]{:S(2)}) collective-permute-start(bf16[64,2048]{1,0:T(8,128)(2,1)} %get-tuple-element.37), channel_id=1, source_target_pairs={{0,16},{4,0},{8,4},{12,8},{28,12},{24,28},{20,24},{16,20},{1,17},{... | collective-permute-start | bytes 786440 | tf_op jit(solution)/shard_map/ppermute | solution.py:324
  86.4 40.6 %collective-permute-start.18 = (bf16[2,2304,128]{2,1,0:T(8,128)(2,1)}, bf16[2,2304,128]{2,1,0:T(8,128)(2,1)}, u32[]{:S(2)}, u32[]{:S(2)}) collective-permute-start(bf16[2,2304,128]{2,1,0:T(8,128)(2,1)} %get-tuple-element.42), channel_id=1, source_target_pairs={{0,3},{1,2},{2,1},{3,0},{4,7},{5,6},{6,5},{7,4},{8,11},{9,10},{10,... | collective-permute-start | bytes 3538952 | tf_op jit(solution)/shard_map/ppermute | solution.py:13
  95.4 14.0 %copy-start.7 = (bf16[256,1024]{1,0:T(8,128)(2,1)}, bf16[256,1024]{1,0:T(8,128)(2,1)S(1)}, u32[]{:S(2)}) copy-start(bf16[256,1024]{1,0:T(8,128)(2,1)S(1)} %collective-permute-done.14.refs_2_) | copy-start | bytes 1572868
  95.4 14.0 %collective-permute-start.13 = (bf16[256,1024]{1,0:T(8,128)(2,1)S(1)}, bf16[256,1024]{1,0:T(8,128)(2,1)}, u32[]{:S(2)}, u32[]{:S(2)}) collective-permute-start(bf16[256,1024]{1,0:T(8,128)(2,1)S(1)} %constant_dynamic-slice_fusion.2.refs_0_), channel_id=1, source_target_pairs={{0,4},{4,8},{8,12},{12,28},{28,24},{24,20},{20,16},{16,0},{1,5},{5... | collective-permute-start | bytes 1572872 | tf_op jit(solution)/shard_map/ppermute | solution.py:324
  99.5 0.7 copy-start.14
  101.9 9.3 %collective-permute-start.16 = (bf16[256,1024]{1,0:T(8,128)(2,1)S(1)}, bf16[256,1024]{1,0:T(8,128)(2,1)}, u32[]{:S(2)}, u32[]{:S(2)}) collective-permute-start(bf16[256,1024]{1,0:T(8,128)(2,1)S(1)} %collective-permute-done.14.refs_2_), channel_id=1, source_target_pairs={{0,16},{4,0},{8,4},{12,8},{28,12},{24,28},{20,24},{16,20},{1,17},{... | collective-permute-start | bytes 1572872 | tf_op jit(solution)/shard_map/ppermute | solution.py:324
  109.3 3.4 %collective-permute-start.11 = (f32[576,64]{1,0:T(8,128)}, f32[576,64]{1,0:T(8,128)S(1)}, u32[]{:S(2)}, u32[]{:S(2)}) collective-permute-start(f32[576,64]{1,0:T(8,128)} %rank.3), channel_id=1, source_target_pairs={{0,1},{1,0},{2,3},{3,2},{4,5},{5,4},{6,7},{7,6},{8,9},{9,8},{10,11... | collective-permute-start | bytes 442376 | tf_op jit(solution)/shard_map/ppermute | solution.py:13
  109.4 33.5 %collective-permute-start.22 = (bf16[2,2304,128]{2,1,0:T(8,128)(2,1)}, bf16[2,2304,128]{2,1,0:T(8,128)(2,1)}, u32[]{:S(2)}, u32[]{:S(2)}) collective-permute-start(bf16[2,2304,128]{2,1,0:T(8,128)(2,1)} %get-tuple-element.44), channel_id=1, source_target_pairs={{0,1},{1,0},{2,3},{3,2},{4,5},{5,4},{6,7},{7,6},{8,9},{9,8},{10,11... | collective-permute-start | bytes 3538952 | tf_op jit(solution)/shard_map/ppermute | solution.py:13
  111.2 15.7 %collective-permute-start.15 = (bf16[256,1024]{1,0:T(8,128)(2,1)}, bf16[256,1024]{1,0:T(8,128)(2,1)S(1)}, u32[]{:S(2)}, u32[]{:S(2)}) collective-permute-start(bf16[256,1024]{1,0:T(8,128)(2,1)} %collective-permute-done.13.refs_1_), channel_id=1, source_target_pairs={{0,4},{4,8},{8,12},{12,28},{28,24},{24,20},{20,16},{16,0},{1,5},{5... | collective-permute-start | bytes 1572872 | tf_op jit(solution)/shard_map/ppermute | solution.py:324
  112.7 15.8 %collective-permute-start.20 = (bf16[256,1024]{1,0:T(8,128)(2,1)}, bf16[256,1024]{1,0:T(8,128)(2,1)}, u32[]{:S(2)}, u32[]{:S(2)}) collective-permute-start(bf16[256,1024]{1,0:T(8,128)(2,1)} %collective-permute-done.16.refs_4_), channel_id=1, source_target_pairs={{0,16},{4,0},{8,4},{12,8},{28,12},{24,28},{20,24},{16,20},{1,17},{... | collective-permute-start | bytes 1572872 | tf_op jit(solution)/shard_map/ppermute | solution.py:324
  114.9 19.5 %copy-start.12 = (s32[192]{0:T(256)S(1)}, s32[192]{0:T(256)}, u32[]{:S(2)}) copy-start(s32[192]{0:T(256)} %param.18) | copy-start | bytes 2308
  126.9 9.6 %copy-start.8 = (bf16[256,1024]{1,0:T(8,128)(2,1)}, bf16[256,1024]{1,0:T(8,128)(2,1)S(1)}, u32[]{:S(2)}) copy-start(bf16[256,1024]{1,0:T(8,128)(2,1)S(1)} %collective-permute-done.15.refs_3_) | copy-start | bytes 1572868
  127.0 16.0 %collective-permute-start.19 = (bf16[256,1024]{1,0:T(8,128)(2,1)S(1)}, bf16[256,1024]{1,0:T(8,128)(2,1)S(1)}, u32[]{:S(2)}, u32[]{:S(2)}) collective-permute-start(bf16[256,1024]{1,0:T(8,128)(2,1)S(1)} %collective-permute-done.15.refs_3_), channel_id=1, source_target_pairs={{0,4},{4,8},{8,12},{12,28},{28,24},{24,20},{20,16},{16,0},{1,5},{5... | collective-permute-start | bytes 1572872 | tf_op jit(solution)/shard_map/ppermute | solution.py:324
  128.5 15.2 %collective-permute-start.21 = (bf16[256,1024]{1,0:T(8,128)(2,1)}, bf16[256,1024]{1,0:T(8,128)(2,1)S(1)}, u32[]{:S(2)}, u32[]{:S(2)}) collective-permute-start(bf16[256,1024]{1,0:T(8,128)(2,1)} %collective-permute-done.20.refs_4_), channel_id=1, source_target_pairs={{0,16},{4,0},{8,4},{12,8},{28,12},{24,28},{20,24},{16,20},{1,17},{... | collective-permute-start | bytes 1572872 | tf_op jit(solution)/shard_map/ppermute | solution.py:324
  129.0 6.7 %collective-permute-start.12 = (f32[576,64]{1,0:T(8,128)S(1)}, f32[576,64]{1,0:T(8,128)S(1)}, u32[]{:S(2)}, u32[]{:S(2)}) collective-permute-start(f32[576,64]{1,0:T(8,128)S(1)} %add.119), channel_id=1, source_target_pairs={{0,2},{1,3},{2,0},{3,1},{4,6},{5,7},{6,4},{7,5},{8,10},{9,11},{10,... | collective-permute-start | bytes 442376 | tf_op jit(solution)/shard_map/ppermute | solution.py:13
  142.9 0.8 copy-start.9
  143.7 0.8 copy-start.10
  144.5 10.8 %copy-start.1 = (bf16[8,2048,64]{1,2,0:T(8,128)(2,1)S(1)}, bf16[8,2048,64]{1,2,0:T(8,128)(2,1)}, u32[]{:S(2)}) copy-start(bf16[8,2048,64]{1,2,0:T(8,128)(2,1)} %param.12) | copy-start | bytes 6291460

commit v9 on v8

--- a/solution.py
+++ b/solution.py
@@ -459,14 +459,14 @@
         starts[early:], flat_tokens, row_adapters, groups, rank, earlier=ranks, last=True
     )
     for k in range(2, owners + 1):
-        from_after.append(ring_hop(gate(from_after[-1], *(down[-1] if k == 2 else [])), -1, owners))
+        from_after.append(ring_hop(gate(from_after[-1], *([down[-1], base] if k == 2 else [])), -1, owners))
     bits = [1 << i for i in range((count - 1).bit_length())]
-    ranks = ranks + swap(ranks, bits[0], count)
     for k in range(2, owners):
-        wait = [ranks] + ([third, base] if paired else []) if k == owners - 1 else []
+        if k == owners - 1:
+            for bit in bits:
+                ranks = ranks + swap(ranks, bit, count)
+        wait = [ranks] + ([third] if paired and k == owners - 1 else [])
         from_before.append(ring_hop(gate(from_before[-1], *wait), 1, owners))
-    for bit in bits[1:]:
-        ranks = ranks + swap(ranks, bit, count)
     up = [part for pair in zip(from_before, from_after) for part in pair] + [from_after[-1]]
     groups = [[own_up]] + [[part] for part in up[: early - 1]]
     query = early_query(starts[:early], base, ranks, row_adapters, groups)

time: 156 us -> 160 us (1.026)
  waiting for transfers between devices: 52.7 us -> 57.8 us
    ppermute x8, waiting for transfers between devices: 4.13 us -> 36.2 us  [swap(): return lax.ppermute(array, 'tensor', [(i, i ^ bit) for i in range(count)])]
    ppermute x15, waiting for transfers between devices: 48.5 us -> 21.6 us  [ring_hop(): return lax.ppermute(array, ('rep', 'dp'), pairs)]
    ppermute x8, starting transfers between devices: 7.01 us -> 5.02 us  [swap(): return lax.ppermute(array, 'tensor', [(i, i ^ bit) for i in range(count)])]
    unnamed x33 -> x35, local copies, waits for them, and re-layouts: 8.34 us -> 7.79 us
  transfers between devices with their start and end apart: 23 -> 23, of which waited for: 12 -> 9; matrix products, arithmetic and copies ran while one was open for 13% -> 12% of each run, Pallas kernels for 29% -> 29%
where the time goes in v9:
time: 160 us; the launch traced here: 159 us
  waiting for transfers between devices  57.8 us (36%)
  Pallas kernels  56.6 us (35%)
  starting transfers between devices  22 us (14%)
  local copies, waits for them, and re-layouts  19.1 us (12%)
  other arithmetic  3.59 us (2%)
    ppermute x8, waiting for transfers between devices, swap(): return lax.ppermute(array, 'tensor', [(i, i ^ bit) for i in range(count)])  36.2 us
    pallas_call x2, Pallas kernels, project_pair(): pl.pallas_call(kernel, out_shape=jax.ShapeDtypeStruct((rows, columns), jn...  22.9 us
    ppermute x15, waiting for transfers between devices, ring_hop(): return lax.ppermute(array, ('rep', 'dp'), pairs)  21.6 us
    ppermute x15, starting transfers between devices, ring_hop(): return lax.ppermute(array, ('rep', 'dp'), pairs)  17 us
    pallas_call x2, Pallas kernels, add_ranks(): pl.pallas_call(kernel, out_shape=jax.ShapeDtypeStruct((rows, out_width),...  14.3 us
    pallas_call x1, Pallas kernels, attend(): pl.pallas_call(kernel, out_shape=jax.ShapeDtypeStruct((steps, rows, width...  10.8 us
    unnamed x35, local copies, waits for them, and re-layouts  7.79 us
    pallas_call x1, Pallas kernels, early_query(): pl.pallas_call(kernel, out_shape=jax.ShapeDtypeStruct((rows, columns), jn...  6.39 us
  transfers between devices with their start and end apart: 23, of which 9 were waited for; matrix products, arithmetic and copies ran while one was open for 12% of the time, Pallas kernels for 29%

profile of v9, /device:TPU:0, one launch (start us, length us, event | category | flops | bytes accessed | tf_op | source)
XLA Modules:
  0.0 159.2 jit_solution(15860192963758780912)
XLA Ops:
  0.5 1.1 copy-done
  1.7 3.1 %collective-permute-start.1 = (bf16[256,2048]{1,0:T(8,128)(2,1)S(1)}, bf16[256,2048]{1,0:T(8,128)(2,1)}, u32[]{:S(2)}, u32[]{:S(2)}) collective-permute-start(bf16[256,2048]{1,0:T(8,128)(2,1)S(1)} %constant_dynamic-slice_fusion.3.refs_0_), channel_id=1, source_target_pairs={{0,4},{4,8},{8,12},{12,28},{28,24},{24,20},{20,16},{16,0},{1,5},{5... | collective-permute-start | bytes 3145736 | tf_op jit(solution)/shard_map/ppermute | solution.py:324
  4.8 1.9 %collective-permute-start = (bf16[576,2048]{1,0:T(8,128)(2,1)}, bf16[576,2048]{1,0:T(8,128)(2,1)S(1)}, u32[]{:S(2)}, u32[]{:S(2)}) collective-permute-start(bf16[576,2048]{1,0:T(8,128)(2,1)} %bitcast.42), channel_id=1, source_target_pairs={{0,2},{1,3},{2,0},{3,1},{4,6},{5,7},{6,4},{7,5},{8,10},{9,11},{10,... | collective-permute-start | bytes 7077896 | tf_op jit(solution)/shard_map/ppermute | solution.py:13
  6.7 3.5 %copy_dynamic-update-slice_fusion.1 = bf16[4,2,2304,128]{3,2,1,0:T(8,128)(2,1)} fusion(bf16[4,1,2304,128]{3,0,2,1:T(4,128)(2,1)} %bitcast.39), kind=kLoop, calls=%fused_computation.1 | loop fusion | bytes 4718592
  10.3 1.7 %copy_dynamic-update-slice_fusion = bf16[4,2,2304,128]{3,2,1,0:T(8,128)(2,1)} fusion(bf16[4,2,2304,128]{3,2,1,0:T(8,128)(2,1)} %copy_dynamic-update-slice_fusion.1, bf16[4,1,2304,128]{3,0,2,1:T(4,128)(2,1)S(1)} %bitcast.40), kind=kLoop, calls=%fused_computation | loop fusion | bytes 4718592 | tf_op jit(solution)/shard_map/stack | solution.py:411
  12.0 4.6 %dynamic-slice_bitcast_fusion = (bf16[2,2304,128]{2,1,0:T(8,128)(2,1)}, bf16[2,2304,128]{2,1,0:T(8,128)(2,1)}, bf16[2,2304,128]{2,1,0:T(8,128)(2,1)}, bf16[2,2304,128]{2,1,0:T(8,128)(2,1)}) fusion(bf16[4,2,2304,128]{3,2,1,0:T(8,128)(2,1)} %copy_dynamic-update-slice_fusion, s32[]{:T(128)S(6)} %select_n.67, s32[]{:T(128)S(6)} %select_n.66, s32[]{:T(128)S(6)} %select_n.65, ...), kind=kLoop, calls=%fused_computation.2 | loop fusion | bytes 9437200 | tf_op jit(solution)/shard_map/jit(dynamic_index_in_dim)/squeeze | solution.py:420
  16.6 0.7 pad_add_fusion.1.ids_ref
  17.2 10.8 %project.2.refs_4_ = f32[576,1024]{1,0:T(8,128)} custom-call(s32[2]{0:T(128)} %pad_add_fusion.1.ids_ref, bf16[576,2048]{1,0:T(8,128)(2,1)} %bitcast.43, bf16[576,2048]{1,0:T(8,128)(2,1)} %collective-permute-done.3.refs_1_, bf16[8192,1024]{1,0:T(8,128)(2,1)} %refs_3_.3, bf16[8192,1024]{1,0:T(8,128)(2,1)} %refs_3_.3), custom_call_target="tpu_custom_call" | custom-call | flops 4831838208 | bytes 15466496 | tf_op jit(solution)/shard_map/project/pallas_call | solution.py:54
  28.1 1.4 collective-permute-done.2.refs_2_
  29.5 1.6 collective-permute-start.4
  31.5 26.2 %collective-permute-done.refs_0_ = bf16[576,2048]{1,0:T(8,128)(2,1)S(1)} collective-permute-done((bf16[576,2048]{1,0:T(8,128)(2,1)}, bf16[576,2048]{1,0:T(8,128)(2,1)S(1)}, u32[]{:S(2)}, u32[]{:S(2)}) %collective-permute-start) | collective-permute-done | bytes 2359328 | tf_op jit(solution)/shard_map/ppermute | solution.py:13
  57.8 1.8 %collective-permute-start.7 = (bf16[256,2048]{1,0:T(8,128)(2,1)}, bf16[256,2048]{1,0:T(8,128)(2,1)S(1)}, u32[]{:S(2)}, u32[]{:S(2)}) collective-permute-start(bf16[256,2048]{1,0:T(8,128)(2,1)} %collective-permute-done.4.refs_3_), channel_id=1, source_target_pairs={{0,4},{4,8},{8,12},{12,28},{28,24},{24,20},{20,16},{16,0},{1,5},{5... | collective-permute-start | bytes 3145736 | tf_op jit(solution)/shard_map/ppermute | solution.py:324
  59.9 1.7 %collective-permute-start.17 = (bf16[2,2304,128]{2,1,0:T(8,128)(2,1)}, bf16[2,2304,128]{2,1,0:T(8,128)(2,1)}, u32[]{:S(2)}, u32[]{:S(2)}) collective-permute-start(bf16[2,2304,128]{2,1,0:T(8,128)(2,1)} %get-tuple-element.43), channel_id=1, source_target_pairs={{0,2},{1,3},{2,0},{3,1},{4,6},{5,7},{6,4},{7,5},{8,10},{9,11},{10,... | collective-permute-start | bytes 3538952 | tf_op jit(solution)/shard_map/ppermute | solution.py:13
  61.5 1.0 reshape_tile.4.adapter_ref.refs_2_
  62.5 0.7 stack.61.starts_ref
  63.2 8.0 %rank.2.refs_4_ = f32[576,256]{1,0:T(8,128)} custom-call(s32[5]{0:T(128)} %stack.61.starts_ref, bf16[576,2048]{1,0:T(8,128)(2,1)} %bitcast.44, s32[576,1]{1,0:T(8,128)} %reshape_tile.4.adapter_ref.refs_2_, bf16[256,2048]{1,0:T(8,128)(2,1)} %copy-done.7, bf16[256,2048]{1,0:T(8,128)(2,1)} %collective-permute-done.1.refs_1_, ...), custom_call_target="tpu_custom_call" | custom-call | flops 3019898880 | bytes 7602176 | tf_op jit(solution)/shard_map/rank/pallas_call | solution.py:101
  71.2 12.4 %collective-permute-done.7.before_ref.refs_0_ = bf16[256,2048]{1,0:T(8,128)(2,1)S(1)} collective-permute-done((bf16[256,2048]{1,0:T(8,128)(2,1)}, bf16[256,2048]{1,0:T(8,128)(2,1)S(1)}, u32[]{:S(2)}, u32[]{:S(2)}) %collective-permute-start.7) | collective-permute-done | bytes 1048608 | tf_op jit(solution)/shard_map/ppermute | solution.py:324
  83.6 1.6 collective-permute-done.8.after_ref.refs_1_
  85.1 2.2 %split.1 = (bf16[192,2048]{1,0:T(8,128)(2,1)}, bf16[64,2048]{1,0:T(8,128)(2,1)}) custom-call(bf16[256,2048]{1,0:T(8,128)(2,1)} %copy-done.8, bf16[256,2048]{1,0:T(8,128)(2,1)} %collective-permute-done.8.after_ref.refs_1_), custom_call_target="tpu_custom_call" | custom-call | bytes 2097152 | tf_op jit(solution)/shard_map/split/pallas_call | solution.py:343
  87.4 1.6 collective-permute-start.9
  89.5 0.6 pad_add_fusion.ids_ref
  90.1 1.1 collective-permute-start.10
  91.2 0.9 collective-permute-start.13
  92.1 12.0 %project.3.base_ref = f32[576,1024]{1,0:T(8,128)} custom-call(s32[2]{0:T(128)} %pad_add_fusion.ids_ref, bf16[576,2048]{1,0:T(8,128)(2,1)} %copy-done.2, bf16[576,2048]{1,0:T(8,128)(2,1)} %collective-permute-done.6.refs_1_, bf16[8192,1024]{1,0:T(8,128)(2,1)} %refs_3_.3, bf16[8192,1024]{1,0:T(8,128)(2,1)} %refs_3_.3, f32[576,1024]{1,0:T(8,128)} %project.2.refs_4_), custom_call_target="tpu_custom_call" | custom-call | flops 4831838208 | bytes 15466496 | tf_op jit(solution)/shard_map/project/pallas_call | solution.py:54
  104.2 3.4 %collective-permute-done.10.refs_3_ = bf16[64,2048]{1,0:T(8,128)(2,1)S(1)} collective-permute-done((bf16[64,2048]{1,0:T(8,128)(2,1)}, bf16[64,2048]{1,0:T(8,128)(2,1)S(1)}, u32[]{:S(2)}, u32[]{:S(2)}) %collective-permute-start.10) | collective-permute-done | bytes 262176 | tf_op jit(solution)/shard_map/ppermute | solution.py:324
  107.6 0.7 copy-done.15
  108.3 0.9 collective-permute-start.16
  109.2 0.6 pad_add_fusion.2.starts_ref
  109.8 6.3 %rank.3 = f32[576,64]{1,0:T(8,128)} custom-call(s32[3]{0:T(128)} %pad_add_fusion.2.starts_ref, bf16[576,2048]{1,0:T(8,128)(2,1)} %bitcast.45, s32[576,1]{1,0:T(8,128)} %reshape_tile.4.adapter_ref.refs_2_, bf16[256,2048]{1,0:T(8,128)(2,1)} %copy-done.8, bf16[256,2048]{1,0:T(8,128)(2,1)} %collective-permute-done.8.after_ref.refs_1_, ...), custom_call_target="tpu_custom_call" | custom-call | flops 1811939328 | bytes 5505024 | tf_op jit(solution)/shard_map/rank/pallas_call | solution.py:101
  116.1 1.6 collective-permute-done.13.refs_1_
  117.7 1.6 collective-permute-start.15
  119.3 1.2 collective-permute-done.16.refs_4_
  120.5 1.1 collective-permute-start.20
  121.5 1.8 %collective-permute-done.11 = f32[576,64]{1,0:T(8,128)S(1)} collective-permute-done((f32[576,64]{1,0:T(8,128)}, f32[576,64]{1,0:T(8,128)S(1)}, u32[]{:S(2)}, u32[]{:S(2)}) %collective-permute-start.11) | collective-permute-done | bytes 147488 | tf_op jit(solution)/shard_map/ppermute | solution.py:13
  123.3 1.0 add.119
  124.3 0.9 collective-permute-start.12
  125.3 8.2 %collective-permute-done.12 = f32[576,64]{1,0:T(8,128)S(1)} collective-permute-done((f32[576,64]{1,0:T(8,128)S(1)}, f32[576,64]{1,0:T(8,128)S(1)}, u32[]{:S(2)}, u32[]{:S(2)}) %collective-permute-start.12) | collective-permute-done | bytes 147488 | tf_op jit(solution)/shard_map/ppermute | solution.py:13
  133.5 0.7 add.120.rank_ref.refs_1_
  134.2 1.0 collective-permute-start.19
  135.2 1.1 collective-permute-start.21
  136.3 0.6 concatenate.9.scalars_ref
  136.9 1.9 %constant_dynamic-slice_fusion = (bf16[3,192,1,128]{3,2,1,0:T(2,128)(2,1)S(1)}, bf16[3,192,1,128]{3,2,1,0:T(2,128)(2,1)S(1)}) fusion(bf16[3,192,4,128]{3,2,1,0:T(4,128)(2,1)} %param.17, s32[]{:T(128)S(6)} %select_n.69, bf16[3,192,4,128]{3,2,1,0:T(4,128)(2,1)} %param.16), kind=kLoop, calls=%fused_computation.8 | loop fusion | bytes 589828 | tf_op jit(solution)/shard_map/jit(dynamic_index_in_dim)/dynamic_slice | solution.py:477
  138.8 0.7 copy.28
  139.5 0.7 copy.29
  140.1 0.8 copy.21.refs_6_
  140.9 6.4 %delta.1.refs_0_ = f32[576,1024]{1,0:T(8,128)} custom-call(s32[5]{0:T(128)} %stack.61.starts_ref, f32[576,1024]{1,0:T(8,128)} %project.3.base_ref, f32[576,64]{1,0:T(8,128)} %add.120.rank_ref.refs_1_, s32[576,1]{1,0:T(8,128)} %reshape_tile.4.adapter_ref.refs_2_, bf16[256,1024]{1,0:T(8,128)(2,1)} %copy-done.4, ...), custom_call_target="tpu_custom_call" | custom-call | flops 1509949440 | bytes 7340032 | tf_op jit(solution)/shard_map/delta/pallas_call | solution.py:147
  147.3 1.0 copy-done.6
  148.3 10.8 %attend.1 = bf16[3,192,1024]{2,1,0:T(8,128)(2,1)} custom-call(s32[7]{0:T(128)} %concatenate.9.scalars_ref, f32[576,1024]{1,0:T(8,128)} %delta.1.refs_0_, f32[576,64]{1,0:T(8,128)} %add.120.rank_ref.refs_1_, s32[576,1]{1,0:T(8,128)} %reshape_tile.4.adapter_ref.refs_2_, bf16[256,1024]{1,0:T(8,128)(2,1)} %collective-permute-done.19.refs_3_, ...), custom_call_target="tpu_custom_call" | custom-call | flops 481296384 | bytes 7077888 | tf_op jit(solution)/shard_map/attend/pallas_call | solution.py:297
  (55 shorter events, 2.0 us)
Async XLA Ops:
  0.0 1.6 copy-start
  0.0 17.2 %collective-permute-start.3 = (bf16[576,2048]{1,0:T(8,128)(2,1)}, bf16[576,2048]{1,0:T(8,128)(2,1)}, u32[]{:S(2)}, u32[]{:S(2)}) collective-permute-start(bf16[576,2048]{1,0:T(8,128)(2,1)} %bitcast.41), channel_id=1, source_target_pairs={{0,1},{1,0},{2,3},{3,2},{4,5},{5,4},{6,7},{7,6},{8,9},{9,8},{10,11... | collective-permute-start | bytes 7077896 | tf_op jit(solution)/shard_map/ppermute | solution.py:13
  1.7 8.6 %copy-start.7 = (bf16[256,2048]{1,0:T(8,128)(2,1)}, bf16[256,2048]{1,0:T(8,128)(2,1)S(1)}, u32[]{:S(2)}) copy-start(bf16[256,2048]{1,0:T(8,128)(2,1)S(1)} %constant_dynamic-slice_fusion.3.refs_0_) | copy-start | bytes 3145732
  1.7 26.4 %collective-permute-start.1 = (bf16[256,2048]{1,0:T(8,128)(2,1)S(1)}, bf16[256,2048]{1,0:T(8,128)(2,1)}, u32[]{:S(2)}, u32[]{:S(2)}) collective-permute-start(bf16[256,2048]{1,0:T(8,128)(2,1)S(1)} %constant_dynamic-slice_fusion.3.refs_0_), channel_id=1, source_target_pairs={{0,4},{4,8},{8,12},{12,28},{28,24},{24,20},{20,16},{16,0},{1,5},{5... | collective-permute-start | bytes 3145736 | tf_op jit(solution)/shard_map/ppermute | solution.py:324
  4.8 24.7 %collective-permute-start.2 = (bf16[256,2048]{1,0:T(8,128)(2,1)S(1)}, bf16[256,2048]{1,0:T(8,128)(2,1)}, u32[]{:S(2)}, u32[]{:S(2)}) collective-permute-start(bf16[256,2048]{1,0:T(8,128)(2,1)S(1)} %constant_dynamic-slice_fusion.3.refs_0_), channel_id=1, source_target_pairs={{0,16},{4,0},{8,4},{12,8},{28,12},{24,28},{20,24},{16,20},{1,17},{... | collective-permute-start | bytes 3145736 | tf_op jit(solution)/shard_map/ppermute | solution.py:324
  4.8 52.9 %collective-permute-start = (bf16[576,2048]{1,0:T(8,128)(2,1)}, bf16[576,2048]{1,0:T(8,128)(2,1)S(1)}, u32[]{:S(2)}, u32[]{:S(2)}) collective-permute-start(bf16[576,2048]{1,0:T(8,128)(2,1)} %bitcast.42), channel_id=1, source_target_pairs={{0,2},{1,3},{2,0},{3,1},{4,6},{5,7},{6,4},{7,5},{8,10},{9,11},{10,... | collective-permute-start | bytes 7077896 | tf_op jit(solution)/shard_map/ppermute | solution.py:13
  6.7 3.6 %copy-start.3 = (bf16[192,4,12,128]{3,1,2,0:T(4,128)(2,1)S(1)}, bf16[192,4,12,128]{3,1,2,0:T(4,128)(2,1)}, u32[]{:S(2)}) copy-start(bf16[192,4,12,128]{3,1,2,0:T(4,128)(2,1)} %param.15) | copy-start | bytes 7077892
  17.2 44.3 %copy-start.14 = (s32[192]{0:T(256)S(1)}, s32[192]{0:T(256)}, u32[]{:S(2)}) copy-start(s32[192]{0:T(256)} %param.19) | copy-start | bytes 2308
  29.5 28.2 %collective-permute-start.4 = (bf16[256,2048]{1,0:T(8,128)(2,1)}, bf16[256,2048]{1,0:T(8,128)(2,1)}, u32[]{:S(2)}, u32[]{:S(2)}) collective-permute-start(bf16[256,2048]{1,0:T(8,128)(2,1)} %collective-permute-done.1.refs_1_), channel_id=1, source_target_pairs={{0,4},{4,8},{8,12},{12,28},{28,24},{24,20},{20,16},{16,0},{1,5},{5... | collective-permute-start | bytes 3145736 | tf_op jit(solution)/shard_map/ppermute | solution.py:324
  31.1 26.6 %collective-permute-start.5 = (bf16[256,2048]{1,0:T(8,128)(2,1)}, bf16[256,2048]{1,0:T(8,128)(2,1)}, u32[]{:S(2)}, u32[]{:S(2)}) collective-permute-start(bf16[256,2048]{1,0:T(8,128)(2,1)} %collective-permute-done.2.refs_2_), channel_id=1, source_target_pairs={{0,16},{4,0},{8,4},{12,8},{28,12},{24,28},{20,24},{16,20},{1,17},{... | collective-permute-start | bytes 3145736 | tf_op jit(solution)/shard_map/ppermute | solution.py:324
  57.7 13.5 %copy-start.2 = (bf16[576,2048]{1,0:T(8,128)(2,1)}, bf16[576,2048]{1,0:T(8,128)(2,1)S(1)}, u32[]{:S(2)}) copy-start(bf16[576,2048]{1,0:T(8,128)(2,1)S(1)} %collective-permute-done.refs_0_) | copy-start | bytes 7077892
  57.7 34.4 %collective-permute-start.6 = (bf16[576,2048]{1,0:T(8,128)(2,1)S(1)}, bf16[576,2048]{1,0:T(8,128)(2,1)}, u32[]{:S(2)}, u32[]{:S(2)}) collective-permute-start(bf16[576,2048]{1,0:T(8,128)(2,1)S(1)} %collective-permute-done.refs_0_), channel_id=1, source_target_pairs={{0,1},{1,0},{2,3},{3,2},{4,5},{5,4},{6,7},{7,6},{8,9},{9,8},{10,11... | collective-permute-start | bytes 7077896 | tf_op jit(solution)/shard_map/ppermute | solution.py:13
  57.8 25.8 %collective-permute-start.7 = (bf16[256,2048]{1,0:T(8,128)(2,1)}, bf16[256,2048]{1,0:T(8,128)(2,1)S(1)}, u32[]{:S(2)}, u32[]{:S(2)}) collective-permute-start(bf16[256,2048]{1,0:T(8,128)(2,1)} %collective-permute-done.4.refs_3_), channel_id=1, source_target_pairs={{0,4},{4,8},{8,12},{12,28},{28,24},{24,20},{20,16},{16,0},{1,5},{5... | collective-permute-start | bytes 3145736 | tf_op jit(solution)/shard_map/ppermute | solution.py:324
  59.6 25.5 %collective-permute-start.8 = (bf16[256,2048]{1,0:T(8,128)(2,1)}, bf16[256,2048]{1,0:T(8,128)(2,1)}, u32[]{:S(2)}, u32[]{:S(2)}) collective-permute-start(bf16[256,2048]{1,0:T(8,128)(2,1)} %collective-permute-done.5.refs_4_), channel_id=1, source_target_pairs={{0,16},{4,0},{8,4},{12,8},{28,12},{24,28},{20,24},{16,20},{1,17},{... | collective-permute-start | bytes 3145736 | tf_op jit(solution)/shard_map/ppermute | solution.py:324
  59.9 31.3 %collective-permute-start.17 = (bf16[2,2304,128]{2,1,0:T(8,128)(2,1)}, bf16[2,2304,128]{2,1,0:T(8,128)(2,1)}, u32[]{:S(2)}, u32[]{:S(2)}) collective-permute-start(bf16[2,2304,128]{2,1,0:T(8,128)(2,1)} %get-tuple-element.43), channel_id=1, source_target_pairs={{0,2},{1,3},{2,0},{3,1},{4,6},{5,7},{6,4},{7,5},{8,10},{9,11},{10,... | collective-permute-start | bytes 3538952 | tf_op jit(solution)/shard_map/ppermute | solution.py:13
  71.2 17.8 %copy-start.12 = (bf16[8,64,1024]{2,1,0:T(8,128)(2,1)S(1)}, bf16[8,64,1024]{2,1,0:T(8,128)(2,1)}, u32[]{:S(2)}) copy-start(bf16[8,64,1024]{2,1,0:T(8,128)(2,1)} %param.13) | copy-start | bytes 3145732
  83.6 1.6 copy-start.8
  87.4 20.9 %collective-permute-start.9 = (bf16[192,2048]{1,0:T(8,128)(2,1)}, bf16[192,2048]{1,0:T(8,128)(2,1)}, u32[]{:S(2)}, u32[]{:S(2)}) collective-permute-start(bf16[192,2048]{1,0:T(8,128)(2,1)} %get-tuple-element.37), channel_id=1, source_target_pairs={{0,4},{4,8},{8,12},{12,28},{28,24},{24,20},{20,16},{16,0},{1,5},{5... | collective-permute-start | bytes 2359304 | tf_op jit(solution)/shard_map/ppermute | solution.py:324
  89.0 15.2 %copy-start.4 = (bf16[256,1024]{1,0:T(8,128)(2,1)}, bf16[256,1024]{1,0:T(8,128)(2,1)S(1)}, u32[]{:S(2)}) copy-start(bf16[256,1024]{1,0:T(8,128)(2,1)S(1)} %constant_dynamic-slice_fusion.2.refs_0_) | copy-start | bytes 1572868
  89.0 15.1 %collective-permute-start.14 = (bf16[256,1024]{1,0:T(8,128)(2,1)S(1)}, bf16[256,1024]{1,0:T(8,128)(2,1)S(1)}, u32[]{:S(2)}, u32[]{:S(2)}) collective-permute-start(bf16[256,1024]{1,0:T(8,128)(2,1)S(1)} %constant_dynamic-slice_fusion.2.refs_0_), channel_id=1, source_target_pairs={{0,16},{4,0},{8,4},{12,8},{28,12},{24,28},{20,24},{16,20},{1,17},{... | collective-permute-start | bytes 1572872 | tf_op jit(solution)/shard_map/ppermute | solution.py:324
  90.1 17.5 %collective-permute-start.10 = (bf16[64,2048]{1,0:T(8,128)(2,1)}, bf16[64,2048]{1,0:T(8,128)(2,1)S(1)}, u32[]{:S(2)}, u32[]{:S(2)}) collective-permute-start(bf16[64,2048]{1,0:T(8,128)(2,1)} %get-tuple-element.38), channel_id=1, source_target_pairs={{0,16},{4,0},{8,4},{12,8},{28,12},{24,28},{20,24},{16,20},{1,17},{... | collective-permute-start | bytes 786440 | tf_op jit(solution)/shard_map/ppermute | solution.py:324
  91.2 26.5 %collective-permute-start.13 = (bf16[256,1024]{1,0:T(8,128)(2,1)S(1)}, bf16[256,1024]{1,0:T(8,128)(2,1)}, u32[]{:S(2)}, u32[]{:S(2)}) collective-permute-start(bf16[256,1024]{1,0:T(8,128)(2,1)S(1)} %constant_dynamic-slice_fusion.2.refs_0_), channel_id=1, source_target_pairs={{0,4},{4,8},{8,12},{12,28},{28,24},{24,20},{20,16},{16,0},{1,5},{5... | collective-permute-start | bytes 1572872 | tf_op jit(solution)/shard_map/ppermute | solution.py:324
  92.1 42.1 %collective-permute-start.18 = (bf16[2,2304,128]{2,1,0:T(8,128)(2,1)}, bf16[2,2304,128]{2,1,0:T(8,128)(2,1)S(1)}, u32[]{:S(2)}, u32[]{:S(2)}) collective-permute-start(bf16[2,2304,128]{2,1,0:T(8,128)(2,1)} %get-tuple-element.44), channel_id=1, source_target_pairs={{0,3},{1,2},{2,1},{3,0},{4,7},{5,6},{6,5},{7,4},{8,11},{9,10},{10,... | collective-permute-start | bytes 3538952 | tf_op jit(solution)/shard_map/ppermute | solution.py:13
  104.2 12.0 %copy-start.9 = (bf16[256,1024]{1,0:T(8,128)(2,1)}, bf16[256,1024]{1,0:T(8,128)(2,1)S(1)}, u32[]{:S(2)}) copy-start(bf16[256,1024]{1,0:T(8,128)(2,1)S(1)} %collective-permute-done.14.refs_2_) | copy-start | bytes 1572868
  107.6 0.7 copy-start.15
  108.3 12.2 %collective-permute-start.16 = (bf16[256,1024]{1,0:T(8,128)(2,1)S(1)}, bf16[256,1024]{1,0:T(8,128)(2,1)}, u32[]{:S(2)}, u32[]{:S(2)}) collective-permute-start(bf16[256,1024]{1,0:T(8,128)(2,1)S(1)} %collective-permute-done.14.refs_2_), channel_id=1, source_target_pairs={{0,16},{4,0},{8,4},{12,8},{28,12},{24,28},{20,24},{16,20},{1,17},{... | collective-permute-start | bytes 1572872 | tf_op jit(solution)/shard_map/ppermute | solution.py:324
  109.8 37.5 %collective-permute-start.22 = (bf16[2,2304,128]{2,1,0:T(8,128)(2,1)}, bf16[2,2304,128]{2,1,0:T(8,128)(2,1)S(1)}, u32[]{:S(2)}, u32[]{:S(2)}) collective-permute-start(bf16[2,2304,128]{2,1,0:T(8,128)(2,1)} %get-tuple-element.46), channel_id=1, source_target_pairs={{0,1},{1,0},{2,3},{3,2},{4,5},{5,4},{6,7},{7,6},{8,9},{9,8},{10,11... | collective-permute-start | bytes 3538952 | tf_op jit(solution)/shard_map/ppermute | solution.py:13
  116.1 24.0 %copy-start.13 = (s32[192]{0:T(256)S(1)}, s32[192]{0:T(256)}, u32[]{:S(2)}) copy-start(s32[192]{0:T(256)} %param.18) | copy-start | bytes 2308
  117.7 16.5 %collective-permute-start.15 = (bf16[256,1024]{1,0:T(8,128)(2,1)}, bf16[256,1024]{1,0:T(8,128)(2,1)S(1)}, u32[]{:S(2)}, u32[]{:S(2)}) collective-permute-start(bf16[256,1024]{1,0:T(8,128)(2,1)} %collective-permute-done.13.refs_1_), channel_id=1, source_target_pairs={{0,4},{4,8},{8,12},{12,28},{28,24},{24,20},{20,16},{16,0},{1,5},{5... | collective-permute-start | bytes 1572872 | tf_op jit(solution)/shard_map/ppermute | solution.py:324
  120.5 14.8 %collective-permute-start.20 = (bf16[256,1024]{1,0:T(8,128)(2,1)}, bf16[256,1024]{1,0:T(8,128)(2,1)S(1)}, u32[]{:S(2)}, u32[]{:S(2)}) collective-permute-start(bf16[256,1024]{1,0:T(8,128)(2,1)} %collective-permute-done.16.refs_4_), channel_id=1, source_target_pairs={{0,16},{4,0},{8,4},{12,8},{28,12},{24,28},{20,24},{16,20},{1,17},{... | collective-permute-start | bytes 1572872 | tf_op jit(solution)/shard_map/ppermute | solution.py:324
  121.5 1.8 %collective-permute-start.11 = (f32[576,64]{1,0:T(8,128)}, f32[576,64]{1,0:T(8,128)S(1)}, u32[]{:S(2)}, u32[]{:S(2)}) collective-permute-start(f32[576,64]{1,0:T(8,128)} %rank.3), channel_id=1, source_target_pairs={{0,1},{1,0},{2,3},{3,2},{4,5},{5,4},{6,7},{7,6},{8,9},{9,8},{10,11... | collective-permute-start | bytes 442376 | tf_op jit(solution)/shard_map/ppermute | solution.py:13
  124.3 9.1 %collective-permute-start.12 = (f32[576,64]{1,0:T(8,128)S(1)}, f32[576,64]{1,0:T(8,128)S(1)}, u32[]{:S(2)}, u32[]{:S(2)}) collective-permute-start(f32[576,64]{1,0:T(8,128)S(1)} %add.119), channel_id=1, source_target_pairs={{0,2},{1,3},{2,0},{3,1},{4,6},{5,7},{6,4},{7,5},{8,10},{9,11},{10,... | collective-permute-start | bytes 442376 | tf_op jit(solution)/shard_map/ppermute | solution.py:13
  134.2 6.7 %copy-start.10 = (bf16[256,1024]{1,0:T(8,128)(2,1)}, bf16[256,1024]{1,0:T(8,128)(2,1)S(1)}, u32[]{:S(2)}) copy-start(bf16[256,1024]{1,0:T(8,128)(2,1)S(1)} %collective-permute-done.15.refs_3_) | copy-start | bytes 1572868
  134.2 13.1 %copy-start.5 = (bf16[2,2304,128]{2,1,0:T(8,128)(2,1)}, bf16[2,2304,128]{2,1,0:T(8,128)(2,1)S(1)}, u32[]{:S(2)}) copy-start(bf16[2,2304,128]{2,1,0:T(8,128)(2,1)S(1)} %collective-permute-done.18.refs_10_) | copy-start | bytes 3538948
  134.2 14.1 %collective-permute-start.19 = (bf16[256,1024]{1,0:T(8,128)(2,1)S(1)}, bf16[256,1024]{1,0:T(8,128)(2,1)}, u32[]{:S(2)}, u32[]{:S(2)}) collective-permute-start(bf16[256,1024]{1,0:T(8,128)(2,1)S(1)} %collective-permute-done.15.refs_3_), channel_id=1, source_target_pairs={{0,4},{4,8},{8,12},{12,28},{28,24},{24,20},{20,16},{16,0},{1,5},{5... | collective-permute-start | bytes 1572872 | tf_op jit(solution)/shard_map/ppermute | solution.py:324
  135.2 12.1 %copy-start.11 = (bf16[256,1024]{1,0:T(8,128)(2,1)}, bf16[256,1024]{1,0:T(8,128)(2,1)S(1)}, u32[]{:S(2)}) copy-start(bf16[256,1024]{1,0:T(8,128)(2,1)S(1)} %collective-permute-done.20.refs_4_) | copy-start | bytes 1572868
  135.2 13.1 %collective-permute-start.21 = (bf16[256,1024]{1,0:T(8,128)(2,1)S(1)}, bf16[256,1024]{1,0:T(8,128)(2,1)}, u32[]{:S(2)}, u32[]{:S(2)}) collective-permute-start(bf16[256,1024]{1,0:T(8,128)(2,1)S(1)} %collective-permute-done.20.refs_4_), channel_id=1, source_target_pairs={{0,16},{4,0},{8,4},{12,8},{28,12},{24,28},{20,24},{16,20},{1,17},{... | collective-permute-start | bytes 1572872 | tf_op jit(solution)/shard_map/ppermute | solution.py:324
  147.3 1.0 copy-start.6
  148.3 10.8 %copy-start.1 = (bf16[8,2048,64]{1,2,0:T(8,128)(2,1)S(1)}, bf16[8,2048,64]{1,2,0:T(8,128)(2,1)}, u32[]{:S(2)}) copy-start(bf16[8,2048,64]{1,2,0:T(8,128)(2,1)} %param.12) | copy-start | bytes 6291460

commit v10 on v8

--- a/solution.py
+++ b/solution.py
@@ -173,7 +173,7 @@
     sizes = [len(group) for group in groups]
     ups = [part for group in groups for part in group]
     positions = key_values[0].shape[1] // rows
-    bundle = 32
+    bundle = 64
     sub = 4 if 4 * positions % 16 == 0 and heads % 2 == 0 else 16
     slab = max(sub, 8)
     pack = slab // sub

time: 156 us -> 154 us (0.987)
  transfers between devices with their start and end apart: 23 -> 23, of which waited for: 12 -> 12; matrix products, arithmetic and copies ran while one was open for 13% -> 13% of each run, Pallas kernels for 29% -> 30%
where the time goes in v10:
time: 154 us
  Pallas kernels  55.1 us (36%)
  waiting for transfers between devices  52.7 us (34%)
  starting transfers between devices  22.7 us (15%)
  local copies, waits for them, and re-layouts  19.5 us (13%)
  other arithmetic  3.65 us (2%)
    ppermute x15, waiting for transfers between devices, ring_hop(): return lax.ppermute(array, ('rep', 'dp'), pairs)  48.5 us
    pallas_call x2, Pallas kernels, project_pair(): pl.pallas_call(kernel, out_shape=jax.ShapeDtypeStruct((rows, columns), jn...  22.9 us
    ppermute x15, starting transfers between devices, ring_hop(): return lax.ppermute(array, ('rep', 'dp'), pairs)  15.7 us
    pallas_call x2, Pallas kernels, add_ranks(): pl.pallas_call(kernel, out_shape=jax.ShapeDtypeStruct((rows, out_width),...  14.3 us
    pallas_call x1, Pallas kernels, attend(): pl.pallas_call(kernel, out_shape=jax.ShapeDtypeStruct((steps, rows, width...  9.25 us
    unnamed x33, local copies, waits for them, and re-layouts  8.34 us
    ppermute x8, starting transfers between devices, swap(): return lax.ppermute(array, 'tensor', [(i, i ^ bit) for i in range(count)])  7.01 us
    pallas_call x1, Pallas kernels, early_query(): pl.pallas_call(kernel, out_shape=jax.ShapeDtypeStruct((rows, columns), jn...  6.39 us
  transfers between devices with their start and end apart: 23, of which 12 were waited for; matrix products, arithmetic and copies ran while one was open for 13% of the time, Pallas kernels for 30%

profile of v10, /device:TPU:0, one launch (start us, length us, event | category | flops | bytes accessed | tf_op | source)
XLA Modules:
  0.0 153.9 jit_solution(12569419473234758108)
XLA Ops:
  0.5 1.1 copy-done
  1.7 3.1 %collective-permute-start.1 = (bf16[256,2048]{1,0:T(8,128)(2,1)S(1)}, bf16[256,2048]{1,0:T(8,128)(2,1)}, u32[]{:S(2)}, u32[]{:S(2)}) collective-permute-start(bf16[256,2048]{1,0:T(8,128)(2,1)S(1)} %constant_dynamic-slice_fusion.3.refs_0_), channel_id=1, source_target_pairs={{0,4},{4,8},{8,12},{12,28},{28,24},{24,20},{20,16},{16,0},{1,5},{5... | collective-permute-start | bytes 3145736 | tf_op jit(solution)/shard_map/ppermute | solution.py:324
  4.8 1.9 %collective-permute-start = (bf16[576,2048]{1,0:T(8,128)(2,1)}, bf16[576,2048]{1,0:T(8,128)(2,1)S(1)}, u32[]{:S(2)}, u32[]{:S(2)}) collective-permute-start(bf16[576,2048]{1,0:T(8,128)(2,1)} %bitcast.42), channel_id=1, source_target_pairs={{0,2},{1,3},{2,0},{3,1},{4,6},{5,7},{6,4},{7,5},{8,10},{9,11},{10,... | collective-permute-start | bytes 7077896 | tf_op jit(solution)/shard_map/ppermute | solution.py:13
  6.7 3.5 %copy_dynamic-update-slice_fusion.1 = bf16[4,2,2304,128]{3,2,1,0:T(8,128)(2,1)} fusion(bf16[4,1,2304,128]{3,0,2,1:T(4,128)(2,1)} %bitcast.39), kind=kLoop, calls=%fused_computation.1 | loop fusion | bytes 4718592
  10.2 1.7 %copy_dynamic-update-slice_fusion = bf16[4,2,2304,128]{3,2,1,0:T(8,128)(2,1)} fusion(bf16[4,2,2304,128]{3,2,1,0:T(8,128)(2,1)} %copy_dynamic-update-slice_fusion.1, bf16[4,1,2304,128]{3,0,2,1:T(4,128)(2,1)S(1)} %bitcast.40), kind=kLoop, calls=%fused_computation | loop fusion | bytes 4718592 | tf_op jit(solution)/shard_map/stack | solution.py:411
  11.9 4.6 %dynamic-slice_bitcast_fusion = (bf16[2,2304,128]{2,1,0:T(8,128)(2,1)}, bf16[2,2304,128]{2,1,0:T(8,128)(2,1)}, bf16[2,2304,128]{2,1,0:T(8,128)(2,1)}, bf16[2,2304,128]{2,1,0:T(8,128)(2,1)}) fusion(bf16[4,2,2304,128]{3,2,1,0:T(8,128)(2,1)} %copy_dynamic-update-slice_fusion, s32[]{:T(128)S(6)} %select_n.67, s32[]{:T(128)S(6)} %select_n.66, s32[]{:T(128)S(6)} %select_n.65, ...), kind=kLoop, calls=%fused_computation.2 | loop fusion | bytes 9437200 | tf_op jit(solution)/shard_map/jit(dynamic_index_in_dim)/squeeze | solution.py:420
  16.5 0.6 pad_add_fusion.1.ids_ref
  17.2 10.9 %project.2.refs_4_ = f32[576,1024]{1,0:T(8,128)} custom-call(s32[2]{0:T(128)} %pad_add_fusion.1.ids_ref, bf16[576,2048]{1,0:T(8,128)(2,1)} %bitcast.43, bf16[576,2048]{1,0:T(8,128)(2,1)} %collective-permute-done.3.refs_1_, bf16[8192,1024]{1,0:T(8,128)(2,1)} %refs_3_.3, bf16[8192,1024]{1,0:T(8,128)(2,1)} %refs_3_.3), custom_call_target="tpu_custom_call" | custom-call | flops 4831838208 | bytes 15466496 | tf_op jit(solution)/shard_map/project/pallas_call | solution.py:54
  28.0 1.4 collective-permute-done.2.refs_2_
  29.5 1.6 %collective-permute-start.4 = (bf16[256,2048]{1,0:T(8,128)(2,1)}, bf16[256,2048]{1,0:T(8,128)(2,1)}, u32[]{:S(2)}, u32[]{:S(2)}) collective-permute-start(bf16[256,2048]{1,0:T(8,128)(2,1)} %collective-permute-done.1.refs_1_), channel_id=1, source_target_pairs={{0,4},{4,8},{8,12},{12,28},{28,24},{24,20},{20,16},{16,0},{1,5},{5... | collective-permute-start | bytes 3145736 | tf_op jit(solution)/shard_map/ppermute | solution.py:324
  31.5 22.0 %collective-permute-done.4.refs_3_ = bf16[256,2048]{1,0:T(8,128)(2,1)} collective-permute-done((bf16[256,2048]{1,0:T(8,128)(2,1)}, bf16[256,2048]{1,0:T(8,128)(2,1)}, u32[]{:S(2)}, u32[]{:S(2)}) %collective-permute-start.4) | collective-permute-done | bytes 1048608 | tf_op jit(solution)/shard_map/ppermute | solution.py:324
  53.5 1.3 collective-permute-done.5.refs_4_
  54.8 1.6 %collective-permute-start.7 = (bf16[256,2048]{1,0:T(8,128)(2,1)}, bf16[256,2048]{1,0:T(8,128)(2,1)S(1)}, u32[]{:S(2)}, u32[]{:S(2)}) collective-permute-start(bf16[256,2048]{1,0:T(8,128)(2,1)} %collective-permute-done.4.refs_3_), channel_id=1, source_target_pairs={{0,4},{4,8},{8,12},{12,28},{28,24},{24,20},{20,16},{16,0},{1,5},{5... | collective-permute-start | bytes 3145736 | tf_op jit(solution)/shard_map/ppermute | solution.py:324
  56.8 0.9 collective-permute-done.refs_0_
  57.7 1.7 %collective-permute-start.17 = (bf16[2,2304,128]{2,1,0:T(8,128)(2,1)}, bf16[2,2304,128]{2,1,0:T(8,128)(2,1)}, u32[]{:S(2)}, u32[]{:S(2)}) collective-permute-start(bf16[2,2304,128]{2,1,0:T(8,128)(2,1)} %get-tuple-element.41), channel_id=1, source_target_pairs={{0,2},{1,3},{2,0},{3,1},{4,6},{5,7},{6,4},{7,5},{8,10},{9,11},{10,... | collective-permute-start | bytes 3538952 | tf_op jit(solution)/shard_map/ppermute | solution.py:13
  59.3 0.9 reshape_tile.4.adapter_ref.refs_2_
  60.8 8.0 %rank.2.refs_4_ = f32[576,256]{1,0:T(8,128)} custom-call(s32[5]{0:T(128)} %stack.61.starts_ref, bf16[576,2048]{1,0:T(8,128)(2,1)} %bitcast.44, s32[576,1]{1,0:T(8,128)} %reshape_tile.4.adapter_ref.refs_2_, bf16[256,2048]{1,0:T(8,128)(2,1)} %copy-done.5, bf16[256,2048]{1,0:T(8,128)(2,1)} %collective-permute-done.1.refs_1_, ...), custom_call_target="tpu_custom_call" | custom-call | flops 3019898880 | bytes 7602176 | tf_op jit(solution)/shard_map/rank/pallas_call | solution.py:101
  68.9 8.7 %collective-permute-done.7.before_ref.refs_0_ = bf16[256,2048]{1,0:T(8,128)(2,1)S(1)} collective-permute-done((bf16[256,2048]{1,0:T(8,128)(2,1)}, bf16[256,2048]{1,0:T(8,128)(2,1)S(1)}, u32[]{:S(2)}, u32[]{:S(2)}) %collective-permute-start.7) | collective-permute-done | bytes 1048608 | tf_op jit(solution)/shard_map/ppermute | solution.py:324
  77.5 1.4 collective-permute-done.8.after_ref.refs_1_
  78.9 2.2 %split.1 = (bf16[192,2048]{1,0:T(8,128)(2,1)}, bf16[64,2048]{1,0:T(8,128)(2,1)}) custom-call(bf16[256,2048]{1,0:T(8,128)(2,1)} %copy-done.6, bf16[256,2048]{1,0:T(8,128)(2,1)} %collective-permute-done.8.after_ref.refs_1_), custom_call_target="tpu_custom_call" | custom-call | bytes 2097152 | tf_op jit(solution)/shard_map/split/pallas_call | solution.py:343
  81.1 1.5 collective-permute-start.9
  83.7 2.7 %collective-permute-done.17.refs_9_ = bf16[2,2304,128]{2,1,0:T(8,128)(2,1)} collective-permute-done((bf16[2,2304,128]{2,1,0:T(8,128)(2,1)}, bf16[2,2304,128]{2,1,0:T(8,128)(2,1)}, u32[]{:S(2)}, u32[]{:S(2)}) %collective-permute-start.17) | collective-permute-done | bytes 1179680 | tf_op jit(solution)/shard_map/ppermute | solution.py:13
  86.4 1.0 collective-permute-start.18
  87.4 8.0 %collective-permute-done.14.refs_2_ = bf16[256,1024]{1,0:T(8,128)(2,1)S(1)} collective-permute-done((bf16[256,1024]{1,0:T(8,128)(2,1)S(1)}, bf16[256,1024]{1,0:T(8,128)(2,1)S(1)}, u32[]{:S(2)}, u32[]{:S(2)}) %collective-permute-start.14) | collective-permute-done | bytes 524320 | tf_op jit(solution)/shard_map/ppermute | solution.py:324
  95.4 1.5 collective-permute-start.13
  96.9 2.6 %collective-permute-done.10.refs_3_ = bf16[64,2048]{1,0:T(8,128)(2,1)S(1)} collective-permute-done((bf16[64,2048]{1,0:T(8,128)(2,1)}, bf16[64,2048]{1,0:T(8,128)(2,1)S(1)}, u32[]{:S(2)}, u32[]{:S(2)}) %collective-permute-start.10) | collective-permute-done | bytes 262176 | tf_op jit(solution)/shard_map/ppermute | solution.py:324
  99.5 0.7 copy-done.14
  100.2 1.7 %collective-permute-done.9.refs_2_ = bf16[192,2048]{1,0:T(8,128)(2,1)} collective-permute-done((bf16[192,2048]{1,0:T(8,128)(2,1)}, bf16[192,2048]{1,0:T(8,128)(2,1)}, u32[]{:S(2)}, u32[]{:S(2)}) %collective-permute-start.9) | collective-permute-done | bytes 786464 | tf_op jit(solution)/shard_map/ppermute | solution.py:324
  102.4 0.7 pad_add_fusion.2.starts_ref
  103.1 6.3 %rank.3 = f32[576,64]{1,0:T(8,128)} custom-call(s32[3]{0:T(128)} %pad_add_fusion.2.starts_ref, bf16[576,2048]{1,0:T(8,128)(2,1)} %bitcast.45, s32[576,1]{1,0:T(8,128)} %reshape_tile.4.adapter_ref.refs_2_, bf16[256,2048]{1,0:T(8,128)(2,1)} %copy-done.6, bf16[256,2048]{1,0:T(8,128)(2,1)} %collective-permute-done.8.after_ref.refs_1_, ...), custom_call_target="tpu_custom_call" | custom-call | flops 1811939328 | bytes 5505024 | tf_op jit(solution)/shard_map/rank/pallas_call | solution.py:101
  109.9 1.4 collective-permute-done.16.refs_4_
  111.2 1.5 collective-permute-start.15
  113.3 0.6 pad_add_fusion.ids_ref
  113.8 1.0 add.119
  114.9 12.1 %project.3.base_ref = f32[576,1024]{1,0:T(8,128)} custom-call(s32[2]{0:T(128)} %pad_add_fusion.ids_ref, bf16[576,2048]{1,0:T(8,128)(2,1)} %copy-done.2, bf16[576,2048]{1,0:T(8,128)(2,1)} %collective-permute-done.6.refs_1_, bf16[8192,1024]{1,0:T(8,128)(2,1)} %refs_3_.3, bf16[8192,1024]{1,0:T(8,128)(2,1)} %refs_3_.3, f32[576,1024]{1,0:T(8,128)} %project.2.refs_4_), custom_call_target="tpu_custom_call" | custom-call | flops 4831838208 | bytes 15466496 | tf_op jit(solution)/shard_map/project/pallas_call | solution.py:54
  127.0 1.6 %collective-permute-start.19 = (bf16[256,1024]{1,0:T(8,128)(2,1)S(1)}, bf16[256,1024]{1,0:T(8,128)(2,1)S(1)}, u32[]{:S(2)}, u32[]{:S(2)}) collective-permute-start(bf16[256,1024]{1,0:T(8,128)(2,1)S(1)} %collective-permute-done.15.refs_3_), channel_id=1, source_target_pairs={{0,4},{4,8},{8,12},{12,28},{28,24},{24,20},{20,16},{16,0},{1,5},{5... | collective-permute-start | bytes 1572872 | tf_op jit(solution)/shard_map/ppermute | solution.py:324
  129.0 1.5 collective-permute-start.12
  130.5 0.7 concatenate.9.scalars_ref
  131.2 1.9 %constant_dynamic-slice_fusion = (bf16[3,192,1,128]{3,2,1,0:T(2,128)(2,1)S(1)}, bf16[3,192,1,128]{3,2,1,0:T(2,128)(2,1)S(1)}) fusion(bf16[3,192,4,128]{3,2,1,0:T(4,128)(2,1)} %param.17, s32[]{:T(128)S(6)} %select_n.69, bf16[3,192,4,128]{3,2,1,0:T(4,128)(2,1)} %param.16), kind=kLoop, calls=%fused_computation.8 | loop fusion | bytes 589828 | tf_op jit(solution)/shard_map/jit(dynamic_index_in_dim)/dynamic_slice | solution.py:477
  133.0 0.7 copy.28
  133.7 0.7 copy.29
  134.4 0.8 copy.21.refs_6_
  135.2 0.6 collective-permute-done.12
  135.8 0.7 add.120.rank_ref.refs_1_
  136.5 6.4 %delta.1.refs_0_ = f32[576,1024]{1,0:T(8,128)} custom-call(s32[5]{0:T(128)} %stack.61.starts_ref, f32[576,1024]{1,0:T(8,128)} %project.3.base_ref, f32[576,64]{1,0:T(8,128)} %add.120.rank_ref.refs_1_, s32[576,1]{1,0:T(8,128)} %reshape_tile.4.adapter_ref.refs_2_, bf16[256,1024]{1,0:T(8,128)(2,1)} %copy-done.4, ...), custom_call_target="tpu_custom_call" | custom-call | flops 1509949440 | bytes 7340032 | tf_op jit(solution)/shard_map/delta/pallas_call | solution.py:147
  142.9 0.8 copy-done.9
  143.7 0.8 copy-done.10
  144.5 9.2 %attend.1 = bf16[3,192,1024]{2,1,0:T(8,128)(2,1)} custom-call(s32[7]{0:T(128)} %concatenate.9.scalars_ref, f32[576,1024]{1,0:T(8,128)} %delta.1.refs_0_, f32[576,64]{1,0:T(8,128)} %add.120.rank_ref.refs_1_, s32[576,1]{1,0:T(8,128)} %reshape_tile.4.adapter_ref.refs_2_, bf16[256,1024]{1,0:T(8,128)(2,1)} %copy-done.9, ...), custom_call_target="tpu_custom_call" | custom-call | flops 481296384 | bytes 7077888 | tf_op jit(solution)/shard_map/attend/pallas_call | solution.py:297
  (53 shorter events, 5.1 us)
Async XLA Ops:
  0.0 1.6 %copy-start = (bf16[8,2048,64]{1,2,0:T(8,128)(2,1)S(1)}, bf16[8,2048,64]{1,2,0:T(8,128)(2,1)}, u32[]{:S(2)}) copy-start(bf16[8,2048,64]{1,2,0:T(8,128)(2,1)} %param.12) | copy-start | bytes 6291460
  0.0 17.2 %collective-permute-start.3 = (bf16[576,2048]{1,0:T(8,128)(2,1)}, bf16[576,2048]{1,0:T(8,128)(2,1)}, u32[]{:S(2)}, u32[]{:S(2)}) collective-permute-start(bf16[576,2048]{1,0:T(8,128)(2,1)} %bitcast.41), channel_id=1, source_target_pairs={{0,1},{1,0},{2,3},{3,2},{4,5},{5,4},{6,7},{7,6},{8,9},{9,8},{10,11... | collective-permute-start | bytes 7077896 | tf_op jit(solution)/shard_map/ppermute | solution.py:13
  1.7 8.6 %copy-start.5 = (bf16[256,2048]{1,0:T(8,128)(2,1)}, bf16[256,2048]{1,0:T(8,128)(2,1)S(1)}, u32[]{:S(2)}) copy-start(bf16[256,2048]{1,0:T(8,128)(2,1)S(1)} %constant_dynamic-slice_fusion.3.refs_0_) | copy-start | bytes 3145732
  1.7 26.4 %collective-permute-start.1 = (bf16[256,2048]{1,0:T(8,128)(2,1)S(1)}, bf16[256,2048]{1,0:T(8,128)(2,1)}, u32[]{:S(2)}, u32[]{:S(2)}) collective-permute-start(bf16[256,2048]{1,0:T(8,128)(2,1)S(1)} %constant_dynamic-slice_fusion.3.refs_0_), channel_id=1, source_target_pairs={{0,4},{4,8},{8,12},{12,28},{28,24},{24,20},{20,16},{16,0},{1,5},{5... | collective-permute-start | bytes 3145736 | tf_op jit(solution)/shard_map/ppermute | solution.py:324
  4.8 24.7 %collective-permute-start.2 = (bf16[256,2048]{1,0:T(8,128)(2,1)S(1)}, bf16[256,2048]{1,0:T(8,128)(2,1)}, u32[]{:S(2)}, u32[]{:S(2)}) collective-permute-start(bf16[256,2048]{1,0:T(8,128)(2,1)S(1)} %constant_dynamic-slice_fusion.3.refs_0_), channel_id=1, source_target_pairs={{0,16},{4,0},{8,4},{12,8},{28,12},{24,28},{20,24},{16,20},{1,17},{... | collective-permute-start | bytes 3145736 | tf_op jit(solution)/shard_map/ppermute | solution.py:324
  4.8 52.9 %collective-permute-start = (bf16[576,2048]{1,0:T(8,128)(2,1)}, bf16[576,2048]{1,0:T(8,128)(2,1)S(1)}, u32[]{:S(2)}, u32[]{:S(2)}) collective-permute-start(bf16[576,2048]{1,0:T(8,128)(2,1)} %bitcast.42), channel_id=1, source_target_pairs={{0,2},{1,3},{2,0},{3,1},{4,6},{5,7},{6,4},{7,5},{8,10},{9,11},{10,... | collective-permute-start | bytes 7077896 | tf_op jit(solution)/shard_map/ppermute | solution.py:13
  6.7 3.5 %copy-start.3 = (bf16[192,4,12,128]{3,1,2,0:T(4,128)(2,1)S(1)}, bf16[192,4,12,128]{3,1,2,0:T(4,128)(2,1)}, u32[]{:S(2)}) copy-start(bf16[192,4,12,128]{3,1,2,0:T(4,128)(2,1)} %param.15) | copy-start | bytes 7077892
  17.2 42.2 %copy-start.13 = (s32[192]{0:T(256)S(1)}, s32[192]{0:T(256)}, u32[]{:S(2)}) copy-start(s32[192]{0:T(256)} %param.19) | copy-start | bytes 2308
  29.5 24.0 %collective-permute-start.4 = (bf16[256,2048]{1,0:T(8,128)(2,1)}, bf16[256,2048]{1,0:T(8,128)(2,1)}, u32[]{:S(2)}, u32[]{:S(2)}) collective-permute-start(bf16[256,2048]{1,0:T(8,128)(2,1)} %collective-permute-done.1.refs_1_), channel_id=1, source_target_pairs={{0,4},{4,8},{8,12},{12,28},{28,24},{24,20},{20,16},{16,0},{1,5},{5... | collective-permute-start | bytes 3145736 | tf_op jit(solution)/shard_map/ppermute | solution.py:324
  31.1 23.7 %collective-permute-start.5 = (bf16[256,2048]{1,0:T(8,128)(2,1)}, bf16[256,2048]{1,0:T(8,128)(2,1)}, u32[]{:S(2)}, u32[]{:S(2)}) collective-permute-start(bf16[256,2048]{1,0:T(8,128)(2,1)} %collective-permute-done.2.refs_2_), channel_id=1, source_target_pairs={{0,16},{4,0},{8,4},{12,8},{28,12},{24,28},{20,24},{16,20},{1,17},{... | collective-permute-start | bytes 3145736 | tf_op jit(solution)/shard_map/ppermute | solution.py:324
  54.8 22.7 %collective-permute-start.7 = (bf16[256,2048]{1,0:T(8,128)(2,1)}, bf16[256,2048]{1,0:T(8,128)(2,1)S(1)}, u32[]{:S(2)}, u32[]{:S(2)}) collective-permute-start(bf16[256,2048]{1,0:T(8,128)(2,1)} %collective-permute-done.4.refs_3_), channel_id=1, source_target_pairs={{0,4},{4,8},{8,12},{12,28},{28,24},{24,20},{20,16},{16,0},{1,5},{5... | collective-permute-start | bytes 3145736 | tf_op jit(solution)/shard_map/ppermute | solution.py:324
  56.4 22.5 %collective-permute-start.8 = (bf16[256,2048]{1,0:T(8,128)(2,1)}, bf16[256,2048]{1,0:T(8,128)(2,1)}, u32[]{:S(2)}, u32[]{:S(2)}) collective-permute-start(bf16[256,2048]{1,0:T(8,128)(2,1)} %collective-permute-done.5.refs_4_), channel_id=1, source_target_pairs={{0,16},{4,0},{8,4},{12,8},{28,12},{24,28},{20,24},{16,20},{1,17},{... | collective-permute-start | bytes 3145736 | tf_op jit(solution)/shard_map/ppermute | solution.py:324
  57.7 11.2 %copy-start.2 = (bf16[576,2048]{1,0:T(8,128)(2,1)}, bf16[576,2048]{1,0:T(8,128)(2,1)S(1)}, u32[]{:S(2)}) copy-start(bf16[576,2048]{1,0:T(8,128)(2,1)S(1)} %collective-permute-done.refs_0_) | copy-start | bytes 7077892
  57.7 57.2 %collective-permute-start.6 = (bf16[576,2048]{1,0:T(8,128)(2,1)S(1)}, bf16[576,2048]{1,0:T(8,128)(2,1)}, u32[]{:S(2)}, u32[]{:S(2)}) collective-permute-start(bf16[576,2048]{1,0:T(8,128)(2,1)S(1)} %collective-permute-done.refs_0_), channel_id=1, source_target_pairs={{0,1},{1,0},{2,3},{3,2},{4,5},{5,4},{6,7},{7,6},{8,9},{9,8},{10,11... | collective-permute-start | bytes 7077896 | tf_op jit(solution)/shard_map/ppermute | solution.py:13
  57.7 28.7 %collective-permute-start.17 = (bf16[2,2304,128]{2,1,0:T(8,128)(2,1)}, bf16[2,2304,128]{2,1,0:T(8,128)(2,1)}, u32[]{:S(2)}, u32[]{:S(2)}) collective-permute-start(bf16[2,2304,128]{2,1,0:T(8,128)(2,1)} %get-tuple-element.41), channel_id=1, source_target_pairs={{0,2},{1,3},{2,0},{3,1},{4,6},{5,7},{6,4},{7,5},{8,10},{9,11},{10,... | collective-permute-start | bytes 3538952 | tf_op jit(solution)/shard_map/ppermute | solution.py:13
  68.8 13.8 %copy-start.11 = (bf16[8,64,1024]{2,1,0:T(8,128)(2,1)S(1)}, bf16[8,64,1024]{2,1,0:T(8,128)(2,1)}, u32[]{:S(2)}) copy-start(bf16[8,64,1024]{2,1,0:T(8,128)(2,1)} %param.13) | copy-start | bytes 3145732
  77.5 1.4 copy-start.6
  81.1 20.8 %collective-permute-start.9 = (bf16[192,2048]{1,0:T(8,128)(2,1)}, bf16[192,2048]{1,0:T(8,128)(2,1)}, u32[]{:S(2)}, u32[]{:S(2)}) collective-permute-start(bf16[192,2048]{1,0:T(8,128)(2,1)} %get-tuple-element.36), channel_id=1, source_target_pairs={{0,4},{4,8},{8,12},{12,28},{28,24},{24,20},{20,16},{16,0},{1,5},{5... | collective-permute-start | bytes 2359304 | tf_op jit(solution)/shard_map/ppermute | solution.py:324
  82.7 26.6 %copy-start.4 = (bf16[256,1024]{1,0:T(8,128)(2,1)}, bf16[256,1024]{1,0:T(8,128)(2,1)S(1)}, u32[]{:S(2)}) copy-start(bf16[256,1024]{1,0:T(8,128)(2,1)S(1)} %constant_dynamic-slice_fusion.2.refs_0_) | copy-start | bytes 1572868
  82.7 12.7 %collective-permute-start.14 = (bf16[256,1024]{1,0:T(8,128)(2,1)S(1)}, bf16[256,1024]{1,0:T(8,128)(2,1)S(1)}, u32[]{:S(2)}, u32[]{:S(2)}) collective-permute-start(bf16[256,1024]{1,0:T(8,128)(2,1)S(1)} %constant_dynamic-slice_fusion.2.refs_0_), channel_id=1, source_target_pairs={{0,16},{4,0},{8,4},{12,8},{28,12},{24,28},{20,24},{16,20},{1,17},{... | collective-permute-start | bytes 1572872 | tf_op jit(solution)/shard_map/ppermute | solution.py:324
  83.3 16.3 %collective-permute-start.10 = (bf16[64,2048]{1,0:T(8,128)(2,1)}, bf16[64,2048]{1,0:T(8,128)(2,1)S(1)}, u32[]{:S(2)}, u32[]{:S(2)}) collective-permute-start(bf16[64,2048]{1,0:T(8,128)(2,1)} %get-tuple-element.37), channel_id=1, source_target_pairs={{0,16},{4,0},{8,4},{12,8},{28,12},{24,28},{20,24},{16,20},{1,17},{... | collective-permute-start | bytes 786440 | tf_op jit(solution)/shard_map/ppermute | solution.py:324
  86.4 40.6 %collective-permute-start.18 = (bf16[2,2304,128]{2,1,0:T(8,128)(2,1)}, bf16[2,2304,128]{2,1,0:T(8,128)(2,1)}, u32[]{:S(2)}, u32[]{:S(2)}) collective-permute-start(bf16[2,2304,128]{2,1,0:T(8,128)(2,1)} %get-tuple-element.42), channel_id=1, source_target_pairs={{0,3},{1,2},{2,1},{3,0},{4,7},{5,6},{6,5},{7,4},{8,11},{9,10},{10,... | collective-permute-start | bytes 3538952 | tf_op jit(solution)/shard_map/ppermute | solution.py:13
  95.4 14.0 %copy-start.7 = (bf16[256,1024]{1,0:T(8,128)(2,1)}, bf16[256,1024]{1,0:T(8,128)(2,1)S(1)}, u32[]{:S(2)}) copy-start(bf16[256,1024]{1,0:T(8,128)(2,1)S(1)} %collective-permute-done.14.refs_2_) | copy-start | bytes 1572868
  95.4 14.0 %collective-permute-start.13 = (bf16[256,1024]{1,0:T(8,128)(2,1)S(1)}, bf16[256,1024]{1,0:T(8,128)(2,1)}, u32[]{:S(2)}, u32[]{:S(2)}) collective-permute-start(bf16[256,1024]{1,0:T(8,128)(2,1)S(1)} %constant_dynamic-slice_fusion.2.refs_0_), channel_id=1, source_target_pairs={{0,4},{4,8},{8,12},{12,28},{28,24},{24,20},{20,16},{16,0},{1,5},{5... | collective-permute-start | bytes 1572872 | tf_op jit(solution)/shard_map/ppermute | solution.py:324
  99.5 0.7 copy-start.14
  101.9 9.3 %collective-permute-start.16 = (bf16[256,1024]{1,0:T(8,128)(2,1)S(1)}, bf16[256,1024]{1,0:T(8,128)(2,1)}, u32[]{:S(2)}, u32[]{:S(2)}) collective-permute-start(bf16[256,1024]{1,0:T(8,128)(2,1)S(1)} %collective-permute-done.14.refs_2_), channel_id=1, source_target_pairs={{0,16},{4,0},{8,4},{12,8},{28,12},{24,28},{20,24},{16,20},{1,17},{... | collective-permute-start | bytes 1572872 | tf_op jit(solution)/shard_map/ppermute | solution.py:324
  109.3 3.4 %collective-permute-start.11 = (f32[576,64]{1,0:T(8,128)}, f32[576,64]{1,0:T(8,128)S(1)}, u32[]{:S(2)}, u32[]{:S(2)}) collective-permute-start(f32[576,64]{1,0:T(8,128)} %rank.3), channel_id=1, source_target_pairs={{0,1},{1,0},{2,3},{3,2},{4,5},{5,4},{6,7},{7,6},{8,9},{9,8},{10,11... | collective-permute-start | bytes 442376 | tf_op jit(solution)/shard_map/ppermute | solution.py:13
  109.4 33.5 %collective-permute-start.22 = (bf16[2,2304,128]{2,1,0:T(8,128)(2,1)}, bf16[2,2304,128]{2,1,0:T(8,128)(2,1)}, u32[]{:S(2)}, u32[]{:S(2)}) collective-permute-start(bf16[2,2304,128]{2,1,0:T(8,128)(2,1)} %get-tuple-element.44), channel_id=1, source_target_pairs={{0,1},{1,0},{2,3},{3,2},{4,5},{5,4},{6,7},{7,6},{8,9},{9,8},{10,11... | collective-permute-start | bytes 3538952 | tf_op jit(solution)/shard_map/ppermute | solution.py:13
  111.2 15.7 %collective-permute-start.15 = (bf16[256,1024]{1,0:T(8,128)(2,1)}, bf16[256,1024]{1,0:T(8,128)(2,1)S(1)}, u32[]{:S(2)}, u32[]{:S(2)}) collective-permute-start(bf16[256,1024]{1,0:T(8,128)(2,1)} %collective-permute-done.13.refs_1_), channel_id=1, source_target_pairs={{0,4},{4,8},{8,12},{12,28},{28,24},{24,20},{20,16},{16,0},{1,5},{5... | collective-permute-start | bytes 1572872 | tf_op jit(solution)/shard_map/ppermute | solution.py:324
  112.7 15.8 %collective-permute-start.20 = (bf16[256,1024]{1,0:T(8,128)(2,1)}, bf16[256,1024]{1,0:T(8,128)(2,1)}, u32[]{:S(2)}, u32[]{:S(2)}) collective-permute-start(bf16[256,1024]{1,0:T(8,128)(2,1)} %collective-permute-done.16.refs_4_), channel_id=1, source_target_pairs={{0,16},{4,0},{8,4},{12,8},{28,12},{24,28},{20,24},{16,20},{1,17},{... | collective-permute-start | bytes 1572872 | tf_op jit(solution)/shard_map/ppermute | solution.py:324
  114.9 19.5 %copy-start.12 = (s32[192]{0:T(256)S(1)}, s32[192]{0:T(256)}, u32[]{:S(2)}) copy-start(s32[192]{0:T(256)} %param.18) | copy-start | bytes 2308
  126.9 9.6 %copy-start.8 = (bf16[256,1024]{1,0:T(8,128)(2,1)}, bf16[256,1024]{1,0:T(8,128)(2,1)S(1)}, u32[]{:S(2)}) copy-start(bf16[256,1024]{1,0:T(8,128)(2,1)S(1)} %collective-permute-done.15.refs_3_) | copy-start | bytes 1572868
  127.0 16.0 %collective-permute-start.19 = (bf16[256,1024]{1,0:T(8,128)(2,1)S(1)}, bf16[256,1024]{1,0:T(8,128)(2,1)S(1)}, u32[]{:S(2)}, u32[]{:S(2)}) collective-permute-start(bf16[256,1024]{1,0:T(8,128)(2,1)S(1)} %collective-permute-done.15.refs_3_), channel_id=1, source_target_pairs={{0,4},{4,8},{8,12},{12,28},{28,24},{24,20},{20,16},{16,0},{1,5},{5... | collective-permute-start | bytes 1572872 | tf_op jit(solution)/shard_map/ppermute | solution.py:324
  128.5 15.2 %collective-permute-start.21 = (bf16[256,1024]{1,0:T(8,128)(2,1)}, bf16[256,1024]{1,0:T(8,128)(2,1)S(1)}, u32[]{:S(2)}, u32[]{:S(2)}) collective-permute-start(bf16[256,1024]{1,0:T(8,128)(2,1)} %collective-permute-done.20.refs_4_), channel_id=1, source_target_pairs={{0,16},{4,0},{8,4},{12,8},{28,12},{24,28},{20,24},{16,20},{1,17},{... | collective-permute-start | bytes 1572872 | tf_op jit(solution)/shard_map/ppermute | solution.py:324
  129.0 6.7 %collective-permute-start.12 = (f32[576,64]{1,0:T(8,128)S(1)}, f32[576,64]{1,0:T(8,128)S(1)}, u32[]{:S(2)}, u32[]{:S(2)}) collective-permute-start(f32[576,64]{1,0:T(8,128)S(1)} %add.119), channel_id=1, source_target_pairs={{0,2},{1,3},{2,0},{3,1},{4,6},{5,7},{6,4},{7,5},{8,10},{9,11},{10,... | collective-permute-start | bytes 442376 | tf_op jit(solution)/shard_map/ppermute | solution.py:13
  142.9 0.8 copy-start.9
  143.7 0.8 copy-start.10
  144.5 9.3 %copy-start.1 = (bf16[8,2048,64]{1,2,0:T(8,128)(2,1)S(1)}, bf16[8,2048,64]{1,2,0:T(8,128)(2,1)}, u32[]{:S(2)}) copy-start(bf16[8,2048,64]{1,2,0:T(8,128)(2,1)} %param.12) | copy-start | bytes 6291460
